TPU v7x, 32 devices: a whole 2x2x4 slice. The times are simulated.
32 devices in a mesh: dp: 8 (over z, y), tensor: 4 (over x, core).
Axes of the slice: x: 2, y: 2, z: 4, core: 2. Of those that a mesh axis runs over, the one named last changes fastest.
Arguments:
- patch_tokens: bfloat16 [64, 196, 768], P('dp', 'tensor'), may hold values from -6 to 6
- class_tokens: bfloat16 [24, 768], P('dp'), may hold values from -6 to 6
- frame_counts: int32 [8, 3], P('dp'), may hold values from 1 to 4, 8 in all within a row
- patch_cotangent: bfloat16 [64, 196, 768], P('dp', 'tensor'), may hold values from -6 to 6
- class_cotangent: bfloat16 [24, 768], P('dp'), may hold values from -6 to 6
- temporal_in: bfloat16 [2, 768, 2304], replicated, may hold values from -0.21875 to 0.21875
- temporal_out: bfloat16 [2, 768, 768], replicated, may hold values from -0.3125 to 0.3125
- temporal_mix: bfloat16 [2, 768, 768], replicated, may hold values from -0.21875 to 0.21875
- spatial_in: bfloat16 [2, 768, 2304], replicated, may hold values from -0.21875 to 0.21875
- spatial_out: bfloat16 [2, 768, 768], replicated, may hold values from -1.75 to 1.75
- hidden_up: bfloat16 [2, 768, 3072], P(None, None, 'tensor'), may hold values from -0.21875 to 0.21875
- hidden_down: bfloat16 [2, 3072, 768], P(None, 'tensor'), may hold values from -0.3125 to 0.3125
- norm_gain: float32 [2, 3, 768], replicated, may hold values from 0.5 to 1.5
- norm_shift: float32 [2, 3, 768], replicated, may hold values from -3 to 3
Outputs:
- patch_output: bfloat16 [64, 196, 768], P('dp', 'tensor')
- class_output: bfloat16 [24, 768], P('dp')
- patch_grad: float32 [64, 196, 768], P('dp', 'tensor')
- class_grad: float32 [24, 768], P('dp')
- grad_temporal_in: float32 [2, 768, 2304], P(None, 'dp')
- grad_temporal_out: float32 [2, 768, 768], P(None, 'dp')
- grad_temporal_mix: float32 [2, 768, 768], P(None, 'dp')
- grad_spatial_in: float32 [2, 768, 2304], P(None, 'dp')
- grad_spatial_out: float32 [2, 768, 768], P(None, 'dp')
- grad_hidden_up: float32 [2, 768, 3072], P(None, 'dp', 'tensor')
- grad_hidden_down: float32 [2, 3072, 768], P(None, 'tensor', 'dp')
- grad_norm_gain: float32 [2, 3, 768], P(None, None, 'dp')
- grad_norm_shift: float32 [2, 3, 768], P(None, None, 'dp')
Inputs may be any that keep to these rules, and one draw needn't show every extreme that they name: `frame_counts`: each row sums to 8, and in each row the longest clip has exactly 4 frames.
All inputs are finite; a program needn't handle non-finite values.
Results may differ from a plain program's by a relative error of at most 0.02.
Values may be sent and summed in bfloat16 or wider, within the bound.
No kernel may reach another device: no remote copies, remote signals or barrier semaphores. Data moves between devices by JAX's collectives and lax.ppermute only.
A program may use at most 320 MiB of HBM per device.

v0:
```python
from functools import partial

import jax
import jax.numpy as jnp
from jax import lax
from jax.experimental import pallas as pl
from jax.experimental.pallas import tpu as pltpu
from jax.sharding import PartitionSpec as P

HEADS = 12
EPS = 1e-06
HIGH = lax.Precision.HIGHEST
HALF = jnp.bfloat16
FULL = jnp.float32
NEAR = 4
TENSOR = "tensor"
DP = "dp"
TILE = 256
VMEM_BYTES = 56 << 20
SMEM = pl.BlockSpec(memory_space=pltpu.SMEM)
VMEM = pl.BlockSpec(memory_space=pltpu.VMEM)
ANY = pl.BlockSpec(memory_space=pl.ANY)
ROOT_HALF = 0.5**0.5
DENSITY = (2.0 * 3.141592653589793) ** -0.5


def up_to(value, step):
    return -(-value // step) * step


def dot(left, right):
    return jnp.dot(left, right, preferred_element_type=FULL)


def dot_back(left, right):
    return lax.dot_general(left, right, (((1,), (1,)), ((), ())), preferred_element_type=FULL)


def dot_outer(left, right):
    return lax.dot_general(left, right, (((0,), (0,)), ((), ())), preferred_element_type=FULL)


def unit_of(values):
    centred = values - jnp.mean(values, -1, keepdims=True)
    inverse = lax.rsqrt(jnp.mean(centred * centred, -1, keepdims=True) + EPS)
    return centred * inverse, inverse


def unit_back(grad, unit, inverse, gain):
    scaled = grad * gain
    inner = (
        scaled
        - jnp.mean(scaled, -1, keepdims=True)
        - unit * jnp.mean(scaled * unit, -1, keepdims=True)
    )
    return inner * inverse


def head_lanes(head_size, half):
    lane = lax.broadcasted_iota(jnp.int32, (1, 2 * head_size), 1)
    return (lane // head_size) == half


def row_chunk(rows):
    return next(step for step in (80, 104, 64, 48, 32, 16, 8) if rows % step == 0)


def over_rows(rows, step, run):
    def one(index, carry):
        run(pl.ds(pl.multiple_of(index * step, step), step))
        return carry

    lax.fori_loop(0, rows // step, one, 0)


def interleave(order, frame, frames, values):
    for group in range(order.shape[0]):
        part = values[:, group * 128 : (group + 1) * 128]
        order[group, pl.ds(frame, values.shape[0], stride=frames), :] = part


def pick(order, frame, frames, patches):
    own = pl.ds(frame, patches, stride=frames)
    return jnp.concatenate([order[group, own, :] for group in range(order.shape[0])], 1)


def shard_copies(place_ref, refs, target):
    own, core, far_first, far_second, core_first, core_second = refs
    half = far_first.shape[0]
    first = pl.multiple_of(place_ref[1] * half, half)
    second = pl.multiple_of((1 - place_ref[1]) * half, half)
    return [
        [(own, target.at[0])],
        [(core, target.at[1])],
        [
            (far_first, target.at[2, pl.ds(first, half)]),
            (far_second, target.at[2, pl.ds(second, half)]),
        ],
        [
            (core_first, target.at[3, pl.ds(first, half)]),
            (core_second, target.at[3, pl.ds(second, half)]),
        ],
    ]


def start_shards(place_ref, ups, downs, up_ref, down_ref, sems):
    waits = []
    index = 0
    for pairs in zip(
        shard_copies(place_ref, ups, up_ref), shard_copies(place_ref, downs, down_ref)
    ):
        group = []
        for source, target in pairs[0] + pairs[1]:
            copy = pltpu.make_async_copy(source, target, sems.at[index])
            copy.start()
            group.append(copy)
            index += 1
        waits.append(group)
    return waits


def fetch(sources, targets, sems):
    copies = [
        pltpu.make_async_copy(source, target, sems.at[index])
        for index, (source, target) in enumerate(zip(sources, targets))
    ]
    for copy in copies:
        copy.start()
    return copies


def attend_forward(load, store, store_total, heads, head_size, bias):
    scale = head_size**-0.5
    totals = None
    lanes = None
    for pair in range(heads // 2):
        query, key, value = (load(part, pair) for part in range(3))
        sides = []
        for half in range(2):
            mine = head_lanes(head_size, half)
            scores = dot_back(jnp.where(mine, query, 0), key) * scale + bias
            top = jnp.max(scores, -1, keepdims=True)
            raised = jnp.exp(scores - top)
            total = jnp.sum(raised, -1, keepdims=True)
            sides.append(dot(raised.astype(HALF), value) * (1.0 / total))
            log_total = top + jnp.log(total)
            if totals is None:
                lanes = lax.broadcasted_iota(jnp.int32, (query.shape[0], 128), 1)
                totals = jnp.zeros(lanes.shape, FULL)
            totals = jnp.where(lanes == pair * 2 + half, log_total, totals)
        store(pair, jnp.where(head_lanes(head_size, 0), sides[0], sides[1]))
    store_total(totals)


def attend_backward(load, load_grad, totals, store, heads, head_size, bias):
    scale = head_size**-0.5
    for pair in range(heads // 2):
        query, key, value = (load(part, pair) for part in range(3))
        grad = load_grad(pair)
        sides = []
        for half in range(2):
            mine = head_lanes(head_size, half)
            head = pair * 2 + half
            scores = dot_back(jnp.where(mine, query, 0), key) * scale + bias
            prob = jnp.exp(scores - totals[:, head : head + 1])
            grad_prob = dot_back(jnp.where(mine, grad, 0), value)
            delta = jnp.sum(prob * grad_prob, -1, keepdims=True)
            grad_score = (prob * (grad_prob - delta)).astype(HALF)
            sides.append(
                (
                    dot(grad_score, key) * scale,
                    dot_outer(grad_score, query) * scale,
                    dot_outer(prob.astype(HALF), grad),
                )
            )
        for part in range(3):
            first = head_lanes(head_size, 0)
            store(part, pair, jnp.where(first, sides[0][part], sides[1][part]))


def time_forward(dims, layer, place_ref, x_ref, bias_ref, gain_ref, shift_ref, in_hbm, out_hbm, mix_hbm,
                 normed_ref, triple_ref, total_ref, mixed_ref, projected_ref, after_ref,
                 send0, send1, send2, send3, class_ref,
                 in_ref, out_ref, mix_ref, order, plain, blocks, sems):
    frames, patches, width, heads, groups = dims
    count = frames * patches
    rows = x_ref.shape[0]
    step = bias_ref.shape[0]
    copies = fetch(
        (in_hbm.at[layer], out_hbm.at[layer], mix_hbm.at[layer]), (in_ref, out_ref, mix_ref), sems
    )
    gain = gain_ref[layer, 0:1, :]
    shift = shift_ref[layer, 0:1, :]
    for frame in range(frames):
        unit, unused = unit_of(x_ref[frame * patches : (frame + 1) * patches, :])
        interleave(order, frame, frames, unit * gain + shift)
    for group in range(width // 128):
        order[group, count:, :] = jnp.zeros((rows - count, 128), FULL)
        normed_ref[:, group * 128 : (group + 1) * 128] = order[group].astype(HALF)
    copies[0].wait()
    for column in range(0, 3 * width, TILE):
        part = slice(column, column + TILE)
        triple_ref[:, part] = dot(normed_ref[...], in_ref[:, part]).astype(HALF)

    def block(index, carry):
        own = pl.ds(pl.multiple_of(index * step, step), step)

        def load(part, pair):
            start = part * width + pair * 128
            return triple_ref[own, start : start + 128]

        def store(pair, mixed):
            order[pair, own, :] = mixed

        def store_total(totals):
            total_ref[own, :] = totals

        attend_forward(load, store, store_total, heads, width // heads, bias_ref[...])
        return carry

    lax.fori_loop(0, rows // step, block, 0)
    for frame in range(frames):
        plain[frame * patches : (frame + 1) * patches, :] = pick(order, frame, frames, patches)
    plain[count:, :] = jnp.zeros((rows - count, width), FULL)
    mixed_ref[...] = plain[...].astype(HALF)
    copies[1].wait()
    for column in range(0, width, TILE):
        part = slice(column, column + TILE)
        projected_ref[:, part] = dot(mixed_ref[...], out_ref[:, part]).astype(HALF)
    copies[2].wait()
    for column in range(0, width, TILE):
        part = slice(column, column + TILE)
        after_ref[:, part] = x_ref[:, part] + dot(projected_ref[...], mix_ref[:, part])
    gain = gain_ref[layer, 1:2, :]
    shift = shift_ref[layer, 1:2, :]

    def norm(own):
        unit, unused = unit_of(after_ref[own, :])
        plain[own, :] = unit * gain + shift

    over_rows(rows, row_chunk(rows), norm)
    send_blocks(plain, blocks, (send0, send1, send2, send3), place_ref[0], count // groups)
    class_ref[...] = plain[count:, :]


def send_blocks(plain, blocks, sends, place, size):
    groups = len(sends)
    for group in range(groups):
        blocks[group, 0:size, :] = plain[group * size : (group + 1) * size, :]
    for away in range(groups):
        sends[away][...] = blocks[place ^ away][0:size].astype(HALF)


def space_forward(dims, layer, place_ref, clip_ref, class_ref, piece0, piece1, piece2, piece3, in_hbm,
                  normed_ref, triple_ref, total_ref, send0, send1, send2, send3,
                  in_ref, plain, sems):
    frames, patches, width, heads, groups = dims
    own_frames = frames // groups
    seq = groups * patches
    rows = normed_ref.shape[0] // own_frames
    copies = fetch((in_hbm.at[layer],), (in_ref,), sems)
    pieces = [piece0, piece1, piece2, piece3]
    for away, piece in enumerate(pieces):
        values = piece[...].astype(FULL)
        for frame in range(own_frames):
            start = frame * rows + away * patches
            plain[start : start + patches, :] = values[frame * patches : (frame + 1) * patches]
    for frame in range(own_frames):
        start = frame * rows + seq
        plain[start : start + rows - seq, :] = jnp.zeros((rows - seq, width), FULL)
        clip = clip_ref[place_ref[0] * own_frames + frame]
        plain[start : start + 1, :] = class_ref[pl.ds(clip, 1), :]
    normed_ref[...] = plain[...].astype(HALF)
    copies[0].wait()
    for column in range(0, 3 * width, TILE):
        part = slice(column, column + TILE)
        triple_ref[:, part] = dot(normed_ref[...], in_ref[:, part]).astype(HALF)
    keys = lax.broadcasted_iota(jnp.int32, (1, rows), 1)
    bias = jnp.where(keys <= seq, 0.0, -1e30)

    def block(index, carry):
        own = pl.ds(pl.multiple_of(index * rows, rows), rows)

        def load(part, pair):
            start = part * width + pair * 128
            return triple_ref[own, start : start + 128]

        def store(pair, mixed):
            plain[own, pair * 128 : (pair + 1) * 128] = mixed

        def store_total(totals):
            total_ref[own, :] = totals

        attend_forward(load, store, store_total, heads, width // heads, bias)
        return carry

    lax.fori_loop(0, own_frames, block, 0)
    return_pieces(plain, (send0, send1, send2, send3), own_frames, patches, rows)


def return_pieces(plain, sends, own_frames, patches, rows):
    seq = len(sends) * patches
    tail = []
    for frame in range(own_frames):
        row = plain[frame * rows + seq : frame * rows + seq + 1, :]
        high = row.astype(HALF).astype(FULL)
        tail += [high, row - high]
    size = own_frames * patches
    spare = sends[0].shape[0] - size - len(tail)
    tail.append(jnp.zeros((spare, plain.shape[1]), FULL))
    for away, send in enumerate(sends):
        kept = [
            plain[frame * rows + away * patches : frame * rows + (away + 1) * patches, :]
            for frame in range(own_frames)
        ]
        send[...] = jnp.concatenate(kept + tail, 0).astype(HALF)


def take_pieces(pieces, blocks, plain, frame_rows, place, size, own_frames):
    for away, piece in enumerate(pieces):
        blocks[place ^ away] = piece[...].astype(FULL)
    for group in range(len(pieces)):
        plain[group * size : (group + 1) * size, :] = blocks[group, 0:size, :]
        for frame in range(own_frames):
            start = size + 2 * frame
            frame_rows[group * own_frames + frame : group * own_frames + frame + 1, :] = (
                blocks[group, start : start + 1, :] + blocks[group, start + 1 : start + 2, :]
            )


def feed_forward(dims, layer, place_ref, piece0, piece1, piece2, piece3, share_ref, after_ref,
                 gain_ref, shift_ref, out_hbm,
                 up0, up1, up2, up3, up4, up5, down0, down1, down2, down3, down4, down5,
                 mixed_ref, rows_ref, normed_ref, active_ref, slope_ref, next_ref,
                 out_ref, up_ref, down_ref, plain, blocks, frame_rows, whole, out_sem, sems):
    frames, patches, width, heads, groups = dims
    count = frames * patches
    rows = after_ref.shape[0]
    size = count // groups
    place = place_ref[0]
    copies = fetch((out_hbm.at[layer],), (out_ref,), out_sem)
    ups, downs = (up0, up1, up2, up3, up4, up5), (down0, down1, down2, down3, down4, down5)
    shards = start_shards(place_ref, ups, downs, up_ref, down_ref, sems)
    take_pieces(
        (piece0, piece1, piece2, piece3), blocks, plain, frame_rows, place, size, frames // groups
    )
    plain[count:, :] = jnp.dot(
        share_ref[...], frame_rows[...], precision=HIGH, preferred_element_type=FULL
    )
    whole[...] = plain[...].astype(HALF)
    leader = jnp.where(place == 0, 1.0, 0.0).astype(FULL)
    kept = lax.broadcasted_iota(jnp.int32, (rows, 1), 0) < count
    kept = jnp.where(kept, 1.0, leader)
    mixed_ref[...] = (plain[...] * kept).astype(HALF)
    copies[0].wait()
    for column in range(0, width, TILE):
        part = slice(column, column + TILE)
        rows_ref[:, part] = after_ref[:, part] + dot(whole[...], out_ref[:, part])
    gain = gain_ref[layer, 2:3, :]
    shift = shift_ref[layer, 2:3, :]

    def norm(own):
        unit, unused = unit_of(rows_ref[own, :])
        plain[own, :] = unit * gain + shift

    over_rows(rows, row_chunk(rows), norm)
    whole[...] = plain[...].astype(HALF)
    normed_ref[...] = (plain[...] * kept).astype(HALF)
    next_ref[...] = rows_ref[...]
    for away in range(groups):
        for copy in shards[away]:
            copy.wait()
        for column in range(0, width, TILE):
            part = slice(column, column + TILE)
            hidden = dot(whole[...], up_ref[away, :, part])
            below = 0.5 + 0.5 * lax.erf(hidden * ROOT_HALF)
            active = (hidden * below).astype(HALF)
            slope = below + hidden * (jnp.exp(hidden * hidden * -0.5) * DENSITY)
            start = away * width + column
            active_ref[:, start : start + TILE] = active
            slope_ref[:, start : start + TILE] = slope.astype(HALF)
            next_ref[...] += dot(active, down_ref[away, part, :])
    start = count // 16 * 16
    active_ref[start:, :] = (active_ref[start:, :].astype(FULL) * kept[start:]).astype(HALF)


def feed_backward(dims, layer, place_ref, clip_ref, grad_ref, slope_ref, rows_ref, share_ref, gain_ref,
                  out_hbm, up0, up1, up2, up3, up4, up5, down0, down1, down2, down3, down4, down5,
                  update_ref, hidden_ref, branch_ref, back_ref, norms_ref,
                  send0, send1, send2, send3, class_ref,
                  out_ref, up_ref, down_ref, total, plain, blocks, out_sem, sems):
    frames, patches, width, heads, groups = dims
    count = frames * patches
    rows = grad_ref.shape[0]
    place = place_ref[0]
    own_frames = frames // groups
    ups, downs = (up0, up1, up2, up3, up4, up5), (down0, down1, down2, down3, down4, down5)
    shards = start_shards(place_ref, ups, downs, up_ref, down_ref, sems)
    copies = fetch((out_hbm.at[layer],), (out_ref,), out_sem)
    update_ref[...] = grad_ref[...].astype(HALF)
    for away in range(groups):
        for copy in shards[away]:
            copy.wait()
        for column in range(0, width, TILE):
            part = slice(column, column + TILE)
            start = away * width + column
            grad_active = dot_back(update_ref[...], down_ref[away, part, :])
            slope = slope_ref[:, start : start + TILE].astype(FULL)
            grad_hidden = (grad_active * slope).astype(HALF)
            hidden_ref[:, start : start + TILE] = grad_hidden
            term = dot_back(grad_hidden, up_ref[away, :, part])
            if start == 0:
                total[...] = term
            else:
                total[...] += term
    gain = gain_ref[layer, 2:3, :]
    leader = jnp.where(place == 0, 1.0, 0.0).astype(FULL)
    norms_ref[...] = jnp.zeros(norms_ref.shape, FULL)
    step = row_chunk(rows)

    def norm(own):
        unit, inverse = unit_of(rows_ref[own, :])
        grad = total[own, :]
        back = grad_ref[own, :] + unit_back(grad, unit, inverse, gain)
        back_ref[own, :] = back
        branch_ref[own, :] = back.astype(HALF)
        kept = lax.broadcasted_iota(jnp.int32, (step, 1), 0) + own.start < count
        grad = jnp.where(kept, grad, grad * leader)
        norms_ref[0:1, :] += jnp.sum(grad * unit, 0, keepdims=True)
        norms_ref[1:2, :] += jnp.sum(grad, 0, keepdims=True)

    over_rows(rows, step, norm)
    copies[-1].wait()
    for column in range(0, width, TILE):
        part = slice(column, column + TILE)
        plain[:, part] = dot_back(branch_ref[...], out_ref[part, :])
    send_blocks(plain, blocks, (send0, send1, send2, send3), place, count // groups)
    for frame in range(own_frames):
        clip = clip_ref[place * own_frames + frame]
        class_ref[frame : frame + 1, :] = (
            plain[pl.ds(count + clip, 1), :] * share_ref[pl.ds(clip, 1), 0:1]
        )


def space_backward(dims, layer, piece0, piece1, piece2, piece3, class_ref, triple_ref, total_ref, in_hbm,
                   grad_ref, send0, send1, send2, send3,
                   in_ref, plain, mixed, sems):
    frames, patches, width, heads, groups = dims
    own_frames = frames // groups
    seq = groups * patches
    rows = triple_ref.shape[0] // own_frames
    copies = fetch((in_hbm.at[layer],), (in_ref,), sems)
    for away, piece in enumerate((piece0, piece1, piece2, piece3)):
        values = piece[...].astype(FULL)
        for frame in range(own_frames):
            start = frame * rows + away * patches
            plain[start : start + patches, :] = values[frame * patches : (frame + 1) * patches]
    for frame in range(own_frames):
        start = frame * rows + seq
        plain[start : start + rows - seq, :] = jnp.zeros((rows - seq, width), FULL)
        plain[start : start + 1, :] = class_ref[frame : frame + 1, :]
    mixed[...] = plain[...].astype(HALF)
    keys = lax.broadcasted_iota(jnp.int32, (1, rows), 1)
    bias = jnp.where(keys <= seq, 0.0, -1e30)

    def block(index, carry):
        own = pl.ds(pl.multiple_of(index * rows, rows), rows)

        def load(part, pair):
            start = part * width + pair * 128
            return triple_ref[own, start : start + 128]

        def load_grad(pair):
            return mixed[own, pair * 128 : (pair + 1) * 128]

        def store(part, pair, grad):
            start = part * width + pair * 128
            grad_ref[own, start : start + 128] = grad.astype(HALF)

        attend_backward(load, load_grad, total_ref[own, :], store, heads, width // heads, bias)
        return carry

    lax.fori_loop(0, own_frames, block, 0)
    copies[0].wait()
    for column in range(0, width, TILE):
        part = slice(column, column + TILE)
        plain[:, part] = dot_back(grad_ref[...], in_ref[part, :])
    return_pieces(plain, (send0, send1, send2, send3), own_frames, patches, rows)


def time_backward(dims, layer, place_ref, piece0, piece1, piece2, piece3, member_ref, back_ref, after_ref, x_ref,
                  triple_ref, total_ref, bias_ref, gain_ref, in_hbm, out_hbm, mix_hbm,
                  branch_ref, projected_ref, grad_ref, next_ref, norms_ref,
                  in_ref, out_ref, mix_ref, order, plain, blocks, frame_rows, mixed, sems):
    frames, patches, width, heads, groups = dims
    count = frames * patches
    rows = x_ref.shape[0]
    step = bias_ref.shape[0]
    place = place_ref[0]
    copies = fetch(
        (mix_hbm.at[layer], out_hbm.at[layer], in_hbm.at[layer]), (mix_ref, out_ref, in_ref), sems
    )
    take_pieces(
        (piece0, piece1, piece2, piece3),
        blocks,
        plain,
        frame_rows,
        place,
        count // groups,
        frames // groups,
    )
    plain[count:, :] = jnp.dot(
        member_ref[...], frame_rows[...], precision=HIGH, preferred_element_type=FULL
    )
    leader = jnp.where(place == 0, 1.0, 0.0).astype(FULL)
    norms_ref[...] = jnp.zeros(norms_ref.shape, FULL)
    gain = gain_ref[layer, 1:2, :]
    chunk = row_chunk(rows)

    def space_norm(own):
        unit, inverse = unit_of(after_ref[own, :])
        grad = plain[own, :]
        back = back_ref[own, :] + unit_back(grad, unit, inverse, gain)
        next_ref[own, :] = back
        kept = lax.broadcasted_iota(jnp.int32, (chunk, 1), 0) + own.start < count
        branch_ref[own, :] = jnp.where(kept, back, 0.0).astype(HALF)
        grad = jnp.where(kept, grad, grad * leader)
        norms_ref[0:1, :] += jnp.sum(grad * unit, 0, keepdims=True)
        norms_ref[1:2, :] += jnp.sum(grad, 0, keepdims=True)

    over_rows(rows, chunk, space_norm)
    copies[0].wait()
    for column in range(0, width, TILE):
        part = slice(column, column + TILE)
        projected_ref[:, part] = dot_back(branch_ref[...], mix_ref[part, :]).astype(HALF)
    copies[1].wait()
    for column in range(0, width, TILE):
        part = slice(column, column + TILE)
        plain[:, part] = dot_back(projected_ref[...], out_ref[part, :])
    for frame in range(frames):
        interleave(order, frame, frames, plain[frame * patches : (frame + 1) * patches, :])
    for group in range(width // 128):
        order[group, count:, :] = jnp.zeros((rows - count, 128), FULL)
        mixed[:, group * 128 : (group + 1) * 128] = order[group].astype(HALF)

    def block(index, carry):
        own = pl.ds(pl.multiple_of(index * step, step), step)

        def load(part, pair):
            start = part * width + pair * 128
            return triple_ref[own, start : start + 128]

        def load_grad(pair):
            return mixed[own, pair * 128 : (pair + 1) * 128]

        def store(part, pair, grad):
            start = part * width + pair * 128
            grad_ref[own, start : start + 128] = grad.astype(HALF)

        attend_backward(
            load, load_grad, total_ref[own, :], store, heads, width // heads, bias_ref[...]
        )
        return carry

    lax.fori_loop(0, rows // step, block, 0)
    copies[2].wait()
    for column in range(0, width, TILE):
        part = slice(column, column + TILE)
        grad = dot_back(grad_ref[...], in_ref[part, :])
        for group in range(TILE // 128):
            order[column // 128 + group] = grad[:, group * 128 : (group + 1) * 128]
    gain = gain_ref[layer, 0:1, :]
    for frame in range(frames):
        own = slice(frame * patches, (frame + 1) * patches)
        grad = pick(order, frame, frames, patches)
        unit, inverse = unit_of(x_ref[own, :])
        next_ref[own, :] += unit_back(grad, unit, inverse, gain)
        norms_ref[2:3, :] += jnp.sum(grad * unit, 0, keepdims=True)
        norms_ref[3:4, :] += jnp.sum(grad, 0, keepdims=True)


def cost(micros):
    return pl.CostEstimate(flops=micros * 10**9, bytes_accessed=micros * 10**6, transcendentals=0)


def call(kernel, outs, scratch, specs, micros):
    return pl.pallas_call(
        kernel,
        out_shape=[jax.ShapeDtypeStruct(shape, kind) for shape, kind in outs],
        in_specs=specs,
        out_specs=[VMEM] * len(outs),
        scratch_shapes=scratch,
        compiler_params=pltpu.CompilerParams(vmem_limit_bytes=VMEM_BYTES),
        cost_estimate=cost(micros),
    )


def outer_kernel(split, steps, place_ref, *refs):
    count = len(steps)
    lefts, rights, send_ref, keep_ref, turned = (
        refs[:count],
        refs[count : 2 * count],
        refs[2 * count],
        refs[2 * count + 1],
        refs[2 * count + 2 :],
    )
    step = pl.program_id(0)
    half = pl.num_programs(0) // 2

    def store(target, terms):
        if split:
            blocks, rows = target.shape[1], target.shape[2]
            far = place_ref[0] // 2 % 2
            for index in range(blocks):
                for side in range(2):
                    start = (index * 2 + side) * rows
                    target[far ^ side, index] = terms[start : start + rows]
        else:
            target[0] = terms

    for index, (first, last) in enumerate(steps):

        @pl.when(step == first)
        def _():
            turned[index][...] = lefts[index][...].astype(FULL).T.astype(HALF)

        @pl.when(jnp.logical_and(step >= first, step < last))
        def _():
            store(send_ref, dot(turned[index][...], rights[index][...]).astype(HALF))

        @pl.when(jnp.logical_and(step >= first + half, step < last + half))
        def _():
            store(keep_ref, dot(turned[index][...], rights[index][...]).astype(HALF))


def outer_group(place, pairs, groups, blocks, split, micros):
    rows = pairs[0][0].shape[1]
    parts = 2 if split else groups
    sizes = [right.shape[1] // parts for left, right in pairs]
    tile = 384 if all(size % 384 == 0 for size in sizes) else 128
    tiles = [size // tile for size in sizes]
    inner = 1 if split else 2
    total = sum(tiles)
    half = inner * total
    starts = [inner * sum(tiles[:index]) for index in range(len(tiles))]
    steps = [(start, start + inner * own) for start, own in zip(starts, tiles)]

    def right_map(start, own, step, place_ref):
        keep = step >= half
        local = jnp.clip(jnp.where(keep, step - half, step) - start, 0, inner * own - 1)
        if split:
            side = place_ref[0] % 2
            return (0, jnp.where(keep, side, 1 - side) * own + local)
        shard = local // own * 2 + jnp.where(keep, 0, 1)
        return (0, shard * own + local % own)

    def out_map(step):
        if split:
            return (0, 0, 0, step)
        shard = step * 0
        column = step * 0
        for start, own, base in zip(starts, tiles, [s // inner for s in starts]):
            here = jnp.logical_and(step >= start, step < start + inner * own)
            shard = jnp.where(here, (step - start) // own, shard)
            column = jnp.where(here, base + (step - start) % own, column)
        return (shard, 0, column)

    if split:
        size = rows // blocks // 2
        shape, block = (2, blocks, size, total * tile), (2, blocks, size, tile)
    else:
        shape, block = (2, rows, total * tile), (1, rows, tile)
    shape = jax.ShapeDtypeStruct(shape, HALF)
    lefts, rights = zip(*pairs)
    send, keep = pl.pallas_call(
        partial(outer_kernel, split, steps),
        out_shape=[shape, shape],
        grid_spec=pltpu.PrefetchScalarGridSpec(
            num_scalar_prefetch=1,
            grid=(2 * half,),
            in_specs=[pl.BlockSpec(left.shape, lambda step, place_ref: (0, 0)) for left in lefts]
            + [
                pl.BlockSpec((right.shape[0], tile), partial(right_map, start, own))
                for right, start, own in zip(rights, starts, tiles)
            ],
            out_specs=[
                pl.BlockSpec(block, lambda step, place_ref: out_map(jnp.minimum(step, half - 1))),
                pl.BlockSpec(block, lambda step, place_ref: out_map(jnp.maximum(step - half, 0))),
            ],
            scratch_shapes=[pltpu.VMEM((rows, left.shape[0]), HALF) for left in lefts],
        ),
        compiler_params=pltpu.CompilerParams(vmem_limit_bytes=VMEM_BYTES),
        cost_estimate=cost(micros),
    )(place, *lefts, *rights)
    if split:
        return send, keep
    shape = (2, blocks, rows // blocks, total * tile)
    return send.reshape(shape), keep.reshape(shape)


def swap(values, axis, bit):
    size = lax.axis_size(axis)
    return lax.ppermute(values, axis, [(index, index ^ bit) for index in range(size)])


def ring(values, far, step):
    return lax.ppermute(
        values,
        DP,
        [
            (start * 2 + near, (start + step) % far * 2 + near)
            for start in range(far)
            for near in range(2)
        ],
    )


def reduce_group(parts, order):
    send, keep = parts
    other = yield swap(send, TENSOR, 1)
    values = keep + other
    blocks, rows, columns = values.shape[1:]
    far = blocks // 2
    near_index = lax.axis_index(DP) % 2
    far_index = lax.axis_index(DP) // 2
    values = values.reshape(2, far, 2, rows, columns)
    dims = [0, 1, 2]
    for axis in order:
        dim = dims.index(axis)
        if axis == 0:
            keep = lax.index_in_dim(values, 0, dim, False)
            other = yield swap(lax.index_in_dim(values, 1, dim, False), TENSOR, 2)
            values = keep + other
        elif axis == 2:
            keep = lax.dynamic_index_in_dim(values, near_index, dim, False)
            send = lax.dynamic_index_in_dim(values, 1 - near_index, dim, False)
            other = yield swap(send, DP, 1)
            values = keep + other
        else:
            keep = lax.dynamic_index_in_dim(values, far_index, dim, False).astype(FULL)
            others = yield [
                ring(
                    lax.dynamic_index_in_dim(values, (far_index + step) % far, dim, False),
                    far,
                    step,
                )
                for step in range(1, far)
            ]
            for other in others:
                keep = keep + other.astype(FULL)
            values = keep.astype(HALF) if axis != order[-1] else keep
        dims.remove(axis)
    return values.astype(FULL)


def reduce_attention(parts, order, sizes):
    values = (yield from reduce_group(parts, order)).astype(HALF)
    other = yield swap(values, TENSOR, 2)
    values = in_order(values, other, 2, 0)
    other = yield swap(values, TENSOR, 1)
    matrices = []
    begin = 0
    for size in sizes:
        end = begin + size // 2
        matrices.append(in_order(values[:, begin:end], other[:, begin:end], 1, 1).astype(FULL))
        begin = end
    return matrices


def in_order(values, other, bit, dim):
    first = lax.axis_index(TENSOR) // bit % 2 == 0
    return jnp.where(
        first,
        jnp.concatenate([values, other], dim),
        jnp.concatenate([other, values], dim),
    )


def reduce_far(parts):
    send, keep = parts
    other = yield swap(send, TENSOR, 1)
    values = keep + other
    values = values[0] + swap(values[1], TENSOR, 2)
    values = values.reshape(-1, values.shape[-1])
    return lax.psum_scatter(values, DP, scatter_dimension=0, tiled=True).astype(FULL)


def reduce_whole(pairs):
    totals = yield [lax.psum(dot_outer(*pair).astype(HALF), TENSOR) for pair in pairs]
    return [
        lax.psum_scatter(total, DP, scatter_dimension=0, tiled=True).astype(FULL)
        for total in totals
    ]


class Flights:
    def __init__(self):
        self.running = {}
        self.results = {}

    def start(self, name, steps):
        self.running[name] = (steps, next(steps))

    def land(self, names, values):
        names = [name for name in names if name in self.running]
        held = [self.running[name][1] for name in names]
        values, held = lax.optimization_barrier((values, held))
        for name, arrived in zip(names, held):
            steps = self.running.pop(name)[0]
            try:
                self.running[name] = (steps, steps.send(arrived))
            except StopIteration as stop:
                self.results[name] = stop.value
        return values

    def finish(self):
        while self.running:
            for name in list(self.running):
                steps, arrived = self.running.pop(name)
                try:
                    self.running[name] = (steps, steps.send(arrived))
                except StopIteration as stop:
                    self.results[name] = stop.value


def reduce_norms(values):
    count = lax.axis_size(DP)
    far = count // 2
    if count > 2 * NEAR:
        values = yield lax.psum(values, TENSOR)
        return lax.psum_scatter(values, DP, scatter_dimension=1, tiled=True)
    for axis, bit in ((TENSOR, 1), (TENSOR, 2), (DP, 1)):
        other = yield swap(values, axis, bit)
        values = values + other
    others = yield [ring(values, far, step) for step in range(1, far)]
    for other in others:
        values = values + other
    lanes = values.shape[1] // count
    return lax.dynamic_slice_in_dim(values, lax.axis_index(DP) * lanes, lanes, 1)


def spread(pieces):
    return [pieces[0]] + [swap(piece, TENSOR, away) for away, piece in enumerate(pieces) if away]


def gather_shards(values):
    half = values.shape[0] // 2
    near = lax.axis_index(DP) % 2
    first = swap(lax.dynamic_slice_in_dim(values, near * half, half, 0), TENSOR, 2)
    second = swap(first, DP, 1)
    return [
        values,
        swap(values, TENSOR, 1),
        first,
        second,
        swap(first, TENSOR, 1),
        swap(second, TENSOR, 1),
    ]


def body(
    patch_tokens,
    class_tokens,
    frame_counts,
    patch_cotangent,
    class_cotangent,
    temporal_in,
    temporal_out,
    temporal_mix,
    spatial_in,
    spatial_out,
    hidden_up,
    hidden_down,
    norm_gain,
    norm_shift,
):
    frames, patches, width = patch_tokens.shape
    clips = class_tokens.shape[0]
    layers = temporal_in.shape[0]
    groups = lax.axis_size(TENSOR)
    place = jnp.stack([lax.axis_index(TENSOR), lax.axis_index(DP) % 2]).astype(jnp.int32)
    blocks_dp = lax.axis_size(DP)
    dims = (frames, patches, width, HEADS, groups)
    count = frames * patches
    rows = up_to(count + up_to(clips, 8), 80)
    spare = rows - count
    own_frames = frames // groups
    seq = groups * patches
    frame_span = up_to(seq + 1, 16)
    span = own_frames * frame_span
    hidden = groups * hidden_up.shape[2]
    piece_rows = own_frames * patches
    back_rows = up_to(piece_rows + 2 * own_frames, 8)

    ends = jnp.cumsum(frame_counts[0])
    frame_index = jnp.arange(frames, dtype=jnp.int32)
    clip_of = jnp.sum((frame_index[:, None] >= ends[None, :]).astype(jnp.int32), 1)
    clip_index = jnp.arange(spare, dtype=jnp.int32)
    member = (clip_index[:, None] == clip_of[None, :]).astype(FULL)
    counts = jnp.concatenate([frame_counts[0].astype(FULL), jnp.ones((spare - clips,), FULL)])
    share = member / counts[:, None]
    inverse_counts = 1.0 / counts
    row_index = jnp.arange(80, dtype=jnp.int32)
    row_clip = jnp.sum(
        jnp.where(row_index[:, None] % frames == frame_index[None, :], clip_of[None, :], 0), 1
    )
    same = jnp.logical_and(
        row_index[:, None] // frames == row_index[None, :] // frames,
        row_clip[:, None] == row_clip[None, :],
    )
    bias = jnp.where(same, 0.0, -1e30)

    def rows_of(patch, per_clip):
        return jnp.concatenate(
            [
                patch.reshape(count, width),
                per_clip,
                jnp.zeros((spare - clips, width), patch.dtype),
            ],
            0,
        ).astype(FULL)

    ups = [gather_shards(hidden_up[0])]
    downs = [gather_shards(hidden_down[0])]
    patch_rows = rows_of(patch_tokens, class_tokens)
    pieces_out = [((piece_rows, width), HALF)] * groups
    backs_out = [((back_rows, width), HALF)] * groups
    lane_buffer = pltpu.VMEM((width // 128, rows, 128), FULL)
    row_buffer = pltpu.VMEM((rows, width), FULL)
    square = pltpu.VMEM((width, width), HALF)
    wide = pltpu.VMEM((width, 3 * width), HALF)
    shards = pltpu.VMEM((groups, width, width), HALF)
    blocks = pltpu.VMEM((groups, back_rows, width), FULL)
    frame_rows = pltpu.VMEM((frames, width), FULL)
    saved = []
    for layer in range(layers):
        time = call(
            partial(time_forward, dims, layer),
            [
                ((rows, width), HALF),
                ((rows, 3 * width), HALF),
                ((rows, 128), FULL),
                ((rows, width), HALF),
                ((rows, width), HALF),
                ((rows, width), FULL),
            ]
            + pieces_out
            + [((spare, width), FULL)],
            [wide, square, square, lane_buffer, row_buffer, blocks, pltpu.SemaphoreType.DMA((3,))],
            [SMEM, VMEM, VMEM, VMEM, VMEM, ANY, ANY, ANY],
            14,
        )(place, patch_rows, bias, norm_gain, norm_shift, temporal_in, temporal_out, temporal_mix)
        space = call(
            partial(space_forward, dims, layer),
            [((span, width), HALF), ((span, 3 * width), HALF), ((span, 128), FULL)] + backs_out,
            [wide, pltpu.VMEM((span, width), FULL), pltpu.SemaphoreType.DMA((1,))],
            [SMEM, SMEM, VMEM] + [VMEM] * groups + [ANY],
            9,
        )(place, clip_of, time[10], *spread(time[6:10]), spatial_in)
        if layer + 1 < layers:
            later = lax.optimization_barrier((hidden_up[layer + 1], hidden_down[layer + 1], *space))
            ups.append(gather_shards(later[0]))
            downs.append(gather_shards(later[1]))
            space = later[2:]
        feed = call(
            partial(feed_forward, dims, layer),
            [
                ((rows, width), HALF),
                ((rows, width), FULL),
                ((rows, width), HALF),
                ((rows, hidden), HALF),
                ((rows, hidden), HALF),
                ((rows, width), FULL),
            ],
            [
                square,
                shards,
                shards,
                row_buffer,
                blocks,
                frame_rows,
                pltpu.VMEM((rows, width), HALF),
                pltpu.SemaphoreType.DMA((1,)),
                pltpu.SemaphoreType.DMA((12,)),
            ],
            [SMEM] + [VMEM] * groups + [VMEM] * 4 + [ANY] * 13,
            15,
        )(
            place, *spread(space[3:]), share, time[5], norm_gain, norm_shift, spatial_out,
            *ups[layer], *downs[layer],
        )
        saved.append((patch_rows, time, space, feed))
        patch_rows = feed[5]
    patch_output = patch_rows[:count].reshape(frames, patches, width).astype(HALF)
    class_output = patch_rows[count : count + clips].astype(HALF)

    grad_rows = rows_of(patch_cotangent, class_cotangent)
    near = blocks_dp <= 2 * NEAR
    flights = Flights()
    norms = [None] * layers

    def start(name, pairs, order, split, micros):
        if split and not near:
            flights.start(name, reduce_whole(pairs))
            return
        parts = outer_group(place, pairs, groups, blocks_dp, split, micros)
        if split:
            flights.start(name, reduce_attention(parts, order, [right.shape[1] for left, right in pairs]))
        elif near:
            flights.start(name, reduce_group(parts, order))
        else:
            flights.start(name, reduce_far(parts))

    for layer in reversed(range(layers)):
        first, time, space, feed = saved[layer]
        last = layer == 0
        feed_back = call(
            partial(feed_backward, dims, layer),
            [
                ((rows, width), HALF),
                ((rows, hidden), HALF),
                ((rows, width), HALF),
                ((rows, width), FULL),
                ((8, width), FULL),
            ]
            + pieces_out
            + [((8, width), FULL)],
            [
                square,
                shards,
                shards,
                row_buffer,
                row_buffer,
                blocks,
                pltpu.SemaphoreType.DMA((1,)),
                pltpu.SemaphoreType.DMA((12,)),
            ],
            [SMEM, SMEM] + [VMEM] * 5 + [ANY] * 13,
            23,
        )(
            place, clip_of, grad_rows, feed[4], feed[1],
            jnp.broadcast_to(inverse_counts[:, None], (spare, 128)), norm_gain, spatial_out,
            *ups[layer], *downs[layer],
        )
        update, grad_hidden, branch, back, feed_norms = feed_back[:5]
        arrived = spread(feed_back[5:9])
        pairs = ((feed[2], grad_hidden), (update, feed[3]))
        if last:
            pairs = flights.land(("feed1", "space1"), pairs)
            start("up0", pairs[:1], (0, 2, 1), False, 10)
            start("down0", pairs[1:], (2, 0, 1), False, 10)
            arrived = flights.land(("space1", "time1"), arrived)
        else:
            start("feed1", pairs, (2, 1, 0), False, 19)
        space_back = call(
            partial(space_backward, dims, layer),
            [((span, 3 * width), HALF)] + backs_out,
            [
                wide,
                pltpu.VMEM((span, width), FULL),
                pltpu.VMEM((span, width), HALF),
                pltpu.SemaphoreType.DMA((1,)),
            ],
            [VMEM] * groups + [VMEM] * 3 + [ANY],
            29,
        )(*arrived, feed_back[9], space[1], space[2], spatial_in)
        arrived = spread(space_back[1:])
        pairs = ((space[0], space_back[0]), (feed[0], branch))
        if last:
            pairs = flights.land(("up0", "down0"), pairs)
            start("space0", pairs, (2, 0, 1), True, 11)
            arrived = flights.land(("feed1", "space1", "time1"), arrived)
        else:
            pairs = flights.land(("feed1",), pairs)
            start("space1", pairs, (0, 2, 1), True, 11)
        time_back = call(
            partial(time_backward, dims, layer),
            [
                ((rows, width), HALF),
                ((rows, width), HALF),
                ((rows, 3 * width), HALF),
                ((rows, width), FULL),
                ((8, width), FULL),
            ],
            [
                wide,
                square,
                square,
                lane_buffer,
                row_buffer,
                blocks,
                frame_rows,
                pltpu.VMEM((rows, width), HALF),
                pltpu.SemaphoreType.DMA((3,)),
            ],
            [SMEM] + [VMEM] * groups + [VMEM] * 8 + [ANY] * 3,
            14,
        )(
            place, *arrived, member, back, time[5], first, time[1], time[2], bias,
            norm_gain, temporal_in, temporal_out, temporal_mix,
        )
        grad_rows = time_back[3]
        norms[layer] = (time_back[4], feed_norms)
        pairs = ((time[0], time_back[2]), (time[3], time_back[1]), (time[4], time_back[0]))
        if last:
            pairs = flights.land(("feed1", "space1", "space0", "up0", "down0"), pairs)
            ordered = [
                entry[at : at + 1]
                for part, at in ((0, 2), (0, 0), (1, 0), (0, 3), (0, 1), (1, 1))
                for entry in [norms[index][part] for index in range(layers)]
            ]
            flights.start("norms", reduce_norms(jnp.concatenate(ordered, 0)))
            start("others0", pairs[1:], (2, 0, 1), True, 8)
            start("time0", pairs[:1], (0, 2, 1), True, 8)
        else:
            start("time1", pairs, (0, 2, 1), True, 15)
            grad_rows = flights.land(("space1",), grad_rows)
    flights.finish()
    results = flights.results
    lanes = width // blocks_dp

    norm_sums = results["norms"].reshape(2, 3, layers, lanes).transpose(0, 2, 1, 3)
    time_sums = (results["time0"] + results["others0"], results["time1"])
    space_sums = (results["space0"], results["space1"])
    gradients = (
        *[jnp.stack([sums[index] for sums in time_sums]) for index in range(3)],
        *[jnp.stack([sums[index] for sums in space_sums]) for index in range(2)],
        jnp.stack([results["up0"], results["feed1"][:, :width]]),
        jnp.stack([results["down0"].T, results["feed1"][:, width:].T]),
        norm_sums[0],
        norm_sums[1],
    )
    patch_grad = grad_rows[:count].reshape(frames, patches, width)
    class_grad = grad_rows[count : count + clips]
    return (patch_output, class_output, patch_grad, class_grad, *gradients)


def solution(mesh):
    placed = (
        P(DP, TENSOR, None),
        P(DP, None),
        P(DP, None),
        P(DP, TENSOR, None),
        P(DP, None),
        P(),
        P(),
        P(),
        P(),
        P(),
        P(None, None, TENSOR),
        P(None, TENSOR, None),
        P(),
        P(),
    )
    return jax.shard_map(
        body,
        mesh=mesh,
        in_specs=placed,
        out_specs=(
            P(DP, TENSOR, None),
            P(DP, None),
            P(DP, TENSOR, None),
            P(DP, None),
            P(None, DP, None),
            P(None, DP, None),
            P(None, DP, None),
            P(None, DP, None),
            P(None, DP, None),
            P(None, DP, TENSOR),
            P(None, TENSOR, DP),
            P(None, None, DP),
            P(None, None, DP),
        ),
        check_vma=False,
    )
```

profile of v0, /device:TPU:0, one launch (start us, length us, event | category | flops | bytes accessed | tf_op | source)
XLA Modules:
  0.0 767.2 jit_solution(6368959220380020795)
XLA Ops:
  8.2 14.4 %shard_map.237 = (bf16[400,768]{1,0:T(8,128)(2,1)}, bf16[400,2304]{1,0:T(8,128)(2,1)}, f32[400,128]{1,0:T(8,128)}, bf16[400,768]{1,0:T(8,128)(2,1)}, bf16[400,76...) custom-call(s32[2]{0:T(128)} %pad_add_fusion.place_ref, ...), custom_call_target="tpu_custom_call" | custom-call | flops 14000000000 | bytes 14000000 | tf_op jit(solution)/shard_map/pallas_call | solution.py:937
  33.8 9.0 %shard_map.238 = (bf16[416,768]{1,0:T(8,128)(2,1)}, bf16[416,2304]{1,0:T(8,128)(2,1)}, f32[416,128]{1,0:T(8,128)}, bf16[104,768]{1,0:T(8,128)(2,1)}, bf16[104,76...) custom-call(s32[2]{0:T(128)} %pad_add_fusion.place_ref, s32[8]{0:T(128)} %copy-done.54, ...), custom_call_target="tpu_custom_call" | custom-call | flops 8999999488 | bytes 9000000 | tf_op jit(solution)/shard_map/pallas_call | solution.py:953
  46.6 28.7 %collective-permute-done.4.piece2 = bf16[104,768]{1,0:T(8,128)(2,1)S(1)} collective-permute-done((bf16[104,768]{1,0:T(8,128)(2,1)}, bf16[104,768]{1,0:T(8,128)(2,1)S(1)}, u32[]{:S(2)}, u32[]{:S(2)}) %collective-permute-start.4) | collective-permute-done | bytes 159776 | tf_op jit(solution)/shard_map/ppermute | solution.py:703
  77.1 5.2 collective-permute-done.5.piece3
  87.2 10.6 %collective-permute-done.28.down2 = bf16[384,768]{1,0:T(8,128)(2,1)} collective-permute-done((bf16[384,768]{1,0:T(8,128)(2,1)S(1)}, bf16[384,768]{1,0:T(8,128)(2,1)}, u32[]{:S(2)}, u32[]{:S(2)}) %collective-permute-start.28) | collective-permute-done | bytes 589856 | tf_op jit(solution)/shard_map/ppermute | solution.py:703
  98.3 3.2 collective-permute-done.8.up3
  101.5 12.2 %collective-permute-done.13.down3 = bf16[384,768]{1,0:T(8,128)(2,1)S(1)} collective-permute-done((bf16[384,768]{1,0:T(8,128)(2,1)}, bf16[384,768]{1,0:T(8,128)(2,1)S(1)}, u32[]{:S(2)}, u32[]{:S(2)}) %collective-permute-start.13) | collective-permute-done | bytes 589856 | tf_op jit(solution)/shard_map/ppermute | solution.py:703
  118.3 17.9 %shard_map.239 = (bf16[400,768]{1,0:T(8,128)(2,1)}, f32[400,768]{1,0:T(8,128)}, bf16[400,768]{1,0:T(8,128)(2,1)}, bf16[400,3072]{1,0:T(8,128)(2,1)}, bf16[400,3072]{1,0:T(8,128)(2,1)}, /*index=5*/f32[400,768]{1,0:T(8,128)}) custom-call(s32[2]{0:T(128)} %pad_add_fusion.place_ref, bf16[104,768]{1,0:T(8,128)(2,1)} %get-tuple-element.185.piece0, ...), custom_call_target="tpu_custom_call" | custom-call | flops 15000000512 | bytes 15000000 | tf_op jit(solution)/shard_map/pallas_call | solution.py:965
  136.2 14.4 %shard_map.240 = (bf16[400,768]{1,0:T(8,128)(2,1)}, bf16[400,2304]{1,0:T(8,128)(2,1)}, f32[400,128]{1,0:T(8,128)}, bf16[400,768]{1,0:T(8,128)(2,1)}, bf16[400,76...) custom-call(s32[2]{0:T(128)} %pad_add_fusion.place_ref, ...), custom_call_target="tpu_custom_call" | custom-call | flops 14000000000 | bytes 14000000 | tf_op jit(solution)/shard_map/pallas_call | solution.py:937
  153.0 4.9 collective-permute-done.17.piece2
  160.9 9.4 %shard_map.241 = (bf16[416,768]{1,0:T(8,128)(2,1)}, bf16[416,2304]{1,0:T(8,128)(2,1)}, f32[416,128]{1,0:T(8,128)}, bf16[104,768]{1,0:T(8,128)(2,1)}, bf16[104,76...) custom-call(s32[2]{0:T(128)} %pad_add_fusion.place_ref, s32[8]{0:T(128)} %copy-done.54, ...), custom_call_target="tpu_custom_call" | custom-call | flops 8999999488 | bytes 9000000 | tf_op jit(solution)/shard_map/pallas_call | solution.py:953
  172.3 5.7 collective-permute-done.20.piece2
  180.4 17.7 %shard_map.242 = (bf16[400,768]{1,0:T(8,128)(2,1)}, f32[400,768]{1,0:T(8,128)}, bf16[400,768]{1,0:T(8,128)(2,1)}, bf16[400,3072]{1,0:T(8,128)(2,1)}, bf16[400,3072]{1,0:T(8,128)(2,1)}, /*index=5*/f32[400,768]{1,0:T(8,128)}) custom-call(s32[2]{0:T(128)} %pad_add_fusion.place_ref, bf16[104,768]{1,0:T(8,128)(2,1)} %get-tuple-element.196.piece0, ...), custom_call_target="tpu_custom_call" | custom-call | flops 15000000512 | bytes 15000000 | tf_op jit(solution)/shard_map/pallas_call | solution.py:965
  198.8 13.9 %shard_map.243 = (bf16[400,768]{1,0:T(8,128)(2,1)}, bf16[400,3072]{1,0:T(8,128)(2,1)}, bf16[400,768]{1,0:T(8,128)(2,1)}, f32[400,768]{1,0:T(8,128)}, f32[8,768]{...) custom-call(s32[2]{0:T(128)} %pad_add_fusion.place_ref, ...), custom_call_target="tpu_custom_call" | custom-call | flops 23000000512 | bytes 23000000 | tf_op jit(solution)/shard_map/pallas_call | solution.py:1017
  212.8 17.8 %shard_map.246 = (bf16[2,768,1536]{2,1,0:T(8,128)(2,1)}, bf16[2,768,1536]{2,1,0:T(8,128)(2,1)}) custom-call(s32[2]{0:T(128)} %pad_add_fusion.place_ref, bf16[400,768]{1,0:T(8,128)(2,1)} %get-tuple-element.225.refs_0_, bf16[400,768]{1,0:T(8,128)(2,1)} %get-tuple-element.226.refs_1_, bf16[400,3072]{1,0:T(8,128)(2,1)} %get-tuple-element.227.refs_2_, ...), custom_call_target="tpu_custom_call" | custom-call | flops 19000000512 | bytes 19000000 | tf_op jit(solution)/shard_map/pallas_call | solution.py:675
  235.1 3.7 collective-permute-done.32.piece1
  242.0 14.4 %shard_map.244 = (bf16[416,2304]{1,0:T(8,128)(2,1)}, bf16[104,768]{1,0:T(8,128)(2,1)}, bf16[104,768]{1,0:T(8,128)(2,1)}, bf16[104,768]{1,0:T(8,128)(2,1)}, bf16[104,768]{1,0:T(8,128)(2,1)}) custom-call(bf16[98,768]{1,0:T(8,128)(2,1)} %get-tuple-element.206.piece0, bf16[98,768]{1,0:T(8,128)(2,1)} %copy-done.90, bf16[98,768]{1,0:T(8,128)(2,1)} %copy-done.91, ...), custom_call_target="tpu_custom_call" | custom-call | flops 28999999488 | bytes 29000000 | tf_op jit(solution)/shard_map/pallas_call | solution.py:1055
  258.3 10.3 %shard_map.247 = (bf16[2,8,48,1536]{3,2,1,0:T(8,128)(2,1)}, bf16[2,8,48,1536]{3,2,1,0:T(8,128)(2,1)}) custom-call(s32[2]{0:T(128)} %pad_add_fusion.place_ref, bf16[416,768]{1,0:T(8,128)(2,1)} %get-tuple-element.230.refs_0_, bf16[400,768]{1,0:T(8,128)(2,1)} %get-tuple-element.231.refs_1_, bf16[416,2304]{1,0:T(8,128)(2,1)} %get-tuple-element.232.refs_2_, ...), custom_call_target="tpu_custom_call" | custom-call | flops 11000000512 | bytes 11000000 | tf_op jit(solution)/shard_map/pallas_call | solution.py:675
  269.9 28.8 %shard_map.245 = (bf16[400,768]{1,0:T(8,128)(2,1)}, bf16[400,768]{1,0:T(8,128)(2,1)}, bf16[400,2304]{1,0:T(8,128)(2,1)}, f32[400,768]{1,0:T(8,128)}, f32[8,768]{1,0:T(8,128)}) custom-call(s32[2]{0:T(128)} %pad_add_fusion.place_ref, bf16[104,768]{1,0:T(8,128)(2,1)} %get-tuple-element.213.piece0, bf16[104,768]{1,0:T(8,128)(2,1)} %copy-done.83, ...), custom_call_target="tpu_custom_call" | custom-call | flops 14000000000 | bytes 14000000 | tf_op jit(solution)/shard_map/pallas_call | solution.py:1076
  298.8 13.4 %shard_map.249 = (bf16[2,8,48,1920]{3,2,1,0:T(8,128)(2,1)}, bf16[2,8,48,1920]{3,2,1,0:T(8,128)(2,1)}) custom-call(s32[2]{0:T(128)} %pad_add_fusion.place_ref, bf16[400,768]{1,0:T(8,128)(2,1)} %get-tuple-element.251.refs_0_, bf16[400,768]{1,0:T(8,128)(2,1)} %get-tuple-element.252.refs_1_, bf16[400,768]{1,0:T(8,128)(2,1)} %get-tuple-element.253.refs_2_, ...), custom_call_target="tpu_custom_call" | custom-call | flops 15000000512 | bytes 15000000 | tf_op jit(solution)/shard_map/pallas_call | solution.py:675
  312.3 3.9 add.373
  321.3 13.7 %shard_map.248 = (bf16[400,768]{1,0:T(8,128)(2,1)}, bf16[400,3072]{1,0:T(8,128)(2,1)}, bf16[400,768]{1,0:T(8,128)(2,1)}, f32[400,768]{1,0:T(8,128)}, f32[8,768]{...) custom-call(s32[2]{0:T(128)} %pad_add_fusion.place_ref, ...), custom_call_target="tpu_custom_call" | custom-call | flops 23000000512 | bytes 23000000 | tf_op jit(solution)/shard_map/pallas_call | solution.py:1017
  337.9 34.2 %collective-permute-done.43 = bf16[2,4,96,1536]{3,2,0,1:T(8,128)(2,1)S(1)} collective-permute-done((bf16[2,4,96,1536]{3,2,0,1:T(8,128)(2,1)}, bf16[2,4,96,1536]{3,2,0,1:T(8,128)(2,1)S(1)}, u32[]{:S(2)}, u32[]{:S(2)}) %collective-permute-start.43) | collective-permute-done | bytes 2359328 | tf_op jit(solution)/shard_map/ppermute | solution.py:703
  375.4 9.9 %shard_map.252 = (bf16[2,768,768]{2,1,0:T(8,128)(2,1)}, bf16[2,768,768]{2,1,0:T(8,128)(2,1)}) custom-call(s32[2]{0:T(128)} %pad_add_fusion.place_ref, bf16[400,768]{1,0:T(8,128)(2,1)} %get-tuple-element.297.refs_0_, bf16[400,3072]{1,0:T(8,128)(2,1)} %get-tuple-element.298.refs_1_), custom_call_target="tpu_custom_call" | custom-call | flops 10000000000 | bytes 10000000 | tf_op jit(solution)/shard_map/pallas_call | solution.py:675
  400.1 6.5 collective-permute-done.50
  407.2 14.5 %shard_map.250 = (bf16[416,2304]{1,0:T(8,128)(2,1)}, bf16[104,768]{1,0:T(8,128)(2,1)}, bf16[104,768]{1,0:T(8,128)(2,1)}, bf16[104,768]{1,0:T(8,128)(2,1)}, bf16[104,768]{1,0:T(8,128)(2,1)}) custom-call(bf16[98,768]{1,0:T(8,128)(2,1)} %get-tuple-element.258.piece0, bf16[98,768]{1,0:T(8,128)(2,1)} %collective-permute-done.40.piece1, ...), custom_call_target="tpu_custom_call" | custom-call | flops 28999999488 | bytes 29000000 | tf_op jit(solution)/shard_map/pallas_call | solution.py:1055
  421.8 10.1 %collective-permute-done.51 = bf16[2,96,1536]{2,1,0:T(8,128)(2,1)S(1)} collective-permute-done((bf16[2,96,1536]{2,1,0:T(8,128)(2,1)}, bf16[2,96,1536]{2,1,0:T(8,128)(2,1)S(1)}, u32[]{:S(2)}, u32[]{:S(2)}) %collective-permute-start.51) | collective-permute-done | bytes 589856 | tf_op jit(solution)/shard_map/ppermute | solution.py:707
  435.1 17.3 %collective-permute-done.54 = bf16[48,1536]{1,0:T(8,128)(2,1)S(1)} collective-permute-done((bf16[48,1536]{1,0:T(8,128)(2,1)S(1)}, bf16[48,1536]{1,0:T(8,128)(2,1)S(1)}, u32[]{:S(2)}, u32[]{:S(2)}) %collective-permute-start.54) | collective-permute-done | bytes 147488 | tf_op jit(solution)/shard_map/ppermute | solution.py:707
  454.0 9.9 %shard_map.253 = (bf16[2,768,768]{2,1,0:T(8,128)(2,1)}, bf16[2,768,768]{2,1,0:T(8,128)(2,1)}) custom-call(s32[2]{0:T(128)} %pad_add_fusion.place_ref, bf16[400,768]{1,0:T(8,128)(2,1)} %get-tuple-element.300.refs_0_, bf16[400,3072]{1,0:T(8,128)(2,1)} %get-tuple-element.301.refs_1_), custom_call_target="tpu_custom_call" | custom-call | flops 10000000000 | bytes 10000000 | tf_op jit(solution)/shard_map/pallas_call | solution.py:675
  465.2 28.7 %shard_map.251 = (bf16[400,768]{1,0:T(8,128)(2,1)}, bf16[400,768]{1,0:T(8,128)(2,1)}, bf16[400,2304]{1,0:T(8,128)(2,1)}, f32[400,768]{1,0:T(8,128)}, f32[8,768]{1,0:T(8,128)}) custom-call(s32[2]{0:T(128)} %pad_add_fusion.place_ref, bf16[104,768]{1,0:T(8,128)(2,1)} %get-tuple-element.273.piece0, bf16[104,768]{1,0:T(8,128)(2,1)} %copy-done.79, ...), custom_call_target="tpu_custom_call" | custom-call | flops 14000000000 | bytes 14000000 | tf_op jit(solution)/shard_map/pallas_call | solution.py:1076
  507.5 16.6 %collective-permute-done.104 = f32[12,768]{1,0:T(8,128)S(1)} collective-permute-done((f32[12,768]{1,0:T(8,128)S(1)}, f32[12,768]{1,0:T(8,128)S(1)}, u32[]{:S(2)}, u32[]{:S(2)}) %collective-permute-start.104) | collective-permute-done | bytes 36896 | tf_op jit(solution)/shard_map/ppermute | solution.py:703
  540.0 10.6 %shard_map.254 = (bf16[2,8,48,1536]{3,2,1,0:T(8,128)(2,1)}, bf16[2,8,48,1536]{3,2,1,0:T(8,128)(2,1)}) custom-call(s32[2]{0:T(128)} %pad_add_fusion.place_ref, bf16[416,768]{1,0:T(8,128)(2,1)} %get-tuple-element.303.refs_0_, bf16[400,768]{1,0:T(8,128)(2,1)} %get-tuple-element.304.refs_1_, bf16[416,2304]{1,0:T(8,128)(2,1)} %get-tuple-element.305.refs_2_, ...), custom_call_target="tpu_custom_call" | custom-call | flops 11000000512 | bytes 11000000 | tf_op jit(solution)/shard_map/pallas_call | solution.py:675
  565.2 23.5 %collective-permute-done.58 = bf16[48,1536]{1,0:T(8,128)(2,1)S(1)} collective-permute-done((bf16[48,1536]{1,0:T(8,128)(2,1)S(1)}, bf16[48,1536]{1,0:T(8,128)(2,1)S(1)}, u32[]{:S(2)}, u32[]{:S(2)}) %collective-permute-start.58) | collective-permute-done | bytes 147488 | tf_op jit(solution)/shard_map/ppermute | solution.py:703
  593.1 8.1 %shard_map.255 = (bf16[2,8,48,1152]{3,2,1,0:T(8,128)(2,1)}, bf16[2,8,48,1152]{3,2,1,0:T(8,128)(2,1)}) custom-call(s32[2]{0:T(128)} %pad_add_fusion.place_ref, bf16[400,768]{1,0:T(8,128)(2,1)} %get-tuple-element.312.refs_0_, bf16[400,2304]{1,0:T(8,128)(2,1)} %get-tuple-element.313.refs_1_), custom_call_target="tpu_custom_call" | custom-call | flops 8000000000 | bytes 8000000 | tf_op jit(solution)/shard_map/pallas_call | solution.py:675
  607.5 6.6 shard_map.256
  617.3 28.8 %collective-permute-done.94 = bf16[4,96,768]{2,1,0:T(8,128)(2,1)} collective-permute-done((bf16[4,96,768]{2,1,0:T(8,128)(2,1)S(1)}, bf16[4,96,768]{2,1,0:T(8,128)(2,1)}, u32[]{:S(2)}, u32[]{:S(2)}) %collective-permute-start.94) | collective-permute-done | bytes 589856 | tf_op jit(solution)/shard_map/ppermute | solution.py:703
  650.5 3.5 collective-permute-done.97
  654.1 4.3 collective-permute-start.101
  658.4 5.1 collective-permute-done.96
  663.5 6.4 collective-permute-start.99
  670.1 4.8 collective-permute-done.100
  684.0 10.5 %collective-permute-done.87 = bf16[4,48,1536]{2,1,0:T(8,128)(2,1)S(1)} collective-permute-done((bf16[4,48,1536]{2,1,0:T(8,128)(2,1)S(1)}, bf16[4,48,1536]{2,1,0:T(8,128)(2,1)S(1)}, u32[]{:S(2)}, u32[]{:S(2)}) %collective-permute-start.87) | collective-permute-done | bytes 589856 | tf_op jit(solution)/shard_map/ppermute | solution.py:703
  694.6 3.2 collective-permute-start.90
  702.5 5.6 collective-permute-done.89
  709.2 10.5 %collective-permute-done.80 = bf16[4,48,768]{2,1,0:T(8,128)(2,1)S(1)} collective-permute-done((bf16[4,48,768]{2,1,0:T(8,128)(2,1)S(1)}, bf16[4,48,768]{2,1,0:T(8,128)(2,1)S(1)}, u32[]{:S(2)}, u32[]{:S(2)}) %collective-permute-start.80) | collective-permute-done | bytes 294944 | tf_op jit(solution)/shard_map/ppermute | solution.py:703
  730.0 3.3 collective-permute-done.84
  736.8 10.8 %collective-permute-done.66 = bf16[4,48,1152]{2,1,0:T(8,128)(2,1)S(1)} collective-permute-done((bf16[4,48,1152]{2,1,0:T(8,128)(2,1)S(1)}, bf16[4,48,1152]{2,1,0:T(8,128)(2,1)S(1)}, u32[]{:S(2)}, u32[]{:S(2)}) %collective-permute-start.66) | collective-permute-done | bytes 442400 | tf_op jit(solution)/shard_map/ppermute | solution.py:703
  753.0 5.9 collective-permute-done.68
  (523 shorter events, 192.0 us)
Async XLA Ops:
  26.0 71.8 %collective-permute-start.6 = (bf16[768,768]{1,0:T(8,128)(2,1)S(1)}, bf16[768,768]{1,0:T(8,128)(2,1)}, u32[]{:S(2)}, u32[]{:S(2)}) collective-permute-start(bf16[768,768]{1,0:T(8,128)(2,1)S(1)} %get-tuple-element.387.up0), channel_id=1, source_target_pairs={{0,1},{1,0},{2,3},{3,2},{4,5},{5,4},{6,7},{7,6},{8,9},{9,8},{10,11... | collective-permute-start | bytes 3538952 | tf_op jit(solution)/shard_map/ppermute | solution.py:703
  26.2 58.0 %collective-permute-start.7 = (bf16[384,768]{1,0:T(8,128)(2,1)S(1)}, bf16[384,768]{1,0:T(8,128)(2,1)S(1)}, u32[]{:S(2)}, u32[]{:S(2)}) collective-permute-start(bf16[384,768]{1,0:T(8,128)(2,1)S(1)} %dynamic-slice_bitcast_fusion.10), channel_id=1, source_target_pairs={{0,2},{1,3},{2,0},{3,1},{4,6},{5,7},{6,4},{7,5},{8,10},{9,11},{10,... | collective-permute-start | bytes 1769480 | tf_op jit(solution)/shard_map/ppermute | solution.py:703
  30.2 54.9 %collective-permute-start.12 = (bf16[384,768]{1,0:T(8,128)(2,1)S(1)}, bf16[384,768]{1,0:T(8,128)(2,1)}, u32[]{:S(2)}, u32[]{:S(2)}) collective-permute-start(bf16[384,768]{1,0:T(8,128)(2,1)S(1)} %dynamic-slice_bitcast_fusion.9), channel_id=1, source_target_pairs={{0,2},{1,3},{2,0},{3,1},{4,6},{5,7},{6,4},{7,5},{8,10},{9,11},{10,... | collective-permute-start | bytes 1769480 | tf_op jit(solution)/shard_map/ppermute | solution.py:703
  42.9 43.8 %collective-permute-start.23 = (bf16[384,768]{1,0:T(8,128)(2,1)S(1)}, bf16[384,768]{1,0:T(8,128)(2,1)}, u32[]{:S(2)}, u32[]{:S(2)}) collective-permute-start(bf16[384,768]{1,0:T(8,128)(2,1)S(1)} %constant_dynamic-slice_fusion.7), channel_id=1, source_target_pairs={{0,2},{1,3},{2,0},{3,1},{4,6},{5,7},{6,4},{7,5},{8,10},{9,11},{10,... | collective-permute-start | bytes 1769480 | tf_op jit(solution)/shard_map/ppermute | solution.py:703
  46.2 29.1 %collective-permute-start.4 = (bf16[104,768]{1,0:T(8,128)(2,1)}, bf16[104,768]{1,0:T(8,128)(2,1)S(1)}, u32[]{:S(2)}, u32[]{:S(2)}) collective-permute-start(bf16[104,768]{1,0:T(8,128)(2,1)} %get-tuple-element.187), channel_id=1, source_target_pairs={{0,2},{1,3},{2,0},{3,1},{4,6},{5,7},{6,4},{7,5},{8,10},{9,11},{10,... | collective-permute-start | bytes 479240 | tf_op jit(solution)/shard_map/ppermute | solution.py:703
  85.1 29.8 %collective-permute-start.11 = (bf16[768,768]{1,0:T(8,128)(2,1)S(1)}, bf16[768,768]{1,0:T(8,128)(2,1)S(1)}, u32[]{:S(2)}, u32[]{:S(2)}) collective-permute-start(bf16[768,768]{1,0:T(8,128)(2,1)S(1)} %get-tuple-element.384.down0), channel_id=1, source_target_pairs={{0,1},{1,0},{2,3},{3,2},{4,5},{5,4},{6,7},{7,6},{8,9},{9,8},{10,11... | collective-permute-start | bytes 3538952 | tf_op jit(solution)/shard_map/ppermute | solution.py:703
  86.7 27.0 %collective-permute-start.13 = (bf16[384,768]{1,0:T(8,128)(2,1)}, bf16[384,768]{1,0:T(8,128)(2,1)S(1)}, u32[]{:S(2)}, u32[]{:S(2)}) collective-permute-start(bf16[384,768]{1,0:T(8,128)(2,1)} %collective-permute-done.12.down2), channel_id=1, source_target_pairs={{0,4},{4,0},{8,12},{12,8},{16,20},{20,16},{24,28},{28,24},{1,5},{5... | collective-permute-start | bytes 1769480 | tf_op jit(solution)/shard_map/ppermute | solution.py:703
  114.5 36.3 %collective-permute-start.22 = (bf16[768,768]{1,0:T(8,128)(2,1)S(1)}, bf16[768,768]{1,0:T(8,128)(2,1)S(1)}, u32[]{:S(2)}, u32[]{:S(2)}) collective-permute-start(bf16[768,768]{1,0:T(8,128)(2,1)S(1)} %get-tuple-element.201.up0), channel_id=1, source_target_pairs={{0,1},{1,0},{2,3},{3,2},{4,5},{5,4},{6,7},{7,6},{8,9},{9,8},{10,11... | collective-permute-start | bytes 3538952 | tf_op jit(solution)/shard_map/ppermute | solution.py:703
  114.9 55.9 %collective-permute-start.27 = (bf16[768,768]{1,0:T(8,128)(2,1)S(1)}, bf16[768,768]{1,0:T(8,128)(2,1)S(1)}, u32[]{:S(2)}, u32[]{:S(2)}) collective-permute-start(bf16[768,768]{1,0:T(8,128)(2,1)S(1)} %get-tuple-element.202.down0), channel_id=1, source_target_pairs={{0,1},{1,0},{2,3},{3,2},{4,5},{5,4},{6,7},{7,6},{8,9},{9,8},{10,11... | collective-permute-start | bytes 3538952 | tf_op jit(solution)/shard_map/ppermute | solution.py:703
  115.0 36.5 %collective-permute-start.24 = (bf16[384,768]{1,0:T(8,128)(2,1)}, bf16[384,768]{1,0:T(8,128)(2,1)S(1)}, u32[]{:S(2)}, u32[]{:S(2)}) collective-permute-start(bf16[384,768]{1,0:T(8,128)(2,1)} %collective-permute-done.23.up2), channel_id=1, source_target_pairs={{0,4},{4,0},{8,12},{12,8},{16,20},{20,16},{24,28},{28,24},{1,5},{5... | collective-permute-start | bytes 1769480 | tf_op jit(solution)/shard_map/ppermute | solution.py:703
  116.6 35.9 %collective-permute-start.29 = (bf16[384,768]{1,0:T(8,128)(2,1)}, bf16[384,768]{1,0:T(8,128)(2,1)S(1)}, u32[]{:S(2)}, u32[]{:S(2)}) collective-permute-start(bf16[384,768]{1,0:T(8,128)(2,1)} %collective-permute-done.28.down2), channel_id=1, source_target_pairs={{0,4},{4,0},{8,12},{12,8},{16,20},{20,16},{24,28},{28,24},{1,5},{5... | collective-permute-start | bytes 1769480 | tf_op jit(solution)/shard_map/ppermute | solution.py:703
  152.5 17.8 %collective-permute-start.25 = (bf16[384,768]{1,0:T(8,128)(2,1)}, bf16[384,768]{1,0:T(8,128)(2,1)S(1)}, u32[]{:S(2)}, u32[]{:S(2)}) collective-permute-start(bf16[384,768]{1,0:T(8,128)(2,1)} %collective-permute-done.23.up2), channel_id=1, source_target_pairs={{0,1},{1,0},{2,3},{3,2},{4,5},{5,4},{6,7},{7,6},{8,9},{9,8},{10,11... | collective-permute-start | bytes 1769480 | tf_op jit(solution)/shard_map/ppermute | solution.py:703
  152.9 18.6 %collective-permute-start.30 = (bf16[384,768]{1,0:T(8,128)(2,1)}, bf16[384,768]{1,0:T(8,128)(2,1)S(1)}, u32[]{:S(2)}, u32[]{:S(2)}) collective-permute-start(bf16[384,768]{1,0:T(8,128)(2,1)} %collective-permute-done.28.down2), channel_id=1, source_target_pairs={{0,1},{1,0},{2,3},{3,2},{4,5},{5,4},{6,7},{7,6},{8,9},{9,8},{10,11... | collective-permute-start | bytes 1769480 | tf_op jit(solution)/shard_map/ppermute | solution.py:703
  230.6 27.7 %collective-permute-start.38 = (bf16[2,8,96,1536]{3,2,1,0:T(8,128)(2,1)}, bf16[2,8,96,1536]{3,2,1,0:T(8,128)(2,1)}, u32[]{:S(2)}, u32[]{:S(2)}) collective-permute-start(bf16[2,8,96,1536]{3,2,1,0:T(8,128)(2,1)} %bitcast.251), channel_id=1, source_target_pairs={{0,1},{1,0},{2,3},{3,2},{4,5},{5,4},{6,7},{7,6},{8,9},{9,8},{10,11... | collective-permute-start | bytes 14155784 | tf_op jit(solution)/shard_map/ppermute | solution.py:703
  268.5 51.2 %collective-permute-start.39 = (bf16[2,8,48,1536]{3,2,1,0:T(8,128)(2,1)}, bf16[2,8,48,1536]{3,2,1,0:T(8,128)(2,1)S(1)}, u32[]{:S(2)}, u32[]{:S(2)}) collective-permute-start(bf16[2,8,48,1536]{3,2,1,0:T(8,128)(2,1)} %get-tuple-element.234), channel_id=1, source_target_pairs={{0,1},{1,0},{2,3},{3,2},{4,5},{5,4},{6,7},{7,6},{8,9},{9,8},{10,11... | collective-permute-start | bytes 7077896 | tf_op jit(solution)/shard_map/ppermute | solution.py:703
  312.1 76.3 %collective-permute-start.46 = (bf16[2,8,48,1920]{3,2,1,0:T(8,128)(2,1)}, bf16[2,8,48,1920]{3,2,1,0:T(8,128)(2,1)}, u32[]{:S(2)}, u32[]{:S(2)}) collective-permute-start(bf16[2,8,48,1920]{3,2,1,0:T(8,128)(2,1)} %get-tuple-element.257), channel_id=1, source_target_pairs={{0,1},{1,0},{2,3},{3,2},{4,5},{5,4},{6,7},{7,6},{8,9},{9,8},{10,11... | collective-permute-start | bytes 8847368 | tf_op jit(solution)/shard_map/ppermute | solution.py:703
  318.3 53.8 %collective-permute-start.43 = (bf16[2,4,96,1536]{3,2,0,1:T(8,128)(2,1)}, bf16[2,4,96,1536]{3,2,0,1:T(8,128)(2,1)S(1)}, u32[]{:S(2)}, u32[]{:S(2)}) collective-permute-start(bf16[2,4,96,1536]{3,2,0,1:T(8,128)(2,1)} %bitcast.227), channel_id=1, source_target_pairs={{0,4},{4,0},{8,12},{12,8},{16,20},{20,16},{24,28},{28,24},{1,5},{5... | collective-permute-start | bytes 7077896 | tf_op jit(solution)/shard_map/ppermute | solution.py:703
  320.6 51.6 %collective-permute-start.44 = (bf16[4,2,48,1536]{3,2,1,0:T(8,128)(2,1)S(1)}, bf16[4,2,48,1536]{3,2,1,0:T(8,128)(2,1)S(1)}, u32[]{:S(2)}, u32[]{:S(2)}) collective-permute-start(bf16[4,2,48,1536]{3,2,1,0:T(8,128)(2,1)S(1)} %bitcast.246), channel_id=1, source_target_pairs={{0,2},{1,3},{2,0},{3,1},{4,6},{5,7},{6,4},{7,5},{8,10},{9,11},{10,... | collective-permute-start | bytes 3538952 | tf_op jit(solution)/shard_map/ppermute | solution.py:703
  335.1 54.9 %collective-permute-start.40 = (bf16[98,768]{1,0:T(8,128)(2,1)}, bf16[98,768]{1,0:T(8,128)(2,1)}, u32[]{:S(2)}, u32[]{:S(2)}) collective-permute-start(bf16[98,768]{1,0:T(8,128)(2,1)} %get-tuple-element.239), channel_id=1, source_target_pairs={{0,1},{1,0},{2,3},{3,2},{4,5},{5,4},{6,7},{7,6},{8,9},{9,8},{10,11... | collective-permute-start | bytes 451592 | tf_op jit(solution)/shard_map/ppermute | solution.py:703
  335.1 57.4 %collective-permute-start.41 = (bf16[98,768]{1,0:T(8,128)(2,1)}, bf16[98,768]{1,0:T(8,128)(2,1)}, u32[]{:S(2)}, u32[]{:S(2)}) collective-permute-start(bf16[98,768]{1,0:T(8,128)(2,1)} %get-tuple-element.240), channel_id=1, source_target_pairs={{0,2},{1,3},{2,0},{3,1},{4,6},{5,7},{6,4},{7,5},{8,10},{9,11},{10,... | collective-permute-start | bytes 451592 | tf_op jit(solution)/shard_map/ppermute | solution.py:703
  372.1 21.8 %collective-permute-start.42 = (bf16[98,768]{1,0:T(8,128)(2,1)}, bf16[98,768]{1,0:T(8,128)(2,1)}, u32[]{:S(2)}, u32[]{:S(2)}) collective-permute-start(bf16[98,768]{1,0:T(8,128)(2,1)} %get-tuple-element.241), channel_id=1, source_target_pairs={{0,3},{1,2},{2,1},{3,0},{4,7},{5,6},{6,5},{7,4},{8,11},{9,10},{10,... | collective-permute-start | bytes 451592 | tf_op jit(solution)/shard_map/ppermute | solution.py:703
  374.0 20.0 %collective-permute-start.45 = (bf16[4,48,1536]{2,1,0:T(8,128)(2,1)S(1)}, bf16[4,48,1536]{2,1,0:T(8,128)(2,1)}, u32[]{:S(2)}, u32[]{:S(2)}) collective-permute-start(bf16[4,48,1536]{2,1,0:T(8,128)(2,1)S(1)} %dynamic-slice_bitcast_fusion.8), channel_id=1, source_target_pairs={{0,4},{4,0},{8,12},{12,8},{16,20},{20,16},{24,28},{28,24},{1,5},{5... | collective-permute-start | bytes 1769480 | tf_op jit(solution)/shard_map/ppermute | solution.py:703
  388.4 18.2 %collective-permute-start.50 = (bf16[2,96,1536]{2,1,0:T(8,128)(2,1)S(1)}, bf16[2,96,1536]{2,1,0:T(8,128)(2,1)S(1)}, u32[]{:S(2)}, u32[]{:S(2)}) collective-permute-start(bf16[2,96,1536]{2,1,0:T(8,128)(2,1)S(1)} %get-tuple-element.380), channel_id=1, source_target_pairs={{0,8},{4,12},{8,16},{12,20},{16,24},{20,28},{24,0},{28,4},{1,9},{5... | collective-permute-start | bytes 1769480 | tf_op jit(solution)/shard_map/ppermute | solution.py:707
  390.0 41.9 %collective-permute-start.51 = (bf16[2,96,1536]{2,1,0:T(8,128)(2,1)}, bf16[2,96,1536]{2,1,0:T(8,128)(2,1)S(1)}, u32[]{:S(2)}, u32[]{:S(2)}) collective-permute-start(bf16[2,96,1536]{2,1,0:T(8,128)(2,1)} %get-tuple-element.379), channel_id=1, source_target_pairs={{0,16},{4,20},{8,24},{12,28},{16,0},{20,4},{24,8},{28,12},{1,17},{... | collective-permute-start | bytes 1769480 | tf_op jit(solution)/shard_map/ppermute | solution.py:707
  392.6 39.3 %collective-permute-start.52 = (bf16[2,96,1536]{2,1,0:T(8,128)(2,1)}, bf16[2,96,1536]{2,1,0:T(8,128)(2,1)S(1)}, u32[]{:S(2)}, u32[]{:S(2)}) collective-permute-start(bf16[2,96,1536]{2,1,0:T(8,128)(2,1)} %get-tuple-element.378), channel_id=1, source_target_pairs={{0,24},{4,28},{8,0},{12,4},{16,8},{20,12},{24,16},{28,20},{1,25},{... | collective-permute-start | bytes 1769480 | tf_op jit(solution)/shard_map/ppermute | solution.py:707
  395.1 40.0 %collective-permute-start.53 = (bf16[48,1536]{1,0:T(8,128)(2,1)S(1)}, bf16[48,1536]{1,0:T(8,128)(2,1)S(1)}, u32[]{:S(2)}, u32[]{:S(2)}) collective-permute-start(bf16[48,1536]{1,0:T(8,128)(2,1)S(1)} %get-tuple-element.407), channel_id=1, source_target_pairs={{0,8},{4,12},{8,16},{12,20},{16,24},{20,28},{24,0},{28,4},{1,9},{5... | collective-permute-start | bytes 442376 | tf_op jit(solution)/shard_map/ppermute | solution.py:707
  395.9 56.5 %collective-permute-start.54 = (bf16[48,1536]{1,0:T(8,128)(2,1)S(1)}, bf16[48,1536]{1,0:T(8,128)(2,1)S(1)}, u32[]{:S(2)}, u32[]{:S(2)}) collective-permute-start(bf16[48,1536]{1,0:T(8,128)(2,1)S(1)} %get-tuple-element.406), channel_id=1, source_target_pairs={{0,16},{4,20},{8,24},{12,28},{16,0},{20,4},{24,8},{28,12},{1,17},{... | collective-permute-start | bytes 442376 | tf_op jit(solution)/shard_map/ppermute | solution.py:707
  406.6 57.9 %collective-permute-start.56 = (bf16[4,2,48,1920]{3,2,1,0:T(8,128)(2,1)S(1)}, bf16[4,2,48,1920]{3,2,1,0:T(8,128)(2,1)S(1)}, u32[]{:S(2)}, u32[]{:S(2)}) collective-permute-start(bf16[4,2,48,1920]{3,2,1,0:T(8,128)(2,1)S(1)} %bitcast.245), channel_id=1, source_target_pairs={{0,2},{1,3},{2,0},{3,1},{4,6},{5,7},{6,4},{7,5},{8,10},{9,11},{10,... | collective-permute-start | bytes 4423688 | tf_op jit(solution)/shard_map/ppermute | solution.py:703
  431.9 32.1 %collective-permute-start.47 = (bf16[104,768]{1,0:T(8,128)(2,1)}, bf16[104,768]{1,0:T(8,128)(2,1)S(1)}, u32[]{:S(2)}, u32[]{:S(2)}) collective-permute-start(bf16[104,768]{1,0:T(8,128)(2,1)} %get-tuple-element.266), channel_id=1, source_target_pairs={{0,1},{1,0},{2,3},{3,2},{4,5},{5,4},{6,7},{7,6},{8,9},{9,8},{10,11... | collective-permute-start | bytes 479240 | tf_op jit(solution)/shard_map/ppermute | solution.py:703
  431.9 32.5 %collective-permute-start.48 = (bf16[104,768]{1,0:T(8,128)(2,1)}, bf16[104,768]{1,0:T(8,128)(2,1)S(1)}, u32[]{:S(2)}, u32[]{:S(2)}) collective-permute-start(bf16[104,768]{1,0:T(8,128)(2,1)} %get-tuple-element.267), channel_id=1, source_target_pairs={{0,2},{1,3},{2,0},{3,1},{4,6},{5,7},{6,4},{7,5},{8,10},{9,11},{10,... | collective-permute-start | bytes 479240 | tf_op jit(solution)/shard_map/ppermute | solution.py:703
  435.1 29.4 %collective-permute-start.49 = (bf16[104,768]{1,0:T(8,128)(2,1)}, bf16[104,768]{1,0:T(8,128)(2,1)S(1)}, u32[]{:S(2)}, u32[]{:S(2)}) collective-permute-start(bf16[104,768]{1,0:T(8,128)(2,1)} %get-tuple-element.268), channel_id=1, source_target_pairs={{0,3},{1,2},{2,1},{3,0},{4,7},{5,6},{6,5},{7,4},{8,11},{9,10},{10,... | collective-permute-start | bytes 479240 | tf_op jit(solution)/shard_map/ppermute | solution.py:703
  463.9 70.6 %collective-permute-start.59 = (bf16[2,8,96,768]{3,2,1,0:T(8,128)(2,1)}, bf16[2,8,96,768]{3,2,1,0:T(8,128)(2,1)}, u32[]{:S(2)}, u32[]{:S(2)}) collective-permute-start(bf16[2,8,96,768]{3,2,1,0:T(8,128)(2,1)} %bitcast.252), channel_id=1, source_target_pairs={{0,1},{1,0},{2,3},{3,2},{4,5},{5,4},{6,7},{7,6},{8,9},{9,8},{10,11... | collective-permute-start | bytes 7077896 | tf_op jit(solution)/shard_map/ppermute | solution.py:703
  464.0 70.5 %collective-permute-start.60 = (bf16[2,8,96,768]{3,2,1,0:T(8,128)(2,1)}, bf16[2,8,96,768]{3,2,1,0:T(8,128)(2,1)}, u32[]{:S(2)}, u32[]{:S(2)}) collective-permute-start(bf16[2,8,96,768]{3,2,1,0:T(8,128)(2,1)} %bitcast.253), channel_id=1, source_target_pairs={{0,1},{1,0},{2,3},{3,2},{4,5},{5,4},{6,7},{7,6},{8,9},{9,8},{10,11... | collective-permute-start | bytes 7077896 | tf_op jit(solution)/shard_map/ppermute | solution.py:703
  504.3 30.2 %collective-permute-start.72 = (bf16[4,48,1920]{2,1,0:T(8,128)(2,1)}, bf16[4,48,1920]{2,1,0:T(8,128)(2,1)}, u32[]{:S(2)}, u32[]{:S(2)}) collective-permute-start(bf16[4,48,1920]{2,1,0:T(8,128)(2,1)} %dynamic-slice_bitcast_fusion.2), channel_id=1, source_target_pairs={{0,4},{4,0},{8,12},{12,8},{16,20},{20,16},{24,28},{28,24},{1,5},{5... | collective-permute-start | bytes 2211848 | tf_op jit(solution)/shard_map/ppermute | solution.py:703
  506.5 17.6 %collective-permute-start.104 = (f32[12,768]{1,0:T(8,128)S(1)}, f32[12,768]{1,0:T(8,128)S(1)}, u32[]{:S(2)}, u32[]{:S(2)}) collective-permute-start(f32[12,768]{1,0:T(8,128)S(1)} %add.435), channel_id=1, source_target_pairs={{0,4},{4,0},{8,12},{12,8},{16,20},{20,16},{24,28},{28,24},{1,5},{5... | collective-permute-start | bytes 110600 | tf_op jit(solution)/shard_map/ppermute | solution.py:703
  532.0 56.7 %collective-permute-start.57 = (bf16[96,1536]{1,0:T(8,128)(2,1)S(1)}, bf16[96,1536]{1,0:T(8,128)(2,1)S(1)}, u32[]{:S(2)}, u32[]{:S(2)}) collective-permute-start(bf16[96,1536]{1,0:T(8,128)(2,1)S(1)} %slice_bitcast_fusion.11), channel_id=1, source_target_pairs={{0,2},{1,3},{2,0},{3,1},{4,6},{5,7},{6,4},{7,5},{8,10},{9,11},{10,... | collective-permute-start | bytes 884744 | tf_op jit(solution)/shard_map/ppermute | solution.py:703
  550.7 38.1 %collective-permute-start.61 = (bf16[2,8,48,1536]{3,2,1,0:T(8,128)(2,1)}, bf16[2,8,48,1536]{3,2,1,0:T(8,128)(2,1)S(1)}, u32[]{:S(2)}, u32[]{:S(2)}) collective-permute-start(bf16[2,8,48,1536]{3,2,1,0:T(8,128)(2,1)} %get-tuple-element.307), channel_id=1, source_target_pairs={{0,1},{1,0},{2,3},{3,2},{4,5},{5,4},{6,7},{7,6},{8,9},{9,8},{10,11... | collective-permute-start | bytes 7077896 | tf_op jit(solution)/shard_map/ppermute | solution.py:703
  554.5 34.3 %collective-permute-start.62 = (bf16[4,2,96,768]{3,2,0,1:T(8,128)(2,1)S(1)}, bf16[4,2,96,768]{3,2,0,1:T(8,128)(2,1)S(1)}, u32[]{:S(2)}, u32[]{:S(2)}) collective-permute-start(bf16[4,2,96,768]{3,2,0,1:T(8,128)(2,1)S(1)} %copy.87), channel_id=1, source_target_pairs={{0,2},{1,3},{2,0},{3,1},{4,6},{5,7},{6,4},{7,5},{8,10},{9,11},{10,... | collective-permute-start | bytes 3538952 | tf_op jit(solution)/shard_map/ppermute | solution.py:703
  558.5 30.2 %collective-permute-start.63 = (bf16[2,4,96,768]{3,2,1,0:T(8,128)(2,1)S(1)}, bf16[2,4,96,768]{3,2,1,0:T(8,128)(2,1)S(1)}, u32[]{:S(2)}, u32[]{:S(2)}) collective-permute-start(bf16[2,4,96,768]{3,2,1,0:T(8,128)(2,1)S(1)} %dynamic-slice_bitcast_fusion.1), channel_id=1, source_target_pairs={{0,4},{4,0},{8,12},{12,8},{16,20},{20,16},{24,28},{28,24},{1,5},{5... | collective-permute-start | bytes 3538952 | tf_op jit(solution)/shard_map/ppermute | solution.py:703
  562.5 26.2 %collective-permute-start.58 = (bf16[48,1536]{1,0:T(8,128)(2,1)S(1)}, bf16[48,1536]{1,0:T(8,128)(2,1)S(1)}, u32[]{:S(2)}, u32[]{:S(2)}) collective-permute-start(bf16[48,1536]{1,0:T(8,128)(2,1)S(1)} %fusion.23), channel_id=1, source_target_pairs={{0,2},{1,3},{2,0},{3,1},{4,6},{5,7},{6,4},{7,5},{8,10},{9,11},{10,... | collective-permute-start | bytes 442376 | tf_op jit(solution)/shard_map/ppermute | solution.py:703
  589.7 25.6 %collective-permute-start.93 = (bf16[96,1536]{1,0:T(8,128)(2,1)}, bf16[96,1536]{1,0:T(8,128)(2,1)}, u32[]{:S(2)}, u32[]{:S(2)}) collective-permute-start(bf16[96,1536]{1,0:T(8,128)(2,1)} %maximum_select_fusion.6), channel_id=1, source_target_pairs={{0,1},{1,0},{2,3},{3,2},{4,5},{5,4},{6,7},{7,6},{8,9},{9,8},{10,11... | collective-permute-start | bytes 884744 | tf_op jit(solution)/shard_map/ppermute | solution.py:703
  601.2 79.3 %collective-permute-start.64 = (bf16[2,8,48,1152]{3,2,1,0:T(8,128)(2,1)}, bf16[2,8,48,1152]{3,2,1,0:T(8,128)(2,1)}, u32[]{:S(2)}, u32[]{:S(2)}) collective-permute-start(bf16[2,8,48,1152]{3,2,1,0:T(8,128)(2,1)} %get-tuple-element.315), channel_id=1, source_target_pairs={{0,1},{1,0},{2,3},{3,2},{4,5},{5,4},{6,7},{7,6},{8,9},{9,8},{10,11... | collective-permute-start | bytes 5308424 | tf_op jit(solution)/shard_map/ppermute | solution.py:703
  605.0 71.7 %collective-permute-start.86 = (bf16[2,4,48,1536]{3,2,1,0:T(8,128)(2,1)}, bf16[2,4,48,1536]{3,2,1,0:T(8,128)(2,1)}, u32[]{:S(2)}, u32[]{:S(2)}) collective-permute-start(bf16[2,4,48,1536]{3,2,1,0:T(8,128)(2,1)} %dynamic-slice_bitcast_fusion), channel_id=1, source_target_pairs={{0,4},{4,0},{8,12},{12,8},{16,20},{20,16},{24,28},{28,24},{1,5},{5... | collective-permute-start | bytes 3538952 | tf_op jit(solution)/shard_map/ppermute | solution.py:703
  606.0 40.1 %collective-permute-start.94 = (bf16[4,96,768]{2,1,0:T(8,128)(2,1)S(1)}, bf16[4,96,768]{2,1,0:T(8,128)(2,1)}, u32[]{:S(2)}, u32[]{:S(2)}) collective-permute-start(bf16[4,96,768]{2,1,0:T(8,128)(2,1)S(1)} %dynamic-slice_bitcast_fusion.3), channel_id=1, source_target_pairs={{0,4},{4,0},{8,12},{12,8},{16,20},{20,16},{24,28},{28,24},{1,5},{5... | collective-permute-start | bytes 1769480 | tf_op jit(solution)/shard_map/ppermute | solution.py:703
  614.2 35.6 %collective-permute-start.98 = (bf16[4,96,768]{2,1,0:T(8,128)(2,1)S(1)}, bf16[4,96,768]{2,1,0:T(8,128)(2,1)S(1)}, u32[]{:S(2)}, u32[]{:S(2)}) collective-permute-start(bf16[4,96,768]{2,1,0:T(8,128)(2,1)S(1)} %slice_bitcast_fusion.2), channel_id=1, source_target_pairs={{0,2},{1,3},{2,0},{3,1},{4,6},{5,7},{6,4},{7,5},{8,10},{9,11},{10,... | collective-permute-start | bytes 1769480 | tf_op jit(solution)/shard_map/ppermute | solution.py:703
  679.7 19.5 %collective-permute-start.79 = (bf16[2,4,48,768]{3,2,1,0:T(8,128)(2,1)S(1)}, bf16[2,4,48,768]{3,2,1,0:T(8,128)(2,1)S(1)}, u32[]{:S(2)}, u32[]{:S(2)}) collective-permute-start(bf16[2,4,48,768]{3,2,1,0:T(8,128)(2,1)S(1)} %dynamic-slice_bitcast_fusion.4), channel_id=1, source_target_pairs={{0,4},{4,0},{8,12},{12,8},{16,20},{20,16},{24,28},{28,24},{1,5},{5... | collective-permute-start | bytes 1769480 | tf_op jit(solution)/shard_map/ppermute | solution.py:703
  682.9 52.1 %collective-permute-start.65 = (bf16[4,2,48,1152]{3,2,1,0:T(8,128)(2,1)S(1)}, bf16[4,2,48,1152]{3,2,1,0:T(8,128)(2,1)S(1)}, u32[]{:S(2)}, u32[]{:S(2)}) collective-permute-start(bf16[4,2,48,1152]{3,2,1,0:T(8,128)(2,1)S(1)} %bitcast.247), channel_id=1, source_target_pairs={{0,2},{1,3},{2,0},{3,1},{4,6},{5,7},{6,4},{7,5},{8,10},{9,11},{10,... | collective-permute-start | bytes 2654216 | tf_op jit(solution)/shard_map/ppermute | solution.py:703
  699.3 20.4 %collective-permute-start.80 = (bf16[4,48,768]{2,1,0:T(8,128)(2,1)S(1)}, bf16[4,48,768]{2,1,0:T(8,128)(2,1)S(1)}, u32[]{:S(2)}, u32[]{:S(2)}) collective-permute-start(bf16[4,48,768]{2,1,0:T(8,128)(2,1)S(1)} %slice_bitcast_fusion.9), channel_id=1, source_target_pairs={{0,2},{1,3},{2,0},{3,1},{4,6},{5,7},{6,4},{7,5},{8,10},{9,11},{10,... | collective-permute-start | bytes 884744 | tf_op jit(solution)/shard_map/ppermute | solution.py:703
  (157 other events, 1808.7 us)
where the time goes:
time: 778 us; the launch traced here: 767 us
  waiting for transfers between devices  306 us (39%)
  Pallas kernels  283 us (36%)
  starting transfers between devices  91.4 us (12%)
  other arithmetic  45.2 us (6%)
  local copies, waits for them, and re-layouts  38.4 us (5%)
    ppermute x81, waiting for transfers between devices, swap(): lax.ppermute(values, axis, [(index, index ^ bit) for index in range(size)])  233 us
    pallas_call x8, Pallas kernels, outer_group(): pl.pallas_call(partial(outer_kernel, split, steps), out_shape=[shape, sha...  86.5 us
    ppermute x27, waiting for transfers between devices, ring(): lax.ppermute(values, DP, [(start * 2 + near, (start + step) % far * 2 + n...  73.1 us
    pallas_call x2, Pallas kernels, body(): call(partial(time_backward, dims, layer), [((rows, width), HALF), ((rows,...  57.5 us
    ppermute x81, starting transfers between devices, swap(): lax.ppermute(values, axis, [(index, index ^ bit) for index in range(size)])  51.5 us
    ppermute x27, starting transfers between devices, ring(): lax.ppermute(values, DP, [(start * 2 + near, (start + step) % far * 2 + n...  39.9 us
    pallas_call x2, Pallas kernels, body(): call(partial(feed_forward, dims, layer), [((rows, width), HALF), ((rows,...  35.6 us
    pallas_call x2, Pallas kernels, body(): call(partial(space_backward, dims, layer), [((span, 3 * width), HALF)] +...  28.8 us
  transfers between devices with their start and end apart: 108, of which 44 were waited for; matrix products, arithmetic and copies ran while one was open for 8% of the time, Pallas kernels for 29%

commit v1 on v0

v1 whole, which is shorter than its diff:
```python
from functools import partial

import jax
import jax.numpy as jnp
from jax import lax
from jax.experimental import pallas as pl
from jax.experimental.pallas import tpu as pltpu
from jax.sharding import PartitionSpec as P

HEADS = 12
EPS = 1e-06
HIGH = lax.Precision.HIGHEST
HALF = jnp.bfloat16
FULL = jnp.float32
NEAR = 4
TENSOR = "tensor"
DP = "dp"
TILE = 256
VMEM_BYTES = 58 << 20
SMEM = pl.BlockSpec(memory_space=pltpu.SMEM)
SMALL, ROWS, FAR = range(3)
HBM = pl.BlockSpec(memory_space=pltpu.HBM)
ROOT_HALF = 0.5**0.5
DENSITY = (2.0 * 3.141592653589793) ** -0.5


def up_to(value, step):
    return -(-value // step) * step


def dot(left, right):
    return jnp.dot(left, right, preferred_element_type=FULL)


def dot_back(left, right):
    return lax.dot_general(left, right, (((1,), (1,)), ((), ())), preferred_element_type=FULL)


def dot_outer(left, right):
    return lax.dot_general(left, right, (((0,), (0,)), ((), ())), preferred_element_type=FULL)


def unit_of(values):
    centred = values - jnp.mean(values, -1, keepdims=True)
    inverse = lax.rsqrt(jnp.mean(centred * centred, -1, keepdims=True) + EPS)
    return centred * inverse, inverse


def unit_back(grad, unit, inverse, gain):
    scaled = grad * gain
    inner = (
        scaled
        - jnp.mean(scaled, -1, keepdims=True)
        - unit * jnp.mean(scaled * unit, -1, keepdims=True)
    )
    return inner * inverse


def head_lanes(head_size, half):
    lane = lax.broadcasted_iota(jnp.int32, (1, 2 * head_size), 1)
    return (lane // head_size) == half


def over_rows(rows, step, run):
    for start in range(0, rows, step):
        run(start, min(step, rows - start))


def two_heads(values, head_size):
    return jnp.concatenate(
        [jnp.where(head_lanes(head_size, half), values, 0) for half in range(2)], 0
    )


def one_of_two(values, head_size):
    rows = values.shape[0] // 2
    return jnp.where(head_lanes(head_size, 0), values[:rows], values[rows:])


def interleave(order, frame, frames, values):
    for group in range(order.shape[0]):
        part = values[:, group * 128 : (group + 1) * 128]
        order[group, pl.ds(frame, values.shape[0], stride=frames), :] = part


def pick(order, frame, frames, patches):
    own = pl.ds(frame, patches, stride=frames)
    return jnp.concatenate([order[group, own, :] for group in range(order.shape[0])], 1)


def shard_copies(place_ref, refs, target, which):
    own, core, far_first, far_second, core_first, core_second = refs
    half = far_first.shape[1]
    first = pl.multiple_of(place_ref[1] * half, half)
    second = pl.multiple_of((1 - place_ref[1]) * half, half)
    return [
        [(own, target.at[0])],
        [(core.at[which], target.at[1])],
        [
            (far_first.at[which], target.at[2, pl.ds(first, half)]),
            (far_second.at[which], target.at[2, pl.ds(second, half)]),
        ],
        [
            (core_first.at[which], target.at[3, pl.ds(first, half)]),
            (core_second.at[which], target.at[3, pl.ds(second, half)]),
        ],
    ]


def start_shards(place_ref, own, peers, up_ref, down_ref, sems):
    waits = []
    index = 0
    for pairs in zip(
        shard_copies(place_ref, (own[0],) + peers, up_ref, 0),
        shard_copies(place_ref, (own[1],) + peers, down_ref, 1),
    ):
        group = []
        for source, target in pairs[0] + pairs[1]:
            copy = pltpu.make_async_copy(source, target, sems.at[index])
            copy.start()
            group.append(copy)
            index += 1
        waits.append(group)
    return waits


def fetch(sources, targets, sems):
    copies = [
        pltpu.make_async_copy(source, target, sems.at[index])
        for index, (source, target) in enumerate(zip(sources, targets))
    ]
    for copy in copies:
        copy.start()
    return copies


def attend_forward(load, store, store_total, heads, head_size, bias):
    scale = head_size**-0.5
    totals = None
    if bias.shape[0] > 1:
        bias = jnp.concatenate([bias, bias], 0)
    for pair in range(heads // 2):
        query, key, value = (load(part, pair) for part in range(3))
        rows = query.shape[0]
        scores = dot_back(two_heads(query, head_size), key) * scale + bias
        top = jnp.max(scores, -1, keepdims=True)
        raised = jnp.exp(scores - top)
        total = jnp.sum(raised, -1, keepdims=True)
        mixed = dot(raised.astype(HALF), value) * (1.0 / total)
        log_total = top + jnp.log(total)
        if totals is None:
            lanes = lax.broadcasted_iota(jnp.int32, (rows, 128), 1)
            totals = jnp.zeros(lanes.shape, FULL)
        totals = jnp.where(lanes == pair * 2, log_total[:rows], totals)
        totals = jnp.where(lanes == pair * 2 + 1, log_total[rows:], totals)
        store(pair, one_of_two(mixed, head_size))
    store_total(totals)


def attend_backward(load, load_grad, totals, store, heads, head_size, bias):
    scale = head_size**-0.5
    totals = totals.T
    if bias.shape[1] > 1:
        bias = jnp.concatenate([bias, bias], 1)
    for pair in range(heads // 2):
        query, key, value = (load(part, pair) for part in range(3))
        query = two_heads(query, head_size)
        grad = two_heads(load_grad(pair), head_size)
        total = jnp.concatenate([totals[2 * pair + half : 2 * pair + half + 1] for half in range(2)], 1)
        prob = jnp.exp(dot_back(key, query) * scale + (bias - total))
        grad_prob = dot_back(value, grad)
        delta = jnp.sum(prob * grad_prob, 0, keepdims=True)
        grad_score = (prob * (grad_prob - delta)).astype(HALF)
        store(0, pair, one_of_two(dot_outer(grad_score, key), head_size) * scale)
        store(1, pair, dot(grad_score, query) * scale)
        store(2, pair, dot(prob.astype(HALF), grad))


def row_blocks(rows, step):
    return [(start, min(step, rows - start)) for start in range(0, rows, step)]


def time_forward(dims, layer, place_ref, x_ref, bias_ref, gain_ref, shift_ref, in_hbm, out_hbm, mix_hbm,
                 normed_ref, triple_ref, total_ref, mixed_ref, projected_ref, after_ref,
                 send0, send1, send2, send3, class_ref,
                 in_ref, out_ref, mix_ref, order, plain, blocks, sems):
    frames, patches, width, heads, groups = dims
    count = frames * patches
    rows = x_ref.shape[0]
    step = bias_ref.shape[0]
    copies = fetch(
        (in_hbm.at[layer], out_hbm.at[layer], mix_hbm.at[layer]), (in_ref, out_ref, mix_ref), sems
    )
    gain = gain_ref[layer, 0:1, :]
    shift = shift_ref[layer, 0:1, :]
    for frame in range(frames):
        unit, unused = unit_of(x_ref[frame * patches : (frame + 1) * patches, :])
        interleave(order, frame, frames, unit * gain + shift)
    for group in range(width // 128):
        order[group, count:, :] = jnp.zeros((rows - count, 128), FULL)
        normed_ref[:, group * 128 : (group + 1) * 128] = order[group].astype(HALF)
    normed_ref.flush()
    copies[0].wait()
    for column in range(0, 3 * width, TILE):
        part = slice(column, column + TILE)
        triple_ref[:, part] = dot(normed_ref[...], in_ref[:, part]).astype(HALF)
    triple_ref.flush()
    for begin, size in row_blocks(rows, step):
        own = slice(begin, begin + size)

        def load(part, pair):
            start = part * width + pair * 128
            return triple_ref[own, start : start + 128]

        def store(pair, mixed):
            order[pair, own, :] = mixed

        def store_total(totals):
            total_ref[own, :] = totals

        attend_forward(
            load, store, store_total, heads, width // heads, bias_ref[0:size, 0:size]
        )
    for frame in range(frames):
        plain[frame * patches : (frame + 1) * patches, :] = pick(order, frame, frames, patches)
    plain[count:, :] = jnp.zeros((rows - count, width), FULL)
    mixed_ref[...] = plain[...].astype(HALF)
    mixed_ref.flush()
    copies[1].wait()
    for column in range(0, width, TILE):
        part = slice(column, column + TILE)
        projected_ref[:, part] = dot(mixed_ref[...], out_ref[:, part]).astype(HALF)
    projected_ref.flush()
    copies[2].wait()
    for column in range(0, width, TILE):
        part = slice(column, column + TILE)
        after_ref[:, part] = x_ref[:, part] + dot(projected_ref[...], mix_ref[:, part])
    after_ref.flush()
    gain = gain_ref[layer, 1:2, :]
    shift = shift_ref[layer, 1:2, :]

    def norm(start, size):
        own = slice(start, start + size)
        unit, unused = unit_of(after_ref[own, :])
        plain[own, :] = unit * gain + shift

    over_rows(rows, 80, norm)
    send_blocks(plain, blocks, (send0, send1, send2, send3), place_ref[0], count // groups)
    class_ref[...] = plain[count:, :]


def send_blocks(plain, blocks, sends, place, size):
    groups = len(sends)
    for group in range(groups):
        blocks[group, 0:size, :] = plain[group * size : (group + 1) * size, :]
    for away in range(groups):
        sends[away][...] = blocks[place ^ away][0:size].astype(HALF)


def space_forward(dims, layer, place_ref, clip_ref, class_ref, piece0, piece1, piece2, piece3, in_hbm,
                  normed_ref, triple_ref, total_ref, send0, send1, send2, send3,
                  in_ref, plain, sems):
    frames, patches, width, heads, groups = dims
    own_frames = frames // groups
    seq = groups * patches
    rows = normed_ref.shape[0] // own_frames
    copies = fetch((in_hbm.at[layer],), (in_ref,), sems)
    pieces = [piece0, piece1, piece2, piece3]
    for away, piece in enumerate(pieces):
        values = piece[...].astype(FULL)
        for frame in range(own_frames):
            start = frame * rows + away * patches
            plain[start : start + patches, :] = values[frame * patches : (frame + 1) * patches]
    for frame in range(own_frames):
        start = frame * rows + seq
        plain[start : start + rows - seq, :] = jnp.zeros((rows - seq, width), FULL)
        clip = clip_ref[place_ref[0] * own_frames + frame]
        plain[start : start + 1, :] = class_ref[pl.ds(clip, 1), :]
    normed_ref[...] = plain[...].astype(HALF)
    normed_ref.flush()
    copies[0].wait()
    for column in range(0, 3 * width, TILE):
        part = slice(column, column + TILE)
        triple_ref[:, part] = dot(normed_ref[...], in_ref[:, part]).astype(HALF)
    triple_ref.flush()
    keys = lax.broadcasted_iota(jnp.int32, (1, rows), 1)
    bias = jnp.where(keys <= seq, 0.0, -1e30)

    for frame in range(own_frames):
        own = slice(frame * rows, (frame + 1) * rows)

        def load(part, pair):
            start = part * width + pair * 128
            return triple_ref[own, start : start + 128]

        def store(pair, mixed):
            plain[own, pair * 128 : (pair + 1) * 128] = mixed

        def store_total(totals):
            total_ref[own, :] = totals

        attend_forward(load, store, store_total, heads, width // heads, bias)
    return_pieces(plain, (send0, send1, send2, send3), own_frames, patches, rows)


def return_pieces(plain, sends, own_frames, patches, rows):
    seq = len(sends) * patches
    tail = []
    for frame in range(own_frames):
        row = plain[frame * rows + seq : frame * rows + seq + 1, :]
        high = row.astype(HALF).astype(FULL)
        tail += [high, row - high]
    size = own_frames * patches
    spare = sends[0].shape[0] - size - len(tail)
    tail.append(jnp.zeros((spare, plain.shape[1]), FULL))
    for away, send in enumerate(sends):
        kept = [
            plain[frame * rows + away * patches : frame * rows + (away + 1) * patches, :]
            for frame in range(own_frames)
        ]
        send[...] = jnp.concatenate(kept + tail, 0).astype(HALF)


def take_pieces(pieces, blocks, plain, frame_rows, place, size, own_frames):
    for away, piece in enumerate(pieces):
        blocks[place ^ away] = piece[...].astype(FULL)
    for group in range(len(pieces)):
        plain[group * size : (group + 1) * size, :] = blocks[group, 0:size, :]
        for frame in range(own_frames):
            start = size + 2 * frame
            frame_rows[group * own_frames + frame : group * own_frames + frame + 1, :] = (
                blocks[group, start : start + 1, :] + blocks[group, start + 1 : start + 2, :]
            )


def feed_forward(dims, layer, place_ref, piece0, piece1, piece2, piece3, share_ref, after_ref,
                 gain_ref, shift_ref, out_hbm,
                 up_hbm, down_hbm, peer1, peer2, peer3, peer4, peer5,
                 mixed_ref, rows_ref, normed_ref, active_ref, slope_ref, next_ref,
                 out_ref, up_ref, down_ref, plain, blocks, frame_rows, whole, out_sem, sems):
    frames, patches, width, heads, groups = dims
    count = frames * patches
    rows = after_ref.shape[0]
    size = count // groups
    place = place_ref[0]
    copies = fetch((out_hbm.at[layer],), (out_ref,), out_sem)
    own = (up_hbm.at[layer], down_hbm.at[layer])
    peers = (peer1, peer2, peer3, peer4, peer5)
    shards = start_shards(place_ref, own, peers, up_ref, down_ref, sems)
    take_pieces(
        (piece0, piece1, piece2, piece3), blocks, plain, frame_rows, place, size, frames // groups
    )
    plain[count:, :] = jnp.dot(
        share_ref[...], frame_rows[...], precision=HIGH, preferred_element_type=FULL
    )
    whole[...] = plain[...].astype(HALF)
    leader = jnp.where(place == 0, 1.0, 0.0).astype(FULL)
    kept = lax.broadcasted_iota(jnp.int32, (rows, 1), 0) < count
    kept = jnp.where(kept, 1.0, leader)
    mixed_ref[...] = (plain[...] * kept).astype(HALF)
    mixed_ref.flush()
    copies[0].wait()
    for column in range(0, width, TILE):
        part = slice(column, column + TILE)
        rows_ref[:, part] = after_ref[:, part] + dot(whole[...], out_ref[:, part])
    rows_ref.flush()
    gain = gain_ref[layer, 2:3, :]
    shift = shift_ref[layer, 2:3, :]

    def norm(start, size):
        own = slice(start, start + size)
        unit, unused = unit_of(rows_ref[own, :])
        plain[own, :] = unit * gain + shift

    over_rows(rows, 80, norm)
    whole[...] = plain[...].astype(HALF)
    normed_ref[...] = (plain[...] * kept).astype(HALF)
    normed_ref.flush()
    next_ref[...] = rows_ref[...]
    for away in range(groups):
        for copy in shards[away]:
            copy.wait()
        for column in range(0, width, TILE):
            part = slice(column, column + TILE)
            hidden = dot(whole[...], up_ref[away, :, part])
            below = 0.5 + 0.5 * lax.erf(hidden * ROOT_HALF)
            active = (hidden * below).astype(HALF)
            slope = below + hidden * (jnp.exp(hidden * hidden * -0.5) * DENSITY)
            start = away * width + column
            active_ref[:, start : start + TILE] = active
            slope_ref[:, start : start + TILE] = slope.astype(HALF)
        own = slice(away * width, (away + 1) * width)
        for column in range(0, width, TILE):
            part = slice(column, column + TILE)
            next_ref[:, part] += dot(active_ref[:, own], down_ref[away, :, part])
        end = count // 16 * 16
        active_ref[end:, own] = (active_ref[end:, own].astype(FULL) * kept[end:]).astype(HALF)
        active_ref.flush(own)
        slope_ref.flush(own)


def feed_backward(dims, layer, place_ref, clip_ref, grad_ref, slope_ref, rows_ref, share_ref, gain_ref,
                  out_hbm, up_hbm, down_hbm, peer1, peer2, peer3, peer4, peer5,
                  update_ref, hidden_ref, branch_ref, back_ref, norms_ref,
                  send0, send1, send2, send3, class_ref,
                  out_ref, up_ref, down_ref, total, plain, blocks, out_sem, sems):
    frames, patches, width, heads, groups = dims
    count = frames * patches
    rows = grad_ref.shape[0]
    place = place_ref[0]
    own_frames = frames // groups
    own = (up_hbm.at[layer], down_hbm.at[layer])
    peers = (peer1, peer2, peer3, peer4, peer5)
    shards = start_shards(place_ref, own, peers, up_ref, down_ref, sems)
    copies = fetch((out_hbm.at[layer],), (out_ref,), out_sem)
    update_ref[...] = grad_ref[...].astype(HALF)
    update_ref.flush()
    for away in range(groups):
        for copy in shards[away]:
            copy.wait()
        for column in range(0, width, TILE):
            part = slice(column, column + TILE)
            start = away * width + column
            grad_active = dot_back(update_ref[...], down_ref[away, part, :])
            slope = slope_ref[:, start : start + TILE].astype(FULL)
            grad_hidden = (grad_active * slope).astype(HALF)
            hidden_ref[:, start : start + TILE] = grad_hidden
        own = slice(away * width, (away + 1) * width)
        for column in range(0, width, TILE):
            part = slice(column, column + TILE)
            term = dot_back(hidden_ref[:, own], up_ref[away, part, :])
            if away == 0:
                total[:, part] = term
            else:
                total[:, part] += term
        hidden_ref.flush(own)
    gain = gain_ref[layer, 2:3, :]
    leader = jnp.where(place == 0, 1.0, 0.0).astype(FULL)
    norms_ref[...] = jnp.zeros(norms_ref.shape, FULL)
    def norm(start, size):
        own = slice(start, start + size)
        unit, inverse = unit_of(rows_ref[own, :])
        grad = total[own, :]
        back = grad_ref[own, :] + unit_back(grad, unit, inverse, gain)
        back_ref[own, :] = back
        branch_ref[own, :] = back.astype(HALF)
        kept = lax.broadcasted_iota(jnp.int32, (size, 1), 0) + start < count
        grad = jnp.where(kept, grad, grad * leader)
        norms_ref[0:1, :] += jnp.sum(grad * unit, 0, keepdims=True)
        norms_ref[1:2, :] += jnp.sum(grad, 0, keepdims=True)

    over_rows(rows, 80, norm)
    back_ref.flush()
    branch_ref.flush()
    copies[-1].wait()
    for column in range(0, width, TILE):
        part = slice(column, column + TILE)
        plain[:, part] = dot_back(branch_ref[...], out_ref[part, :])
    send_blocks(plain, blocks, (send0, send1, send2, send3), place, count // groups)
    for frame in range(own_frames):
        clip = clip_ref[place * own_frames + frame]
        class_ref[frame : frame + 1, :] = (
            plain[pl.ds(count + clip, 1), :] * share_ref[pl.ds(clip, 1), 0:1]
        )


def space_backward(dims, layer, piece0, piece1, piece2, piece3, class_ref, triple_ref, total_ref, in_hbm,
                   grad_ref, send0, send1, send2, send3,
                   in_ref, plain, mixed, sems):
    frames, patches, width, heads, groups = dims
    own_frames = frames // groups
    seq = groups * patches
    rows = triple_ref.shape[0] // own_frames
    copies = fetch((in_hbm.at[layer],), (in_ref,), sems)
    for away, piece in enumerate((piece0, piece1, piece2, piece3)):
        values = piece[...].astype(FULL)
        for frame in range(own_frames):
            start = frame * rows + away * patches
            plain[start : start + patches, :] = values[frame * patches : (frame + 1) * patches]
    for frame in range(own_frames):
        start = frame * rows + seq
        plain[start : start + rows - seq, :] = jnp.zeros((rows - seq, width), FULL)
        plain[start : start + 1, :] = class_ref[frame : frame + 1, :]
    mixed[...] = plain[...].astype(HALF)
    keys = lax.broadcasted_iota(jnp.int32, (rows, 1), 0)
    bias = jnp.where(keys <= seq, 0.0, -1e30)
    for frame in range(own_frames):
        own = slice(frame * rows, (frame + 1) * rows)

        def load(part, pair):
            start = part * width + pair * 128
            return triple_ref[own, start : start + 128]

        def load_grad(pair):
            return mixed[own, pair * 128 : (pair + 1) * 128]

        def store(part, pair, grad):
            start = part * width + pair * 128
            grad_ref[own, start : start + 128] = grad.astype(HALF)

        attend_backward(load, load_grad, total_ref[own, :], store, heads, width // heads, bias)
    grad_ref.flush()
    copies[0].wait()
    for column in range(0, width, TILE):
        part = slice(column, column + TILE)
        plain[:, part] = dot_back(grad_ref[...], in_ref[part, :])
    return_pieces(plain, (send0, send1, send2, send3), own_frames, patches, rows)


def time_backward(dims, layer, place_ref, piece0, piece1, piece2, piece3, member_ref, back_ref, after_ref, x_ref,
                  triple_ref, total_ref, bias_ref, gain_ref, in_hbm, out_hbm, mix_hbm,
                  branch_ref, projected_ref, grad_ref, next_ref, norms_ref,
                  in_ref, out_ref, mix_ref, order, plain, blocks, frame_rows, mixed, sems):
    frames, patches, width, heads, groups = dims
    count = frames * patches
    rows = x_ref.shape[0]
    step = bias_ref.shape[0]
    place = place_ref[0]
    copies = fetch(
        (mix_hbm.at[layer], out_hbm.at[layer], in_hbm.at[layer]), (mix_ref, out_ref, in_ref), sems
    )
    take_pieces(
        (piece0, piece1, piece2, piece3),
        blocks,
        plain,
        frame_rows,
        place,
        count // groups,
        frames // groups,
    )
    plain[count:, :] = jnp.dot(
        member_ref[...], frame_rows[...], precision=HIGH, preferred_element_type=FULL
    )
    leader = jnp.where(place == 0, 1.0, 0.0).astype(FULL)
    norms_ref[...] = jnp.zeros(norms_ref.shape, FULL)
    gain = gain_ref[layer, 1:2, :]

    def space_norm(start, size):
        own = slice(start, start + size)
        unit, inverse = unit_of(after_ref[own, :])
        grad = plain[own, :]
        back = back_ref[own, :] + unit_back(grad, unit, inverse, gain)
        next_ref[own, :] = back
        kept = lax.broadcasted_iota(jnp.int32, (size, 1), 0) + start < count
        branch_ref[own, :] = jnp.where(kept, back, 0.0).astype(HALF)
        grad = jnp.where(kept, grad, grad * leader)
        norms_ref[0:1, :] += jnp.sum(grad * unit, 0, keepdims=True)
        norms_ref[1:2, :] += jnp.sum(grad, 0, keepdims=True)

    over_rows(rows, 80, space_norm)
    branch_ref.flush()
    copies[0].wait()
    for column in range(0, width, TILE):
        part = slice(column, column + TILE)
        projected_ref[:, part] = dot_back(branch_ref[...], mix_ref[part, :]).astype(HALF)
    projected_ref.flush()
    copies[1].wait()
    for column in range(0, width, TILE):
        part = slice(column, column + TILE)
        plain[:, part] = dot_back(projected_ref[...], out_ref[part, :])
    for frame in range(frames):
        interleave(order, frame, frames, plain[frame * patches : (frame + 1) * patches, :])
    for group in range(width // 128):
        order[group, count:, :] = jnp.zeros((rows - count, 128), FULL)
        mixed[:, group * 128 : (group + 1) * 128] = order[group].astype(HALF)

    for begin, size in row_blocks(rows, step):
        own = slice(begin, begin + size)

        def load(part, pair):
            start = part * width + pair * 128
            return triple_ref[own, start : start + 128]

        def load_grad(pair):
            return mixed[own, pair * 128 : (pair + 1) * 128]

        def store(part, pair, grad):
            start = part * width + pair * 128
            grad_ref[own, start : start + 128] = grad.astype(HALF)

        attend_backward(
            load,
            load_grad,
            total_ref[own, :],
            store,
            heads,
            width // heads,
            bias_ref[0:size, 0:size],
        )
    grad_ref.flush()
    copies[2].wait()
    for column in range(0, width, TILE):
        part = slice(column, column + TILE)
        grad = dot_back(grad_ref[...], in_ref[part, :])
        for group in range(TILE // 128):
            order[column // 128 + group] = grad[:, group * 128 : (group + 1) * 128]
    gain = gain_ref[layer, 0:1, :]
    for frame in range(frames):
        own = slice(frame * patches, (frame + 1) * patches)
        grad = pick(order, frame, frames, patches)
        unit, inverse = unit_of(x_ref[own, :])
        next_ref[own, :] += unit_back(grad, unit, inverse, gain)
        norms_ref[2:3, :] += jnp.sum(grad * unit, 0, keepdims=True)
        norms_ref[3:4, :] += jnp.sum(grad, 0, keepdims=True)


def cost(micros):
    return pl.CostEstimate(flops=micros, bytes_accessed=micros, transcendentals=0)


class Fetched:
    def __init__(self, source, target, sem):
        self.target, self.shape = target, target.shape
        self.copy = pltpu.make_async_copy(source, target, sem)
        self.copy.start()

    def wait(self):
        if self.copy is not None:
            self.copy.wait()
            self.copy = None

    def __getitem__(self, index):
        self.wait()
        return self.target[index]


class Written:
    def __init__(self, source, target, sems):
        self.source, self.target, self.sems = source, target, sems
        self.shape = source.shape
        self.copies = []

    def __getitem__(self, index):
        return self.source[index]

    def __setitem__(self, index, values):
        self.source[index] = values

    def flush(self, columns=None):
        parts = (self.source, self.target)
        if columns is not None:
            parts = tuple(ref.at[:, columns] for ref in parts)
        copy = pltpu.make_async_copy(*parts, self.sems.at[len(self.copies)])
        copy.start()
        self.copies.append(copy)

    def wait(self):
        if not self.copies:
            self.flush()
        for copy in self.copies:
            copy.wait()


def call(kernel, outs, scratch, specs, micros):
    def run(*arrays):
        fetched = [index for index, kind in enumerate(specs) if kind == ROWS]
        count, results = len(specs), len(outs)

        def whole(*refs):
            ins, out_refs = list(refs[:count]), refs[count : count + results]
            rest = refs[count + results :]
            in_refs, rest = rest[: len(fetched)], rest[len(fetched) :]
            kept, rest = rest[:results], rest[results:]
            in_sems, out_sems = rest[0], rest[1]
            for place, index in enumerate(fetched):
                ins[index] = Fetched(ins[index], in_refs[place], in_sems.at[place])
            written = [
                Written(source, target, out_sems.at[index])
                for index, (source, target) in enumerate(zip(kept, out_refs))
            ]
            kernel(*ins, *written, *rest[2:])
            for index in fetched:
                ins[index].wait()
            for result in written:
                result.wait()

        return pl.pallas_call(
            whole,
            out_shape=[jax.ShapeDtypeStruct(shape, kind) for shape, kind in outs],
            in_specs=[SMEM if kind == SMALL else HBM for kind in specs],
            out_specs=[HBM] * results,
            scratch_shapes=[pltpu.VMEM(arrays[index].shape, arrays[index].dtype) for index in fetched]
            + [pltpu.VMEM(shape, kind) for shape, kind in outs]
            + [pltpu.SemaphoreType.DMA((len(fetched),)), pltpu.SemaphoreType.DMA((results, 4))]
            + scratch,
            compiler_params=pltpu.CompilerParams(vmem_limit_bytes=VMEM_BYTES),
            cost_estimate=cost(micros),
        )(*arrays)

    return run


def outer_group(place, pairs, groups, split, micros):
    rows = pairs[0][0].shape[1]
    parts = 2 if split else groups
    inner = parts // 2
    sizes = [right.shape[1] // parts for left, right in pairs]
    total = sum(sizes)
    tiles = []
    for side in range(2):
        for index, size in enumerate(sizes):
            for shard in range(inner):
                for start in range(0, size, 768):
                    tiles.append((side, index, shard, start, min(768, size - start)))
    count = len(pairs)

    def kernel(place_ref, *refs):
        lefts, rights = refs[:count], refs[count : 2 * count]
        outs = refs[2 * count : 2 * count + 2]
        left_refs = refs[2 * count + 2 : 3 * count + 2]
        right_refs, stage, left_sems, right_sems, out_sems = refs[3 * count + 2 :]
        arrivals = []
        lefts_here = []
        for number, (side, index, shard, start, size) in enumerate(tiles):
            if index == len(lefts_here):
                copy = pltpu.make_async_copy(lefts[index], left_refs[index], left_sems.at[index])
                copy.start()
                lefts_here.append(copy)
            if split:
                part = jnp.where(place_ref[0] % 2 == 0, 1 - side, side)
                begin = pl.multiple_of(part * sizes[index] + start, 128)
            else:
                begin = (2 * shard + 1 - side) * sizes[index] + start
            copy = pltpu.make_async_copy(
                rights[index].at[:, pl.ds(begin, size)],
                right_refs.at[number, pl.ds(0, rights[index].shape[0]), pl.ds(0, size)],
                right_sems.at[number],
            )
            copy.start()
            arrivals.append(copy)
        leaving = []
        waited = [False] * count
        for number, (side, index, shard, start, size) in enumerate(tiles):
            if not waited[index]:
                lefts_here[index].wait()
                waited[index] = True
            arrivals[number].wait()
            depth = lefts[index].shape[0]
            terms = dot_outer(left_refs[index][...], right_refs[number, 0:depth, 0:size])
            stage[number, :, 0:size] = terms.astype(HALF)
            column = sum(sizes[:index]) + start
            target = outs[side] if split else outs[side].at[shard]
            copy = pltpu.make_async_copy(
                stage.at[number, :, pl.ds(0, size)],
                target.at[:, pl.ds(column, size)],
                out_sems.at[number],
            )
            copy.start()
            leaving.append(copy)
        for copy in leaving:
            copy.wait()

    shape = (rows, total) if split else (inner, rows, total)
    lefts, rights = zip(*pairs)
    width = max(tile[4] for tile in tiles)
    return pl.pallas_call(
        kernel,
        out_shape=[jax.ShapeDtypeStruct(shape, HALF)] * 2,
        in_specs=[SMEM] + [HBM] * (2 * count),
        out_specs=[HBM] * 2,
        scratch_shapes=[pltpu.VMEM(left.shape, HALF) for left in lefts]
        + [
            pltpu.VMEM((len(tiles), max(left.shape[0] for left in lefts), width), HALF),
            pltpu.VMEM((len(tiles), rows, width), HALF),
            pltpu.SemaphoreType.DMA((count,)),
            pltpu.SemaphoreType.DMA((len(tiles),)),
            pltpu.SemaphoreType.DMA((len(tiles),)),
        ],
        compiler_params=pltpu.CompilerParams(vmem_limit_bytes=VMEM_BYTES),
        cost_estimate=cost(micros),
    )(place, *lefts, *rights)


def exchange(axis, bit):
    return (axis, [(index, index ^ bit) for index in range(lax.axis_size(axis))])


def shift(step):
    far = lax.axis_size(DP) // 2
    return (
        DP,
        [
            (start * 2 + near, (start + step) % far * 2 + near)
            for start in range(far)
            for near in range(2)
        ],
    )


def swap(values, axis, bit):
    return lax.ppermute(values, *exchange(axis, bit))


def reduce_group(parts):
    send, keep = parts
    other = yield [(send, exchange(TENSOR, 1))]
    values = keep + other[0]
    columns = values.shape[-1]
    blocks = lax.axis_size(DP)
    far = blocks // 2
    near = lax.axis_index(DP) % 2
    place = lax.axis_index(DP) // 2
    middle = columns // 2 // 128 * 128
    if values.ndim == 3:
        values = values.reshape(2, far, 2, -1, columns)
        x_dim, y_dim, x_place = 0, 2, 0
    else:
        values = values.reshape(far, 2, 2, -1, columns)
        x_dim, y_dim, x_place = 2, 1, lax.axis_index(TENSOR) // 2
    over_x, over_y = values[..., :middle], values[..., middle:]

    def of_x(array, mine, dim):
        return lax.dynamic_index_in_dim(array, x_place if mine else 1 - x_place, dim, False)

    def of_y(array, mine, dim):
        return lax.dynamic_index_in_dim(array, near if mine else 1 - near, dim, False)

    other = yield [
        (of_x(over_x, False, x_dim), exchange(TENSOR, 2)),
        (of_y(over_y, False, y_dim), exchange(DP, 1)),
    ]
    over_x = of_x(over_x, True, x_dim) + other[0]
    over_y = of_y(over_y, True, y_dim) + other[1]
    y_dim -= x_dim < y_dim
    x_dim -= x_dim > 0
    other = yield [
        (of_y(over_x, False, y_dim), exchange(DP, 1)),
        (of_x(over_y, False, x_dim), exchange(TENSOR, 2)),
    ]
    values = jnp.concatenate(
        [of_y(over_x, True, y_dim) + other[0], of_x(over_y, True, x_dim) + other[1]], -1
    )
    others = yield [
        (lax.dynamic_index_in_dim(values, (place + step) % far, 0, False), shift(step))
        for step in range(1, far)
    ]
    total = lax.dynamic_index_in_dim(values, place, 0, False).astype(FULL)
    for other in others:
        total = total + other.astype(FULL)
    return total


def reduce_norms(values):
    count = lax.axis_size(DP)
    far = count // 2
    for axis, bit in ((TENSOR, 1), (TENSOR, 2), (DP, 1)):
        other = yield [(values, exchange(axis, bit))]
        values = values + other[0]
    others = yield [(values, shift(step)) for step in range(1, far)]
    for other in others:
        values = values + other
    lanes = values.shape[1] // count
    return lax.dynamic_slice_in_dim(values, lax.axis_index(DP) * lanes, lanes, 1)


def reduce_attention(parts, sizes):
    values = (yield from reduce_group(parts)).astype(HALF)
    other = yield [(values, exchange(TENSOR, 2))]
    values = in_order(values, other[0], 2, 0)
    other = yield [(values, exchange(TENSOR, 1))]
    matrices = []
    begin = 0
    for size in sizes:
        end = begin + size // 2
        matrices.append(in_order(values[:, begin:end], other[0][:, begin:end], 1, 1).astype(FULL))
        begin = end
    return matrices


def in_order(values, other, bit, dim):
    first = lax.axis_index(TENSOR) // bit % 2 == 0
    return jnp.where(
        first,
        jnp.concatenate([values, other], dim),
        jnp.concatenate([other, values], dim),
    )


def reduce_far(parts):
    send, keep = parts
    other = yield [(send, exchange(TENSOR, 1))]
    values = keep + other[0]
    other = yield [(values[1], exchange(TENSOR, 2))]
    values = values[0] + other[0]
    values = values.reshape(-1, values.shape[-1])
    return lax.psum_scatter(values, DP, scatter_dimension=0, tiled=True).astype(FULL)


def reduce_whole(pairs):
    totals = []
    for left, right in pairs:
        total = lax.psum(dot_outer(left, right).astype(HALF), TENSOR)
        total = lax.psum_scatter(total, DP, scatter_dimension=0, tiled=True)
        totals.append(total.astype(FULL))
    return totals


class Flights:
    def __init__(self):
        self.running = {}
        self.results = {}
        self.asked = {}

    def start(self, name, steps):
        self.asked[name] = (steps, next(steps))

    def leave(self, values):
        sends = [[send for send, way in asked] for steps, asked in self.asked.values()]
        values, sends = lax.optimization_barrier((values, sends))
        for (name, (steps, asked)), ready in zip(self.asked.items(), sends):
            self.running[name] = (
                steps,
                [lax.ppermute(send, *way) for send, (unused, way) in zip(ready, asked)],
            )
        self.asked = {}
        return values

    def land(self, names, values):
        names = [name for name in names if name in self.running]
        held = [self.running[name][1] for name in names]
        values, held = lax.optimization_barrier((values, held))
        for name, arrived in zip(names, held):
            steps = self.running.pop(name)[0]
            try:
                self.asked[name] = (steps, steps.send(arrived))
            except StopIteration as stop:
                self.results[name] = stop.value
        return self.leave(values)


def spread(pieces):
    return [pieces[0]] + [swap(piece, TENSOR, away) for away, piece in enumerate(pieces) if away]


def pass_on(values, way):
    arrived = yield [(values, way)]
    return arrived[0]


def both_matrices(hidden_up, hidden_down, layer, near=None):
    matrices = [hidden_up[layer], hidden_down[layer]]
    if near is not None:
        half = matrices[0].shape[0] // 2
        matrices = [lax.dynamic_slice_in_dim(rows, near * half, half, 0) for rows in matrices]
    return jnp.stack(matrices)


def body(
    patch_tokens,
    class_tokens,
    frame_counts,
    patch_cotangent,
    class_cotangent,
    temporal_in,
    temporal_out,
    temporal_mix,
    spatial_in,
    spatial_out,
    hidden_up,
    hidden_down,
    norm_gain,
    norm_shift,
):
    frames, patches, width = patch_tokens.shape
    clips = class_tokens.shape[0]
    layers = temporal_in.shape[0]
    groups = lax.axis_size(TENSOR)
    place = jnp.stack([lax.axis_index(TENSOR), lax.axis_index(DP) % 2]).astype(jnp.int32)
    blocks_dp = lax.axis_size(DP)
    dims = (frames, patches, width, HEADS, groups)
    count = frames * patches
    rows = up_to(count + up_to(clips, 8), 80)
    spare = rows - count
    own_frames = frames // groups
    seq = groups * patches
    frame_span = up_to(seq + 1, 16)
    span = own_frames * frame_span
    hidden = groups * hidden_up.shape[2]
    piece_rows = own_frames * patches
    back_rows = up_to(piece_rows + 2 * own_frames, 8)

    ends = jnp.cumsum(frame_counts[0])
    frame_index = jnp.arange(frames, dtype=jnp.int32)
    clip_of = jnp.sum((frame_index[:, None] >= ends[None, :]).astype(jnp.int32), 1)
    clip_index = jnp.arange(spare, dtype=jnp.int32)
    member = (clip_index[:, None] == clip_of[None, :]).astype(FULL)
    counts = jnp.concatenate([frame_counts[0].astype(FULL), jnp.ones((spare - clips,), FULL)])
    share = member / counts[:, None]
    inverse_counts = 1.0 / counts
    row_index = jnp.arange(128, dtype=jnp.int32)
    row_clip = jnp.sum(
        jnp.where(row_index[:, None] % frames == frame_index[None, :], clip_of[None, :], 0), 1
    )
    same = jnp.logical_and(
        row_index[:, None] // frames == row_index[None, :] // frames,
        row_clip[:, None] == row_clip[None, :],
    )
    bias = jnp.where(same, 0.0, -1e30)

    def rows_of(patch, per_clip):
        return jnp.concatenate(
            [
                patch.reshape(count, width),
                per_clip,
                jnp.zeros((spare - clips, width), patch.dtype),
            ],
            0,
        ).astype(FULL)

    flights = Flights()
    near = lax.axis_index(DP) % 2
    gathered = [None] * layers
    by_core, by_x, by_y = exchange(TENSOR, 1), exchange(TENSOR, 2), exchange(DP, 1)

    def send(name, values, way):
        flights.start(name, pass_on(values, way))

    def arrived_here(name):
        return flights.results.pop(name)

    send("x0", both_matrices(hidden_up, hidden_down, 0, near), by_x)
    send("core0", both_matrices(hidden_up, hidden_down, 0), by_core)
    patch_rows = flights.leave(rows_of(patch_tokens, class_tokens))
    pieces_out = [((piece_rows, width), HALF)] * groups
    backs_out = [((back_rows, width), HALF)] * groups
    lane_buffer = pltpu.VMEM((width // 128, rows, 128), FULL)
    row_buffer = pltpu.VMEM((rows, width), FULL)
    square = pltpu.VMEM((width, width), HALF)
    wide = pltpu.VMEM((width, 3 * width), HALF)
    shards = pltpu.VMEM((groups, width, width), HALF)
    blocks = pltpu.VMEM((groups, back_rows, width), FULL)
    frame_rows = pltpu.VMEM((frames, width), FULL)
    saved = []
    for layer in range(layers):
        if layer:
            patch_rows = flights.land([f"x{layer}", f"core{layer}"], patch_rows)
            first = arrived_here(f"x{layer}")
            send("y1", first, by_y)
            patch_rows = flights.leave(patch_rows)
        time = call(
            partial(time_forward, dims, layer),
            [
                ((rows, width), HALF),
                ((rows, 3 * width), HALF),
                ((rows, 128), FULL),
                ((rows, width), HALF),
                ((rows, width), HALF),
                ((rows, width), FULL),
            ]
            + pieces_out
            + [((spare, width), FULL)],
            [wide, square, square, lane_buffer, row_buffer, blocks, pltpu.SemaphoreType.DMA((3,))],
            [SMALL, ROWS, ROWS, ROWS, ROWS, FAR, FAR, FAR],
            14,
        )(place, patch_rows, bias, norm_gain, norm_shift, temporal_in, temporal_out, temporal_mix)
        arrived = spread(time[6:10])
        if layer == 0:
            arrived = flights.land(("x0", "core0"), arrived)
            first = arrived_here("x0")
            send("y0", first, by_y)
            send("x1", both_matrices(hidden_up, hidden_down, 1, near), by_x)
        arrived = flights.leave(arrived)
        space = call(
            partial(space_forward, dims, layer),
            [((span, width), HALF), ((span, 3 * width), HALF), ((span, 128), FULL)] + backs_out,
            [wide, pltpu.VMEM((span, width), FULL), pltpu.SemaphoreType.DMA((1,))],
            [SMALL, SMALL, ROWS] + [ROWS] * groups + [FAR],
            9,
        )(place, clip_of, time[10], *arrived, spatial_in)
        arrived = spread(space[3:])
        arrived = flights.land([f"y{layer}"], arrived)
        second = arrived_here(f"y{layer}")
        send("first", first, by_core)
        send("second", second, by_core)
        if layer + 1 < layers:
            send("core1", both_matrices(hidden_up, hidden_down, 1), by_core)
        arrived = flights.leave(arrived)
        arrived = flights.land(("first", "second"), arrived)
        gathered[layer] = (
            arrived_here(f"core{layer}"),
            first,
            second,
            arrived_here("first"),
            arrived_here("second"),
        )
        feed = call(
            partial(feed_forward, dims, layer),
            [
                ((rows, width), HALF),
                ((rows, width), FULL),
                ((rows, width), HALF),
                ((rows, hidden), HALF),
                ((rows, hidden), HALF),
                ((rows, width), FULL),
            ],
            [
                square,
                shards,
                shards,
                row_buffer,
                blocks,
                frame_rows,
                pltpu.VMEM((rows, width), HALF),
                pltpu.SemaphoreType.DMA((1,)),
                pltpu.SemaphoreType.DMA((12,)),
            ],
            [SMALL] + [ROWS] * groups + [ROWS] * 4 + [FAR] * 8,
            15,
        )(
            place, *arrived, share, time[5], norm_gain, norm_shift, spatial_out,
            hidden_up, hidden_down, *gathered[layer],
        )
        saved.append((patch_rows, time, space, feed))
        patch_rows = feed[5]
    patch_output = patch_rows[:count].reshape(frames, patches, width).astype(HALF)
    class_output = patch_rows[count : count + clips].astype(HALF)

    grad_rows = rows_of(patch_cotangent, class_cotangent)
    usual = blocks_dp == 2 * NEAR
    norms = [None] * layers

    def start(name, pairs, split, micros):
        if split and not usual:
            flights.results[name] = reduce_whole(pairs)
            return
        parts = outer_group(place, pairs, groups, split, micros)
        if split:
            flights.start(name, reduce_attention(parts, [right.shape[1] for left, right in pairs]))
        elif usual:
            flights.start(name, reduce_group(parts))
        else:
            flights.start(name, reduce_far(parts))

    for layer in reversed(range(layers)):
        start_rows, time, space, feed = saved[layer]
        last = layer == 0
        feed_back = call(
            partial(feed_backward, dims, layer),
            [
                ((rows, width), HALF),
                ((rows, hidden), HALF),
                ((rows, width), HALF),
                ((rows, width), FULL),
                ((8, width), FULL),
            ]
            + pieces_out
            + [((8, width), FULL)],
            [
                square,
                shards,
                shards,
                row_buffer,
                row_buffer,
                blocks,
                pltpu.SemaphoreType.DMA((1,)),
                pltpu.SemaphoreType.DMA((12,)),
            ],
            [SMALL, SMALL] + [ROWS] * 5 + [FAR] * 8,
            23,
        )(
            place, clip_of, grad_rows, feed[4], feed[1],
            jnp.broadcast_to(inverse_counts[:, None], (spare, 128)), norm_gain, spatial_out,
            hidden_up, hidden_down, *gathered[layer],
        )
        update, grad_hidden, branch, back, feed_norms = feed_back[:5]
        arrived = spread(feed_back[5:9])
        pairs = ((feed[2], grad_hidden), (update, feed[3]))
        if last:
            start("feed0", pairs, False, 10)
            arrived = flights.land(("feed1", "attention1"), arrived)
        else:
            start("feed1", pairs, False, 10)
            arrived = flights.leave(arrived)
        space_back = call(
            partial(space_backward, dims, layer),
            [((span, 3 * width), HALF)] + backs_out,
            [
                wide,
                pltpu.VMEM((span, width), FULL),
                pltpu.VMEM((span, width), HALF),
                pltpu.SemaphoreType.DMA((1,)),
            ],
            [ROWS] * groups + [ROWS] * 3 + [FAR],
            29,
        )(*arrived, feed_back[9], space[1], space[2], spatial_in)
        arrived = spread(space_back[1:])
        pairs = ((space[0], space_back[0]), (feed[0], branch))
        if last:
            start("space0", pairs, True, 8)
            arrived = flights.land(("feed1", "feed0", "attention1"), arrived)
        else:
            space_pairs = pairs
            arrived = flights.land(("feed1",), arrived)
        time_back = call(
            partial(time_backward, dims, layer),
            [
                ((rows, width), HALF),
                ((rows, width), HALF),
                ((rows, 3 * width), HALF),
                ((rows, width), FULL),
                ((8, width), FULL),
            ],
            [
                wide,
                square,
                square,
                lane_buffer,
                row_buffer,
                blocks,
                frame_rows,
                pltpu.VMEM((rows, width), HALF),
                pltpu.SemaphoreType.DMA((3,)),
            ],
            [SMALL] + [ROWS] * groups + [ROWS] * 8 + [FAR] * 3,
            14,
        )(
            place, *arrived, member, back, time[5], start_rows, time[1], time[2], bias,
            norm_gain, temporal_in, temporal_out, temporal_mix,
        )
        grad_rows = time_back[3]
        norms[layer] = (time_back[4], feed_norms)
        pairs = ((time[0], time_back[2]), (time[3], time_back[1]), (time[4], time_back[0]))
        if last:
            ordered = [
                entry[at : at + 1]
                for part, at in ((0, 2), (0, 0), (1, 0), (0, 3), (0, 1), (1, 1))
                for entry in [norms[index][part] for index in range(layers)]
            ]
            ordered = jnp.concatenate(ordered, 0)
            if usual:
                flights.start("norms", reduce_norms(ordered))
            else:
                total = lax.psum(ordered, TENSOR)
                flights.results["norms"] = lax.psum_scatter(
                    total, DP, scatter_dimension=1, tiled=True
                )
            start("time0", pairs, True, 9)
            token = flights.land(("feed1", "attention1"), time_back[4])
        else:
            start("attention1", space_pairs + pairs, True, 17)
            grad_rows = flights.land(("feed1",), grad_rows)
    for names in (
        ("feed0", "space0"),
        ("time0", "attention1"),
        ("feed0", "space0"),
        ("time0", "attention1", "norms"),
        ("feed0", "space0"),
        ("time0", "attention1", "norms"),
        ("feed0", "space0"),
        ("time0", "norms"),
        ("space0",),
        ("time0", "norms"),
    ):
        token = flights.land(names, token)
    while flights.running:
        token = flights.land(list(flights.running), token)
    results = flights.results
    lanes = width // blocks_dp

    norm_sums = results["norms"].reshape(2, 3, layers, lanes).transpose(0, 2, 1, 3)
    feeds = (results["feed0"], results["feed1"])
    late = results["attention1"]
    time_sums = (results["time0"], late[2:])
    space_sums = (results["space0"], late[:2])
    gradients = (
        *[jnp.stack([sums[index] for sums in time_sums]) for index in range(3)],
        *[jnp.stack([sums[index] for sums in space_sums]) for index in range(2)],
        jnp.stack([sums[:, :width] for sums in feeds]),
        jnp.stack([sums[:, width:].T for sums in feeds]),
        norm_sums[0],
        norm_sums[1],
    )
    patch_grad = grad_rows[:count].reshape(frames, patches, width)
    class_grad = grad_rows[count : count + clips]
    return (patch_output, class_output, patch_grad, class_grad, *gradients)


def solution(mesh):
    placed = (
        P(DP, TENSOR, None),
        P(DP, None),
        P(DP, None),
        P(DP, TENSOR, None),
        P(DP, None),
        P(),
        P(),
        P(),
        P(),
        P(),
        P(None, None, TENSOR),
        P(None, TENSOR, None),
        P(),
        P(),
    )
    return jax.shard_map(
        body,
        mesh=mesh,
        in_specs=placed,
        out_specs=(
            P(DP, TENSOR, None),
            P(DP, None),
            P(DP, TENSOR, None),
            P(DP, None),
            P(None, DP, None),
            P(None, DP, None),
            P(None, DP, None),
            P(None, DP, None),
            P(None, DP, None),
            P(None, DP, TENSOR),
            P(None, TENSOR, DP),
            P(None, None, DP),
            P(None, None, DP),
        ),
        check_vma=False,
    )
```

time: 778 us -> 649 us (0.83)
  waiting for transfers between devices: 306 us -> 182 us
  Pallas kernels: 283 us -> 234 us
  starting transfers between devices: 91.4 us -> 110 us
  other arithmetic: 45.2 us -> 59.3 us
  local copies, waits for them, and re-layouts: 38.4 us -> 50 us
    ppermute x108 -> x86, waiting for transfers between devices: 306 us -> 182 us  [the longest x62 119 us: leave(): lax.ppermute(send, *way)]
    pallas_call x20 -> x17, Pallas kernels: 283 us -> 234 us  [the longest x12 180 us: run(): pl.pallas_call(whole, out_shape=[jax.ShapeDtypeStruct(shape, kind) for sh...]
    ppermute x108 -> x86, starting transfers between devices: 91.4 us -> 110 us  [the longest x62 93.2 us: leave(): lax.ppermute(send, *way)]
    add x23 -> x30, other arithmetic: 26.4 us -> 37.5 us  [the longest x5 19.4 us: reduce_group(): values = keep + other[0]]
    unnamed x201 -> x168, local copies, waits for them, and re-layouts: 15.4 us -> 20.3 us
  transfers between devices with their start and end apart: 108 -> 86, of which waited for: 44 -> 36; matrix products, arithmetic and copies ran while one was open for 8% -> 5% of each run, Pallas kernels for 29% -> 32%
where the time goes in v1:
time: 649 us; the launch traced here: 638 us
  Pallas kernels  234 us (36%)
  waiting for transfers between devices  182 us (28%)
  starting transfers between devices  110 us (17%)
  other arithmetic  59.3 us (9%)
  local copies, waits for them, and re-layouts  50 us (8%)
    pallas_call x12, Pallas kernels, run(): pl.pallas_call(whole, out_shape=[jax.ShapeDtypeStruct(shape, kind) for sh...  180 us
    ppermute x62, waiting for transfers between devices, leave(): lax.ppermute(send, *way)  119 us
    ppermute x62, starting transfers between devices, leave(): lax.ppermute(send, *way)  93.2 us
    ppermute x24, waiting for transfers between devices, swap(): return lax.ppermute(values, *exchange(axis, bit))  63.9 us
    pallas_call x5, Pallas kernels, outer_group(): pl.pallas_call(kernel, out_shape=[jax.ShapeDtypeStruct(shape, HALF)] * 2,...  54.4 us
    unnamed x168, local copies, waits for them, and re-layouts  20.3 us
    add x5, other arithmetic, reduce_group(): values = keep + other[0]  19.4 us
    ppermute x24, starting transfers between devices, swap(): return lax.ppermute(values, *exchange(axis, bit))  16.9 us
  transfers between devices with their start and end apart: 86, of which 36 were waited for; matrix products, arithmetic and copies ran while one was open for 5% of the time, Pallas kernels for 32%

profile of v1, /device:TPU:0, one launch (start us, length us, event | category | flops | bytes accessed | tf_op | source)
XLA Modules:
  0.0 638.4 jit_solution(7371052010407567154)
XLA Ops:
  23.6 15.0 %shard_map.237 = (bf16[400,768]{1,0:T(8,128)(2,1)}, bf16[400,2304]{1,0:T(8,128)(2,1)}, f32[400,128]{1,0:T(8,128)}, bf16[400,768]{1,0:T(8,128)(2,1)}, bf16[400,76...) custom-call(s32[2]{0:T(128)} %pad_add_fusion.refs_0_.place_ref, ...), custom_call_target="tpu_custom_call" | custom-call | flops 14 | bytes 14 | tf_op jit(solution)/shard_map/pallas_call | solution.py:677
  41.7 8.0 %collective-permute-done.1.refs_5_ = bf16[98,768]{1,0:T(8,128)(2,1)S(1)} collective-permute-done((bf16[98,768]{1,0:T(8,128)(2,1)}, bf16[98,768]{1,0:T(8,128)(2,1)S(1)}, u32[]{:S(2)}, u32[]{:S(2)}) %collective-permute-start.1) | collective-permute-done | bytes 150560 | tf_op jit(solution)/shard_map/ppermute | solution.py:791
  54.4 11.1 %shard_map.238 = (bf16[416,768]{1,0:T(8,128)(2,1)}, bf16[416,2304]{1,0:T(8,128)(2,1)}, f32[416,128]{1,0:T(8,128)}, bf16[104,768]{1,0:T(8,128)(2,1)}, bf16[104,76...) custom-call(s32[2]{0:T(128)} %pad_add_fusion.refs_0_.place_ref, s32[8]{0:T(128)} %copy-done.73, ...), custom_call_target="tpu_custom_call" | custom-call | flops 9 | bytes 9 | tf_op jit(solution)/shard_map/pallas_call | solution.py:677
  67.4 5.3 collective-permute-done.6.refs_3_
  75.3 5.8 collective-permute-done.8.refs_14_.refs_12_
  83.9 5.2 collective-permute-done.9.refs_15_.refs_13_
  90.6 14.5 %shard_map.239 = (bf16[400,768]{1,0:T(8,128)(2,1)}, f32[400,768]{1,0:T(8,128)}, bf16[400,768]{1,0:T(8,128)(2,1)}, bf16[400,3072]{1,0:T(8,128)(2,1)}, bf16[400,3072]{1,0:T(8,128)(2,1)}, /*index=5*/f32[400,768]{1,0:T(8,128)}) custom-call(s32[2]{0:T(128)} %pad_add_fusion.refs_0_.place_ref, bf16[104,768]{1,0:T(8,128)(2,1)} %get-tuple-element.373.refs_1_, ...), custom_call_target="tpu_custom_call" | custom-call | flops 15 | bytes 15 | tf_op jit(solution)/shard_map/pallas_call | solution.py:677
  105.1 5.2 collective-permute-done.11.refs_13_.refs_11_
  111.9 14.8 %shard_map.240 = (bf16[400,768]{1,0:T(8,128)(2,1)}, bf16[400,2304]{1,0:T(8,128)(2,1)}, f32[400,128]{1,0:T(8,128)}, bf16[400,768]{1,0:T(8,128)(2,1)}, bf16[400,76...) custom-call(s32[2]{0:T(128)} %pad_add_fusion.refs_0_.place_ref, ...), custom_call_target="tpu_custom_call" | custom-call | flops 14 | bytes 14 | tf_op jit(solution)/shard_map/pallas_call | solution.py:677
  128.9 5.3 collective-permute-done.14.refs_5_
  137.4 11.0 %shard_map.241 = (bf16[416,768]{1,0:T(8,128)(2,1)}, bf16[416,2304]{1,0:T(8,128)(2,1)}, f32[416,128]{1,0:T(8,128)}, bf16[104,768]{1,0:T(8,128)(2,1)}, bf16[104,76...) custom-call(s32[2]{0:T(128)} %pad_add_fusion.refs_0_.place_ref, s32[8]{0:T(128)} %copy-done.73, ...), custom_call_target="tpu_custom_call" | custom-call | flops 9 | bytes 9 | tf_op jit(solution)/shard_map/pallas_call | solution.py:677
  150.5 5.7 collective-permute-done.17.refs_3_
  158.7 3.5 collective-permute-done.20.refs_15_.refs_13_
  163.8 14.4 %shard_map.242 = (bf16[400,768]{1,0:T(8,128)(2,1)}, f32[400,768]{1,0:T(8,128)}, bf16[400,768]{1,0:T(8,128)(2,1)}, bf16[400,3072]{1,0:T(8,128)(2,1)}, bf16[400,3072]{1,0:T(8,128)(2,1)}, /*index=5*/f32[400,768]{1,0:T(8,128)}) custom-call(s32[2]{0:T(128)} %pad_add_fusion.refs_0_.place_ref, bf16[104,768]{1,0:T(8,128)(2,1)} %get-tuple-element.420.refs_1_, ...), custom_call_target="tpu_custom_call" | custom-call | flops 15 | bytes 15 | tf_op jit(solution)/shard_map/pallas_call | solution.py:677
  178.9 17.1 %shard_map.243 = (bf16[400,768]{1,0:T(8,128)(2,1)}, bf16[400,3072]{1,0:T(8,128)(2,1)}, bf16[400,768]{1,0:T(8,128)(2,1)}, f32[400,768]{1,0:T(8,128)}, f32[8,768]{...) custom-call(s32[2]{0:T(128)} %pad_add_fusion.refs_0_.place_ref, ...), custom_call_target="tpu_custom_call" | custom-call | flops 23 | bytes 23 | tf_op jit(solution)/shard_map/pallas_call | solution.py:677
  197.9 12.2 %shard_map.244 = (bf16[2,768,1536]{2,1,0:T(8,128)(2,1)}, bf16[2,768,1536]{2,1,0:T(8,128)(2,1)}) custom-call(s32[2]{0:T(128)} %pad_add_fusion.refs_0_.place_ref, bf16[400,768]{1,0:T(8,128)(2,1)} %get-tuple-element.435.refs_0_, bf16[400,768]{1,0:T(8,128)(2,1)} %get-tuple-element.436.refs_1_, bf16[400,3072]{1,0:T(8,128)(2,1)} %get-tuple-element.437.refs_2_, ...), custom_call_target="tpu_custom_call" | custom-call | flops 10 | bytes 10 | tf_op jit(solution)/shard_map/pallas_call | solution.py:756
  210.9 13.4 %shard_map.245 = (bf16[416,2304]{1,0:T(8,128)(2,1)}, bf16[104,768]{1,0:T(8,128)(2,1)}, bf16[104,768]{1,0:T(8,128)(2,1)}, bf16[104,768]{1,0:T(8,128)(2,1)}, bf16[104,768]{1,0:T(8,128)(2,1)}) custom-call(bf16[98,768]{1,0:T(8,128)(2,1)} %get-tuple-element.440.refs_0_, bf16[98,768]{1,0:T(8,128)(2,1)} %copy-done.58, bf16[98,768]{1,0:T(8,128)(2,1)} %copy-done.59, ...), custom_call_target="tpu_custom_call" | custom-call | flops 29 | bytes 29 | tf_op jit(solution)/shard_map/pallas_call | solution.py:677
  226.6 5.6 collective-permute-done.26.refs_3_
  233.9 5.1 add.344
  245.2 19.4 %shard_map.246 = (bf16[400,768]{1,0:T(8,128)(2,1)}, bf16[400,768]{1,0:T(8,128)(2,1)}, bf16[400,2304]{1,0:T(8,128)(2,1)}, f32[400,768]{1,0:T(8,128)}, f32[8,768]{1,0:T(8,128)}) custom-call(s32[2]{0:T(128)} %pad_add_fusion.refs_0_.place_ref, bf16[104,768]{1,0:T(8,128)(2,1)} %get-tuple-element.458.refs_1_, bf16[104,768]{1,0:T(8,128)(2,1)} %copy-done.64, ...), custom_call_target="tpu_custom_call" | custom-call | flops 14 | bytes 14 | tf_op jit(solution)/shard_map/pallas_call | solution.py:677
  264.6 13.9 %shard_map.247 = (bf16[768,3456]{1,0:T(8,128)(2,1)}, bf16[768,3456]{1,0:T(8,128)(2,1)}) custom-call(s32[2]{0:T(128)} %pad_add_fusion.refs_0_.place_ref, bf16[416,768]{1,0:T(8,128)(2,1)} %get-tuple-element.469.refs_0_, bf16[400,768]{1,0:T(8,128)(2,1)} %get-tuple-element.470.refs_1_, bf16[400,768]{1,0:T(8,128)(2,1)} %get-tuple-element.471.refs_2_, ...), custom_call_target="tpu_custom_call" | custom-call | flops 17 | bytes 17 | tf_op jit(solution)/shard_map/pallas_call | solution.py:756
  285.0 16.5 %shard_map.248 = (bf16[400,768]{1,0:T(8,128)(2,1)}, bf16[400,3072]{1,0:T(8,128)(2,1)}, bf16[400,768]{1,0:T(8,128)(2,1)}, f32[400,768]{1,0:T(8,128)}, f32[8,768]{...) custom-call(s32[2]{0:T(128)} %pad_add_fusion.refs_0_.place_ref, ...), custom_call_target="tpu_custom_call" | custom-call | flops 23 | bytes 23 | tf_op jit(solution)/shard_map/pallas_call | solution.py:677
  304.5 12.2 %shard_map.249 = (bf16[2,768,1536]{2,1,0:T(8,128)(2,1)}, bf16[2,768,1536]{2,1,0:T(8,128)(2,1)}) custom-call(s32[2]{0:T(128)} %pad_add_fusion.refs_0_.place_ref, bf16[400,768]{1,0:T(8,128)(2,1)} %get-tuple-element.496.refs_0_, bf16[400,768]{1,0:T(8,128)(2,1)} %get-tuple-element.497.refs_1_, bf16[400,3072]{1,0:T(8,128)(2,1)} %get-tuple-element.498.refs_2_, ...), custom_call_target="tpu_custom_call" | custom-call | flops 10 | bytes 10 | tf_op jit(solution)/shard_map/pallas_call | solution.py:756
  316.8 6.0 add.360
  331.2 13.0 %shard_map.250 = (bf16[416,2304]{1,0:T(8,128)(2,1)}, bf16[104,768]{1,0:T(8,128)(2,1)}, bf16[104,768]{1,0:T(8,128)(2,1)}, bf16[104,768]{1,0:T(8,128)(2,1)}, bf16[104,768]{1,0:T(8,128)(2,1)}) custom-call(bf16[98,768]{1,0:T(8,128)(2,1)} %get-tuple-element.505.refs_0_, bf16[98,768]{1,0:T(8,128)(2,1)} %copy-done.55, bf16[98,768]{1,0:T(8,128)(2,1)} %copy-done.56, ...), custom_call_target="tpu_custom_call" | custom-call | flops 29 | bytes 29 | tf_op jit(solution)/shard_map/pallas_call | solution.py:677
  347.6 16.7 %collective-permute-done.38.refs_3_ = bf16[104,768]{1,0:T(8,128)(2,1)S(1)} collective-permute-done((bf16[104,768]{1,0:T(8,128)(2,1)}, bf16[104,768]{1,0:T(8,128)(2,1)S(1)}, u32[]{:S(2)}, u32[]{:S(2)}) %collective-permute-start.38) | collective-permute-done | bytes 159776 | tf_op jit(solution)/shard_map/ppermute | solution.py:791
  364.2 5.8 collective-permute-done.39.refs_4_
  374.5 7.4 %shard_map.251 = (bf16[768,1536]{1,0:T(8,128)(2,1)}, bf16[768,1536]{1,0:T(8,128)(2,1)}) custom-call(s32[2]{0:T(128)} %pad_add_fusion.refs_0_.place_ref, bf16[416,768]{1,0:T(8,128)(2,1)} %get-tuple-element.526.refs_0_, bf16[400,768]{1,0:T(8,128)(2,1)} %get-tuple-element.527.refs_1_, bf16[416,2304]{1,0:T(8,128)(2,1)} %get-tuple-element.528.refs_2_, ...), custom_call_target="tpu_custom_call" | custom-call | flops 8 | bytes 8 | tf_op jit(solution)/shard_map/pallas_call | solution.py:756
  381.9 5.1 collective-permute-done.41
  387.0 5.1 add.362
  407.9 19.6 %shard_map.252 = (bf16[400,768]{1,0:T(8,128)(2,1)}, bf16[400,768]{1,0:T(8,128)(2,1)}, bf16[400,2304]{1,0:T(8,128)(2,1)}, f32[400,768]{1,0:T(8,128)}, f32[8,768]{1,0:T(8,128)}) custom-call(s32[2]{0:T(128)} %pad_add_fusion.refs_0_.place_ref, bf16[104,768]{1,0:T(8,128)(2,1)} %get-tuple-element.535.refs_1_, bf16[104,768]{1,0:T(8,128)(2,1)} %copy-done.61, ...), custom_call_target="tpu_custom_call" | custom-call | flops 14 | bytes 14 | tf_op jit(solution)/shard_map/pallas_call | solution.py:677
  427.5 8.8 %shard_map.253 = (bf16[768,1920]{1,0:T(8,128)(2,1)}, bf16[768,1920]{1,0:T(8,128)(2,1)}) custom-call(s32[2]{0:T(128)} %pad_add_fusion.refs_0_.place_ref, bf16[400,768]{1,0:T(8,128)(2,1)} %get-tuple-element.543.refs_0_, bf16[400,768]{1,0:T(8,128)(2,1)} %get-tuple-element.544.refs_1_, bf16[400,768]{1,0:T(8,128)(2,1)} %get-tuple-element.545.refs_2_, ...), custom_call_target="tpu_custom_call" | custom-call | flops 9 | bytes 9 | tf_op jit(solution)/shard_map/pallas_call | solution.py:756
  436.4 9.7 %collective-permute-done.46 = bf16[4,48,1664]{2,1,0:T(8,128)(2,1)} collective-permute-done((bf16[4,48,1664]{2,1,0:T(8,128)(2,1)}, bf16[4,48,1664]{2,1,0:T(8,128)(2,1)}, u32[]{:S(2)}, u32[]{:S(2)}) %collective-permute-start.46) | collective-permute-done | bytes 639008 | tf_op jit(solution)/shard_map/ppermute | solution.py:913
  458.0 9.9 %collective-permute-done.55 = bf16[4,96,768]{2,1,0:T(8,128)(2,1)S(1)} collective-permute-done((bf16[4,96,768]{2,1,0:T(8,128)(2,1)S(1)}, bf16[4,96,768]{2,1,0:T(8,128)(2,1)S(1)}, u32[]{:S(2)}, u32[]{:S(2)}) %collective-permute-start.55) | collective-permute-done | bytes 589856 | tf_op jit(solution)/shard_map/ppermute | solution.py:913
  469.4 10.7 %collective-permute-done.57 = bf16[4,2,48,768]{3,2,1,0:T(8,128)(2,1)S(1)} collective-permute-done((bf16[4,2,48,768]{3,2,1,0:T(8,128)(2,1)S(1)}, bf16[4,2,48,768]{3,2,1,0:T(8,128)(2,1)S(1)}, u32[]{:S(2)}, u32[]{:S(2)}) %collective-permute-start.57) | collective-permute-done | bytes 589856 | tf_op jit(solution)/shard_map/ppermute | solution.py:913
  484.0 6.2 collective-permute-start.75
  496.2 3.4 collective-permute-start.76
  508.4 5.1 collective-permute-done.76
  513.5 6.0 collective-permute-start.52
  529.6 4.7 collective-permute-done.80
  534.5 6.2 collective-permute-done.81
  540.6 9.7 %collective-permute-start.54 = (bf16[48,3456]{1,0:T(8,128)(2,1)S(1)}, bf16[48,3456]{1,0:T(8,128)(2,1)S(1)}, u32[]{:S(2)}, u32[]{:S(2)}) collective-permute-start(bf16[48,3456]{1,0:T(8,128)(2,1)S(1)} %copy-done.46), channel_id=1, source_target_pairs={{0,24},{4,28},{8,0},{12,4},{16,8},{20,12},{24,16},{28,20},{1,25},{... | collective-permute-start | bytes 995336 | tf_op jit(solution)/shard_map/ppermute | solution.py:913
  557.1 3.7 collective-permute-done.54
  566.8 19.6 %collective-permute-done.61 = bf16[48,3456]{1,0:T(8,128)(2,1)S(1)} collective-permute-done((bf16[48,3456]{1,0:T(8,128)(2,1)S(1)}, bf16[48,3456]{1,0:T(8,128)(2,1)S(1)}, u32[]{:S(2)}, u32[]{:S(2)}) %collective-permute-start.61) | collective-permute-done | bytes 331808 | tf_op jit(solution)/shard_map/ppermute | solution.py:913
  590.9 6.7 %collective-permute-done.66 = f32[12,768]{1,0:T(8,128)S(1)} collective-permute-done((f32[12,768]{1,0:T(8,128)S(1)}, f32[12,768]{1,0:T(8,128)S(1)}, u32[]{:S(2)}, u32[]{:S(2)}) %collective-permute-start.66) | collective-permute-done | bytes 36896 | tf_op jit(solution)/shard_map/ppermute | solution.py:913
  597.8 8.0 %collective-permute-start.67 = (bf16[48,1920]{1,0:T(8,128)(2,1)S(1)}, bf16[48,1920]{1,0:T(8,128)(2,1)S(1)}, u32[]{:S(2)}, u32[]{:S(2)}) collective-permute-start(bf16[48,1920]{1,0:T(8,128)(2,1)S(1)} %get-tuple-element.605), channel_id=1, source_target_pairs={{0,8},{4,12},{8,16},{12,20},{16,24},{20,28},{24,0},{28,4},{1,9},{5... | collective-permute-start | bytes 552968 | tf_op jit(solution)/shard_map/ppermute | solution.py:913
  612.3 3.7 collective-permute-done.68
  617.7 5.3 collective-permute-start.72
  (446 shorter events, 190.1 us)
Async XLA Ops:
  16.3 36.5 %collective-permute-start.4 = (bf16[2,768,768]{2,1,0:T(8,128)(2,1)}, bf16[2,768,768]{2,1,0:T(8,128)(2,1)S(1)}, u32[]{:S(2)}, u32[]{:S(2)}) collective-permute-start(bf16[2,768,768]{2,1,0:T(8,128)(2,1)} %get-tuple-element.335), channel_id=1, source_target_pairs={{0,1},{1,0},{2,3},{3,2},{4,5},{5,4},{6,7},{7,6},{8,9},{9,8},{10,11... | collective-permute-start | bytes 7077896 | tf_op jit(solution)/shard_map/ppermute | solution.py:913
  16.7 36.0 %collective-permute-start.3 = (bf16[2,384,768]{2,1,0:T(8,128)(2,1)}, bf16[2,384,768]{2,1,0:T(8,128)(2,1)}, u32[]{:S(2)}, u32[]{:S(2)}) collective-permute-start(bf16[2,384,768]{2,1,0:T(8,128)(2,1)} %pad_maximum_fusion.2), channel_id=1, source_target_pairs={{0,2},{1,3},{2,0},{3,1},{4,6},{5,7},{6,4},{7,5},{8,10},{9,11},{10,... | collective-permute-start | bytes 3538952 | tf_op jit(solution)/shard_map/ppermute | solution.py:913
  52.8 28.3 %collective-permute-start.8 = (bf16[2,384,768]{2,1,0:T(8,128)(2,1)}, bf16[2,384,768]{2,1,0:T(8,128)(2,1)S(1)}, u32[]{:S(2)}, u32[]{:S(2)}) collective-permute-start(bf16[2,384,768]{2,1,0:T(8,128)(2,1)} %collective-permute-done.3.refs_13_.refs_11_), channel_id=1, source_target_pairs={{0,4},{4,0},{8,12},{12,8},{16,20},{20,16},{24,28},{28,24},{1,5},{5... | collective-permute-start | bytes 3538952 | tf_op jit(solution)/shard_map/ppermute | solution.py:913
  81.0 29.2 %collective-permute-start.12 = (bf16[2,768,768]{2,1,0:T(8,128)(2,1)}, bf16[2,768,768]{2,1,0:T(8,128)(2,1)S(1)}, u32[]{:S(2)}, u32[]{:S(2)}) collective-permute-start(bf16[2,768,768]{2,1,0:T(8,128)(2,1)} %get-tuple-element.383), channel_id=1, source_target_pairs={{0,1},{1,0},{2,3},{3,2},{4,5},{5,4},{6,7},{7,6},{8,9},{9,8},{10,11... | collective-permute-start | bytes 7077896 | tf_op jit(solution)/shard_map/ppermute | solution.py:913
  81.6 28.6 %collective-permute-start.11 = (bf16[2,384,768]{2,1,0:T(8,128)(2,1)}, bf16[2,384,768]{2,1,0:T(8,128)(2,1)}, u32[]{:S(2)}, u32[]{:S(2)}) collective-permute-start(bf16[2,384,768]{2,1,0:T(8,128)(2,1)} %pad_maximum_fusion.3), channel_id=1, source_target_pairs={{0,2},{1,3},{2,0},{3,1},{4,6},{5,7},{6,4},{7,5},{8,10},{9,11},{10,... | collective-permute-start | bytes 3538952 | tf_op jit(solution)/shard_map/ppermute | solution.py:913
  110.3 47.6 %collective-permute-start.19 = (bf16[2,384,768]{2,1,0:T(8,128)(2,1)}, bf16[2,384,768]{2,1,0:T(8,128)(2,1)S(1)}, u32[]{:S(2)}, u32[]{:S(2)}) collective-permute-start(bf16[2,384,768]{2,1,0:T(8,128)(2,1)} %collective-permute-done.11.refs_13_.refs_11_), channel_id=1, source_target_pairs={{0,4},{4,0},{8,12},{12,8},{16,20},{20,16},{24,28},{28,24},{1,5},{5... | collective-permute-start | bytes 3538952 | tf_op jit(solution)/shard_map/ppermute | solution.py:913
  196.0 14.2 %collective-permute-start.22 = (bf16[98,768]{1,0:T(8,128)(2,1)}, bf16[98,768]{1,0:T(8,128)(2,1)S(1)}, u32[]{:S(2)}, u32[]{:S(2)}) collective-permute-start(bf16[98,768]{1,0:T(8,128)(2,1)} %get-tuple-element.432), channel_id=1, source_target_pairs={{0,1},{1,0},{2,3},{3,2},{4,5},{5,4},{6,7},{7,6},{8,9},{9,8},{10,11... | collective-permute-start | bytes 451592 | tf_op jit(solution)/shard_map/ppermute | solution.py:791
  196.4 13.7 %collective-permute-start.23 = (bf16[98,768]{1,0:T(8,128)(2,1)}, bf16[98,768]{1,0:T(8,128)(2,1)S(1)}, u32[]{:S(2)}, u32[]{:S(2)}) collective-permute-start(bf16[98,768]{1,0:T(8,128)(2,1)} %get-tuple-element.433), channel_id=1, source_target_pairs={{0,2},{1,3},{2,0},{3,1},{4,6},{5,7},{6,4},{7,5},{8,10},{9,11},{10,... | collective-permute-start | bytes 451592 | tf_op jit(solution)/shard_map/ppermute | solution.py:791
  210.2 23.7 %collective-permute-start.28 = (bf16[2,768,1536]{2,1,0:T(8,128)(2,1)}, bf16[2,768,1536]{2,1,0:T(8,128)(2,1)}, u32[]{:S(2)}, u32[]{:S(2)}) collective-permute-start(bf16[2,768,1536]{2,1,0:T(8,128)(2,1)} %get-tuple-element.451), channel_id=1, source_target_pairs={{0,1},{1,0},{2,3},{3,2},{4,5},{5,4},{6,7},{7,6},{8,9},{9,8},{10,11... | collective-permute-start | bytes 14155784 | tf_op jit(solution)/shard_map/ppermute | solution.py:913
  242.6 35.9 %collective-permute-start.29 = (bf16[4,2,96,768]{3,2,1,0:T(8,128)(2,1)}, bf16[4,2,96,768]{3,2,1,0:T(8,128)(2,1)S(1)}, u32[]{:S(2)}, u32[]{:S(2)}) collective-permute-start(bf16[4,2,96,768]{3,2,1,0:T(8,128)(2,1)} %slice_bitcast_fusion.3), channel_id=1, source_target_pairs={{0,2},{1,3},{2,0},{3,1},{4,6},{5,7},{6,4},{7,5},{8,10},{9,11},{10,... | collective-permute-start | bytes 3538952 | tf_op jit(solution)/shard_map/ppermute | solution.py:913
  244.1 34.4 %collective-permute-start.30 = (bf16[2,4,96,768]{3,2,1,0:T(8,128)(2,1)}, bf16[2,4,96,768]{3,2,1,0:T(8,128)(2,1)}, u32[]{:S(2)}, u32[]{:S(2)}) collective-permute-start(bf16[2,4,96,768]{3,2,1,0:T(8,128)(2,1)} %dynamic-slice_bitcast_fusion.3), channel_id=1, source_target_pairs={{0,4},{4,0},{8,12},{12,8},{16,20},{20,16},{24,28},{28,24},{1,5},{5... | collective-permute-start | bytes 3538952 | tf_op jit(solution)/shard_map/ppermute | solution.py:913
  282.8 34.0 %collective-permute-start.36 = (bf16[768,3456]{1,0:T(8,128)(2,1)}, bf16[768,3456]{1,0:T(8,128)(2,1)}, u32[]{:S(2)}, u32[]{:S(2)}) collective-permute-start(bf16[768,3456]{1,0:T(8,128)(2,1)} %get-tuple-element.491), channel_id=1, source_target_pairs={{0,1},{1,0},{2,3},{3,2},{4,5},{5,4},{6,7},{7,6},{8,9},{9,8},{10,11... | collective-permute-start | bytes 15925256 | tf_op jit(solution)/shard_map/ppermute | solution.py:913
  283.0 33.8 %collective-permute-start.34 = (bf16[4,96,768]{2,1,0:T(8,128)(2,1)S(1)}, bf16[4,96,768]{2,1,0:T(8,128)(2,1)S(1)}, u32[]{:S(2)}, u32[]{:S(2)}) collective-permute-start(bf16[4,96,768]{2,1,0:T(8,128)(2,1)S(1)} %dynamic-slice_bitcast_fusion.11), channel_id=1, source_target_pairs={{0,4},{4,0},{8,12},{12,8},{16,20},{20,16},{24,28},{28,24},{1,5},{5... | collective-permute-start | bytes 1769480 | tf_op jit(solution)/shard_map/ppermute | solution.py:913
  284.5 32.2 %collective-permute-start.35 = (bf16[4,96,768]{2,1,0:T(8,128)(2,1)S(1)}, bf16[4,96,768]{2,1,0:T(8,128)(2,1)S(1)}, u32[]{:S(2)}, u32[]{:S(2)}) collective-permute-start(bf16[4,96,768]{2,1,0:T(8,128)(2,1)S(1)} %slice_bitcast_fusion.7), channel_id=1, source_target_pairs={{0,2},{1,3},{2,0},{3,1},{4,6},{5,7},{6,4},{7,5},{8,10},{9,11},{10,... | collective-permute-start | bytes 1769480 | tf_op jit(solution)/shard_map/ppermute | solution.py:913
  301.6 15.1 %collective-permute-start.32 = (bf16[98,768]{1,0:T(8,128)(2,1)}, bf16[98,768]{1,0:T(8,128)(2,1)S(1)}, u32[]{:S(2)}, u32[]{:S(2)}) collective-permute-start(bf16[98,768]{1,0:T(8,128)(2,1)} %get-tuple-element.487), channel_id=1, source_target_pairs={{0,2},{1,3},{2,0},{3,1},{4,6},{5,7},{6,4},{7,5},{8,10},{9,11},{10,... | collective-permute-start | bytes 451592 | tf_op jit(solution)/shard_map/ppermute | solution.py:791
  329.9 57.1 %collective-permute-start.43 = (bf16[2,768,1536]{2,1,0:T(8,128)(2,1)}, bf16[2,768,1536]{2,1,0:T(8,128)(2,1)}, u32[]{:S(2)}, u32[]{:S(2)}) collective-permute-start(bf16[2,768,1536]{2,1,0:T(8,128)(2,1)} %get-tuple-element.519), channel_id=1, source_target_pairs={{0,1},{1,0},{2,3},{3,2},{4,5},{5,4},{6,7},{7,6},{8,9},{9,8},{10,11... | collective-permute-start | bytes 14155784 | tf_op jit(solution)/shard_map/ppermute | solution.py:913
  330.2 56.7 %collective-permute-start.45 = (bf16[4,2,48,1792]{3,2,1,0:T(8,128)(2,1)}, bf16[4,2,48,1792]{3,2,1,0:T(8,128)(2,1)}, u32[]{:S(2)}, u32[]{:S(2)}) collective-permute-start(bf16[4,2,48,1792]{3,2,1,0:T(8,128)(2,1)} %dynamic-slice_bitcast_fusion), channel_id=1, source_target_pairs={{0,4},{4,0},{8,12},{12,8},{16,20},{20,16},{24,28},{28,24},{1,5},{5... | collective-permute-start | bytes 4128776 | tf_op jit(solution)/shard_map/ppermute | solution.py:913
  330.7 56.3 %collective-permute-start.44 = (bf16[4,2,48,1664]{3,2,1,0:T(8,128)(2,1)}, bf16[4,2,48,1664]{3,2,1,0:T(8,128)(2,1)}, u32[]{:S(2)}, u32[]{:S(2)}) collective-permute-start(bf16[4,2,48,1664]{3,2,1,0:T(8,128)(2,1)} %dynamic-slice_bitcast_fusion.1), channel_id=1, source_target_pairs={{0,2},{1,3},{2,0},{3,1},{4,6},{5,7},{6,4},{7,5},{8,10},{9,11},{10,... | collective-permute-start | bytes 3833864 | tf_op jit(solution)/shard_map/ppermute | solution.py:913
  344.4 19.8 %collective-permute-start.38 = (bf16[104,768]{1,0:T(8,128)(2,1)}, bf16[104,768]{1,0:T(8,128)(2,1)S(1)}, u32[]{:S(2)}, u32[]{:S(2)}) collective-permute-start(bf16[104,768]{1,0:T(8,128)(2,1)} %get-tuple-element.514), channel_id=1, source_target_pairs={{0,2},{1,3},{2,0},{3,1},{4,6},{5,7},{6,4},{7,5},{8,10},{9,11},{10,... | collective-permute-start | bytes 479240 | tf_op jit(solution)/shard_map/ppermute | solution.py:791
  345.9 26.7 %collective-permute-start.40 = (bf16[96,1536]{1,0:T(8,128)(2,1)S(1)}, bf16[96,1536]{1,0:T(8,128)(2,1)}, u32[]{:S(2)}, u32[]{:S(2)}) collective-permute-start(bf16[96,1536]{1,0:T(8,128)(2,1)S(1)} %get-tuple-element.516), channel_id=1, source_target_pairs={{0,8},{4,12},{8,16},{12,20},{16,24},{20,28},{24,0},{28,4},{1,9},{5... | collective-permute-start | bytes 884744 | tf_op jit(solution)/shard_map/ppermute | solution.py:913
  370.0 17.0 %collective-permute-start.41 = (bf16[96,1536]{1,0:T(8,128)(2,1)}, bf16[96,1536]{1,0:T(8,128)(2,1)}, u32[]{:S(2)}, u32[]{:S(2)}) collective-permute-start(bf16[96,1536]{1,0:T(8,128)(2,1)} %get-tuple-element.517), channel_id=1, source_target_pairs={{0,16},{4,20},{8,24},{12,28},{16,0},{20,4},{24,8},{28,12},{1,17},{... | collective-permute-start | bytes 884744 | tf_op jit(solution)/shard_map/ppermute | solution.py:913
  372.6 14.3 %collective-permute-start.42 = (bf16[96,1536]{1,0:T(8,128)(2,1)}, bf16[96,1536]{1,0:T(8,128)(2,1)}, u32[]{:S(2)}, u32[]{:S(2)}) collective-permute-start(bf16[96,1536]{1,0:T(8,128)(2,1)} %get-tuple-element.518), channel_id=1, source_target_pairs={{0,24},{4,28},{8,0},{12,4},{16,8},{20,12},{24,16},{28,20},{1,25},{... | collective-permute-start | bytes 884744 | tf_op jit(solution)/shard_map/ppermute | solution.py:913
  402.2 43.9 %collective-permute-start.50 = (bf16[768,1536]{1,0:T(8,128)(2,1)}, bf16[768,1536]{1,0:T(8,128)(2,1)S(1)}, u32[]{:S(2)}, u32[]{:S(2)}) collective-permute-start(bf16[768,1536]{1,0:T(8,128)(2,1)} %get-tuple-element.563), channel_id=1, source_target_pairs={{0,1},{1,0},{2,3},{3,2},{4,5},{5,4},{6,7},{7,6},{8,9},{9,8},{10,11... | collective-permute-start | bytes 7077896 | tf_op jit(solution)/shard_map/ppermute | solution.py:913
  402.2 43.9 %collective-permute-start.48 = (bf16[4,2,96,768]{3,2,1,0:T(8,128)(2,1)}, bf16[4,2,96,768]{3,2,1,0:T(8,128)(2,1)}, u32[]{:S(2)}, u32[]{:S(2)}) collective-permute-start(bf16[4,2,96,768]{3,2,1,0:T(8,128)(2,1)} %slice_bitcast_fusion.1), channel_id=1, source_target_pairs={{0,2},{1,3},{2,0},{3,1},{4,6},{5,7},{6,4},{7,5},{8,10},{9,11},{10,... | collective-permute-start | bytes 3538952 | tf_op jit(solution)/shard_map/ppermute | solution.py:913
  404.0 42.1 %collective-permute-start.49 = (bf16[2,4,96,768]{3,2,1,0:T(8,128)(2,1)}, bf16[2,4,96,768]{3,2,1,0:T(8,128)(2,1)}, u32[]{:S(2)}, u32[]{:S(2)}) collective-permute-start(bf16[2,4,96,768]{3,2,1,0:T(8,128)(2,1)} %dynamic-slice_bitcast_fusion.2), channel_id=1, source_target_pairs={{0,4},{4,0},{8,12},{12,8},{16,20},{20,16},{24,28},{28,24},{1,5},{5... | collective-permute-start | bytes 3538952 | tf_op jit(solution)/shard_map/ppermute | solution.py:913
  405.5 40.6 %collective-permute-start.47 = (bf16[4,48,1792]{2,1,0:T(8,128)(2,1)}, bf16[4,48,1792]{2,1,0:T(8,128)(2,1)}, u32[]{:S(2)}, u32[]{:S(2)}) collective-permute-start(bf16[4,48,1792]{2,1,0:T(8,128)(2,1)} %dynamic-slice_bitcast_fusion.6), channel_id=1, source_target_pairs={{0,2},{1,3},{2,0},{3,1},{4,6},{5,7},{6,4},{7,5},{8,10},{9,11},{10,... | collective-permute-start | bytes 2064392 | tf_op jit(solution)/shard_map/ppermute | solution.py:913
  406.6 39.5 %collective-permute-start.46 = (bf16[4,48,1664]{2,1,0:T(8,128)(2,1)}, bf16[4,48,1664]{2,1,0:T(8,128)(2,1)}, u32[]{:S(2)}, u32[]{:S(2)}) collective-permute-start(bf16[4,48,1664]{2,1,0:T(8,128)(2,1)} %dynamic-slice_bitcast_fusion.7), channel_id=1, source_target_pairs={{0,4},{4,0},{8,12},{12,8},{16,20},{20,16},{24,28},{28,24},{1,5},{5... | collective-permute-start | bytes 1916936 | tf_op jit(solution)/shard_map/ppermute | solution.py:913
  451.5 16.3 %collective-permute-start.55 = (bf16[4,96,768]{2,1,0:T(8,128)(2,1)S(1)}, bf16[4,96,768]{2,1,0:T(8,128)(2,1)S(1)}, u32[]{:S(2)}, u32[]{:S(2)}) collective-permute-start(bf16[4,96,768]{2,1,0:T(8,128)(2,1)S(1)} %dynamic-slice_bitcast_fusion.10), channel_id=1, source_target_pairs={{0,4},{4,0},{8,12},{12,8},{16,20},{20,16},{24,28},{28,24},{1,5},{5... | collective-permute-start | bytes 1769480 | tf_op jit(solution)/shard_map/ppermute | solution.py:913
  453.1 16.3 %collective-permute-start.56 = (bf16[4,96,768]{2,1,0:T(8,128)(2,1)S(1)}, bf16[4,96,768]{2,1,0:T(8,128)(2,1)S(1)}, u32[]{:S(2)}, u32[]{:S(2)}) collective-permute-start(bf16[4,96,768]{2,1,0:T(8,128)(2,1)S(1)} %slice_bitcast_fusion.5), channel_id=1, source_target_pairs={{0,2},{1,3},{2,0},{3,1},{4,6},{5,7},{6,4},{7,5},{8,10},{9,11},{10,... | collective-permute-start | bytes 1769480 | tf_op jit(solution)/shard_map/ppermute | solution.py:913
  454.5 25.7 %collective-permute-start.57 = (bf16[4,2,48,768]{3,2,1,0:T(8,128)(2,1)S(1)}, bf16[4,2,48,768]{3,2,1,0:T(8,128)(2,1)S(1)}, u32[]{:S(2)}, u32[]{:S(2)}) collective-permute-start(bf16[4,2,48,768]{3,2,1,0:T(8,128)(2,1)S(1)} %dynamic-slice_bitcast_fusion.9), channel_id=1, source_target_pairs={{0,2},{1,3},{2,0},{3,1},{4,6},{5,7},{6,4},{7,5},{8,10},{9,11},{10,... | collective-permute-start | bytes 1769480 | tf_op jit(solution)/shard_map/ppermute | solution.py:913
  455.2 25.0 %collective-permute-start.58 = (bf16[4,2,48,768]{3,2,1,0:T(8,128)(2,1)S(1)}, bf16[4,2,48,768]{3,2,1,0:T(8,128)(2,1)S(1)}, u32[]{:S(2)}, u32[]{:S(2)}) collective-permute-start(bf16[4,2,48,768]{3,2,1,0:T(8,128)(2,1)S(1)} %dynamic-slice_bitcast_fusion.8), channel_id=1, source_target_pairs={{0,4},{4,0},{8,12},{12,8},{16,20},{20,16},{24,28},{28,24},{1,5},{5... | collective-permute-start | bytes 1769480 | tf_op jit(solution)/shard_map/ppermute | solution.py:913
  484.0 16.2 %collective-permute-start.75 = (bf16[96,1536]{1,0:T(8,128)(2,1)}, bf16[96,1536]{1,0:T(8,128)(2,1)}, u32[]{:S(2)}, u32[]{:S(2)}) collective-permute-start(bf16[96,1536]{1,0:T(8,128)(2,1)} %get-tuple-element.618), channel_id=1, source_target_pairs={{0,8},{4,12},{8,16},{12,20},{16,24},{20,28},{24,0},{28,4},{1,9},{5... | collective-permute-start | bytes 884744 | tf_op jit(solution)/shard_map/ppermute | solution.py:913
  491.2 69.6 %collective-permute-start.51 = (bf16[768,1920]{1,0:T(8,128)(2,1)}, bf16[768,1920]{1,0:T(8,128)(2,1)}, u32[]{:S(2)}, u32[]{:S(2)}) collective-permute-start(bf16[768,1920]{1,0:T(8,128)(2,1)} %get-tuple-element.570), channel_id=1, source_target_pairs={{0,1},{1,0},{2,3},{3,2},{4,5},{5,4},{6,7},{7,6},{8,9},{9,8},{10,11... | collective-permute-start | bytes 8847368 | tf_op jit(solution)/shard_map/ppermute | solution.py:913
  496.2 17.2 %collective-permute-start.76 = (bf16[96,1536]{1,0:T(8,128)(2,1)}, bf16[96,1536]{1,0:T(8,128)(2,1)}, u32[]{:S(2)}, u32[]{:S(2)}) collective-permute-start(bf16[96,1536]{1,0:T(8,128)(2,1)} %get-tuple-element.619), channel_id=1, source_target_pairs={{0,16},{4,20},{8,24},{12,28},{16,0},{20,4},{24,8},{28,12},{1,17},{... | collective-permute-start | bytes 884744 | tf_op jit(solution)/shard_map/ppermute | solution.py:913
  499.6 19.9 %collective-permute-start.77 = (bf16[96,1536]{1,0:T(8,128)(2,1)}, bf16[96,1536]{1,0:T(8,128)(2,1)}, u32[]{:S(2)}, u32[]{:S(2)}) collective-permute-start(bf16[96,1536]{1,0:T(8,128)(2,1)} %get-tuple-element.620), channel_id=1, source_target_pairs={{0,24},{4,28},{8,0},{12,4},{16,8},{20,12},{24,16},{28,20},{1,25},{... | collective-permute-start | bytes 884744 | tf_op jit(solution)/shard_map/ppermute | solution.py:913
  499.6 19.9 %collective-permute-start.78 = (bf16[4,48,768]{2,1,0:T(8,128)(2,1)}, bf16[4,48,768]{2,1,0:T(8,128)(2,1)}, u32[]{:S(2)}, u32[]{:S(2)}) collective-permute-start(bf16[4,48,768]{2,1,0:T(8,128)(2,1)} %dynamic-slice_bitcast_fusion.15), channel_id=1, source_target_pairs={{0,4},{4,0},{8,12},{12,8},{16,20},{20,16},{24,28},{28,24},{1,5},{5... | collective-permute-start | bytes 884744 | tf_op jit(solution)/shard_map/ppermute | solution.py:913
  500.1 19.4 %collective-permute-start.79 = (bf16[4,48,768]{2,1,0:T(8,128)(2,1)}, bf16[4,48,768]{2,1,0:T(8,128)(2,1)}, u32[]{:S(2)}, u32[]{:S(2)}) collective-permute-start(bf16[4,48,768]{2,1,0:T(8,128)(2,1)} %dynamic-slice_bitcast_fusion.14), channel_id=1, source_target_pairs={{0,2},{1,3},{2,0},{3,1},{4,6},{5,7},{6,4},{7,5},{8,10},{9,11},{10,... | collective-permute-start | bytes 884744 | tf_op jit(solution)/shard_map/ppermute | solution.py:913
  513.5 42.1 %collective-permute-start.52 = (bf16[48,3456]{1,0:T(8,128)(2,1)S(1)}, bf16[48,3456]{1,0:T(8,128)(2,1)S(1)}, u32[]{:S(2)}, u32[]{:S(2)}) collective-permute-start(bf16[48,3456]{1,0:T(8,128)(2,1)S(1)} %copy-done.48), channel_id=1, source_target_pairs={{0,8},{4,12},{8,16},{12,20},{16,24},{20,28},{24,0},{28,4},{1,9},{5... | collective-permute-start | bytes 995336 | tf_op jit(solution)/shard_map/ppermute | solution.py:913
  522.5 18.1 %collective-permute-start.81 = (bf16[48,1536]{1,0:T(8,128)(2,1)S(1)}, bf16[48,1536]{1,0:T(8,128)(2,1)S(1)}, u32[]{:S(2)}, u32[]{:S(2)}) collective-permute-start(bf16[48,1536]{1,0:T(8,128)(2,1)S(1)} %get-tuple-element.626), channel_id=1, source_target_pairs={{0,16},{4,20},{8,24},{12,28},{16,0},{20,4},{24,8},{28,12},{1,17},{... | collective-permute-start | bytes 442376 | tf_op jit(solution)/shard_map/ppermute | solution.py:913
  525.2 25.1 %collective-permute-start.82 = (bf16[48,1536]{1,0:T(8,128)(2,1)S(1)}, bf16[48,1536]{1,0:T(8,128)(2,1)S(1)}, u32[]{:S(2)}, u32[]{:S(2)}) collective-permute-start(bf16[48,1536]{1,0:T(8,128)(2,1)S(1)} %get-tuple-element.627), channel_id=1, source_target_pairs={{0,24},{4,28},{8,0},{12,4},{16,8},{20,12},{24,16},{28,20},{1,25},{... | collective-permute-start | bytes 442376 | tf_op jit(solution)/shard_map/ppermute | solution.py:913
  534.3 22.8 %collective-permute-start.53 = (bf16[48,3456]{1,0:T(8,128)(2,1)S(1)}, bf16[48,3456]{1,0:T(8,128)(2,1)S(1)}, u32[]{:S(2)}, u32[]{:S(2)}) collective-permute-start(bf16[48,3456]{1,0:T(8,128)(2,1)S(1)} %copy-done.47), channel_id=1, source_target_pairs={{0,16},{4,20},{8,24},{12,28},{16,0},{20,4},{24,8},{28,12},{1,17},{... | collective-permute-start | bytes 995336 | tf_op jit(solution)/shard_map/ppermute | solution.py:913
  540.6 20.1 %collective-permute-start.54 = (bf16[48,3456]{1,0:T(8,128)(2,1)S(1)}, bf16[48,3456]{1,0:T(8,128)(2,1)S(1)}, u32[]{:S(2)}, u32[]{:S(2)}) collective-permute-start(bf16[48,3456]{1,0:T(8,128)(2,1)S(1)} %copy-done.46), channel_id=1, source_target_pairs={{0,24},{4,28},{8,0},{12,4},{16,8},{20,12},{24,16},{28,20},{1,25},{... | collective-permute-start | bytes 995336 | tf_op jit(solution)/shard_map/ppermute | solution.py:913
  564.0 22.4 %collective-permute-start.60 = (bf16[4,2,48,1024]{3,2,1,0:T(8,128)(2,1)S(1)}, bf16[4,2,48,1024]{3,2,1,0:T(8,128)(2,1)S(1)}, u32[]{:S(2)}, u32[]{:S(2)}) collective-permute-start(bf16[4,2,48,1024]{3,2,1,0:T(8,128)(2,1)S(1)} %dynamic-slice_bitcast_fusion.4), channel_id=1, source_target_pairs={{0,4},{4,0},{8,12},{12,8},{16,20},{20,16},{24,28},{28,24},{1,5},{5... | collective-permute-start | bytes 2359304 | tf_op jit(solution)/shard_map/ppermute | solution.py:913
  564.6 21.8 %collective-permute-start.59 = (bf16[4,2,48,896]{3,2,1,0:T(8,128)(2,1)S(1)}, bf16[4,2,48,896]{3,2,1,0:T(8,128)(2,1)S(1)}, u32[]{:S(2)}, u32[]{:S(2)}) collective-permute-start(bf16[4,2,48,896]{3,2,1,0:T(8,128)(2,1)S(1)} %dynamic-slice_bitcast_fusion.5), channel_id=1, source_target_pairs={{0,2},{1,3},{2,0},{3,1},{4,6},{5,7},{6,4},{7,5},{8,10},{9,11},{10,... | collective-permute-start | bytes 2064392 | tf_op jit(solution)/shard_map/ppermute | solution.py:913
  566.2 20.2 %collective-permute-start.61 = (bf16[48,3456]{1,0:T(8,128)(2,1)S(1)}, bf16[48,3456]{1,0:T(8,128)(2,1)S(1)}, u32[]{:S(2)}, u32[]{:S(2)}) collective-permute-start(bf16[48,3456]{1,0:T(8,128)(2,1)S(1)} %fusion.4), channel_id=1, source_target_pairs={{0,2},{1,3},{2,0},{3,1},{4,6},{5,7},{6,4},{7,5},{8,10},{9,11},{10,... | collective-permute-start | bytes 995336 | tf_op jit(solution)/shard_map/ppermute | solution.py:913
  566.8 64.6 %collective-permute-start.84 = (bf16[96,1536]{1,0:T(8,128)(2,1)S(1)}, bf16[96,1536]{1,0:T(8,128)(2,1)S(1)}, u32[]{:S(2)}, u32[]{:S(2)}) collective-permute-start(bf16[96,1536]{1,0:T(8,128)(2,1)S(1)} %maximum_select_fusion.6), channel_id=1, source_target_pairs={{0,1},{1,0},{2,3},{3,2},{4,5},{5,4},{6,7},{7,6},{8,9},{9,8},{10,11... | collective-permute-start | bytes 884744 | tf_op jit(solution)/shard_map/ppermute | solution.py:913
  597.8 14.5 %collective-permute-start.67 = (bf16[48,1920]{1,0:T(8,128)(2,1)S(1)}, bf16[48,1920]{1,0:T(8,128)(2,1)S(1)}, u32[]{:S(2)}, u32[]{:S(2)}) collective-permute-start(bf16[48,1920]{1,0:T(8,128)(2,1)S(1)} %get-tuple-element.605), channel_id=1, source_target_pairs={{0,8},{4,12},{8,16},{12,20},{16,24},{20,28},{24,0},{28,4},{1,9},{5... | collective-permute-start | bytes 552968 | tf_op jit(solution)/shard_map/ppermute | solution.py:913
  616.2 14.3 %collective-permute-start.71 = (bf16[48,1920]{1,0:T(8,128)(2,1)S(1)}, bf16[48,1920]{1,0:T(8,128)(2,1)S(1)}, u32[]{:S(2)}, u32[]{:S(2)}) collective-permute-start(bf16[48,1920]{1,0:T(8,128)(2,1)S(1)} %fusion.13), channel_id=1, source_target_pairs={{0,2},{1,3},{2,0},{3,1},{4,6},{5,7},{6,4},{7,5},{8,10},{9,11},{10,... | collective-permute-start | bytes 552968 | tf_op jit(solution)/shard_map/ppermute | solution.py:913
  (119 other events, 788.0 us)

commit v2 on v1

--- a/solution.py
+++ b/solution.py
@@ -690,7 +690,7 @@
     return run
 
 
-def outer_group(place, pairs, groups, split, micros):
+def outer_group(place, pairs, groups, split, micros, whole=False):
     rows = pairs[0][0].shape[1]
     parts = 2 if split else groups
     inner = parts // 2
@@ -703,12 +703,13 @@
                 for start in range(0, size, 768):
                     tiles.append((side, index, shard, start, min(768, size - start)))
     count = len(pairs)
+    results = 1 if whole else 2
 
     def kernel(place_ref, *refs):
         lefts, rights = refs[:count], refs[count : 2 * count]
-        outs = refs[2 * count : 2 * count + 2]
-        left_refs = refs[2 * count + 2 : 3 * count + 2]
-        right_refs, stage, left_sems, right_sems, out_sems = refs[3 * count + 2 :]
+        outs = refs[2 * count : 2 * count + results]
+        left_refs = refs[2 * count + results : 3 * count + results]
+        right_refs, stage, left_sems, right_sems, out_sems = refs[3 * count + results :]
         arrivals = []
         lefts_here = []
         for number, (side, index, shard, start, size) in enumerate(tiles):
@@ -739,7 +740,10 @@
             terms = dot_outer(left_refs[index][...], right_refs[number, 0:depth, 0:size])
             stage[number, :, 0:size] = terms.astype(HALF)
             column = sum(sizes[:index]) + start
-            target = outs[side] if split else outs[side].at[shard]
+            if whole:
+                target = outs[0].at[(2 * shard + 1 - side) ^ place_ref[0]]
+            else:
+                target = outs[side] if split else outs[side].at[shard]
             copy = pltpu.make_async_copy(
                 stage.at[number, :, pl.ds(0, size)],
                 target.at[:, pl.ds(column, size)],
@@ -750,14 +754,14 @@
         for copy in leaving:
             copy.wait()
 
-    shape = (rows, total) if split else (inner, rows, total)
+    shape = (rows, total) if split else (groups if whole else inner, rows, total)
     lefts, rights = zip(*pairs)
     width = max(tile[4] for tile in tiles)
     return pl.pallas_call(
         kernel,
-        out_shape=[jax.ShapeDtypeStruct(shape, HALF)] * 2,
+        out_shape=[jax.ShapeDtypeStruct(shape, HALF)] * results,
         in_specs=[SMEM] + [HBM] * (2 * count),
-        out_specs=[HBM] * 2,
+        out_specs=[HBM] * results,
         scratch_shapes=[pltpu.VMEM(left.shape, HALF) for left in lefts]
         + [
             pltpu.VMEM((len(tiles), max(left.shape[0] for left in lefts), width), HALF),
@@ -775,86 +779,72 @@
     return (axis, [(index, index ^ bit) for index in range(lax.axis_size(axis))])
 
 
-def shift(step):
-    far = lax.axis_size(DP) // 2
-    return (
-        DP,
-        [
-            (start * 2 + near, (start + step) % far * 2 + near)
-            for start in range(far)
-            for near in range(2)
-        ],
-    )
-
-
 def swap(values, axis, bit):
     return lax.ppermute(values, *exchange(axis, bit))
 
 
-def reduce_group(parts):
-    send, keep = parts
-    other = yield [(send, exchange(TENSOR, 1))]
-    values = keep + other[0]
+def reduce_group(groups, path):
+    others = yield [(send, exchange(TENSOR, 1)) for send, keep in groups]
+    sums = [keep + other for (send, keep), other in zip(groups, others)]
+    values = sums[0] if len(sums) == 1 else jnp.concatenate(sums, -1)
     columns = values.shape[-1]
     blocks = lax.axis_size(DP)
     far = blocks // 2
-    near = lax.axis_index(DP) % 2
-    place = lax.axis_index(DP) // 2
-    middle = columns // 2 // 128 * 128
+    place = lax.axis_index(DP)
+    bits = {"x": lax.axis_index(TENSOR) // 2, "y": place % 2, "u": place // 2 % 2, "w": place // 4}
+    ways = {
+        "x": exchange(TENSOR, 2),
+        "y": exchange(DP, 1),
+        "u": exchange(DP, 2),
+        "w": exchange(DP, 4),
+    }
     if values.ndim == 3:
-        values = values.reshape(2, far, 2, -1, columns)
-        x_dim, y_dim, x_place = 0, 2, 0
+        values = values.reshape(2, 2, 2, 2, -1, columns)
+        dims = "xwuy"
+        bits["x"] = 0
     else:
-        values = values.reshape(far, 2, 2, -1, columns)
-        x_dim, y_dim, x_place = 2, 1, lax.axis_index(TENSOR) // 2
-    over_x, over_y = values[..., :middle], values[..., middle:]
-
-    def of_x(array, mine, dim):
-        return lax.dynamic_index_in_dim(array, x_place if mine else 1 - x_place, dim, False)
-
-    def of_y(array, mine, dim):
-        return lax.dynamic_index_in_dim(array, near if mine else 1 - near, dim, False)
-
-    other = yield [
-        (of_x(over_x, False, x_dim), exchange(TENSOR, 2)),
-        (of_y(over_y, False, y_dim), exchange(DP, 1)),
-    ]
-    over_x = of_x(over_x, True, x_dim) + other[0]
-    over_y = of_y(over_y, True, y_dim) + other[1]
-    y_dim -= x_dim < y_dim
-    x_dim -= x_dim > 0
-    other = yield [
-        (of_y(over_x, False, y_dim), exchange(DP, 1)),
-        (of_x(over_y, False, x_dim), exchange(TENSOR, 2)),
-    ]
-    values = jnp.concatenate(
-        [of_y(over_x, True, y_dim) + other[0], of_x(over_y, True, x_dim) + other[1]], -1
-    )
-    others = yield [
-        (lax.dynamic_index_in_dim(values, (place + step) % far, 0, False), shift(step))
-        for step in range(1, far)
-    ]
-    total = lax.dynamic_index_in_dim(values, place, 0, False).astype(FULL)
-    for other in others:
-        total = total + other.astype(FULL)
-    return total
+        values = values.reshape(2, 2, 2, 2, -1, columns)
+        dims = "wuyx"
+
+    def side(array, left, axis, mine):
+        bit = bits[axis] if mine else 1 - bits[axis]
+        return lax.dynamic_index_in_dim(array, bit, left.index(axis), False)
+
+    if path == "both":
+        middle = columns // 2 // 128 * 128
+        tracks = [[values[..., :middle], "xy"], [values[..., middle:], "yx"]]
+        left = [dims, dims]
+        for step in range(2):
+            others = yield [
+                (side(array, rest, way[step], False), ways[way[step]])
+                for (array, way), rest in zip(tracks, left)
+            ]
+            tracks = [
+                [side(array, rest, way[step], True) + other, way]
+                for (array, way), rest, other in zip(tracks, left, others)
+            ]
+            left = [rest.replace(way[step], "") for (array, way), rest in zip(tracks, left)]
+        values = jnp.concatenate([array for array, way in tracks], -1)
+        dims = left[0]
+        path = "uw"
+    for axis in path:
+        other = yield [(side(values, dims, axis, False), ways[axis])]
+        values = side(values, dims, axis, True) + other[0]
+        dims = dims.replace(axis, "")
+    return values
 
 
 def reduce_norms(values):
     count = lax.axis_size(DP)
-    far = count // 2
-    for axis, bit in ((TENSOR, 1), (TENSOR, 2), (DP, 1)):
+    for axis, bit in ((TENSOR, 1), (TENSOR, 2), (DP, 1), (DP, 2), (DP, 4)):
         other = yield [(values, exchange(axis, bit))]
         values = values + other[0]
-    others = yield [(values, shift(step)) for step in range(1, far)]
-    for other in others:
-        values = values + other
     lanes = values.shape[1] // count
     return lax.dynamic_slice_in_dim(values, lax.axis_index(DP) * lanes, lanes, 1)
 
 
-def reduce_attention(parts, sizes):
-    values = (yield from reduce_group(parts)).astype(HALF)
+def reduce_attention(groups, path, sizes):
+    values = yield from reduce_group(groups, path)
     other = yield [(values, exchange(TENSOR, 2))]
     values = in_order(values, other[0], 2, 0)
     other = yield [(values, exchange(TENSOR, 1))]
@@ -904,15 +894,15 @@
     def start(self, name, steps):
         self.asked[name] = (steps, next(steps))
 
-    def leave(self, values):
-        sends = [[send for send, way in asked] for steps, asked in self.asked.values()]
+    def leave(self, values, names=None):
+        asked = {name: self.asked.pop(name) for name in list(names or self.asked) if name in self.asked}
+        sends = [[send for send, way in entry[1]] for entry in asked.values()]
         values, sends = lax.optimization_barrier((values, sends))
-        for (name, (steps, asked)), ready in zip(self.asked.items(), sends):
+        for (name, (steps, entry)), ready in zip(asked.items(), sends):
             self.running[name] = (
                 steps,
-                [lax.ppermute(send, *way) for send, (unused, way) in zip(ready, asked)],
+                [lax.ppermute(send, *way) for send, (unused, way) in zip(ready, entry)],
             )
-        self.asked = {}
         return values
 
     def land(self, names, values):
@@ -925,7 +915,10 @@
                 self.asked[name] = (steps, steps.send(arrived))
             except StopIteration as stop:
                 self.results[name] = stop.value
-        return self.leave(values)
+        return values
+
+    def turn(self, names, values):
+        return self.leave(self.land(names, values), names)
 
 
 def spread(pieces):
@@ -1119,17 +1112,24 @@
     usual = blocks_dp == 2 * NEAR
     norms = [None] * layers
 
-    def start(name, pairs, split, micros):
+    def outer(pairs, split, micros):
+        return outer_group(place, pairs, groups, split, micros)
+
+    def start(name, pairs, path, split, micros, first=()):
+        pairs = tuple(pairs)
         if split and not usual:
-            flights.results[name] = reduce_whole(pairs)
+            flights.results[name] = reduce_whole([pair for early in first for pair in early[0]] + list(pairs))
             return
-        parts = outer_group(place, pairs, groups, split, micros)
+        parts = [early[1] for early in first] + [outer(pairs, split, micros)]
         if split:
-            flights.start(name, reduce_attention(parts, [right.shape[1] for left, right in pairs]))
+            sizes = []
+            for own in [early[0] for early in first] + [pairs]:
+                sizes.append([right.shape[1] for left, right in own])
+            flights.start(name, reduce_attention(parts, path, sum(sizes, [])))
         elif usual:
-            flights.start(name, reduce_group(parts))
+            flights.start(name, reduce_group(parts, path))
         else:
-            flights.start(name, reduce_far(parts))
+            flights.start(name, reduce_far(parts[0]))
 
     for layer in reversed(range(layers)):
         start_rows, time, space, feed = saved[layer]
@@ -1166,11 +1166,20 @@
         arrived = spread(feed_back[5:9])
         pairs = ((feed[2], grad_hidden), (update, feed[3]))
         if last:
-            start("feed0", pairs, False, 10)
-            arrived = flights.land(("feed1", "attention1"), arrived)
+            pairs = flights.turn(["feed1"], pairs)
+            time_pairs = lax.optimization_barrier((time_pairs, pairs))[0]
+            start("attention1", time_pairs, "both", True, 9, [early])
+            pairs = flights.leave(pairs, ["attention1"])
+            start("feed0", pairs, "both", False, 10)
+            arrived, feed_sum = lax.optimization_barrier((arrived, feed_sum))
+            feed_sum = lax.psum_scatter(feed_sum, DP, scatter_dimension=0, tiled=True)
+            arrived = flights.turn(["feed1", "attention1"], arrived)
         else:
-            start("feed1", pairs, False, 10)
-            arrived = flights.leave(arrived)
+            total = outer_group(place, pairs, groups, False, 10, True)[0]
+            arrived, total = lax.optimization_barrier((arrived, total))
+            total = total.reshape(-1, total.shape[-1])
+            feed_sum = lax.psum_scatter(total, TENSOR, scatter_dimension=0, tiled=True)
+        arrived = flights.leave(arrived)
         space_back = call(
             partial(space_backward, dims, layer),
             [((span, 3 * width), HALF)] + backs_out,
@@ -1183,14 +1192,23 @@
             [ROWS] * groups + [ROWS] * 3 + [FAR],
             29,
         )(*arrived, feed_back[9], space[1], space[2], spatial_in)
-        arrived = spread(space_back[1:])
+        pieces = space_back[1:]
+        if last:
+            pieces = flights.land(["feed1", "feed0"], pieces)
+        arrived = spread(pieces)
         pairs = ((space[0], space_back[0]), (feed[0], branch))
         if last:
-            start("space0", pairs, True, 8)
-            arrived = flights.land(("feed1", "feed0", "attention1"), arrived)
+            start("space0", pairs, "xyuw", True, 8)
+            arrived = flights.land(["attention1"], arrived)
+            arrived = flights.leave(arrived)
         else:
-            space_pairs = pairs
-            arrived = flights.land(("feed1",), arrived)
+            pairs = flights.turn(["feed1"], pairs)
+            if usual:
+                early = (pairs, outer(pairs, True, 8))
+                arrived, parts = lax.optimization_barrier((arrived, early[1]))
+                early = (pairs, parts)
+            else:
+                early = (pairs, None)
         time_back = call(
             partial(time_backward, dims, layer),
             [
@@ -1234,26 +1252,28 @@
                 flights.results["norms"] = lax.psum_scatter(
                     total, DP, scatter_dimension=1, tiled=True
                 )
-            start("time0", pairs, True, 9)
-            token = flights.land(("feed1", "attention1"), time_back[4])
+            start("time0", pairs, "both", True, 9)
+            token = grad_rows[count : count + clips]
+            token = flights.leave(token, ["time0"])
+            token, flights.results["feed1"] = lax.optimization_barrier((token, feed_sum))
         else:
-            start("attention1", space_pairs + pairs, True, 17)
-            grad_rows = flights.land(("feed1",), grad_rows)
+            time_pairs = pairs
+            grad_rows = flights.turn(["feed1"], grad_rows)
     for names in (
-        ("feed0", "space0"),
-        ("time0", "attention1"),
-        ("feed0", "space0"),
-        ("time0", "attention1", "norms"),
-        ("feed0", "space0"),
-        ("time0", "attention1", "norms"),
-        ("feed0", "space0"),
-        ("time0", "norms"),
-        ("space0",),
-        ("time0", "norms"),
+        ("attention1", "feed0", "space0"),
+        ("attention1", "feed0", "time0", "norms"),
+        ("space0", "time0", "norms"),
+        ("attention1", "feed0"),
+        ("space0", "time0", "norms"),
+        ("attention1", "feed0"),
+        ("space0", "time0", "norms"),
+        ("attention1",),
+        ("space0", "time0", "norms"),
+        ("space0", "time0"),
     ):
-        token = flights.land(names, token)
+        token = flights.turn(names, token)
     while flights.running:
-        token = flights.land(list(flights.running), token)
+        token = flights.turn(list(flights.running), token)
     results = flights.results
     lanes = width // blocks_dp
 
@@ -1265,13 +1285,13 @@
     gradients = (
         *[jnp.stack([sums[index] for sums in time_sums]) for index in range(3)],
         *[jnp.stack([sums[index] for sums in space_sums]) for index in range(2)],
-        jnp.stack([sums[:, :width] for sums in feeds]),
-        jnp.stack([sums[:, width:].T for sums in feeds]),
+        jnp.stack([sums[:, :width].astype(FULL) for sums in feeds]),
+        jnp.stack([sums[:, width:].T.astype(FULL) for sums in feeds]),
         norm_sums[0],
         norm_sums[1],
     )
     patch_grad = grad_rows[:count].reshape(frames, patches, width)
-    class_grad = grad_rows[count : count + clips]
+    class_grad = token
     return (patch_output, class_output, patch_grad, class_grad, *gradients)
 
 

time: 649 us -> 584 us (0.90)
  starting transfers between devices: 110 us -> 58.2 us
  waiting for transfers between devices: 182 us -> 155 us
  between operations: 2.46 us -> 15.9 us
  other arithmetic: 59.3 us -> 52.4 us
    ppermute x62 -> x48, starting transfers between devices: 93.2 us -> 41.7 us  [leave(): lax.ppermute(send, *way)]
    ppermute x24, waiting for transfers between devices: 63.9 us -> 34 us  [swap(): return lax.ppermute(values, *exchange(axis, bit))]
    dynamic_slice x0 -> x10, local copies, waits for them, and re-layouts: none -> 10.2 us  [side(): return lax.dynamic_index_in_dim(array, bit, left.index(axis), False)]
    add x28 -> x27, other arithmetic: 37.5 us -> 31.6 us  [the longest x5 15.9 us: reduce_group(): sums = [keep + other for (send, keep), other in zip(groups, others)]]
    ppermute x62 -> x48, waiting for transfers between devices: 119 us -> 121 us  [leave(): lax.ppermute(send, *way)]
    pallas_call x5 -> x6, Pallas kernels: 54.4 us -> 56.9 us  [outer_group(): pl.pallas_call(kernel, out_shape=[jax.ShapeDtypeStruct(shape, HALF)] * re...]
    unnamed x168 -> x158, local copies, waits for them, and re-layouts: 20.3 us -> 17.9 us
  transfers between devices with their start and end apart: 86 -> 74, of which waited for: 36 -> 32; matrix products, arithmetic and copies ran while one was open for 5% -> 11% of each run, Pallas kernels for 32% -> 36%
where the time goes in v2:
time: 584 us; the launch traced here: 573 us
  Pallas kernels  237 us (41%)
  waiting for transfers between devices  155 us (27%)
  starting transfers between devices  58.2 us (10%)
  local copies, waits for them, and re-layouts  53.8 us (9%)
  other arithmetic  52.4 us (9%)
  between operations  15.9 us (3%)
    pallas_call x12, Pallas kernels, run(): pl.pallas_call(whole, out_shape=[jax.ShapeDtypeStruct(shape, kind) for sh...  180 us
    ppermute x48, waiting for transfers between devices, leave(): lax.ppermute(send, *way)  121 us
    pallas_call x6, Pallas kernels, outer_group(): pl.pallas_call(kernel, out_shape=[jax.ShapeDtypeStruct(shape, HALF)] * re...  56.9 us
    ppermute x48, starting transfers between devices, leave(): lax.ppermute(send, *way)  41.7 us
    ppermute x24, waiting for transfers between devices, swap(): return lax.ppermute(values, *exchange(axis, bit))  34 us
    unnamed x158, local copies, waits for them, and re-layouts  17.9 us
    ppermute x24, starting transfers between devices, swap(): return lax.ppermute(values, *exchange(axis, bit))  16.1 us
    add x5, other arithmetic, reduce_group(): sums = [keep + other for (send, keep), other in zip(groups, others)]  15.9 us
  transfers between devices with their start and end apart: 74, of which 32 were waited for; matrix products, arithmetic and copies ran while one was open for 11% of the time, Pallas kernels for 36%

profile of v2, /device:TPU:0, one launch (start us, length us, event | category | flops | bytes accessed | tf_op | source)
XLA Modules:
  0.0 572.6 jit_solution(8721170302882152302)
XLA Ops:
  10.7 2.9 fusion.20
  30.2 15.0 %shard_map.237 = (bf16[400,768]{1,0:T(8,128)(2,1)}, bf16[400,2304]{1,0:T(8,128)(2,1)}, f32[400,128]{1,0:T(8,128)}, bf16[400,768]{1,0:T(8,128)(2,1)}, bf16[400,76...) custom-call(s32[2]{0:T(128)} %pad_add_fusion.refs_0_.place_ref, ...), custom_call_target="tpu_custom_call" | custom-call | flops 14 | bytes 14 | tf_op jit(solution)/shard_map/pallas_call | solution.py:677
  48.3 7.9 %collective-permute-done.1.refs_5_ = bf16[98,768]{1,0:T(8,128)(2,1)S(1)} collective-permute-done((bf16[98,768]{1,0:T(8,128)(2,1)}, bf16[98,768]{1,0:T(8,128)(2,1)S(1)}, u32[]{:S(2)}, u32[]{:S(2)}) %collective-permute-start.1) | collective-permute-done | bytes 150560 | tf_op jit(solution)/shard_map/ppermute | solution.py:783
  56.2 3.1 collective-permute-done.2.refs_6_
  61.5 11.1 %shard_map.238 = (bf16[416,768]{1,0:T(8,128)(2,1)}, bf16[416,2304]{1,0:T(8,128)(2,1)}, f32[416,128]{1,0:T(8,128)}, bf16[104,768]{1,0:T(8,128)(2,1)}, bf16[104,76...) custom-call(s32[2]{0:T(128)} %pad_add_fusion.refs_0_.place_ref, s32[8]{0:T(128)} %copy-done.63, ...), custom_call_target="tpu_custom_call" | custom-call | flops 9 | bytes 9 | tf_op jit(solution)/shard_map/pallas_call | solution.py:677
  74.6 5.3 collective-permute-done.6.refs_3_
  82.4 5.7 %collective-permute-done.8.refs_14_.refs_12_ = bf16[2,384,768]{2,1,0:T(8,128)(2,1)S(1)} collective-permute-done((bf16[2,384,768]{2,1,0:T(8,128)(2,1)}, bf16[2,384,768]{2,1,0:T(8,128)(2,1)S(1)}, u32[]{:S(2)}, u32[]{:S(2)}) %collective-permute-start.8) | collective-permute-done | bytes 1179680 | tf_op jit(solution)/shard_map/ppermute | solution.py:904
  91.1 5.2 collective-permute-done.9.refs_15_.refs_13_
  97.7 14.5 %shard_map.239 = (bf16[400,768]{1,0:T(8,128)(2,1)}, f32[400,768]{1,0:T(8,128)}, bf16[400,768]{1,0:T(8,128)(2,1)}, bf16[400,3072]{1,0:T(8,128)(2,1)}, bf16[400,3072]{1,0:T(8,128)(2,1)}, /*index=5*/f32[400,768]{1,0:T(8,128)}) custom-call(s32[2]{0:T(128)} %pad_add_fusion.refs_0_.place_ref, bf16[104,768]{1,0:T(8,128)(2,1)} %get-tuple-element.364.refs_1_, ...), custom_call_target="tpu_custom_call" | custom-call | flops 15 | bytes 15 | tf_op jit(solution)/shard_map/pallas_call | solution.py:677
  112.2 5.2 collective-permute-done.11.refs_13_.refs_11_
  119.0 14.9 %shard_map.240 = (bf16[400,768]{1,0:T(8,128)(2,1)}, bf16[400,2304]{1,0:T(8,128)(2,1)}, f32[400,128]{1,0:T(8,128)}, bf16[400,768]{1,0:T(8,128)(2,1)}, bf16[400,76...) custom-call(s32[2]{0:T(128)} %pad_add_fusion.refs_0_.place_ref, ...), custom_call_target="tpu_custom_call" | custom-call | flops 14 | bytes 14 | tf_op jit(solution)/shard_map/pallas_call | solution.py:677
  136.1 5.3 collective-permute-done.14.refs_5_
  144.6 10.9 %shard_map.241 = (bf16[416,768]{1,0:T(8,128)(2,1)}, bf16[416,2304]{1,0:T(8,128)(2,1)}, f32[416,128]{1,0:T(8,128)}, bf16[104,768]{1,0:T(8,128)(2,1)}, bf16[104,76...) custom-call(s32[2]{0:T(128)} %pad_add_fusion.refs_0_.place_ref, s32[8]{0:T(128)} %copy-done.63, ...), custom_call_target="tpu_custom_call" | custom-call | flops 9 | bytes 9 | tf_op jit(solution)/shard_map/pallas_call | solution.py:677
  157.7 5.7 collective-permute-done.17.refs_3_
  165.9 3.5 collective-permute-done.20.refs_15_.refs_13_
  171.0 14.4 %shard_map.242 = (bf16[400,768]{1,0:T(8,128)(2,1)}, f32[400,768]{1,0:T(8,128)}, bf16[400,768]{1,0:T(8,128)(2,1)}, bf16[400,3072]{1,0:T(8,128)(2,1)}, bf16[400,3072]{1,0:T(8,128)(2,1)}, /*index=5*/f32[400,768]{1,0:T(8,128)}) custom-call(s32[2]{0:T(128)} %pad_add_fusion.refs_0_.place_ref, bf16[104,768]{1,0:T(8,128)(2,1)} %get-tuple-element.403.refs_1_, ...), custom_call_target="tpu_custom_call" | custom-call | flops 15 | bytes 15 | tf_op jit(solution)/shard_map/pallas_call | solution.py:677
  186.1 17.1 %shard_map.243 = (bf16[400,768]{1,0:T(8,128)(2,1)}, bf16[400,3072]{1,0:T(8,128)(2,1)}, bf16[400,768]{1,0:T(8,128)(2,1)}, f32[400,768]{1,0:T(8,128)}, f32[8,768]{...) custom-call(s32[2]{0:T(128)} %pad_add_fusion.refs_0_.place_ref, ...), custom_call_target="tpu_custom_call" | custom-call | flops 23 | bytes 23 | tf_op jit(solution)/shard_map/pallas_call | solution.py:677
  205.1 12.3 %shard_map.244 = bf16[4,768,1536]{2,1,0:T(8,128)(2,1)} custom-call(s32[2]{0:T(128)} %pad_add_fusion.refs_0_.place_ref, bf16[400,768]{1,0:T(8,128)(2,1)} %get-tuple-element.418.refs_0_, bf16[400,768]{1,0:T(8,128)(2,1)} %get-tuple-element.419.refs_1_, bf16[400,3072]{1,0:T(8,128)(2,1)} %get-tuple-element.420.refs_2_, bf16[400,3072]{1,0:T(8,128)(2,1)} %get-tuple-element.421.refs_3_), custom_call_target="tpu_custom_call" | custom-call | flops 10 | bytes 10 | tf_op jit(solution)/shard_map/pallas_call | solution.py:760
  218.6 13.1 %shard_map.245 = (bf16[416,2304]{1,0:T(8,128)(2,1)}, bf16[104,768]{1,0:T(8,128)(2,1)}, bf16[104,768]{1,0:T(8,128)(2,1)}, bf16[104,768]{1,0:T(8,128)(2,1)}, bf16[104,768]{1,0:T(8,128)(2,1)}) custom-call(bf16[98,768]{1,0:T(8,128)(2,1)} %get-tuple-element.426.refs_0_, bf16[98,768]{1,0:T(8,128)(2,1)} %copy-done.48, bf16[98,768]{1,0:T(8,128)(2,1)} %copy-done.49, ...), custom_call_target="tpu_custom_call" | custom-call | flops 29 | bytes 29 | tf_op jit(solution)/shard_map/pallas_call | solution.py:677
  234.5 7.4 %shard_map.246 = (bf16[768,1536]{1,0:T(8,128)(2,1)}, bf16[768,1536]{1,0:T(8,128)(2,1)}) custom-call(s32[2]{0:T(128)} %pad_add_fusion.refs_0_.place_ref, bf16[416,768]{1,0:T(8,128)(2,1)} %get-tuple-element.441.refs_0_, bf16[400,768]{1,0:T(8,128)(2,1)} %get-tuple-element.442.refs_1_, bf16[416,2304]{1,0:T(8,128)(2,1)} %get-tuple-element.443.refs_2_, ...), custom_call_target="tpu_custom_call" | custom-call | flops 8 | bytes 8 | tf_op jit(solution)/shard_map/pallas_call | solution.py:760
  242.7 19.4 %shard_map.247 = (bf16[400,768]{1,0:T(8,128)(2,1)}, bf16[400,768]{1,0:T(8,128)(2,1)}, bf16[400,2304]{1,0:T(8,128)(2,1)}, f32[400,768]{1,0:T(8,128)}, f32[8,768]{1,0:T(8,128)}) custom-call(s32[2]{0:T(128)} %pad_add_fusion.refs_0_.place_ref, bf16[104,768]{1,0:T(8,128)(2,1)} %get-tuple-element.447.refs_1_, bf16[104,768]{1,0:T(8,128)(2,1)} %copy-done.59, ...), custom_call_target="tpu_custom_call" | custom-call | flops 14 | bytes 14 | tf_op jit(solution)/shard_map/pallas_call | solution.py:677
  262.1 17.3 %shard_map.248 = (bf16[400,768]{1,0:T(8,128)(2,1)}, bf16[400,3072]{1,0:T(8,128)(2,1)}, bf16[400,768]{1,0:T(8,128)(2,1)}, f32[400,768]{1,0:T(8,128)}, f32[8,768]{...) custom-call(s32[2]{0:T(128)} %pad_add_fusion.refs_0_.place_ref, ...), custom_call_target="tpu_custom_call" | custom-call | flops 23 | bytes 23 | tf_op jit(solution)/shard_map/pallas_call | solution.py:677
  279.3 8.6 %shard_map.249 = (bf16[768,1920]{1,0:T(8,128)(2,1)}, bf16[768,1920]{1,0:T(8,128)(2,1)}) custom-call(s32[2]{0:T(128)} %pad_add_fusion.refs_0_.place_ref, bf16[400,768]{1,0:T(8,128)(2,1)} %get-tuple-element.481.refs_0_, bf16[400,768]{1,0:T(8,128)(2,1)} %get-tuple-element.482.refs_1_, bf16[400,768]{1,0:T(8,128)(2,1)} %get-tuple-element.483.refs_2_, ...), custom_call_target="tpu_custom_call" | custom-call | flops 9 | bytes 9 | tf_op jit(solution)/shard_map/pallas_call | solution.py:760
  290.5 12.4 %shard_map.250 = (bf16[2,768,1536]{2,1,0:T(8,128)(2,1)}, bf16[2,768,1536]{2,1,0:T(8,128)(2,1)}) custom-call(s32[2]{0:T(128)} %pad_add_fusion.refs_0_.place_ref, bf16[400,768]{1,0:T(8,128)(2,1)} %get-tuple-element.502.refs_0_, bf16[400,768]{1,0:T(8,128)(2,1)} %get-tuple-element.503.refs_1_, bf16[400,3072]{1,0:T(8,128)(2,1)} %get-tuple-element.504.refs_2_, ...), custom_call_target="tpu_custom_call" | custom-call | flops 10 | bytes 10 | tf_op jit(solution)/shard_map/pallas_call | solution.py:760
  303.0 2.7 add.260
  317.2 13.2 %shard_map.251 = (bf16[416,2304]{1,0:T(8,128)(2,1)}, bf16[104,768]{1,0:T(8,128)(2,1)}, bf16[104,768]{1,0:T(8,128)(2,1)}, bf16[104,768]{1,0:T(8,128)(2,1)}, bf16[104,768]{1,0:T(8,128)(2,1)}) custom-call(bf16[98,768]{1,0:T(8,128)(2,1)} %get-tuple-element.507.refs_0_, bf16[98,768]{1,0:T(8,128)(2,1)} %copy-done.45, bf16[98,768]{1,0:T(8,128)(2,1)} %copy-done.46, ...), custom_call_target="tpu_custom_call" | custom-call | flops 29 | bytes 29 | tf_op jit(solution)/shard_map/pallas_call | solution.py:677
  330.5 7.5 %shard_map.252 = (bf16[768,1536]{1,0:T(8,128)(2,1)}, bf16[768,1536]{1,0:T(8,128)(2,1)}) custom-call(s32[2]{0:T(128)} %pad_add_fusion.refs_0_.place_ref, bf16[416,768]{1,0:T(8,128)(2,1)} %get-tuple-element.531.refs_0_, bf16[400,768]{1,0:T(8,128)(2,1)} %get-tuple-element.532.refs_1_, bf16[416,2304]{1,0:T(8,128)(2,1)} %get-tuple-element.533.refs_2_, ...), custom_call_target="tpu_custom_call" | custom-call | flops 8 | bytes 8 | tf_op jit(solution)/shard_map/pallas_call | solution.py:760
  340.0 3.9 add.263
  347.5 6.0 %collective-permute-done.38 = bf16[2,2,2,48,1792]{4,3,1,0,2:T(8,128)(2,1)} collective-permute-done((bf16[2,2,2,48,1792]{4,3,1,0,2:T(8,128)(2,1)}, bf16[2,2,2,48,1792]{4,3,1,0,2:T(8,128)(2,1)}, u32[]{:S(2)}, u32[]{:S(2)}) %collective-permute-start.38) | collective-permute-done | bytes 1376288 | tf_op jit(solution)/shard_map/ppermute | solution.py:904
  364.8 19.5 %shard_map.253 = (bf16[400,768]{1,0:T(8,128)(2,1)}, bf16[400,768]{1,0:T(8,128)(2,1)}, bf16[400,2304]{1,0:T(8,128)(2,1)}, f32[400,768]{1,0:T(8,128)}, f32[8,768]{1,0:T(8,128)}) custom-call(s32[2]{0:T(128)} %pad_add_fusion.refs_0_.place_ref, bf16[104,768]{1,0:T(8,128)(2,1)} %get-tuple-element.538.refs_1_, bf16[104,768]{1,0:T(8,128)(2,1)} %copy-done.51, ...), custom_call_target="tpu_custom_call" | custom-call | flops 14 | bytes 14 | tf_op jit(solution)/shard_map/pallas_call | solution.py:677
  384.3 8.7 %shard_map.254 = (bf16[768,1920]{1,0:T(8,128)(2,1)}, bf16[768,1920]{1,0:T(8,128)(2,1)}) custom-call(s32[2]{0:T(128)} %pad_add_fusion.refs_0_.place_ref, bf16[400,768]{1,0:T(8,128)(2,1)} %get-tuple-element.546.refs_0_, bf16[400,768]{1,0:T(8,128)(2,1)} %get-tuple-element.547.refs_1_, bf16[400,768]{1,0:T(8,128)(2,1)} %get-tuple-element.548.refs_2_, ...), custom_call_target="tpu_custom_call" | custom-call | flops 9 | bytes 9 | tf_op jit(solution)/shard_map/pallas_call | solution.py:760
  394.3 13.2 %collective-permute-done.39 = bf16[2,2,48,1664]{3,2,1,0:T(8,128)(2,1)} collective-permute-done((bf16[2,2,48,1664]{3,2,1,0:T(8,128)(2,1)}, bf16[2,2,48,1664]{3,2,1,0:T(8,128)(2,1)}, u32[]{:S(2)}, u32[]{:S(2)}) %collective-permute-start.39) | collective-permute-done | bytes 639008 | tf_op jit(solution)/shard_map/ppermute | solution.py:904
  407.5 3.0 add.274
  427.9 11.2 %collective-permute-done.45 = bf16[2,2,96,768]{3,2,1,0:T(8,128)(2,1)} collective-permute-done((bf16[2,2,96,768]{3,2,1,0:T(8,128)(2,1)}, bf16[2,2,96,768]{3,2,1,0:T(8,128)(2,1)}, u32[]{:S(2)}, u32[]{:S(2)}) %collective-permute-start.45) | collective-permute-done | bytes 589856 | tf_op jit(solution)/shard_map/ppermute | solution.py:904
  441.4 3.7 add.280
  467.9 12.5 %collective-permute-done.49 = bf16[2,2,2,48,896]{4,3,1,0,2:T(8,128)(2,1)} collective-permute-done((bf16[2,2,2,48,896]{4,3,1,0,2:T(8,128)(2,1)}, bf16[2,2,2,48,896]{4,3,1,0,2:T(8,128)(2,1)}, u32[]{:S(2)}, u32[]{:S(2)}) %collective-permute-start.49) | collective-permute-done | bytes 688160 | tf_op jit(solution)/shard_map/ppermute | solution.py:904
  485.4 4.2 collective-permute-done.53
  494.9 9.8 %collective-permute-done.57 = f32[12,768]{1,0:T(8,128)S(1)} collective-permute-done((f32[12,768]{1,0:T(8,128)S(1)}, f32[12,768]{1,0:T(8,128)S(1)}, u32[]{:S(2)}, u32[]{:S(2)}) %collective-permute-start.57) | collective-permute-done | bytes 36896 | tf_op jit(solution)/shard_map/ppermute | solution.py:904
  504.7 6.9 %collective-permute-done.55 = bf16[2,2,48,896]{3,2,1,0:T(8,128)(2,1)S(1)} collective-permute-done((bf16[2,2,48,896]{3,2,1,0:T(8,128)(2,1)S(1)}, bf16[2,2,48,896]{3,2,1,0:T(8,128)(2,1)S(1)}, u32[]{:S(2)}, u32[]{:S(2)}) %collective-permute-start.55) | collective-permute-done | bytes 344096 | tf_op jit(solution)/shard_map/ppermute | solution.py:904
  511.9 4.7 collective-permute-done.59
  523.0 3.8 collective-permute-done.60
  526.8 4.9 collective-permute-done.61
  532.1 2.9 collective-permute-start.65
  535.3 3.7 collective-permute-done.66
  539.1 4.1 collective-permute-done.64
  543.1 3.8 collective-permute-done.65
  549.4 4.3 collective-permute-done.67
  553.8 2.9 collective-permute-done.68
  (415 shorter events, 157.5 us)
Async XLA Ops:
  7.2 295.7 %reduce-scatter.3.cloned.1.call-start = ((), (), s32[]{:S(2)}) async-start(), calls=%async_computation.2 | async-start | bytes 11796480 | tf_op jit(solution)/shard_map/reduce_scatter | solution.py:1181
  22.8 36.5 %collective-permute-start.4 = (bf16[2,768,768]{2,1,0:T(8,128)(2,1)}, bf16[2,768,768]{2,1,0:T(8,128)(2,1)S(1)}, u32[]{:S(2)}, u32[]{:S(2)}) collective-permute-start(bf16[2,768,768]{2,1,0:T(8,128)(2,1)} %get-tuple-element.338), channel_id=1, source_target_pairs={{0,1},{1,0},{2,3},{3,2},{4,5},{5,4},{6,7},{7,6},{8,9},{9,8},{10,11... | collective-permute-start | bytes 7077896 | tf_op jit(solution)/shard_map/ppermute | solution.py:904
  23.3 36.0 %collective-permute-start.3 = (bf16[2,384,768]{2,1,0:T(8,128)(2,1)}, bf16[2,384,768]{2,1,0:T(8,128)(2,1)}, u32[]{:S(2)}, u32[]{:S(2)}) collective-permute-start(bf16[2,384,768]{2,1,0:T(8,128)(2,1)} %pad_maximum_fusion.3), channel_id=1, source_target_pairs={{0,2},{1,3},{2,0},{3,1},{4,6},{5,7},{6,4},{7,5},{8,10},{9,11},{10,... | collective-permute-start | bytes 3538952 | tf_op jit(solution)/shard_map/ppermute | solution.py:904
  45.5 10.8 %collective-permute-start.1 = (bf16[98,768]{1,0:T(8,128)(2,1)}, bf16[98,768]{1,0:T(8,128)(2,1)S(1)}, u32[]{:S(2)}, u32[]{:S(2)}) collective-permute-start(bf16[98,768]{1,0:T(8,128)(2,1)} %get-tuple-element.335), channel_id=1, source_target_pairs={{0,2},{1,3},{2,0},{3,1},{4,6},{5,7},{6,4},{7,5},{8,10},{9,11},{10,... | collective-permute-start | bytes 451592 | tf_op jit(solution)/shard_map/ppermute | solution.py:783
  45.7 13.6 %collective-permute-start.2 = (bf16[98,768]{1,0:T(8,128)(2,1)}, bf16[98,768]{1,0:T(8,128)(2,1)S(1)}, u32[]{:S(2)}, u32[]{:S(2)}) collective-permute-start(bf16[98,768]{1,0:T(8,128)(2,1)} %get-tuple-element.336), channel_id=1, source_target_pairs={{0,3},{1,2},{2,1},{3,0},{4,7},{5,6},{6,5},{7,4},{8,11},{9,10},{10,... | collective-permute-start | bytes 451592 | tf_op jit(solution)/shard_map/ppermute | solution.py:783
  60.0 28.2 %collective-permute-start.8 = (bf16[2,384,768]{2,1,0:T(8,128)(2,1)}, bf16[2,384,768]{2,1,0:T(8,128)(2,1)S(1)}, u32[]{:S(2)}, u32[]{:S(2)}) collective-permute-start(bf16[2,384,768]{2,1,0:T(8,128)(2,1)} %collective-permute-done.3.refs_13_.refs_11_), channel_id=1, source_target_pairs={{0,4},{4,0},{8,12},{12,8},{16,20},{20,16},{24,28},{28,24},{1,5},{5... | collective-permute-start | bytes 3538952 | tf_op jit(solution)/shard_map/ppermute | solution.py:904
  88.2 29.2 %collective-permute-start.12 = (bf16[2,768,768]{2,1,0:T(8,128)(2,1)}, bf16[2,768,768]{2,1,0:T(8,128)(2,1)S(1)}, u32[]{:S(2)}, u32[]{:S(2)}) collective-permute-start(bf16[2,768,768]{2,1,0:T(8,128)(2,1)} %get-tuple-element.374), channel_id=1, source_target_pairs={{0,1},{1,0},{2,3},{3,2},{4,5},{5,4},{6,7},{7,6},{8,9},{9,8},{10,11... | collective-permute-start | bytes 7077896 | tf_op jit(solution)/shard_map/ppermute | solution.py:904
  88.8 28.6 %collective-permute-start.11 = (bf16[2,384,768]{2,1,0:T(8,128)(2,1)}, bf16[2,384,768]{2,1,0:T(8,128)(2,1)}, u32[]{:S(2)}, u32[]{:S(2)}) collective-permute-start(bf16[2,384,768]{2,1,0:T(8,128)(2,1)} %pad_maximum_fusion.4), channel_id=1, source_target_pairs={{0,2},{1,3},{2,0},{3,1},{4,6},{5,7},{6,4},{7,5},{8,10},{9,11},{10,... | collective-permute-start | bytes 3538952 | tf_op jit(solution)/shard_map/ppermute | solution.py:904
  117.4 47.6 %collective-permute-start.19 = (bf16[2,384,768]{2,1,0:T(8,128)(2,1)}, bf16[2,384,768]{2,1,0:T(8,128)(2,1)S(1)}, u32[]{:S(2)}, u32[]{:S(2)}) collective-permute-start(bf16[2,384,768]{2,1,0:T(8,128)(2,1)} %collective-permute-done.11.refs_13_.refs_11_), channel_id=1, source_target_pairs={{0,4},{4,0},{8,12},{12,8},{16,20},{20,16},{24,28},{28,24},{1,5},{5... | collective-permute-start | bytes 3538952 | tf_op jit(solution)/shard_map/ppermute | solution.py:904
  203.1 14.3 %collective-permute-start.22 = (bf16[98,768]{1,0:T(8,128)(2,1)}, bf16[98,768]{1,0:T(8,128)(2,1)S(1)}, u32[]{:S(2)}, u32[]{:S(2)}) collective-permute-start(bf16[98,768]{1,0:T(8,128)(2,1)} %get-tuple-element.415), channel_id=1, source_target_pairs={{0,1},{1,0},{2,3},{3,2},{4,5},{5,4},{6,7},{7,6},{8,9},{9,8},{10,11... | collective-permute-start | bytes 451592 | tf_op jit(solution)/shard_map/ppermute | solution.py:783
  203.6 13.8 %collective-permute-start.23 = (bf16[98,768]{1,0:T(8,128)(2,1)}, bf16[98,768]{1,0:T(8,128)(2,1)S(1)}, u32[]{:S(2)}, u32[]{:S(2)}) collective-permute-start(bf16[98,768]{1,0:T(8,128)(2,1)} %get-tuple-element.416), channel_id=1, source_target_pairs={{0,2},{1,3},{2,0},{3,1},{4,6},{5,7},{6,4},{7,5},{8,10},{9,11},{10,... | collective-permute-start | bytes 451592 | tf_op jit(solution)/shard_map/ppermute | solution.py:783
  205.1 12.3 %collective-permute-start.24 = (bf16[98,768]{1,0:T(8,128)(2,1)}, bf16[98,768]{1,0:T(8,128)(2,1)S(1)}, u32[]{:S(2)}, u32[]{:S(2)}) collective-permute-start(bf16[98,768]{1,0:T(8,128)(2,1)} %get-tuple-element.417), channel_id=1, source_target_pairs={{0,3},{1,2},{2,1},{3,0},{4,7},{5,6},{6,5},{7,4},{8,11},{9,10},{10,... | collective-permute-start | bytes 451592 | tf_op jit(solution)/shard_map/ppermute | solution.py:783
  218.2 176.2 %reduce-scatter.5.cloned.1.call-start = ((), (), s32[]{:S(2)}) async-start(), calls=%async_computation.3 | async-start | bytes 2654208 | tf_op jit(solution)/shard_map/reduce_scatter | solution.py:1175
  288.0 15.0 %collective-permute-start.32 = (bf16[768,1920]{1,0:T(8,128)(2,1)}, bf16[768,1920]{1,0:T(8,128)(2,1)}, u32[]{:S(2)}, u32[]{:S(2)}) collective-permute-start(bf16[768,1920]{1,0:T(8,128)(2,1)} %get-tuple-element.489), channel_id=1, source_target_pairs={{0,1},{1,0},{2,3},{3,2},{4,5},{5,4},{6,7},{7,6},{8,9},{9,8},{10,11... | collective-permute-start | bytes 8847368 | tf_op jit(solution)/shard_map/ppermute | solution.py:904
  288.4 14.5 %collective-permute-start.31 = (bf16[768,1536]{1,0:T(8,128)(2,1)}, bf16[768,1536]{1,0:T(8,128)(2,1)}, u32[]{:S(2)}, u32[]{:S(2)}) collective-permute-start(bf16[768,1536]{1,0:T(8,128)(2,1)} %get-tuple-element.488), channel_id=1, source_target_pairs={{0,1},{1,0},{2,3},{3,2},{4,5},{5,4},{6,7},{7,6},{8,9},{9,8},{10,11... | collective-permute-start | bytes 7077896 | tf_op jit(solution)/shard_map/ppermute | solution.py:904
  288.6 14.3 %collective-permute-start.28 = (bf16[98,768]{1,0:T(8,128)(2,1)}, bf16[98,768]{1,0:T(8,128)(2,1)S(1)}, u32[]{:S(2)}, u32[]{:S(2)}) collective-permute-start(bf16[98,768]{1,0:T(8,128)(2,1)} %get-tuple-element.458), channel_id=1, source_target_pairs={{0,1},{1,0},{2,3},{3,2},{4,5},{5,4},{6,7},{7,6},{8,9},{9,8},{10,11... | collective-permute-start | bytes 451592 | tf_op jit(solution)/shard_map/ppermute | solution.py:783
  288.9 13.9 %collective-permute-start.29 = (bf16[98,768]{1,0:T(8,128)(2,1)}, bf16[98,768]{1,0:T(8,128)(2,1)S(1)}, u32[]{:S(2)}, u32[]{:S(2)}) collective-permute-start(bf16[98,768]{1,0:T(8,128)(2,1)} %get-tuple-element.459), channel_id=1, source_target_pairs={{0,2},{1,3},{2,0},{3,1},{4,6},{5,7},{6,4},{7,5},{8,10},{9,11},{10,... | collective-permute-start | bytes 451592 | tf_op jit(solution)/shard_map/ppermute | solution.py:783
  290.4 12.5 %collective-permute-start.30 = (bf16[98,768]{1,0:T(8,128)(2,1)}, bf16[98,768]{1,0:T(8,128)(2,1)S(1)}, u32[]{:S(2)}, u32[]{:S(2)}) collective-permute-start(bf16[98,768]{1,0:T(8,128)(2,1)} %get-tuple-element.460), channel_id=1, source_target_pairs={{0,3},{1,2},{2,1},{3,0},{4,7},{5,6},{6,5},{7,4},{8,11},{9,10},{10,... | collective-permute-start | bytes 451592 | tf_op jit(solution)/shard_map/ppermute | solution.py:783
  314.1 23.9 %collective-permute-start.33 = (bf16[2,768,1536]{2,1,0:T(8,128)(2,1)}, bf16[2,768,1536]{2,1,0:T(8,128)(2,1)}, u32[]{:S(2)}, u32[]{:S(2)}) collective-permute-start(bf16[2,768,1536]{2,1,0:T(8,128)(2,1)} %get-tuple-element.518), channel_id=1, source_target_pairs={{0,1},{1,0},{2,3},{3,2},{4,5},{5,4},{6,7},{7,6},{8,9},{9,8},{10,11... | collective-permute-start | bytes 14155784 | tf_op jit(solution)/shard_map/ppermute | solution.py:904
  314.7 38.9 %collective-permute-start.38 = (bf16[2,2,2,48,1792]{4,3,1,0,2:T(8,128)(2,1)}, bf16[2,2,2,48,1792]{4,3,1,0,2:T(8,128)(2,1)}, u32[]{:S(2)}, u32[]{:S(2)}) collective-permute-start(bf16[2,2,2,48,1792]{4,3,1,0,2:T(8,128)(2,1)} %bitcast.166), channel_id=1, source_target_pairs={{0,4},{4,0},{8,12},{12,8},{16,20},{20,16},{24,28},{28,24},{1,5},{5... | collective-permute-start | bytes 4128776 | tf_op jit(solution)/shard_map/ppermute | solution.py:904
  315.7 31.8 %collective-permute-start.37 = (bf16[2,2,2,48,1664]{4,3,1,0,2:T(8,128)(2,1)}, bf16[2,2,2,48,1664]{4,3,1,0,2:T(8,128)(2,1)}, u32[]{:S(2)}, u32[]{:S(2)}) collective-permute-start(bf16[2,2,2,48,1664]{4,3,1,0,2:T(8,128)(2,1)} %bitcast.167), channel_id=1, source_target_pairs={{0,2},{1,3},{2,0},{3,1},{4,6},{5,7},{6,4},{7,5},{8,10},{9,11},{10,... | collective-permute-start | bytes 3833864 | tf_op jit(solution)/shard_map/ppermute | solution.py:904
  338.0 15.5 %collective-permute-start.34 = (bf16[104,768]{1,0:T(8,128)(2,1)S(1)}, bf16[104,768]{1,0:T(8,128)(2,1)S(1)}, u32[]{:S(2)}, u32[]{:S(2)}) collective-permute-start(bf16[104,768]{1,0:T(8,128)(2,1)S(1)} %copy-done.72), channel_id=1, source_target_pairs={{0,1},{1,0},{2,3},{3,2},{4,5},{5,4},{6,7},{7,6},{8,9},{9,8},{10,11... | collective-permute-start | bytes 479240 | tf_op jit(solution)/shard_map/ppermute | solution.py:783
  338.1 15.5 %collective-permute-start.35 = (bf16[104,768]{1,0:T(8,128)(2,1)S(1)}, bf16[104,768]{1,0:T(8,128)(2,1)S(1)}, u32[]{:S(2)}, u32[]{:S(2)}) collective-permute-start(bf16[104,768]{1,0:T(8,128)(2,1)S(1)} %copy-done.71), channel_id=1, source_target_pairs={{0,2},{1,3},{2,0},{3,1},{4,6},{5,7},{6,4},{7,5},{8,10},{9,11},{10,... | collective-permute-start | bytes 479240 | tf_op jit(solution)/shard_map/ppermute | solution.py:783
  338.7 14.8 %collective-permute-start.36 = (bf16[104,768]{1,0:T(8,128)(2,1)S(1)}, bf16[104,768]{1,0:T(8,128)(2,1)S(1)}, u32[]{:S(2)}, u32[]{:S(2)}) collective-permute-start(bf16[104,768]{1,0:T(8,128)(2,1)S(1)} %copy-done.70), channel_id=1, source_target_pairs={{0,3},{1,2},{2,1},{3,0},{4,7},{5,6},{6,5},{7,4},{8,11},{9,10},{10,... | collective-permute-start | bytes 479240 | tf_op jit(solution)/shard_map/ppermute | solution.py:783
  360.0 47.6 %collective-permute-start.43 = (bf16[768,1536]{1,0:T(8,128)(2,1)}, bf16[768,1536]{1,0:T(8,128)(2,1)}, u32[]{:S(2)}, u32[]{:S(2)}) collective-permute-start(bf16[768,1536]{1,0:T(8,128)(2,1)} %get-tuple-element.560), channel_id=1, source_target_pairs={{0,1},{1,0},{2,3},{3,2},{4,5},{5,4},{6,7},{7,6},{8,9},{9,8},{10,11... | collective-permute-start | bytes 7077896 | tf_op jit(solution)/shard_map/ppermute | solution.py:904
  360.0 47.5 %collective-permute-start.41 = (bf16[2,2,2,96,768]{4,3,2,1,0:T(8,128)(2,1)}, bf16[2,2,2,96,768]{4,3,2,1,0:T(8,128)(2,1)S(1)}, u32[]{:S(2)}, u32[]{:S(2)}) collective-permute-start(bf16[2,2,2,96,768]{4,3,2,1,0:T(8,128)(2,1)} %slice_bitcast_fusion.1), channel_id=1, source_target_pairs={{0,2},{1,3},{2,0},{3,1},{4,6},{5,7},{6,4},{7,5},{8,10},{9,11},{10,... | collective-permute-start | bytes 3538952 | tf_op jit(solution)/shard_map/ppermute | solution.py:904
  361.4 46.1 %collective-permute-start.42 = (bf16[2,2,2,96,768]{4,3,2,1,0:T(8,128)(2,1)}, bf16[2,2,2,96,768]{4,3,2,1,0:T(8,128)(2,1)}, u32[]{:S(2)}, u32[]{:S(2)}) collective-permute-start(bf16[2,2,2,96,768]{4,3,2,1,0:T(8,128)(2,1)} %dynamic-slice_bitcast_fusion), channel_id=1, source_target_pairs={{0,4},{4,0},{8,12},{12,8},{16,20},{20,16},{24,28},{28,24},{1,5},{5... | collective-permute-start | bytes 3538952 | tf_op jit(solution)/shard_map/ppermute | solution.py:904
  362.6 44.9 %collective-permute-start.40 = (bf16[2,2,48,1792]{3,2,1,0:T(8,128)(2,1)}, bf16[2,2,48,1792]{3,2,1,0:T(8,128)(2,1)}, u32[]{:S(2)}, u32[]{:S(2)}) collective-permute-start(bf16[2,2,48,1792]{3,2,1,0:T(8,128)(2,1)} %dynamic-slice_bitcast_fusion.1), channel_id=1, source_target_pairs={{0,2},{1,3},{2,0},{3,1},{4,6},{5,7},{6,4},{7,5},{8,10},{9,11},{10,... | collective-permute-start | bytes 2064392 | tf_op jit(solution)/shard_map/ppermute | solution.py:904
  363.6 43.9 %collective-permute-start.39 = (bf16[2,2,48,1664]{3,2,1,0:T(8,128)(2,1)}, bf16[2,2,48,1664]{3,2,1,0:T(8,128)(2,1)}, u32[]{:S(2)}, u32[]{:S(2)}) collective-permute-start(bf16[2,2,48,1664]{3,2,1,0:T(8,128)(2,1)} %dynamic-slice_bitcast_fusion.2), channel_id=1, source_target_pairs={{0,4},{4,0},{8,12},{12,8},{16,20},{20,16},{24,28},{28,24},{1,5},{5... | collective-permute-start | bytes 1916936 | tf_op jit(solution)/shard_map/ppermute | solution.py:904
  407.5 33.9 %collective-permute-start.47 = (bf16[768,1920]{1,0:T(8,128)(2,1)}, bf16[768,1920]{1,0:T(8,128)(2,1)}, u32[]{:S(2)}, u32[]{:S(2)}) collective-permute-start(bf16[768,1920]{1,0:T(8,128)(2,1)} %get-tuple-element.572), channel_id=1, source_target_pairs={{0,1},{1,0},{2,3},{3,2},{4,5},{5,4},{6,7},{7,6},{8,9},{9,8},{10,11... | collective-permute-start | bytes 8847368 | tf_op jit(solution)/shard_map/ppermute | solution.py:904
  421.3 20.1 %collective-permute-start.44 = (bf16[2,48,3456]{2,1,0:T(8,128)(2,1)S(1)}, bf16[2,48,3456]{2,1,0:T(8,128)(2,1)S(1)}, u32[]{:S(2)}, u32[]{:S(2)}) collective-permute-start(bf16[2,48,3456]{2,1,0:T(8,128)(2,1)S(1)} %fusion.5), channel_id=1, source_target_pairs={{0,8},{4,12},{8,0},{12,4},{16,24},{20,28},{24,16},{28,20},{1,9},{5... | collective-permute-start | bytes 1990664 | tf_op jit(solution)/shard_map/ppermute | solution.py:904
  423.3 15.8 %collective-permute-start.45 = (bf16[2,2,96,768]{3,2,1,0:T(8,128)(2,1)}, bf16[2,2,96,768]{3,2,1,0:T(8,128)(2,1)}, u32[]{:S(2)}, u32[]{:S(2)}) collective-permute-start(bf16[2,2,96,768]{3,2,1,0:T(8,128)(2,1)} %dynamic-slice_bitcast_fusion.4), channel_id=1, source_target_pairs={{0,4},{4,0},{8,12},{12,8},{16,20},{20,16},{24,28},{28,24},{1,5},{5... | collective-permute-start | bytes 1769480 | tf_op jit(solution)/shard_map/ppermute | solution.py:904
  424.8 16.5 %collective-permute-start.46 = (bf16[2,2,96,768]{3,2,1,0:T(8,128)(2,1)}, bf16[2,2,96,768]{3,2,1,0:T(8,128)(2,1)}, u32[]{:S(2)}, u32[]{:S(2)}) collective-permute-start(bf16[2,2,96,768]{3,2,1,0:T(8,128)(2,1)} %slice_bitcast_fusion.3), channel_id=1, source_target_pairs={{0,2},{1,3},{2,0},{3,1},{4,6},{5,7},{6,4},{7,5},{8,10},{9,11},{10,... | collective-permute-start | bytes 1769480 | tf_op jit(solution)/shard_map/ppermute | solution.py:904
  427.0 40.9 %collective-permute-start.48 = (bf16[2,2,2,48,1536]{4,3,1,0,2:T(8,128)(2,1)}, bf16[2,2,2,48,1536]{4,3,1,0,2:T(8,128)(2,1)}, u32[]{:S(2)}, u32[]{:S(2)}) collective-permute-start(bf16[2,2,2,48,1536]{4,3,1,0,2:T(8,128)(2,1)} %bitcast.168), channel_id=1, source_target_pairs={{0,2},{1,3},{2,0},{3,1},{4,6},{5,7},{6,4},{7,5},{8,10},{9,11},{10,... | collective-permute-start | bytes 3538952 | tf_op jit(solution)/shard_map/ppermute | solution.py:904
  454.5 25.9 %collective-permute-start.50 = (bf16[2,2,2,48,1024]{4,3,1,0,2:T(8,128)(2,1)}, bf16[2,2,2,48,1024]{4,3,1,0,2:T(8,128)(2,1)}, u32[]{:S(2)}, u32[]{:S(2)}) collective-permute-start(bf16[2,2,2,48,1024]{4,3,1,0,2:T(8,128)(2,1)} %bitcast.169), channel_id=1, source_target_pairs={{0,4},{4,0},{8,12},{12,8},{16,20},{20,16},{24,28},{28,24},{1,5},{5... | collective-permute-start | bytes 2359304 | tf_op jit(solution)/shard_map/ppermute | solution.py:904
  455.0 25.4 %collective-permute-start.49 = (bf16[2,2,2,48,896]{4,3,1,0,2:T(8,128)(2,1)}, bf16[2,2,2,48,896]{4,3,1,0,2:T(8,128)(2,1)}, u32[]{:S(2)}, u32[]{:S(2)}) collective-permute-start(bf16[2,2,2,48,896]{4,3,1,0,2:T(8,128)(2,1)} %bitcast.170), channel_id=1, source_target_pairs={{0,2},{1,3},{2,0},{3,1},{4,6},{5,7},{6,4},{7,5},{8,10},{9,11},{10,... | collective-permute-start | bytes 2064392 | tf_op jit(solution)/shard_map/ppermute | solution.py:904
  465.0 20.4 %collective-permute-start.52 = (bf16[48,3456]{1,0:T(8,128)(2,1)S(1)}, bf16[48,3456]{1,0:T(8,128)(2,1)S(1)}, u32[]{:S(2)}, u32[]{:S(2)}) collective-permute-start(bf16[48,3456]{1,0:T(8,128)(2,1)S(1)} %copy-done.38), channel_id=1, source_target_pairs={{0,16},{4,20},{8,24},{12,28},{16,0},{20,4},{24,8},{28,12},{1,17},{... | collective-permute-start | bytes 995336 | tf_op jit(solution)/shard_map/ppermute | solution.py:904
  467.1 22.5 %collective-permute-start.53 = (bf16[2,96,1536]{2,1,0:T(8,128)(2,1)S(1)}, bf16[2,96,1536]{2,1,0:T(8,128)(2,1)S(1)}, u32[]{:S(2)}, u32[]{:S(2)}) collective-permute-start(bf16[2,96,1536]{2,1,0:T(8,128)(2,1)S(1)} %copy-done.37), channel_id=1, source_target_pairs={{0,8},{4,12},{8,0},{12,4},{16,24},{20,28},{24,16},{28,20},{1,9},{5... | collective-permute-start | bytes 1769480 | tf_op jit(solution)/shard_map/ppermute | solution.py:904
  489.6 22.0 %collective-permute-start.54 = (bf16[2,2,48,1536]{3,2,1,0:T(8,128)(2,1)S(1)}, bf16[2,2,48,1536]{3,2,1,0:T(8,128)(2,1)S(1)}, u32[]{:S(2)}, u32[]{:S(2)}) collective-permute-start(bf16[2,2,48,1536]{3,2,1,0:T(8,128)(2,1)S(1)} %dynamic-slice_bitcast_fusion.3), channel_id=1, source_target_pairs={{0,4},{4,0},{8,12},{12,8},{16,20},{20,16},{24,28},{28,24},{1,5},{5... | collective-permute-start | bytes 1769480 | tf_op jit(solution)/shard_map/ppermute | solution.py:904
  490.9 20.7 %collective-permute-start.55 = (bf16[2,2,48,896]{3,2,1,0:T(8,128)(2,1)S(1)}, bf16[2,2,48,896]{3,2,1,0:T(8,128)(2,1)S(1)}, u32[]{:S(2)}, u32[]{:S(2)}) collective-permute-start(bf16[2,2,48,896]{3,2,1,0:T(8,128)(2,1)S(1)} %dynamic-slice_bitcast_fusion.6), channel_id=1, source_target_pairs={{0,4},{4,0},{8,12},{12,8},{16,20},{20,16},{24,28},{28,24},{1,5},{5... | collective-permute-start | bytes 1032200 | tf_op jit(solution)/shard_map/ppermute | solution.py:904
  491.6 20.0 %collective-permute-start.56 = (bf16[2,2,48,1024]{3,2,1,0:T(8,128)(2,1)S(1)}, bf16[2,2,48,1024]{3,2,1,0:T(8,128)(2,1)S(1)}, u32[]{:S(2)}, u32[]{:S(2)}) collective-permute-start(bf16[2,2,48,1024]{3,2,1,0:T(8,128)(2,1)S(1)} %dynamic-slice_bitcast_fusion.5), channel_id=1, source_target_pairs={{0,2},{1,3},{2,0},{3,1},{4,6},{5,7},{6,4},{7,5},{8,10},{9,11},{10,... | collective-permute-start | bytes 1179656 | tf_op jit(solution)/shard_map/ppermute | solution.py:904
  492.6 12.1 %collective-permute-start.57 = (f32[12,768]{1,0:T(8,128)S(1)}, f32[12,768]{1,0:T(8,128)S(1)}, u32[]{:S(2)}, u32[]{:S(2)}) collective-permute-start(f32[12,768]{1,0:T(8,128)S(1)} %add.284), channel_id=1, source_target_pairs={{0,2},{1,3},{2,0},{3,1},{4,6},{5,7},{6,4},{7,5},{8,10},{9,11},{10,... | collective-permute-start | bytes 110600 | tf_op jit(solution)/shard_map/ppermute | solution.py:904
  493.9 22.7 %collective-permute-start.58 = (bf16[48,3456]{1,0:T(8,128)(2,1)S(1)}, bf16[48,3456]{1,0:T(8,128)(2,1)S(1)}, u32[]{:S(2)}, u32[]{:S(2)}) collective-permute-start(bf16[48,3456]{1,0:T(8,128)(2,1)S(1)} %bitcast_add_fusion.12), channel_id=1, source_target_pairs={{0,2},{1,3},{2,0},{3,1},{4,6},{5,7},{6,4},{7,5},{8,10},{9,11},{10,... | collective-permute-start | bytes 995336 | tf_op jit(solution)/shard_map/ppermute | solution.py:904
  504.7 11.9 %collective-permute-start.59 = (bf16[96,1536]{1,0:T(8,128)(2,1)S(1)}, bf16[96,1536]{1,0:T(8,128)(2,1)S(1)}, u32[]{:S(2)}, u32[]{:S(2)}) collective-permute-start(bf16[96,1536]{1,0:T(8,128)(2,1)S(1)} %dynamic-slice_bitcast_fusion.9), channel_id=1, source_target_pairs={{0,16},{4,20},{8,24},{12,28},{16,0},{20,4},{24,8},{28,12},{1,17},{... | collective-permute-start | bytes 884744 | tf_op jit(solution)/shard_map/ppermute | solution.py:904
  516.9 14.9 %collective-permute-start.61 = (bf16[2,48,1920]{2,1,0:T(8,128)(2,1)S(1)}, bf16[2,48,1920]{2,1,0:T(8,128)(2,1)S(1)}, u32[]{:S(2)}, u32[]{:S(2)}) collective-permute-start(bf16[2,48,1920]{2,1,0:T(8,128)(2,1)S(1)} %fusion.16), channel_id=1, source_target_pairs={{0,8},{4,12},{8,0},{12,4},{16,24},{20,28},{24,16},{28,20},{1,9},{5... | collective-permute-start | bytes 1105928 | tf_op jit(solution)/shard_map/ppermute | solution.py:904
  520.3 15.0 %collective-permute-start.63 = (bf16[96,3456]{1,0:T(8,128)(2,1)S(1)}, bf16[96,3456]{1,0:T(8,128)(2,1)S(1)}, u32[]{:S(2)}, u32[]{:S(2)}) collective-permute-start(bf16[96,3456]{1,0:T(8,128)(2,1)S(1)} %maximum_select_fusion), channel_id=1, source_target_pairs={{0,1},{1,0},{2,3},{3,2},{4,5},{5,4},{6,7},{7,6},{8,9},{9,8},{10,11... | collective-permute-start | bytes 1990664 | tf_op jit(solution)/shard_map/ppermute | solution.py:904
  532.0 11.1 %collective-permute-start.64 = (bf16[48,1536]{1,0:T(8,128)(2,1)S(1)}, bf16[48,1536]{1,0:T(8,128)(2,1)S(1)}, u32[]{:S(2)}, u32[]{:S(2)}) collective-permute-start(bf16[48,1536]{1,0:T(8,128)(2,1)S(1)} %dynamic-slice_bitcast_fusion.11), channel_id=1, source_target_pairs={{0,16},{4,20},{8,24},{12,28},{16,0},{20,4},{24,8},{28,12},{1,17},{... | collective-permute-start | bytes 442376 | tf_op jit(solution)/shard_map/ppermute | solution.py:904
  532.1 14.8 %collective-permute-start.65 = (bf16[48,1920]{1,0:T(8,128)(2,1)S(1)}, bf16[48,1920]{1,0:T(8,128)(2,1)S(1)}, u32[]{:S(2)}, u32[]{:S(2)}) collective-permute-start(bf16[48,1920]{1,0:T(8,128)(2,1)S(1)} %dynamic-slice_bitcast_fusion.10), channel_id=1, source_target_pairs={{0,16},{4,20},{8,24},{12,28},{16,0},{20,4},{24,8},{28,12},{1,17},{... | collective-permute-start | bytes 552968 | tf_op jit(solution)/shard_map/ppermute | solution.py:904
  (102 other events, 567.8 us)
Sparse Core Ops, SparseCore 0:
  217.6 82.4 reduce-scatter.2
  317.3 76.7 reduce-scatter.4

commit v3 on v2

--- a/solution.py
+++ b/solution.py
@@ -95,7 +95,7 @@
     second = pl.multiple_of((1 - place_ref[1]) * half, half)
     return [
         [(own, target.at[0])],
-        [(core.at[which], target.at[1])],
+        [(core, target.at[1])],
         [
             (far_first.at[which], target.at[2, pl.ds(first, half)]),
             (far_second.at[which], target.at[2, pl.ds(second, half)]),
@@ -111,8 +111,8 @@
     waits = []
     index = 0
     for pairs in zip(
-        shard_copies(place_ref, (own[0],) + peers, up_ref, 0),
-        shard_copies(place_ref, (own[1],) + peers, down_ref, 1),
+        shard_copies(place_ref, own[:2] + peers, up_ref, 0),
+        shard_copies(place_ref, own[2:] + peers, down_ref, 1),
     ):
         group = []
         for source, target in pairs[0] + pairs[1]:
@@ -251,10 +251,12 @@
 
 def send_blocks(plain, blocks, sends, place, size):
     groups = len(sends)
+    rows = sends[0].shape[0]
     for group in range(groups):
         blocks[group, 0:size, :] = plain[group * size : (group + 1) * size, :]
+        blocks[group, size:rows, :] = jnp.zeros((rows - size, plain.shape[1]), FULL)
     for away in range(groups):
-        sends[away][...] = blocks[place ^ away][0:size].astype(HALF)
+        sends[away][...] = blocks[place ^ away][0:rows].astype(HALF)
 
 
 def space_forward(dims, layer, place_ref, clip_ref, class_ref, piece0, piece1, piece2, piece3, in_hbm,
@@ -335,7 +337,7 @@
 
 def feed_forward(dims, layer, place_ref, piece0, piece1, piece2, piece3, share_ref, after_ref,
                  gain_ref, shift_ref, out_hbm,
-                 up_hbm, down_hbm, peer1, peer2, peer3, peer4, peer5,
+                 up_hbm, down_hbm, peer_up, peer_down, peer2, peer3, peer4, peer5,
                  mixed_ref, rows_ref, normed_ref, active_ref, slope_ref, next_ref,
                  out_ref, up_ref, down_ref, plain, blocks, frame_rows, whole, out_sem, sems):
     frames, patches, width, heads, groups = dims
@@ -344,8 +346,8 @@
     size = count // groups
     place = place_ref[0]
     copies = fetch((out_hbm.at[layer],), (out_ref,), out_sem)
-    own = (up_hbm.at[layer], down_hbm.at[layer])
-    peers = (peer1, peer2, peer3, peer4, peer5)
+    own = (up_hbm.at[layer], peer_up.at[layer], down_hbm.at[layer], peer_down.at[layer])
+    peers = (peer2, peer3, peer4, peer5)
     shards = start_shards(place_ref, own, peers, up_ref, down_ref, sems)
     take_pieces(
         (piece0, piece1, piece2, piece3), blocks, plain, frame_rows, place, size, frames // groups
@@ -400,7 +402,7 @@
 
 
 def feed_backward(dims, layer, place_ref, clip_ref, grad_ref, slope_ref, rows_ref, share_ref, gain_ref,
-                  out_hbm, up_hbm, down_hbm, peer1, peer2, peer3, peer4, peer5,
+                  out_hbm, up_hbm, down_hbm, peer_up, peer_down, peer2, peer3, peer4, peer5,
                   update_ref, hidden_ref, branch_ref, back_ref, norms_ref,
                   send0, send1, send2, send3, class_ref,
                   out_ref, up_ref, down_ref, total, plain, blocks, out_sem, sems):
@@ -409,8 +411,8 @@
     rows = grad_ref.shape[0]
     place = place_ref[0]
     own_frames = frames // groups
-    own = (up_hbm.at[layer], down_hbm.at[layer])
-    peers = (peer1, peer2, peer3, peer4, peer5)
+    own = (up_hbm.at[layer], peer_up.at[layer], down_hbm.at[layer], peer_down.at[layer])
+    peers = (peer2, peer3, peer4, peer5)
     shards = start_shards(place_ref, own, peers, up_ref, down_ref, sems)
     copies = fetch((out_hbm.at[layer],), (out_ref,), out_sem)
     update_ref[...] = grad_ref[...].astype(HALF)
@@ -930,12 +932,14 @@
     return arrived[0]
 
 
-def both_matrices(hidden_up, hidden_down, layer, near=None):
-    matrices = [hidden_up[layer], hidden_down[layer]]
-    if near is not None:
-        half = matrices[0].shape[0] // 2
-        matrices = [lax.dynamic_slice_in_dim(rows, near * half, half, 0) for rows in matrices]
-    return jnp.stack(matrices)
+def both_matrices(hidden_up, hidden_down, layer, near):
+    half = hidden_up.shape[1] // 2
+    return jnp.stack(
+        [
+            lax.dynamic_slice_in_dim(matrices[layer], near * half, half, 0)
+            for matrices in (hidden_up, hidden_down)
+        ]
+    )
 
 
 def body(
@@ -970,7 +974,7 @@
     span = own_frames * frame_span
     hidden = groups * hidden_up.shape[2]
     piece_rows = own_frames * patches
-    back_rows = up_to(piece_rows + 2 * own_frames, 8)
+    back_rows = up_to(piece_rows + 2 * own_frames, 16)
 
     ends = jnp.cumsum(frame_counts[0])
     frame_index = jnp.arange(frames, dtype=jnp.int32)
@@ -1012,9 +1016,10 @@
         return flights.results.pop(name)
 
     send("x0", both_matrices(hidden_up, hidden_down, 0, near), by_x)
-    send("core0", both_matrices(hidden_up, hidden_down, 0), by_core)
+    send("up", hidden_up, by_core)
+    send("down", hidden_down, by_core)
     patch_rows = flights.leave(rows_of(patch_tokens, class_tokens))
-    pieces_out = [((piece_rows, width), HALF)] * groups
+    pieces_out = [((up_to(piece_rows, 16), width), HALF)] * groups
     backs_out = [((back_rows, width), HALF)] * groups
     lane_buffer = pltpu.VMEM((width // 128, rows, 128), FULL)
     row_buffer = pltpu.VMEM((rows, width), FULL)
@@ -1025,11 +1030,6 @@
     frame_rows = pltpu.VMEM((frames, width), FULL)
     saved = []
     for layer in range(layers):
-        if layer:
-            patch_rows = flights.land([f"x{layer}", f"core{layer}"], patch_rows)
-            first = arrived_here(f"x{layer}")
-            send("y1", first, by_y)
-            patch_rows = flights.leave(patch_rows)
         time = call(
             partial(time_forward, dims, layer),
             [
@@ -1046,9 +1046,16 @@
             [SMALL, ROWS, ROWS, ROWS, ROWS, FAR, FAR, FAR],
             14,
         )(place, patch_rows, bias, norm_gain, norm_shift, temporal_in, temporal_out, temporal_mix)
-        arrived = spread(time[6:10])
+        pieces = time[6:10]
+        if layer:
+            pieces = flights.land(["x1"], pieces)
+            first = arrived_here("x1")
+            send("y1", first, by_y)
+            pieces = flights.leave(pieces)
+        arrived = spread(pieces)
         if layer == 0:
-            arrived = flights.land(("x0", "core0"), arrived)
+            arrived = flights.land(("x0", "up", "down"), arrived)
+            core_shards = (arrived_here("up"), arrived_here("down"))
             first = arrived_here("x0")
             send("y0", first, by_y)
             send("x1", both_matrices(hidden_up, hidden_down, 1, near), by_x)
@@ -1065,12 +1072,10 @@
         second = arrived_here(f"y{layer}")
         send("first", first, by_core)
         send("second", second, by_core)
-        if layer + 1 < layers:
-            send("core1", both_matrices(hidden_up, hidden_down, 1), by_core)
         arrived = flights.leave(arrived)
         arrived = flights.land(("first", "second"), arrived)
         gathered[layer] = (
-            arrived_here(f"core{layer}"),
+            *core_shards,
             first,
             second,
             arrived_here("first"),
@@ -1097,7 +1102,7 @@
                 pltpu.SemaphoreType.DMA((1,)),
                 pltpu.SemaphoreType.DMA((12,)),
             ],
-            [SMALL] + [ROWS] * groups + [ROWS] * 4 + [FAR] * 8,
+            [SMALL] + [ROWS] * groups + [ROWS] * 4 + [FAR] * 9,
             15,
         )(
             place, *arrived, share, time[5], norm_gain, norm_shift, spatial_out,
@@ -1155,7 +1160,7 @@
                 pltpu.SemaphoreType.DMA((1,)),
                 pltpu.SemaphoreType.DMA((12,)),
             ],
-            [SMALL, SMALL] + [ROWS] * 5 + [FAR] * 8,
+            [SMALL, SMALL] + [ROWS] * 5 + [FAR] * 9,
             23,
         )(
             place, clip_of, grad_rows, feed[4], feed[1],

time: 584 us -> 569 us (0.974)
  waiting for transfers between devices: 155 us -> 148 us
    ppermute x48, waiting for transfers between devices: 121 us -> 112 us  [leave(): lax.ppermute(send, *way)]
    unnamed x158 -> x160, local copies, waits for them, and re-layouts: 17.9 us -> 17.2 us
  transfers between devices with their start and end apart: 74 -> 74, of which waited for: 32 -> 33; matrix products, arithmetic and copies ran while one was open for 11% -> 11% of each run, Pallas kernels for 36% -> 37%
where the time goes in v3:
time: 569 us; the launch traced here: 559 us
  Pallas kernels  237 us (42%)
  waiting for transfers between devices  148 us (26%)
  starting transfers between devices  57.4 us (10%)
  local copies, waits for them, and re-layouts  52.7 us (9%)
  other arithmetic  47.9 us (8%)
  between operations  16.1 us (3%)
    pallas_call x12, Pallas kernels, run(): pl.pallas_call(whole, out_shape=[jax.ShapeDtypeStruct(shape, kind) for sh...  180 us
    ppermute x48, waiting for transfers between devices, leave(): lax.ppermute(send, *way)  112 us
    pallas_call x6, Pallas kernels, outer_group(): pl.pallas_call(kernel, out_shape=[jax.ShapeDtypeStruct(shape, HALF)] * re...  56.9 us
    ppermute x48, starting transfers between devices, leave(): lax.ppermute(send, *way)  42.7 us
    ppermute x24, waiting for transfers between devices, swap(): return lax.ppermute(values, *exchange(axis, bit))  36.2 us
    unnamed x160, local copies, waits for them, and re-layouts  17.2 us
    add x5, other arithmetic, reduce_group(): sums = [keep + other for (send, keep), other in zip(groups, others)]  15.9 us
    ppermute x24, starting transfers between devices, swap(): return lax.ppermute(values, *exchange(axis, bit))  14.2 us
  transfers between devices with their start and end apart: 74, of which 33 were waited for; matrix products, arithmetic and copies ran while one was open for 11% of the time, Pallas kernels for 37%

profile of v3, /device:TPU:0, one launch (start us, length us, event | category | flops | bytes accessed | tf_op | source)
XLA Modules:
  0.0 559.1 jit_solution(2273587688899300909)
XLA Ops:
  10.6 2.9 fusion.20
  20.3 2.9 collective-permute-start.3
  27.6 15.0 %shard_map.237 = (bf16[400,768]{1,0:T(8,128)(2,1)}, bf16[400,2304]{1,0:T(8,128)(2,1)}, f32[400,128]{1,0:T(8,128)}, bf16[400,768]{1,0:T(8,128)(2,1)}, bf16[400,76...) custom-call(s32[2]{0:T(128)} %pad_add_fusion.refs_0_.place_ref, ...), custom_call_target="tpu_custom_call" | custom-call | flops 14 | bytes 14 | tf_op jit(solution)/shard_map/pallas_call | solution.py:679
  45.8 8.1 %collective-permute-done.1.refs_5_ = bf16[112,768]{1,0:T(8,128)(2,1)S(1)} collective-permute-done((bf16[112,768]{1,0:T(8,128)(2,1)}, bf16[112,768]{1,0:T(8,128)(2,1)S(1)}, u32[]{:S(2)}, u32[]{:S(2)}) %collective-permute-start.1) | collective-permute-done | bytes 172064 | tf_op jit(solution)/shard_map/ppermute | solution.py:785
  53.9 2.4 collective-permute-done.2.refs_6_
  58.5 11.4 %shard_map.238 = (bf16[416,768]{1,0:T(8,128)(2,1)}, bf16[416,2304]{1,0:T(8,128)(2,1)}, f32[416,128]{1,0:T(8,128)}, bf16[112,768]{1,0:T(8,128)(2,1)}, bf16[112,76...) custom-call(s32[2]{0:T(128)} %pad_add_fusion.refs_0_.place_ref, s32[8]{0:T(128)} %copy-done.64, ...), custom_call_target="tpu_custom_call" | custom-call | flops 9 | bytes 9 | tf_op jit(solution)/shard_map/pallas_call | solution.py:679
  71.9 5.9 %collective-permute-done.7.refs_3_ = bf16[112,768]{1,0:T(8,128)(2,1)S(1)} collective-permute-done((bf16[112,768]{1,0:T(8,128)(2,1)}, bf16[112,768]{1,0:T(8,128)(2,1)S(1)}, u32[]{:S(2)}, u32[]{:S(2)}) %collective-permute-start.7) | collective-permute-done | bytes 172064 | tf_op jit(solution)/shard_map/ppermute | solution.py:785
  79.8 5.6 collective-permute-done.9.refs_15_.refs_13_
  90.9 14.4 %shard_map.239 = (bf16[400,768]{1,0:T(8,128)(2,1)}, f32[400,768]{1,0:T(8,128)}, bf16[400,768]{1,0:T(8,128)(2,1)}, bf16[400,3072]{1,0:T(8,128)(2,1)}, bf16[400,3072]{1,0:T(8,128)(2,1)}, /*index=5*/f32[400,768]{1,0:T(8,128)}) custom-call(s32[2]{0:T(128)} %pad_add_fusion.refs_0_.place_ref, bf16[112,768]{1,0:T(8,128)(2,1)} %get-tuple-element.367.refs_1_, ...), custom_call_target="tpu_custom_call" | custom-call | flops 15 | bytes 15 | tf_op jit(solution)/shard_map/pallas_call | solution.py:679
  105.3 15.0 %shard_map.240 = (bf16[400,768]{1,0:T(8,128)(2,1)}, bf16[400,2304]{1,0:T(8,128)(2,1)}, f32[400,128]{1,0:T(8,128)}, bf16[400,768]{1,0:T(8,128)(2,1)}, bf16[400,76...) custom-call(s32[2]{0:T(128)} %pad_add_fusion.refs_0_.place_ref, ...), custom_call_target="tpu_custom_call" | custom-call | flops 14 | bytes 14 | tf_op jit(solution)/shard_map/pallas_call | solution.py:679
  124.0 5.5 collective-permute-done.14.refs_5_
  129.5 2.9 collective-permute-done.15.refs_6_
  133.1 10.9 %shard_map.241 = (bf16[416,768]{1,0:T(8,128)(2,1)}, bf16[416,2304]{1,0:T(8,128)(2,1)}, f32[416,128]{1,0:T(8,128)}, bf16[112,768]{1,0:T(8,128)(2,1)}, bf16[112,76...) custom-call(s32[2]{0:T(128)} %pad_add_fusion.refs_0_.place_ref, s32[8]{0:T(128)} %copy-done.64, ...), custom_call_target="tpu_custom_call" | custom-call | flops 9 | bytes 9 | tf_op jit(solution)/shard_map/pallas_call | solution.py:679
  146.1 5.9 %collective-permute-done.17.refs_3_ = bf16[112,768]{1,0:T(8,128)(2,1)S(1)} collective-permute-done((bf16[112,768]{1,0:T(8,128)(2,1)}, bf16[112,768]{1,0:T(8,128)(2,1)S(1)}, u32[]{:S(2)}, u32[]{:S(2)}) %collective-permute-start.17) | collective-permute-done | bytes 172064 | tf_op jit(solution)/shard_map/ppermute | solution.py:785
  154.8 2.4 collective-permute-done.20.refs_16_.refs_14_
  159.9 14.5 %shard_map.242 = (bf16[400,768]{1,0:T(8,128)(2,1)}, f32[400,768]{1,0:T(8,128)}, bf16[400,768]{1,0:T(8,128)(2,1)}, bf16[400,3072]{1,0:T(8,128)(2,1)}, bf16[400,3072]{1,0:T(8,128)(2,1)}, /*index=5*/f32[400,768]{1,0:T(8,128)}) custom-call(s32[2]{0:T(128)} %pad_add_fusion.refs_0_.place_ref, bf16[112,768]{1,0:T(8,128)(2,1)} %get-tuple-element.408.refs_1_, ...), custom_call_target="tpu_custom_call" | custom-call | flops 15 | bytes 15 | tf_op jit(solution)/shard_map/pallas_call | solution.py:679
  175.1 16.6 %shard_map.243 = (bf16[400,768]{1,0:T(8,128)(2,1)}, bf16[400,3072]{1,0:T(8,128)(2,1)}, bf16[400,768]{1,0:T(8,128)(2,1)}, f32[400,768]{1,0:T(8,128)}, f32[8,768]{...) custom-call(s32[2]{0:T(128)} %pad_add_fusion.refs_0_.place_ref, ...), custom_call_target="tpu_custom_call" | custom-call | flops 23 | bytes 23 | tf_op jit(solution)/shard_map/pallas_call | solution.py:679
  193.7 12.2 %shard_map.244 = bf16[4,768,1536]{2,1,0:T(8,128)(2,1)} custom-call(s32[2]{0:T(128)} %pad_add_fusion.refs_0_.place_ref, bf16[400,768]{1,0:T(8,128)(2,1)} %get-tuple-element.422.refs_0_, bf16[400,768]{1,0:T(8,128)(2,1)} %get-tuple-element.423.refs_1_, bf16[400,3072]{1,0:T(8,128)(2,1)} %get-tuple-element.424.refs_2_, bf16[400,3072]{1,0:T(8,128)(2,1)} %get-tuple-element.425.refs_3_), custom_call_target="tpu_custom_call" | custom-call | flops 10 | bytes 10 | tf_op jit(solution)/shard_map/pallas_call | solution.py:762
  207.1 13.1 %shard_map.245 = (bf16[416,2304]{1,0:T(8,128)(2,1)}, bf16[112,768]{1,0:T(8,128)(2,1)}, bf16[112,768]{1,0:T(8,128)(2,1)}, bf16[112,768]{1,0:T(8,128)(2,1)}, bf16[112,768]{1,0:T(8,128)(2,1)}) custom-call(bf16[112,768]{1,0:T(8,128)(2,1)} %get-tuple-element.430.refs_0_, bf16[112,768]{1,0:T(8,128)(2,1)} %copy-done.49, bf16[112,768]{1,0:T(8,128)(2,1)} %copy-done.50, ...), custom_call_target="tpu_custom_call" | custom-call | flops 29 | bytes 29 | tf_op jit(solution)/shard_map/pallas_call | solution.py:679
  223.1 7.4 %shard_map.246 = (bf16[768,1536]{1,0:T(8,128)(2,1)}, bf16[768,1536]{1,0:T(8,128)(2,1)}) custom-call(s32[2]{0:T(128)} %pad_add_fusion.refs_0_.place_ref, bf16[416,768]{1,0:T(8,128)(2,1)} %get-tuple-element.445.refs_0_, bf16[400,768]{1,0:T(8,128)(2,1)} %get-tuple-element.446.refs_1_, bf16[416,2304]{1,0:T(8,128)(2,1)} %get-tuple-element.447.refs_2_, ...), custom_call_target="tpu_custom_call" | custom-call | flops 8 | bytes 8 | tf_op jit(solution)/shard_map/pallas_call | solution.py:762
  231.2 19.4 %shard_map.247 = (bf16[400,768]{1,0:T(8,128)(2,1)}, bf16[400,768]{1,0:T(8,128)(2,1)}, bf16[400,2304]{1,0:T(8,128)(2,1)}, f32[400,768]{1,0:T(8,128)}, f32[8,768]{1,0:T(8,128)}) custom-call(s32[2]{0:T(128)} %pad_add_fusion.refs_0_.place_ref, bf16[112,768]{1,0:T(8,128)(2,1)} %get-tuple-element.451.refs_1_, bf16[112,768]{1,0:T(8,128)(2,1)} %copy-done.60, ...), custom_call_target="tpu_custom_call" | custom-call | flops 14 | bytes 14 | tf_op jit(solution)/shard_map/pallas_call | solution.py:679
  250.7 17.1 %shard_map.248 = (bf16[400,768]{1,0:T(8,128)(2,1)}, bf16[400,3072]{1,0:T(8,128)(2,1)}, bf16[400,768]{1,0:T(8,128)(2,1)}, f32[400,768]{1,0:T(8,128)}, f32[8,768]{...) custom-call(s32[2]{0:T(128)} %pad_add_fusion.refs_0_.place_ref, ...), custom_call_target="tpu_custom_call" | custom-call | flops 23 | bytes 23 | tf_op jit(solution)/shard_map/pallas_call | solution.py:679
  267.7 8.7 %shard_map.249 = (bf16[768,1920]{1,0:T(8,128)(2,1)}, bf16[768,1920]{1,0:T(8,128)(2,1)}) custom-call(s32[2]{0:T(128)} %pad_add_fusion.refs_0_.place_ref, bf16[400,768]{1,0:T(8,128)(2,1)} %get-tuple-element.485.refs_0_, bf16[400,768]{1,0:T(8,128)(2,1)} %get-tuple-element.486.refs_1_, bf16[400,768]{1,0:T(8,128)(2,1)} %get-tuple-element.487.refs_2_, ...), custom_call_target="tpu_custom_call" | custom-call | flops 9 | bytes 9 | tf_op jit(solution)/shard_map/pallas_call | solution.py:762
  279.0 12.4 %shard_map.250 = (bf16[2,768,1536]{2,1,0:T(8,128)(2,1)}, bf16[2,768,1536]{2,1,0:T(8,128)(2,1)}) custom-call(s32[2]{0:T(128)} %pad_add_fusion.refs_0_.place_ref, bf16[400,768]{1,0:T(8,128)(2,1)} %get-tuple-element.506.refs_0_, bf16[400,768]{1,0:T(8,128)(2,1)} %get-tuple-element.507.refs_1_, bf16[400,3072]{1,0:T(8,128)(2,1)} %get-tuple-element.508.refs_2_, ...), custom_call_target="tpu_custom_call" | custom-call | flops 10 | bytes 10 | tf_op jit(solution)/shard_map/pallas_call | solution.py:762
  291.6 2.7 add.260
  294.3 2.7 add.259
  305.7 13.2 %shard_map.251 = (bf16[416,2304]{1,0:T(8,128)(2,1)}, bf16[112,768]{1,0:T(8,128)(2,1)}, bf16[112,768]{1,0:T(8,128)(2,1)}, bf16[112,768]{1,0:T(8,128)(2,1)}, bf16[112,768]{1,0:T(8,128)(2,1)}) custom-call(bf16[112,768]{1,0:T(8,128)(2,1)} %get-tuple-element.511.refs_0_, bf16[112,768]{1,0:T(8,128)(2,1)} %copy-done.46, bf16[112,768]{1,0:T(8,128)(2,1)} %copy-done.47, ...), custom_call_target="tpu_custom_call" | custom-call | flops 29 | bytes 29 | tf_op jit(solution)/shard_map/pallas_call | solution.py:679
  319.0 7.5 %shard_map.252 = (bf16[768,1536]{1,0:T(8,128)(2,1)}, bf16[768,1536]{1,0:T(8,128)(2,1)}) custom-call(s32[2]{0:T(128)} %pad_add_fusion.refs_0_.place_ref, bf16[416,768]{1,0:T(8,128)(2,1)} %get-tuple-element.535.refs_0_, bf16[400,768]{1,0:T(8,128)(2,1)} %get-tuple-element.536.refs_1_, bf16[416,2304]{1,0:T(8,128)(2,1)} %get-tuple-element.537.refs_2_, ...), custom_call_target="tpu_custom_call" | custom-call | flops 8 | bytes 8 | tf_op jit(solution)/shard_map/pallas_call | solution.py:762
  328.7 3.7 add.263
  336.0 6.2 %collective-permute-done.38 = bf16[2,2,2,48,1792]{4,3,1,0,2:T(8,128)(2,1)} collective-permute-done((bf16[2,2,2,48,1792]{4,3,1,0,2:T(8,128)(2,1)}, bf16[2,2,2,48,1792]{4,3,1,0,2:T(8,128)(2,1)}, u32[]{:S(2)}, u32[]{:S(2)}) %collective-permute-start.38) | collective-permute-done | bytes 1376288 | tf_op jit(solution)/shard_map/ppermute | solution.py:906
  353.5 19.5 %shard_map.253 = (bf16[400,768]{1,0:T(8,128)(2,1)}, bf16[400,768]{1,0:T(8,128)(2,1)}, bf16[400,2304]{1,0:T(8,128)(2,1)}, f32[400,768]{1,0:T(8,128)}, f32[8,768]{1,0:T(8,128)}) custom-call(s32[2]{0:T(128)} %pad_add_fusion.refs_0_.place_ref, bf16[112,768]{1,0:T(8,128)(2,1)} %get-tuple-element.542.refs_1_, bf16[112,768]{1,0:T(8,128)(2,1)} %copy-done.52, ...), custom_call_target="tpu_custom_call" | custom-call | flops 14 | bytes 14 | tf_op jit(solution)/shard_map/pallas_call | solution.py:679
  373.0 8.7 %shard_map.254 = (bf16[768,1920]{1,0:T(8,128)(2,1)}, bf16[768,1920]{1,0:T(8,128)(2,1)}) custom-call(s32[2]{0:T(128)} %pad_add_fusion.refs_0_.place_ref, bf16[400,768]{1,0:T(8,128)(2,1)} %get-tuple-element.550.refs_0_, bf16[400,768]{1,0:T(8,128)(2,1)} %get-tuple-element.551.refs_1_, bf16[400,768]{1,0:T(8,128)(2,1)} %get-tuple-element.552.refs_2_, ...), custom_call_target="tpu_custom_call" | custom-call | flops 9 | bytes 9 | tf_op jit(solution)/shard_map/pallas_call | solution.py:762
  383.0 13.0 %collective-permute-done.39 = bf16[2,2,48,1664]{3,2,1,0:T(8,128)(2,1)} collective-permute-done((bf16[2,2,48,1664]{3,2,1,0:T(8,128)(2,1)}, bf16[2,2,48,1664]{3,2,1,0:T(8,128)(2,1)}, u32[]{:S(2)}, u32[]{:S(2)}) %collective-permute-start.39) | collective-permute-done | bytes 639008 | tf_op jit(solution)/shard_map/ppermute | solution.py:906
  396.1 3.0 add.274
  416.5 11.2 %collective-permute-done.45 = bf16[2,2,96,768]{3,2,1,0:T(8,128)(2,1)} collective-permute-done((bf16[2,2,96,768]{3,2,1,0:T(8,128)(2,1)}, bf16[2,2,96,768]{3,2,1,0:T(8,128)(2,1)}, u32[]{:S(2)}, u32[]{:S(2)}) %collective-permute-start.45) | collective-permute-done | bytes 589856 | tf_op jit(solution)/shard_map/ppermute | solution.py:906
  429.9 3.9 add.280
  455.3 13.7 %collective-permute-done.49 = bf16[2,2,2,48,896]{4,3,1,0,2:T(8,128)(2,1)} collective-permute-done((bf16[2,2,2,48,896]{4,3,1,0,2:T(8,128)(2,1)}, bf16[2,2,2,48,896]{4,3,1,0,2:T(8,128)(2,1)}, u32[]{:S(2)}, u32[]{:S(2)}) %collective-permute-start.49) | collective-permute-done | bytes 688160 | tf_op jit(solution)/shard_map/ppermute | solution.py:906
  481.5 9.8 %collective-permute-done.57 = f32[12,768]{1,0:T(8,128)S(1)} collective-permute-done((f32[12,768]{1,0:T(8,128)S(1)}, f32[12,768]{1,0:T(8,128)S(1)}, u32[]{:S(2)}, u32[]{:S(2)}) %collective-permute-start.57) | collective-permute-done | bytes 36896 | tf_op jit(solution)/shard_map/ppermute | solution.py:906
  491.6 6.6 %collective-permute-done.55 = bf16[2,2,48,896]{3,2,1,0:T(8,128)(2,1)S(1)} collective-permute-done((bf16[2,2,48,896]{3,2,1,0:T(8,128)(2,1)S(1)}, bf16[2,2,48,896]{3,2,1,0:T(8,128)(2,1)S(1)}, u32[]{:S(2)}, u32[]{:S(2)}) %collective-permute-start.55) | collective-permute-done | bytes 344096 | tf_op jit(solution)/shard_map/ppermute | solution.py:906
  498.5 4.7 collective-permute-done.59
  509.6 3.8 collective-permute-done.60
  513.4 4.9 collective-permute-done.61
  519.0 2.5 collective-permute-start.65
  521.9 3.7 collective-permute-done.66
  525.6 4.1 collective-permute-done.64
  529.7 3.7 collective-permute-done.65
  536.0 4.3 collective-permute-done.67
  540.3 2.9 collective-permute-done.68
  (416 shorter events, 150.3 us)
Async XLA Ops:
  7.2 284.3 %reduce-scatter.3.cloned.1.call-start = ((), (), s32[]{:S(2)}) async-start(), calls=%async_computation.2 | async-start | bytes 11796480 | tf_op jit(solution)/shard_map/reduce_scatter | solution.py:1186
  19.8 36.5 %collective-permute-start.4 = (bf16[2,768,768]{2,1,0:T(8,128)(2,1)S(1)}, bf16[2,768,768]{2,1,0:T(8,128)(2,1)}, u32[]{:S(2)}, u32[]{:S(2)}) collective-permute-start(bf16[2,768,768]{2,1,0:T(8,128)(2,1)S(1)} %copy-done), channel_id=1, source_target_pairs={{0,1},{1,0},{2,3},{3,2},{4,5},{5,4},{6,7},{7,6},{8,9},{9,8},{10,11... | collective-permute-start | bytes 7077896 | tf_op jit(solution)/shard_map/ppermute | solution.py:906
  20.2 36.1 %collective-permute-start.5 = (bf16[2,768,768]{2,1,0:T(8,128)(2,1)}, bf16[2,768,768]{2,1,0:T(8,128)(2,1)}, u32[]{:S(2)}, u32[]{:S(2)}) collective-permute-start(bf16[2,768,768]{2,1,0:T(8,128)(2,1)} %refs_9_.7), channel_id=1, source_target_pairs={{0,1},{1,0},{2,3},{3,2},{4,5},{5,4},{6,7},{7,6},{8,9},{9,8},{10,11... | collective-permute-start | bytes 7077896 | tf_op jit(solution)/shard_map/ppermute | solution.py:906
  20.3 36.0 %collective-permute-start.3 = (bf16[2,384,768]{2,1,0:T(8,128)(2,1)}, bf16[2,384,768]{2,1,0:T(8,128)(2,1)S(1)}, u32[]{:S(2)}, u32[]{:S(2)}) collective-permute-start(bf16[2,384,768]{2,1,0:T(8,128)(2,1)} %pad_maximum_fusion.1), channel_id=1, source_target_pairs={{0,2},{1,3},{2,0},{3,1},{4,6},{5,7},{6,4},{7,5},{8,10},{9,11},{10,... | collective-permute-start | bytes 3538952 | tf_op jit(solution)/shard_map/ppermute | solution.py:906
  42.7 11.2 %collective-permute-start.1 = (bf16[112,768]{1,0:T(8,128)(2,1)}, bf16[112,768]{1,0:T(8,128)(2,1)S(1)}, u32[]{:S(2)}, u32[]{:S(2)}) collective-permute-start(bf16[112,768]{1,0:T(8,128)(2,1)} %get-tuple-element.337), channel_id=1, source_target_pairs={{0,2},{1,3},{2,0},{3,1},{4,6},{5,7},{6,4},{7,5},{8,10},{9,11},{10,... | collective-permute-start | bytes 516104 | tf_op jit(solution)/shard_map/ppermute | solution.py:785
  44.3 12.0 %collective-permute-start.2 = (bf16[112,768]{1,0:T(8,128)(2,1)}, bf16[112,768]{1,0:T(8,128)(2,1)S(1)}, u32[]{:S(2)}, u32[]{:S(2)}) collective-permute-start(bf16[112,768]{1,0:T(8,128)(2,1)} %get-tuple-element.338), channel_id=1, source_target_pairs={{0,3},{1,2},{2,1},{3,0},{4,7},{5,6},{6,5},{7,4},{8,11},{9,10},{10,... | collective-permute-start | bytes 516104 | tf_op jit(solution)/shard_map/ppermute | solution.py:785
  57.0 28.4 %collective-permute-start.9 = (bf16[2,384,768]{2,1,0:T(8,128)(2,1)S(1)}, bf16[2,384,768]{2,1,0:T(8,128)(2,1)S(1)}, u32[]{:S(2)}, u32[]{:S(2)}) collective-permute-start(bf16[2,384,768]{2,1,0:T(8,128)(2,1)S(1)} %collective-permute-done.3.refs_14_.refs_12_), channel_id=1, source_target_pairs={{0,4},{4,0},{8,12},{12,8},{16,20},{20,16},{24,28},{28,24},{1,5},{5... | collective-permute-start | bytes 3538952 | tf_op jit(solution)/shard_map/ppermute | solution.py:906
  85.9 34.4 %collective-permute-start.12 = (bf16[2,384,768]{2,1,0:T(8,128)(2,1)}, bf16[2,384,768]{2,1,0:T(8,128)(2,1)S(1)}, u32[]{:S(2)}, u32[]{:S(2)}) collective-permute-start(bf16[2,384,768]{2,1,0:T(8,128)(2,1)} %pad_maximum_fusion.2), channel_id=1, source_target_pairs={{0,2},{1,3},{2,0},{3,1},{4,6},{5,7},{6,4},{7,5},{8,10},{9,11},{10,... | collective-permute-start | bytes 3538952 | tf_op jit(solution)/shard_map/ppermute | solution.py:906
  120.3 33.7 %collective-permute-start.19 = (bf16[2,384,768]{2,1,0:T(8,128)(2,1)S(1)}, bf16[2,384,768]{2,1,0:T(8,128)(2,1)S(1)}, u32[]{:S(2)}, u32[]{:S(2)}) collective-permute-start(bf16[2,384,768]{2,1,0:T(8,128)(2,1)S(1)} %collective-permute-done.12.refs_14_.refs_12_), channel_id=1, source_target_pairs={{0,4},{4,0},{8,12},{12,8},{16,20},{20,16},{24,28},{28,24},{1,5},{5... | collective-permute-start | bytes 3538952 | tf_op jit(solution)/shard_map/ppermute | solution.py:906
  191.7 14.2 %collective-permute-start.22 = (bf16[112,768]{1,0:T(8,128)(2,1)}, bf16[112,768]{1,0:T(8,128)(2,1)S(1)}, u32[]{:S(2)}, u32[]{:S(2)}) collective-permute-start(bf16[112,768]{1,0:T(8,128)(2,1)} %get-tuple-element.419), channel_id=1, source_target_pairs={{0,1},{1,0},{2,3},{3,2},{4,5},{5,4},{6,7},{7,6},{8,9},{9,8},{10,11... | collective-permute-start | bytes 516104 | tf_op jit(solution)/shard_map/ppermute | solution.py:785
  192.2 13.8 %collective-permute-start.23 = (bf16[112,768]{1,0:T(8,128)(2,1)}, bf16[112,768]{1,0:T(8,128)(2,1)S(1)}, u32[]{:S(2)}, u32[]{:S(2)}) collective-permute-start(bf16[112,768]{1,0:T(8,128)(2,1)} %get-tuple-element.420), channel_id=1, source_target_pairs={{0,2},{1,3},{2,0},{3,1},{4,6},{5,7},{6,4},{7,5},{8,10},{9,11},{10,... | collective-permute-start | bytes 516104 | tf_op jit(solution)/shard_map/ppermute | solution.py:785
  193.7 12.3 %collective-permute-start.24 = (bf16[112,768]{1,0:T(8,128)(2,1)}, bf16[112,768]{1,0:T(8,128)(2,1)S(1)}, u32[]{:S(2)}, u32[]{:S(2)}) collective-permute-start(bf16[112,768]{1,0:T(8,128)(2,1)} %get-tuple-element.421), channel_id=1, source_target_pairs={{0,3},{1,2},{2,1},{3,0},{4,7},{5,6},{6,5},{7,4},{8,11},{9,10},{10,... | collective-permute-start | bytes 516104 | tf_op jit(solution)/shard_map/ppermute | solution.py:785
  206.7 176.3 %reduce-scatter.5.cloned.1.call-start = ((), (), s32[]{:S(2)}) async-start(), calls=%async_computation.3 | async-start | bytes 2654208 | tf_op jit(solution)/shard_map/reduce_scatter | solution.py:1180
  276.4 15.1 %collective-permute-start.32 = (bf16[768,1920]{1,0:T(8,128)(2,1)}, bf16[768,1920]{1,0:T(8,128)(2,1)}, u32[]{:S(2)}, u32[]{:S(2)}) collective-permute-start(bf16[768,1920]{1,0:T(8,128)(2,1)} %get-tuple-element.493), channel_id=1, source_target_pairs={{0,1},{1,0},{2,3},{3,2},{4,5},{5,4},{6,7},{7,6},{8,9},{9,8},{10,11... | collective-permute-start | bytes 8847368 | tf_op jit(solution)/shard_map/ppermute | solution.py:906
  277.1 14.4 %collective-permute-start.31 = (bf16[768,1536]{1,0:T(8,128)(2,1)}, bf16[768,1536]{1,0:T(8,128)(2,1)}, u32[]{:S(2)}, u32[]{:S(2)}) collective-permute-start(bf16[768,1536]{1,0:T(8,128)(2,1)} %get-tuple-element.492), channel_id=1, source_target_pairs={{0,1},{1,0},{2,3},{3,2},{4,5},{5,4},{6,7},{7,6},{8,9},{9,8},{10,11... | collective-permute-start | bytes 7077896 | tf_op jit(solution)/shard_map/ppermute | solution.py:906
  277.2 14.3 %collective-permute-start.28 = (bf16[112,768]{1,0:T(8,128)(2,1)}, bf16[112,768]{1,0:T(8,128)(2,1)S(1)}, u32[]{:S(2)}, u32[]{:S(2)}) collective-permute-start(bf16[112,768]{1,0:T(8,128)(2,1)} %get-tuple-element.462), channel_id=1, source_target_pairs={{0,1},{1,0},{2,3},{3,2},{4,5},{5,4},{6,7},{7,6},{8,9},{9,8},{10,11... | collective-permute-start | bytes 516104 | tf_op jit(solution)/shard_map/ppermute | solution.py:785
  277.6 13.8 %collective-permute-start.29 = (bf16[112,768]{1,0:T(8,128)(2,1)}, bf16[112,768]{1,0:T(8,128)(2,1)S(1)}, u32[]{:S(2)}, u32[]{:S(2)}) collective-permute-start(bf16[112,768]{1,0:T(8,128)(2,1)} %get-tuple-element.463), channel_id=1, source_target_pairs={{0,2},{1,3},{2,0},{3,1},{4,6},{5,7},{6,4},{7,5},{8,10},{9,11},{10,... | collective-permute-start | bytes 516104 | tf_op jit(solution)/shard_map/ppermute | solution.py:785
  279.0 12.5 %collective-permute-start.30 = (bf16[112,768]{1,0:T(8,128)(2,1)}, bf16[112,768]{1,0:T(8,128)(2,1)S(1)}, u32[]{:S(2)}, u32[]{:S(2)}) collective-permute-start(bf16[112,768]{1,0:T(8,128)(2,1)} %get-tuple-element.464), channel_id=1, source_target_pairs={{0,3},{1,2},{2,1},{3,0},{4,7},{5,6},{6,5},{7,4},{8,11},{9,10},{10,... | collective-permute-start | bytes 516104 | tf_op jit(solution)/shard_map/ppermute | solution.py:785
  302.6 23.9 %collective-permute-start.33 = (bf16[2,768,1536]{2,1,0:T(8,128)(2,1)}, bf16[2,768,1536]{2,1,0:T(8,128)(2,1)}, u32[]{:S(2)}, u32[]{:S(2)}) collective-permute-start(bf16[2,768,1536]{2,1,0:T(8,128)(2,1)} %get-tuple-element.522), channel_id=1, source_target_pairs={{0,1},{1,0},{2,3},{3,2},{4,5},{5,4},{6,7},{7,6},{8,9},{9,8},{10,11... | collective-permute-start | bytes 14155784 | tf_op jit(solution)/shard_map/ppermute | solution.py:906
  303.3 38.9 %collective-permute-start.38 = (bf16[2,2,2,48,1792]{4,3,1,0,2:T(8,128)(2,1)}, bf16[2,2,2,48,1792]{4,3,1,0,2:T(8,128)(2,1)}, u32[]{:S(2)}, u32[]{:S(2)}) collective-permute-start(bf16[2,2,2,48,1792]{4,3,1,0,2:T(8,128)(2,1)} %bitcast.166), channel_id=1, source_target_pairs={{0,4},{4,0},{8,12},{12,8},{16,20},{20,16},{24,28},{28,24},{1,5},{5... | collective-permute-start | bytes 4128776 | tf_op jit(solution)/shard_map/ppermute | solution.py:906
  304.1 31.9 %collective-permute-start.37 = (bf16[2,2,2,48,1664]{4,3,1,0,2:T(8,128)(2,1)}, bf16[2,2,2,48,1664]{4,3,1,0,2:T(8,128)(2,1)}, u32[]{:S(2)}, u32[]{:S(2)}) collective-permute-start(bf16[2,2,2,48,1664]{4,3,1,0,2:T(8,128)(2,1)} %bitcast.167), channel_id=1, source_target_pairs={{0,2},{1,3},{2,0},{3,1},{4,6},{5,7},{6,4},{7,5},{8,10},{9,11},{10,... | collective-permute-start | bytes 3833864 | tf_op jit(solution)/shard_map/ppermute | solution.py:906
  326.6 15.6 %collective-permute-start.34 = (bf16[112,768]{1,0:T(8,128)(2,1)S(1)}, bf16[112,768]{1,0:T(8,128)(2,1)S(1)}, u32[]{:S(2)}, u32[]{:S(2)}) collective-permute-start(bf16[112,768]{1,0:T(8,128)(2,1)S(1)} %copy-done.73), channel_id=1, source_target_pairs={{0,1},{1,0},{2,3},{3,2},{4,5},{5,4},{6,7},{7,6},{8,9},{9,8},{10,11... | collective-permute-start | bytes 516104 | tf_op jit(solution)/shard_map/ppermute | solution.py:785
  326.7 15.6 %collective-permute-start.35 = (bf16[112,768]{1,0:T(8,128)(2,1)S(1)}, bf16[112,768]{1,0:T(8,128)(2,1)S(1)}, u32[]{:S(2)}, u32[]{:S(2)}) collective-permute-start(bf16[112,768]{1,0:T(8,128)(2,1)S(1)} %copy-done.72), channel_id=1, source_target_pairs={{0,2},{1,3},{2,0},{3,1},{4,6},{5,7},{6,4},{7,5},{8,10},{9,11},{10,... | collective-permute-start | bytes 516104 | tf_op jit(solution)/shard_map/ppermute | solution.py:785
  327.2 15.1 %collective-permute-start.36 = (bf16[112,768]{1,0:T(8,128)(2,1)S(1)}, bf16[112,768]{1,0:T(8,128)(2,1)S(1)}, u32[]{:S(2)}, u32[]{:S(2)}) collective-permute-start(bf16[112,768]{1,0:T(8,128)(2,1)S(1)} %copy-done.71), channel_id=1, source_target_pairs={{0,3},{1,2},{2,1},{3,0},{4,7},{5,6},{6,5},{7,4},{8,11},{9,10},{10,... | collective-permute-start | bytes 516104 | tf_op jit(solution)/shard_map/ppermute | solution.py:785
  348.6 47.4 %collective-permute-start.43 = (bf16[768,1536]{1,0:T(8,128)(2,1)}, bf16[768,1536]{1,0:T(8,128)(2,1)}, u32[]{:S(2)}, u32[]{:S(2)}) collective-permute-start(bf16[768,1536]{1,0:T(8,128)(2,1)} %get-tuple-element.564), channel_id=1, source_target_pairs={{0,1},{1,0},{2,3},{3,2},{4,5},{5,4},{6,7},{7,6},{8,9},{9,8},{10,11... | collective-permute-start | bytes 7077896 | tf_op jit(solution)/shard_map/ppermute | solution.py:906
  348.7 47.4 %collective-permute-start.41 = (bf16[2,2,2,96,768]{4,3,2,1,0:T(8,128)(2,1)}, bf16[2,2,2,96,768]{4,3,2,1,0:T(8,128)(2,1)S(1)}, u32[]{:S(2)}, u32[]{:S(2)}) collective-permute-start(bf16[2,2,2,96,768]{4,3,2,1,0:T(8,128)(2,1)} %slice_bitcast_fusion.1), channel_id=1, source_target_pairs={{0,2},{1,3},{2,0},{3,1},{4,6},{5,7},{6,4},{7,5},{8,10},{9,11},{10,... | collective-permute-start | bytes 3538952 | tf_op jit(solution)/shard_map/ppermute | solution.py:906
  349.8 46.2 %collective-permute-start.42 = (bf16[2,2,2,96,768]{4,3,2,1,0:T(8,128)(2,1)}, bf16[2,2,2,96,768]{4,3,2,1,0:T(8,128)(2,1)}, u32[]{:S(2)}, u32[]{:S(2)}) collective-permute-start(bf16[2,2,2,96,768]{4,3,2,1,0:T(8,128)(2,1)} %dynamic-slice_bitcast_fusion), channel_id=1, source_target_pairs={{0,4},{4,0},{8,12},{12,8},{16,20},{20,16},{24,28},{28,24},{1,5},{5... | collective-permute-start | bytes 3538952 | tf_op jit(solution)/shard_map/ppermute | solution.py:906
  351.3 44.7 %collective-permute-start.40 = (bf16[2,2,48,1792]{3,2,1,0:T(8,128)(2,1)}, bf16[2,2,48,1792]{3,2,1,0:T(8,128)(2,1)}, u32[]{:S(2)}, u32[]{:S(2)}) collective-permute-start(bf16[2,2,48,1792]{3,2,1,0:T(8,128)(2,1)} %dynamic-slice_bitcast_fusion.1), channel_id=1, source_target_pairs={{0,2},{1,3},{2,0},{3,1},{4,6},{5,7},{6,4},{7,5},{8,10},{9,11},{10,... | collective-permute-start | bytes 2064392 | tf_op jit(solution)/shard_map/ppermute | solution.py:906
  351.7 44.3 %collective-permute-start.39 = (bf16[2,2,48,1664]{3,2,1,0:T(8,128)(2,1)}, bf16[2,2,48,1664]{3,2,1,0:T(8,128)(2,1)}, u32[]{:S(2)}, u32[]{:S(2)}) collective-permute-start(bf16[2,2,48,1664]{3,2,1,0:T(8,128)(2,1)} %dynamic-slice_bitcast_fusion.2), channel_id=1, source_target_pairs={{0,4},{4,0},{8,12},{12,8},{16,20},{20,16},{24,28},{28,24},{1,5},{5... | collective-permute-start | bytes 1916936 | tf_op jit(solution)/shard_map/ppermute | solution.py:906
  396.0 33.9 %collective-permute-start.47 = (bf16[768,1920]{1,0:T(8,128)(2,1)}, bf16[768,1920]{1,0:T(8,128)(2,1)}, u32[]{:S(2)}, u32[]{:S(2)}) collective-permute-start(bf16[768,1920]{1,0:T(8,128)(2,1)} %get-tuple-element.576), channel_id=1, source_target_pairs={{0,1},{1,0},{2,3},{3,2},{4,5},{5,4},{6,7},{7,6},{8,9},{9,8},{10,11... | collective-permute-start | bytes 8847368 | tf_op jit(solution)/shard_map/ppermute | solution.py:906
  409.8 20.1 %collective-permute-start.44 = (bf16[2,48,3456]{2,1,0:T(8,128)(2,1)S(1)}, bf16[2,48,3456]{2,1,0:T(8,128)(2,1)S(1)}, u32[]{:S(2)}, u32[]{:S(2)}) collective-permute-start(bf16[2,48,3456]{2,1,0:T(8,128)(2,1)S(1)} %fusion.5), channel_id=1, source_target_pairs={{0,8},{4,12},{8,0},{12,4},{16,24},{20,28},{24,16},{28,20},{1,9},{5... | collective-permute-start | bytes 1990664 | tf_op jit(solution)/shard_map/ppermute | solution.py:906
  412.0 15.8 %collective-permute-start.45 = (bf16[2,2,96,768]{3,2,1,0:T(8,128)(2,1)}, bf16[2,2,96,768]{3,2,1,0:T(8,128)(2,1)}, u32[]{:S(2)}, u32[]{:S(2)}) collective-permute-start(bf16[2,2,96,768]{3,2,1,0:T(8,128)(2,1)} %dynamic-slice_bitcast_fusion.4), channel_id=1, source_target_pairs={{0,4},{4,0},{8,12},{12,8},{16,20},{20,16},{24,28},{28,24},{1,5},{5... | collective-permute-start | bytes 1769480 | tf_op jit(solution)/shard_map/ppermute | solution.py:906
  413.5 16.4 %collective-permute-start.46 = (bf16[2,2,96,768]{3,2,1,0:T(8,128)(2,1)}, bf16[2,2,96,768]{3,2,1,0:T(8,128)(2,1)S(1)}, u32[]{:S(2)}, u32[]{:S(2)}) collective-permute-start(bf16[2,2,96,768]{3,2,1,0:T(8,128)(2,1)} %slice_bitcast_fusion.3), channel_id=1, source_target_pairs={{0,2},{1,3},{2,0},{3,1},{4,6},{5,7},{6,4},{7,5},{8,10},{9,11},{10,... | collective-permute-start | bytes 1769480 | tf_op jit(solution)/shard_map/ppermute | solution.py:906
  415.4 39.9 %collective-permute-start.48 = (bf16[2,2,2,48,1536]{4,3,1,0,2:T(8,128)(2,1)}, bf16[2,2,2,48,1536]{4,3,1,0,2:T(8,128)(2,1)}, u32[]{:S(2)}, u32[]{:S(2)}) collective-permute-start(bf16[2,2,2,48,1536]{4,3,1,0,2:T(8,128)(2,1)} %bitcast.168), channel_id=1, source_target_pairs={{0,2},{1,3},{2,0},{3,1},{4,6},{5,7},{6,4},{7,5},{8,10},{9,11},{10,... | collective-permute-start | bytes 3538952 | tf_op jit(solution)/shard_map/ppermute | solution.py:906
  442.3 26.7 %collective-permute-start.50 = (bf16[2,2,2,48,1024]{4,3,1,0,2:T(8,128)(2,1)}, bf16[2,2,2,48,1024]{4,3,1,0,2:T(8,128)(2,1)}, u32[]{:S(2)}, u32[]{:S(2)}) collective-permute-start(bf16[2,2,2,48,1024]{4,3,1,0,2:T(8,128)(2,1)} %bitcast.169), channel_id=1, source_target_pairs={{0,4},{4,0},{8,12},{12,8},{16,20},{20,16},{24,28},{28,24},{1,5},{5... | collective-permute-start | bytes 2359304 | tf_op jit(solution)/shard_map/ppermute | solution.py:906
  442.8 26.2 %collective-permute-start.49 = (bf16[2,2,2,48,896]{4,3,1,0,2:T(8,128)(2,1)}, bf16[2,2,2,48,896]{4,3,1,0,2:T(8,128)(2,1)}, u32[]{:S(2)}, u32[]{:S(2)}) collective-permute-start(bf16[2,2,2,48,896]{4,3,1,0,2:T(8,128)(2,1)} %bitcast.170), channel_id=1, source_target_pairs={{0,2},{1,3},{2,0},{3,1},{4,6},{5,7},{6,4},{7,5},{8,10},{9,11},{10,... | collective-permute-start | bytes 2064392 | tf_op jit(solution)/shard_map/ppermute | solution.py:906
  451.5 22.5 %collective-permute-start.52 = (bf16[48,3456]{1,0:T(8,128)(2,1)S(1)}, bf16[48,3456]{1,0:T(8,128)(2,1)S(1)}, u32[]{:S(2)}, u32[]{:S(2)}) collective-permute-start(bf16[48,3456]{1,0:T(8,128)(2,1)S(1)} %copy-done.39), channel_id=1, source_target_pairs={{0,16},{4,20},{8,24},{12,28},{16,0},{20,4},{24,8},{28,12},{1,17},{... | collective-permute-start | bytes 995336 | tf_op jit(solution)/shard_map/ppermute | solution.py:906
  453.7 22.5 %collective-permute-start.53 = (bf16[2,96,1536]{2,1,0:T(8,128)(2,1)S(1)}, bf16[2,96,1536]{2,1,0:T(8,128)(2,1)S(1)}, u32[]{:S(2)}, u32[]{:S(2)}) collective-permute-start(bf16[2,96,1536]{2,1,0:T(8,128)(2,1)S(1)} %copy-done.38), channel_id=1, source_target_pairs={{0,8},{4,12},{8,0},{12,4},{16,24},{20,28},{24,16},{28,20},{1,9},{5... | collective-permute-start | bytes 1769480 | tf_op jit(solution)/shard_map/ppermute | solution.py:906
  476.2 22.0 %collective-permute-start.54 = (bf16[2,2,48,1536]{3,2,1,0:T(8,128)(2,1)S(1)}, bf16[2,2,48,1536]{3,2,1,0:T(8,128)(2,1)S(1)}, u32[]{:S(2)}, u32[]{:S(2)}) collective-permute-start(bf16[2,2,48,1536]{3,2,1,0:T(8,128)(2,1)S(1)} %dynamic-slice_bitcast_fusion.3), channel_id=1, source_target_pairs={{0,4},{4,0},{8,12},{12,8},{16,20},{20,16},{24,28},{28,24},{1,5},{5... | collective-permute-start | bytes 1769480 | tf_op jit(solution)/shard_map/ppermute | solution.py:906
  477.2 20.9 %collective-permute-start.55 = (bf16[2,2,48,896]{3,2,1,0:T(8,128)(2,1)S(1)}, bf16[2,2,48,896]{3,2,1,0:T(8,128)(2,1)S(1)}, u32[]{:S(2)}, u32[]{:S(2)}) collective-permute-start(bf16[2,2,48,896]{3,2,1,0:T(8,128)(2,1)S(1)} %dynamic-slice_bitcast_fusion.6), channel_id=1, source_target_pairs={{0,4},{4,0},{8,12},{12,8},{16,20},{20,16},{24,28},{28,24},{1,5},{5... | collective-permute-start | bytes 1032200 | tf_op jit(solution)/shard_map/ppermute | solution.py:906
  478.2 20.0 %collective-permute-start.56 = (bf16[2,2,48,1024]{3,2,1,0:T(8,128)(2,1)S(1)}, bf16[2,2,48,1024]{3,2,1,0:T(8,128)(2,1)S(1)}, u32[]{:S(2)}, u32[]{:S(2)}) collective-permute-start(bf16[2,2,48,1024]{3,2,1,0:T(8,128)(2,1)S(1)} %dynamic-slice_bitcast_fusion.5), channel_id=1, source_target_pairs={{0,2},{1,3},{2,0},{3,1},{4,6},{5,7},{6,4},{7,5},{8,10},{9,11},{10,... | collective-permute-start | bytes 1179656 | tf_op jit(solution)/shard_map/ppermute | solution.py:906
  479.1 12.1 %collective-permute-start.57 = (f32[12,768]{1,0:T(8,128)S(1)}, f32[12,768]{1,0:T(8,128)S(1)}, u32[]{:S(2)}, u32[]{:S(2)}) collective-permute-start(f32[12,768]{1,0:T(8,128)S(1)} %add.284), channel_id=1, source_target_pairs={{0,2},{1,3},{2,0},{3,1},{4,6},{5,7},{6,4},{7,5},{8,10},{9,11},{10,... | collective-permute-start | bytes 110600 | tf_op jit(solution)/shard_map/ppermute | solution.py:906
  480.5 22.7 %collective-permute-start.58 = (bf16[48,3456]{1,0:T(8,128)(2,1)S(1)}, bf16[48,3456]{1,0:T(8,128)(2,1)S(1)}, u32[]{:S(2)}, u32[]{:S(2)}) collective-permute-start(bf16[48,3456]{1,0:T(8,128)(2,1)S(1)} %bitcast_add_fusion.12), channel_id=1, source_target_pairs={{0,2},{1,3},{2,0},{3,1},{4,6},{5,7},{6,4},{7,5},{8,10},{9,11},{10,... | collective-permute-start | bytes 995336 | tf_op jit(solution)/shard_map/ppermute | solution.py:906
  491.3 11.9 %collective-permute-start.59 = (bf16[96,1536]{1,0:T(8,128)(2,1)S(1)}, bf16[96,1536]{1,0:T(8,128)(2,1)S(1)}, u32[]{:S(2)}, u32[]{:S(2)}) collective-permute-start(bf16[96,1536]{1,0:T(8,128)(2,1)S(1)} %dynamic-slice_bitcast_fusion.9), channel_id=1, source_target_pairs={{0,16},{4,20},{8,24},{12,28},{16,0},{20,4},{24,8},{28,12},{1,17},{... | collective-permute-start | bytes 884744 | tf_op jit(solution)/shard_map/ppermute | solution.py:906
  503.5 14.8 %collective-permute-start.61 = (bf16[2,48,1920]{2,1,0:T(8,128)(2,1)S(1)}, bf16[2,48,1920]{2,1,0:T(8,128)(2,1)S(1)}, u32[]{:S(2)}, u32[]{:S(2)}) collective-permute-start(bf16[2,48,1920]{2,1,0:T(8,128)(2,1)S(1)} %fusion.16), channel_id=1, source_target_pairs={{0,8},{4,12},{8,0},{12,4},{16,24},{20,28},{24,16},{28,20},{1,9},{5... | collective-permute-start | bytes 1105928 | tf_op jit(solution)/shard_map/ppermute | solution.py:906
  506.6 15.2 %collective-permute-start.63 = (bf16[96,3456]{1,0:T(8,128)(2,1)S(1)}, bf16[96,3456]{1,0:T(8,128)(2,1)S(1)}, u32[]{:S(2)}, u32[]{:S(2)}) collective-permute-start(bf16[96,3456]{1,0:T(8,128)(2,1)S(1)} %maximum_select_fusion), channel_id=1, source_target_pairs={{0,1},{1,0},{2,3},{3,2},{4,5},{5,4},{6,7},{7,6},{8,9},{9,8},{10,11... | collective-permute-start | bytes 1990664 | tf_op jit(solution)/shard_map/ppermute | solution.py:906
  518.5 11.2 %collective-permute-start.64 = (bf16[48,1536]{1,0:T(8,128)(2,1)S(1)}, bf16[48,1536]{1,0:T(8,128)(2,1)S(1)}, u32[]{:S(2)}, u32[]{:S(2)}) collective-permute-start(bf16[48,1536]{1,0:T(8,128)(2,1)S(1)} %dynamic-slice_bitcast_fusion.11), channel_id=1, source_target_pairs={{0,16},{4,20},{8,24},{12,28},{16,0},{20,4},{24,8},{28,12},{1,17},{... | collective-permute-start | bytes 442376 | tf_op jit(solution)/shard_map/ppermute | solution.py:906
  519.0 14.4 %collective-permute-start.65 = (bf16[48,1920]{1,0:T(8,128)(2,1)S(1)}, bf16[48,1920]{1,0:T(8,128)(2,1)S(1)}, u32[]{:S(2)}, u32[]{:S(2)}) collective-permute-start(bf16[48,1920]{1,0:T(8,128)(2,1)S(1)} %dynamic-slice_bitcast_fusion.10), channel_id=1, source_target_pairs={{0,16},{4,20},{8,24},{12,28},{16,0},{20,4},{24,8},{28,12},{1,17},{... | collective-permute-start | bytes 552968 | tf_op jit(solution)/shard_map/ppermute | solution.py:906
  (103 other events, 588.1 us)
Sparse Core Ops, SparseCore 0:
  206.1 82.1 reduce-scatter.2
  305.8 77.0 reduce-scatter.4

commit v4 on v3

--- a/solution.py
+++ b/solution.py
@@ -191,6 +191,7 @@
     copies = fetch(
         (in_hbm.at[layer], out_hbm.at[layer], mix_hbm.at[layer]), (in_ref, out_ref, mix_ref), sems
     )
+    yield
     gain = gain_ref[layer, 0:1, :]
     shift = shift_ref[layer, 0:1, :]
     for frame in range(frames):
@@ -267,6 +268,7 @@
     seq = groups * patches
     rows = normed_ref.shape[0] // own_frames
     copies = fetch((in_hbm.at[layer],), (in_ref,), sems)
+    yield
     pieces = [piece0, piece1, piece2, piece3]
     for away, piece in enumerate(pieces):
         values = piece[...].astype(FULL)
@@ -349,6 +351,7 @@
     own = (up_hbm.at[layer], peer_up.at[layer], down_hbm.at[layer], peer_down.at[layer])
     peers = (peer2, peer3, peer4, peer5)
     shards = start_shards(place_ref, own, peers, up_ref, down_ref, sems)
+    yield
     take_pieces(
         (piece0, piece1, piece2, piece3), blocks, plain, frame_rows, place, size, frames // groups
     )
@@ -399,6 +402,7 @@
         active_ref[end:, own] = (active_ref[end:, own].astype(FULL) * kept[end:]).astype(HALF)
         active_ref.flush(own)
         slope_ref.flush(own)
+    next_ref.flush()
 
 
 def feed_backward(dims, layer, place_ref, clip_ref, grad_ref, slope_ref, rows_ref, share_ref, gain_ref,
@@ -415,6 +419,7 @@
     peers = (peer2, peer3, peer4, peer5)
     shards = start_shards(place_ref, own, peers, up_ref, down_ref, sems)
     copies = fetch((out_hbm.at[layer],), (out_ref,), out_sem)
+    yield
     update_ref[...] = grad_ref[...].astype(HALF)
     update_ref.flush()
     for away in range(groups):
@@ -474,6 +479,7 @@
     seq = groups * patches
     rows = triple_ref.shape[0] // own_frames
     copies = fetch((in_hbm.at[layer],), (in_ref,), sems)
+    yield
     for away, piece in enumerate((piece0, piece1, piece2, piece3)):
         values = piece[...].astype(FULL)
         for frame in range(own_frames):
@@ -521,6 +527,7 @@
     copies = fetch(
         (mix_hbm.at[layer], out_hbm.at[layer], in_hbm.at[layer]), (mix_ref, out_ref, in_ref), sems
     )
+    yield
     take_pieces(
         (piece0, piece1, piece2, piece3),
         blocks,
@@ -604,6 +611,7 @@
         next_ref[own, :] += unit_back(grad, unit, inverse, gain)
         norms_ref[2:3, :] += jnp.sum(grad * unit, 0, keepdims=True)
         norms_ref[3:4, :] += jnp.sum(grad, 0, keepdims=True)
+    next_ref.flush()
 
 
 def cost(micros):
@@ -653,7 +661,56 @@
             copy.wait()
 
 
+class Result:
+    def __init__(self, index):
+        self.index = index
+
+
+def step_of(kernel, outs, scratch, specs, micros):
+    return lambda *arrays: (kernel, outs, scratch, specs, micros, arrays)
+
+
 def call(kernel, outs, scratch, specs, micros):
+    return lambda *arrays: call_steps((kernel, outs, scratch, specs, micros, arrays))
+
+
+def call_steps(*steps):
+    outs = sum([list(step[1]) for step in steps], [])
+    scratch = sum([list(step[2]) for step in steps], [])
+    specs, arrays = [], []
+    for step in steps:
+        for kind, array in zip(step[3], step[5]):
+            if not isinstance(array, Result):
+                specs.append(kind)
+                arrays.append(array)
+
+    def kernel(*refs):
+        ins = list(refs[: len(specs)])
+        written = list(refs[len(specs) : len(specs) + len(outs)])
+        rest = list(refs[len(specs) + len(outs) :])
+        before = ()
+        runs = []
+        for unused, own_outs, own_scratch, unused, unused, own_arrays in steps:
+            given = [before[a.index] if isinstance(a, Result) else ins.pop(0) for a in own_arrays]
+            before = [written.pop(0) for out in own_outs]
+            given += before + [rest.pop(0) for buffer in own_scratch]
+            runs.append(given)
+        runs = [step[0](*given) for step, given in zip(steps, runs)]
+        for run in runs:
+            next(run)
+        for run in runs:
+            for unused in run:
+                pass
+
+    results = call_arrays(kernel, outs, scratch, specs, sum(step[4] for step in steps))(*arrays)
+    parts = []
+    for step in steps:
+        parts.append(results[: len(step[1])])
+        results = results[len(step[1]) :]
+    return parts[0] if len(steps) == 1 else parts
+
+
+def call_arrays(kernel, outs, scratch, specs, micros):
     def run(*arrays):
         fetched = [index for index, kind in enumerate(specs) if kind == ROWS]
         count, results = len(specs), len(outs)
@@ -1028,9 +1085,8 @@
     shards = pltpu.VMEM((groups, width, width), HALF)
     blocks = pltpu.VMEM((groups, back_rows, width), FULL)
     frame_rows = pltpu.VMEM((frames, width), FULL)
-    saved = []
-    for layer in range(layers):
-        time = call(
+    def time_step(layer, patch_rows):
+        return step_of(
             partial(time_forward, dims, layer),
             [
                 ((rows, width), HALF),
@@ -1046,6 +1102,98 @@
             [SMALL, ROWS, ROWS, ROWS, ROWS, FAR, FAR, FAR],
             14,
         )(place, patch_rows, bias, norm_gain, norm_shift, temporal_in, temporal_out, temporal_mix)
+
+    def feed_step(layer, arrived, after):
+        return step_of(
+            partial(feed_forward, dims, layer),
+            [
+                ((rows, width), HALF),
+                ((rows, width), FULL),
+                ((rows, width), HALF),
+                ((rows, hidden), HALF),
+                ((rows, hidden), HALF),
+                ((rows, width), FULL),
+            ],
+            [
+                square,
+                shards,
+                shards,
+                row_buffer,
+                blocks,
+                frame_rows,
+                pltpu.VMEM((rows, width), HALF),
+                pltpu.SemaphoreType.DMA((1,)),
+                pltpu.SemaphoreType.DMA((12,)),
+            ],
+            [SMALL] + [ROWS] * groups + [ROWS] * 4 + [FAR] * 9,
+            15,
+        )(
+            place, *arrived, share, after, norm_gain, norm_shift, spatial_out,
+            hidden_up, hidden_down, *gathered[layer],
+        )
+
+    def feed_back_step(layer, grad_rows, slope, rows_in):
+        return step_of(
+            partial(feed_backward, dims, layer),
+            [
+                ((rows, width), HALF),
+                ((rows, hidden), HALF),
+                ((rows, width), HALF),
+                ((rows, width), FULL),
+                ((8, width), FULL),
+            ]
+            + pieces_out
+            + [((8, width), FULL)],
+            [
+                square,
+                shards,
+                shards,
+                row_buffer,
+                row_buffer,
+                blocks,
+                pltpu.SemaphoreType.DMA((1,)),
+                pltpu.SemaphoreType.DMA((12,)),
+            ],
+            [SMALL, SMALL] + [ROWS] * 5 + [FAR] * 9,
+            23,
+        )(
+            place, clip_of, grad_rows, slope, rows_in,
+            jnp.broadcast_to(inverse_counts[:, None], (spare, 128)), norm_gain, spatial_out,
+            hidden_up, hidden_down, *gathered[layer],
+        )
+
+    def time_back_step(layer, arrived, back, time, start_rows):
+        return step_of(
+            partial(time_backward, dims, layer),
+            [
+                ((rows, width), HALF),
+                ((rows, width), HALF),
+                ((rows, 3 * width), HALF),
+                ((rows, width), FULL),
+                ((8, width), FULL),
+            ],
+            [
+                wide,
+                square,
+                square,
+                lane_buffer,
+                row_buffer,
+                blocks,
+                frame_rows,
+                pltpu.VMEM((rows, width), HALF),
+                pltpu.SemaphoreType.DMA((3,)),
+            ],
+            [SMALL] + [ROWS] * groups + [ROWS] * 8 + [FAR] * 3,
+            14,
+        )(
+            place, *arrived, member, back, time[5], start_rows, time[1], time[2], bias,
+            norm_gain, temporal_in, temporal_out, temporal_mix,
+        )
+
+    saved = []
+    grad_rows = rows_of(patch_cotangent, class_cotangent)
+    time = call_steps(time_step(0, patch_rows))
+    for layer in range(layers):
         pieces = time[6:10]
         if layer:
             pieces = flights.land(["x1"], pieces)
@@ -1081,39 +1229,20 @@
             arrived_here("first"),
             arrived_here("second"),
         )
-        feed = call(
-            partial(feed_forward, dims, layer),
-            [
-                ((rows, width), HALF),
-                ((rows, width), FULL),
-                ((rows, width), HALF),
-                ((rows, hidden), HALF),
-                ((rows, hidden), HALF),
-                ((rows, width), FULL),
-            ],
-            [
-                square,
-                shards,
-                shards,
-                row_buffer,
-                blocks,
-                frame_rows,
-                pltpu.VMEM((rows, width), HALF),
-                pltpu.SemaphoreType.DMA((1,)),
-                pltpu.SemaphoreType.DMA((12,)),
-            ],
-            [SMALL] + [ROWS] * groups + [ROWS] * 4 + [FAR] * 9,
-            15,
-        )(
-            place, *arrived, share, time[5], norm_gain, norm_shift, spatial_out,
-            hidden_up, hidden_down, *gathered[layer],
-        )
+        step = feed_step(layer, arrived, time[5])
+        if layer + 1 < layers:
+            feed, later = call_steps(step, time_step(layer + 1, Result(5)))
+        else:
+            feed, later = call_steps(
+                step, feed_back_step(layer, grad_rows, Result(4), Result(1))
+            )
         saved.append((patch_rows, time, space, feed))
         patch_rows = feed[5]
+        time = later
+    feed_back = later
     patch_output = patch_rows[:count].reshape(frames, patches, width).astype(HALF)
     class_output = patch_rows[count : count + clips].astype(HALF)
 
-    grad_rows = rows_of(patch_cotangent, class_cotangent)
     usual = blocks_dp == 2 * NEAR
     norms = [None] * layers
 
@@ -1139,34 +1268,6 @@
     for layer in reversed(range(layers)):
         start_rows, time, space, feed = saved[layer]
         last = layer == 0
-        feed_back = call(
-            partial(feed_backward, dims, layer),
-            [
-                ((rows, width), HALF),
-                ((rows, hidden), HALF),
-                ((rows, width), HALF),
-                ((rows, width), FULL),
-                ((8, width), FULL),
-            ]
-            + pieces_out
-            + [((8, width), FULL)],
-            [
-                square,
-                shards,
-                shards,
-                row_buffer,
-                row_buffer,
-                blocks,
-                pltpu.SemaphoreType.DMA((1,)),
-                pltpu.SemaphoreType.DMA((12,)),
-            ],
-            [SMALL, SMALL] + [ROWS] * 5 + [FAR] * 9,
-            23,
-        )(
-            place, clip_of, grad_rows, feed[4], feed[1],
-            jnp.broadcast_to(inverse_counts[:, None], (spare, 128)), norm_gain, spatial_out,
-            hidden_up, hidden_down, *gathered[layer],
-        )
         update, grad_hidden, branch, back, feed_norms = feed_back[:5]
         arrived = spread(feed_back[5:9])
         pairs = ((feed[2], grad_hidden), (update, feed[3]))
@@ -1214,32 +1315,14 @@
                 early = (pairs, parts)
             else:
                 early = (pairs, None)
-        time_back = call(
-            partial(time_backward, dims, layer),
-            [
-                ((rows, width), HALF),
-                ((rows, width), HALF),
-                ((rows, 3 * width), HALF),
-                ((rows, width), FULL),
-                ((8, width), FULL),
-            ],
-            [
-                wide,
-                square,
-                square,
-                lane_buffer,
-                row_buffer,
-                blocks,
-                frame_rows,
-                pltpu.VMEM((rows, width), HALF),
-                pltpu.SemaphoreType.DMA((3,)),
-            ],
-            [SMALL] + [ROWS] * groups + [ROWS] * 8 + [FAR] * 3,
-            14,
-        )(
-            place, *arrived, member, back, time[5], start_rows, time[1], time[2], bias,
-            norm_gain, temporal_in, temporal_out, temporal_mix,
-        )
+        step = time_back_step(layer, arrived, back, time, start_rows)
+        if last:
+            time_back = call_steps(step)
+        else:
+            ahead = saved[layer - 1][3]
+            time_back, later = call_steps(
+                step, feed_back_step(layer - 1, Result(3), ahead[4], ahead[1])
+            )
         grad_rows = time_back[3]
         norms[layer] = (time_back[4], feed_norms)
         pairs = ((time[0], time_back[2]), (time[3], time_back[1]), (time[4], time_back[0]))
@@ -1263,7 +1346,7 @@
             token, flights.results["feed1"] = lax.optimization_barrier((token, feed_sum))
         else:
             time_pairs = pairs
-            grad_rows = flights.turn(["feed1"], grad_rows)
+            feed_back = later
     for names in (
         ("attention1", "feed0", "space0"),
         ("attention1", "feed0", "time0", "norms"),

time: 569 us -> 561 us (0.986)
  Pallas kernels: 237 us -> 227 us
    pallas_call x12 -> x9, Pallas kernels: 180 us -> 170 us  [run(): pl.pallas_call(whole, out_shape=[jax.ShapeDtypeStruct(shape, kind) for sh...]
    ppermute x48, waiting for transfers between devices: 112 us -> 106 us  [leave(): lax.ppermute(send, *way)]
    unnamed x160 -> x158, local copies, waits for them, and re-layouts: 17.2 us -> 18.4 us
  transfers between devices with their start and end apart: 74 -> 74, of which waited for: 33 -> 35; matrix products, arithmetic and copies ran while one was open for 11% -> 11% of each run, Pallas kernels for 37% -> 36%
where the time goes in v4:
time: 561 us; the launch traced here: 551 us
  Pallas kernels  227 us (40%)
  waiting for transfers between devices  145 us (26%)
  starting transfers between devices  61.2 us (11%)
  local copies, waits for them, and re-layouts  54 us (10%)
  other arithmetic  47.5 us (8%)
  between operations  15.8 us (3%)
    pallas_call x9, Pallas kernels, run(): pl.pallas_call(whole, out_shape=[jax.ShapeDtypeStruct(shape, kind) for sh...  170 us
    ppermute x48, waiting for transfers between devices, leave(): lax.ppermute(send, *way)  106 us
    pallas_call x6, Pallas kernels, outer_group(): pl.pallas_call(kernel, out_shape=[jax.ShapeDtypeStruct(shape, HALF)] * re...  56.8 us
    ppermute x48, starting transfers between devices, leave(): lax.ppermute(send, *way)  46.1 us
    ppermute x24, waiting for transfers between devices, swap(): return lax.ppermute(values, *exchange(axis, bit))  38.9 us
    unnamed x158, local copies, waits for them, and re-layouts  18.4 us
    add x5, other arithmetic, reduce_group(): sums = [keep + other for (send, keep), other in zip(groups, others)]  15.9 us
    ppermute x24, starting transfers between devices, swap(): return lax.ppermute(values, *exchange(axis, bit))  14.7 us
  transfers between devices with their start and end apart: 74, of which 35 were waited for; matrix products, arithmetic and copies ran while one was open for 11% of the time, Pallas kernels for 36%

profile of v4, /device:TPU:0, one launch (start us, length us, event | category | flops | bytes accessed | tf_op | source)
XLA Modules:
  0.0 551.3 jit_solution(4910457005156831140)
XLA Ops:
  13.0 3.2 fusion.20
  21.3 2.9 collective-permute-start.3
  28.5 15.0 %shard_map.237 = (bf16[400,768]{1,0:T(8,128)(2,1)}, bf16[400,2304]{1,0:T(8,128)(2,1)}, f32[400,128]{1,0:T(8,128)}, bf16[400,768]{1,0:T(8,128)(2,1)}, bf16[400,76...) custom-call(s32[2]{0:T(128)} %pad_add_fusion.refs_0_.refs_18_.place_, ...), custom_call_target="tpu_custom_call" | custom-call | flops 14 | bytes 14 | tf_op jit(solution)/shard_map/pallas_call | solution.py:736
  46.6 8.2 %collective-permute-done.1.refs_5_ = bf16[112,768]{1,0:T(8,128)(2,1)S(1)} collective-permute-done((bf16[112,768]{1,0:T(8,128)(2,1)}, bf16[112,768]{1,0:T(8,128)(2,1)S(1)}, u32[]{:S(2)}, u32[]{:S(2)}) %collective-permute-start.1) | collective-permute-done | bytes 172064 | tf_op jit(solution)/shard_map/ppermute | solution.py:842
  54.9 2.4 collective-permute-done.2.refs_6_
  59.5 11.4 %shard_map.238 = (bf16[416,768]{1,0:T(8,128)(2,1)}, bf16[416,2304]{1,0:T(8,128)(2,1)}, f32[416,128]{1,0:T(8,128)}, bf16[112,768]{1,0:T(8,128)(2,1)}, bf16[112,76...) custom-call(s32[2]{0:T(128)} %pad_add_fusion.refs_0_.refs_18_.place_ref.refs_16_, s32[8]{0:T(128)} %copy-done.63, ...), custom_call_target="tpu_custom_call" | custom-call | flops 9 | bytes 9 | tf_op jit(solution)/shard_map/pallas_call | solution.py:736
  72.9 5.9 %collective-permute-done.7.refs_3_ = bf16[112,768]{1,0:T(8,128)(2,1)S(1)} collective-permute-done((bf16[112,768]{1,0:T(8,128)(2,1)}, bf16[112,768]{1,0:T(8,128)(2,1)S(1)}, u32[]{:S(2)}, u32[]{:S(2)}) %collective-permute-start.7) | collective-permute-done | bytes 172064 | tf_op jit(solution)/shard_map/ppermute | solution.py:842
  80.7 5.6 %collective-permute-done.9.refs_15_.refs_28_ = bf16[2,384,768]{2,1,0:T(8,128)(2,1)S(1)} collective-permute-done((bf16[2,384,768]{2,1,0:T(8,128)(2,1)S(1)}, bf16[2,384,768]{2,1,0:T(8,128)(2,1)S(1)}, u32[]{:S(2)}, u32[]{:S(2)}) %collective-permute-start.9) | collective-permute-done | bytes 1179680 | tf_op jit(solution)/shard_map/ppermute | solution.py:963
  91.8 25.8 %shard_map.239 = (bf16[400,768]{1,0:T(8,128)(2,1)}, f32[400,768]{1,0:T(8,128)}, bf16[400,768]{1,0:T(8,128)(2,1)}, bf16[400,3072]{1,0:T(8,128)(2,1)}, bf16[400,30...) custom-call(s32[2]{0:T(128)} %pad_add_fusion.refs_0_.refs_18_.place_, ...), custom_call_target="tpu_custom_call" | custom-call | flops 29 | bytes 29 | tf_op jit(solution)/shard_map/pallas_call | solution.py:736
  121.3 5.5 %collective-permute-done.14.refs_5_ = bf16[112,768]{1,0:T(8,128)(2,1)S(1)} collective-permute-done((bf16[112,768]{1,0:T(8,128)(2,1)}, bf16[112,768]{1,0:T(8,128)(2,1)S(1)}, u32[]{:S(2)}, u32[]{:S(2)}) %collective-permute-start.14) | collective-permute-done | bytes 172064 | tf_op jit(solution)/shard_map/ppermute | solution.py:842
  126.9 2.9 collective-permute-done.15.refs_6_
  130.4 10.9 %shard_map.240 = (bf16[416,768]{1,0:T(8,128)(2,1)}, bf16[416,2304]{1,0:T(8,128)(2,1)}, f32[416,128]{1,0:T(8,128)}, bf16[112,768]{1,0:T(8,128)(2,1)}, bf16[112,76...) custom-call(s32[2]{0:T(128)} %pad_add_fusion.refs_0_.refs_18_.place_ref.refs_16_, s32[8]{0:T(128)} %copy-done.63, ...), custom_call_target="tpu_custom_call" | custom-call | flops 9 | bytes 9 | tf_op jit(solution)/shard_map/pallas_call | solution.py:736
  143.5 5.9 %collective-permute-done.17.refs_3_ = bf16[112,768]{1,0:T(8,128)(2,1)S(1)} collective-permute-done((bf16[112,768]{1,0:T(8,128)(2,1)}, bf16[112,768]{1,0:T(8,128)(2,1)S(1)}, u32[]{:S(2)}, u32[]{:S(2)}) %collective-permute-start.17) | collective-permute-done | bytes 172064 | tf_op jit(solution)/shard_map/ppermute | solution.py:842
  152.2 2.4 collective-permute-done.20.refs_16_.refs_30_
  157.3 28.3 %shard_map.241 = (bf16[400,768]{1,0:T(8,128)(2,1)}, f32[400,768]{1,0:T(8,128)}, bf16[400,768]{1,0:T(8,128)(2,1)}, bf16[400,3072]{1,0:T(8,128)(2,1)}, bf16[400,30...) custom-call(s32[2]{0:T(128)} %pad_add_fusion.refs_0_.refs_18_.place_, ...), custom_call_target="tpu_custom_call" | custom-call | flops 38 | bytes 38 | tf_op jit(solution)/shard_map/pallas_call | solution.py:736
  187.6 12.2 %shard_map.242 = bf16[4,768,1536]{2,1,0:T(8,128)(2,1)} custom-call(s32[2]{0:T(128)} %pad_add_fusion.refs_0_.refs_18_.place_ref.refs_16_, bf16[400,768]{1,0:T(8,128)(2,1)} %get-tuple-element.416.refs_0_, bf16[400,768]{1,0:T(8,128)(2,1)} %get-tuple-element.417.refs_1_, bf16[400,3072]{1,0:T(8,128)(2,1)} %get-tuple-element.418.refs_2_, ...), custom_call_target="tpu_custom_call" | custom-call | flops 10 | bytes 10 | tf_op jit(solution)/shard_map/pallas_call | solution.py:819
  201.1 13.1 %shard_map.243 = (bf16[416,2304]{1,0:T(8,128)(2,1)}, bf16[112,768]{1,0:T(8,128)(2,1)}, bf16[112,768]{1,0:T(8,128)(2,1)}, bf16[112,768]{1,0:T(8,128)(2,1)}, bf16[112,768]{1,0:T(8,128)(2,1)}) custom-call(bf16[112,768]{1,0:T(8,128)(2,1)} %get-tuple-element.424.refs_0_, bf16[112,768]{1,0:T(8,128)(2,1)} %copy-done.57, bf16[112,768]{1,0:T(8,128)(2,1)} %copy-done.58, ...), custom_call_target="tpu_custom_call" | custom-call | flops 29 | bytes 29 | tf_op jit(solution)/shard_map/pallas_call | solution.py:736
  217.0 7.4 %shard_map.244 = (bf16[768,1536]{1,0:T(8,128)(2,1)}, bf16[768,1536]{1,0:T(8,128)(2,1)}) custom-call(s32[2]{0:T(128)} %pad_add_fusion.refs_0_.refs_18_.place_ref.refs_16_, bf16[416,768]{1,0:T(8,128)(2,1)} %get-tuple-element.439.refs_0_, bf16[400,768]{1,0:T(8,128)(2,1)} %get-tuple-element.440.refs_1_, bf16[416,2304]{1,0:T(8,128)(2,1)} %get-tuple-element.441.refs_2_, ...), custom_call_target="tpu_custom_call" | custom-call | flops 8 | bytes 8 | tf_op jit(solution)/shard_map/pallas_call | solution.py:819
  225.2 33.1 %shard_map.245 = (bf16[400,768]{1,0:T(8,128)(2,1)}, bf16[400,768]{1,0:T(8,128)(2,1)}, bf16[400,2304]{1,0:T(8,128)(2,1)}, f32[400,768]{1,0:T(8,128)}, f32[8,768]{...) custom-call(s32[2]{0:T(128)} %pad_add_fusion.refs_0_.refs_18_.place_, ...), custom_call_target="tpu_custom_call" | custom-call | flops 37 | bytes 37 | tf_op jit(solution)/shard_map/pallas_call | solution.py:736
  258.4 8.6 %shard_map.246 = (bf16[768,1920]{1,0:T(8,128)(2,1)}, bf16[768,1920]{1,0:T(8,128)(2,1)}) custom-call(s32[2]{0:T(128)} %pad_add_fusion.refs_0_.refs_18_.place_ref.refs_16_, bf16[400,768]{1,0:T(8,128)(2,1)} %get-tuple-element.479.refs_0_, bf16[400,768]{1,0:T(8,128)(2,1)} %get-tuple-element.480.refs_1_, bf16[400,768]{1,0:T(8,128)(2,1)} %get-tuple-element.481.refs_2_, ...), custom_call_target="tpu_custom_call" | custom-call | flops 9 | bytes 9 | tf_op jit(solution)/shard_map/pallas_call | solution.py:819
  269.7 12.4 %shard_map.247 = (bf16[2,768,1536]{2,1,0:T(8,128)(2,1)}, bf16[2,768,1536]{2,1,0:T(8,128)(2,1)}) custom-call(s32[2]{0:T(128)} %pad_add_fusion.refs_0_.refs_18_.place_ref.refs_16_, bf16[400,768]{1,0:T(8,128)(2,1)} %get-tuple-element.500.refs_0_, bf16[400,768]{1,0:T(8,128)(2,1)} %get-tuple-element.501.refs_1_, bf16[400,3072]{1,0:T(8,128)(2,1)} %get-tuple-element.502.refs_2_, ...), custom_call_target="tpu_custom_call" | custom-call | flops 10 | bytes 10 | tf_op jit(solution)/shard_map/pallas_call | solution.py:819
  282.2 2.5 collective-permute-done.30.refs_3_
  285.6 2.7 add.260
  288.4 2.7 add.259
  299.1 13.3 %shard_map.248 = (bf16[416,2304]{1,0:T(8,128)(2,1)}, bf16[112,768]{1,0:T(8,128)(2,1)}, bf16[112,768]{1,0:T(8,128)(2,1)}, bf16[112,768]{1,0:T(8,128)(2,1)}, bf16[112,768]{1,0:T(8,128)(2,1)}) custom-call(bf16[112,768]{1,0:T(8,128)(2,1)} %get-tuple-element.505.refs_0_, bf16[112,768]{1,0:T(8,128)(2,1)} %copy-done.54, bf16[112,768]{1,0:T(8,128)(2,1)} %copy-done.55, ...), custom_call_target="tpu_custom_call" | custom-call | flops 29 | bytes 29 | tf_op jit(solution)/shard_map/pallas_call | solution.py:736
  312.4 7.6 %shard_map.249 = (bf16[768,1536]{1,0:T(8,128)(2,1)}, bf16[768,1536]{1,0:T(8,128)(2,1)}) custom-call(s32[2]{0:T(128)} %pad_add_fusion.refs_0_.refs_18_.place_ref.refs_16_, bf16[416,768]{1,0:T(8,128)(2,1)} %get-tuple-element.529.refs_0_, bf16[400,768]{1,0:T(8,128)(2,1)} %get-tuple-element.530.refs_1_, bf16[416,2304]{1,0:T(8,128)(2,1)} %get-tuple-element.531.refs_2_, ...), custom_call_target="tpu_custom_call" | custom-call | flops 8 | bytes 8 | tf_op jit(solution)/shard_map/pallas_call | solution.py:819
  322.3 3.9 add.263
  330.2 7.2 %collective-permute-done.38 = bf16[2,2,2,48,1792]{4,3,1,0,2:T(8,128)(2,1)} collective-permute-done((bf16[2,2,2,48,1792]{4,3,1,0,2:T(8,128)(2,1)}, bf16[2,2,2,48,1792]{4,3,1,0,2:T(8,128)(2,1)}, u32[]{:S(2)}, u32[]{:S(2)}) %collective-permute-start.38) | collective-permute-done | bytes 1376288 | tf_op jit(solution)/shard_map/ppermute | solution.py:963
  343.8 2.5 collective-permute-start.42
  349.2 19.5 %shard_map.250 = (bf16[400,768]{1,0:T(8,128)(2,1)}, bf16[400,768]{1,0:T(8,128)(2,1)}, bf16[400,2304]{1,0:T(8,128)(2,1)}, f32[400,768]{1,0:T(8,128)}, f32[8,768]{1,0:T(8,128)}) custom-call(s32[2]{0:T(128)} %pad_add_fusion.refs_0_.refs_18_.place_ref.refs_16_, bf16[112,768]{1,0:T(8,128)(2,1)} %get-tuple-element.536.refs_1_, bf16[112,768]{1,0:T(8,128)(2,1)} %copy-done.60, ...), custom_call_target="tpu_custom_call" | custom-call | flops 14 | bytes 14 | tf_op jit(solution)/shard_map/pallas_call | solution.py:736
  368.7 8.6 %shard_map.251 = (bf16[768,1920]{1,0:T(8,128)(2,1)}, bf16[768,1920]{1,0:T(8,128)(2,1)}) custom-call(s32[2]{0:T(128)} %pad_add_fusion.refs_0_.refs_18_.place_ref.refs_16_, bf16[400,768]{1,0:T(8,128)(2,1)} %get-tuple-element.544.refs_0_, bf16[400,768]{1,0:T(8,128)(2,1)} %get-tuple-element.545.refs_1_, bf16[400,768]{1,0:T(8,128)(2,1)} %get-tuple-element.546.refs_2_, ...), custom_call_target="tpu_custom_call" | custom-call | flops 9 | bytes 9 | tf_op jit(solution)/shard_map/pallas_call | solution.py:819
  378.7 12.1 %collective-permute-done.39 = bf16[2,2,48,1664]{3,2,1,0:T(8,128)(2,1)} collective-permute-done((bf16[2,2,48,1664]{3,2,1,0:T(8,128)(2,1)}, bf16[2,2,48,1664]{3,2,1,0:T(8,128)(2,1)}, u32[]{:S(2)}, u32[]{:S(2)}) %collective-permute-start.39) | collective-permute-done | bytes 639008 | tf_op jit(solution)/shard_map/ppermute | solution.py:963
  390.9 3.0 add.274
  411.0 9.7 %collective-permute-done.45 = bf16[2,2,96,768]{3,2,1,0:T(8,128)(2,1)} collective-permute-done((bf16[2,2,96,768]{3,2,1,0:T(8,128)(2,1)}, bf16[2,2,96,768]{3,2,1,0:T(8,128)(2,1)}, u32[]{:S(2)}, u32[]{:S(2)}) %collective-permute-start.45) | collective-permute-done | bytes 589856 | tf_op jit(solution)/shard_map/ppermute | solution.py:963
  422.2 2.6 collective-permute-done.44
  424.8 3.7 add.280
  445.7 2.7 collective-permute-start.52
  449.6 12.0 %collective-permute-done.49 = bf16[2,2,2,48,896]{4,3,1,0,2:T(8,128)(2,1)} collective-permute-done((bf16[2,2,2,48,896]{4,3,1,0,2:T(8,128)(2,1)}, bf16[2,2,2,48,896]{4,3,1,0,2:T(8,128)(2,1)}, u32[]{:S(2)}, u32[]{:S(2)}) %collective-permute-start.49) | collective-permute-done | bytes 688160 | tf_op jit(solution)/shard_map/ppermute | solution.py:963
  466.8 3.1 collective-permute-done.53
  477.2 5.3 collective-permute-done.55
  482.5 2.7 collective-permute-done.56
  485.2 8.0 %collective-permute-done.54 = bf16[2,2,48,1536]{3,2,1,0:T(8,128)(2,1)S(1)} collective-permute-done((bf16[2,2,48,1536]{3,2,1,0:T(8,128)(2,1)S(1)}, bf16[2,2,48,1536]{3,2,1,0:T(8,128)(2,1)S(1)}, u32[]{:S(2)}, u32[]{:S(2)}) %collective-permute-start.54) | collective-permute-done | bytes 589856 | tf_op jit(solution)/shard_map/ppermute | solution.py:963
  500.1 3.6 collective-permute-done.60
  503.7 5.4 collective-permute-done.61
  514.1 8.5 %collective-permute-done.64 = bf16[48,1536]{1,0:T(8,128)(2,1)S(1)} collective-permute-done((bf16[48,1536]{1,0:T(8,128)(2,1)S(1)}, bf16[48,1536]{1,0:T(8,128)(2,1)S(1)}, u32[]{:S(2)}, u32[]{:S(2)}) %collective-permute-start.64) | collective-permute-done | bytes 147488 | tf_op jit(solution)/shard_map/ppermute | solution.py:963
  522.6 3.3 collective-permute-done.65
  528.6 4.4 collective-permute-done.67
  533.0 2.4 collective-permute-done.68
  (412 shorter events, 149.1 us)
Async XLA Ops:
  7.2 278.4 %reduce-scatter.3.cloned.1.call-start = ((), (), s32[]{:S(2)}) async-start(), calls=%async_computation.2 | async-start | bytes 11796480 | tf_op jit(solution)/shard_map/reduce_scatter | solution.py:1287
  20.7 36.5 %collective-permute-start.4 = (bf16[2,768,768]{2,1,0:T(8,128)(2,1)S(1)}, bf16[2,768,768]{2,1,0:T(8,128)(2,1)}, u32[]{:S(2)}, u32[]{:S(2)}) collective-permute-start(bf16[2,768,768]{2,1,0:T(8,128)(2,1)S(1)} %copy-done), channel_id=1, source_target_pairs={{0,1},{1,0},{2,3},{3,2},{4,5},{5,4},{6,7},{7,6},{8,9},{9,8},{10,11... | collective-permute-start | bytes 7077896 | tf_op jit(solution)/shard_map/ppermute | solution.py:963
  21.2 36.1 %collective-permute-start.5 = (bf16[2,768,768]{2,1,0:T(8,128)(2,1)}, bf16[2,768,768]{2,1,0:T(8,128)(2,1)}, u32[]{:S(2)}, u32[]{:S(2)}) collective-permute-start(bf16[2,768,768]{2,1,0:T(8,128)(2,1)} %refs_24_.5), channel_id=1, source_target_pairs={{0,1},{1,0},{2,3},{3,2},{4,5},{5,4},{6,7},{7,6},{8,9},{9,8},{10,11... | collective-permute-start | bytes 7077896 | tf_op jit(solution)/shard_map/ppermute | solution.py:963
  21.3 36.0 %collective-permute-start.3 = (bf16[2,384,768]{2,1,0:T(8,128)(2,1)}, bf16[2,384,768]{2,1,0:T(8,128)(2,1)S(1)}, u32[]{:S(2)}, u32[]{:S(2)}) collective-permute-start(bf16[2,384,768]{2,1,0:T(8,128)(2,1)} %pad_maximum_fusion.1), channel_id=1, source_target_pairs={{0,2},{1,3},{2,0},{3,1},{4,6},{5,7},{6,4},{7,5},{8,10},{9,11},{10,... | collective-permute-start | bytes 3538952 | tf_op jit(solution)/shard_map/ppermute | solution.py:963
  43.6 11.3 %collective-permute-start.1 = (bf16[112,768]{1,0:T(8,128)(2,1)}, bf16[112,768]{1,0:T(8,128)(2,1)S(1)}, u32[]{:S(2)}, u32[]{:S(2)}) collective-permute-start(bf16[112,768]{1,0:T(8,128)(2,1)} %get-tuple-element.334), channel_id=1, source_target_pairs={{0,2},{1,3},{2,0},{3,1},{4,6},{5,7},{6,4},{7,5},{8,10},{9,11},{10,... | collective-permute-start | bytes 516104 | tf_op jit(solution)/shard_map/ppermute | solution.py:842
  45.2 12.1 %collective-permute-start.2 = (bf16[112,768]{1,0:T(8,128)(2,1)}, bf16[112,768]{1,0:T(8,128)(2,1)S(1)}, u32[]{:S(2)}, u32[]{:S(2)}) collective-permute-start(bf16[112,768]{1,0:T(8,128)(2,1)} %get-tuple-element.335), channel_id=1, source_target_pairs={{0,3},{1,2},{2,1},{3,0},{4,7},{5,6},{6,5},{7,4},{8,11},{9,10},{10,... | collective-permute-start | bytes 516104 | tf_op jit(solution)/shard_map/ppermute | solution.py:842
  57.9 28.4 %collective-permute-start.9 = (bf16[2,384,768]{2,1,0:T(8,128)(2,1)S(1)}, bf16[2,384,768]{2,1,0:T(8,128)(2,1)S(1)}, u32[]{:S(2)}, u32[]{:S(2)}) collective-permute-start(bf16[2,384,768]{2,1,0:T(8,128)(2,1)S(1)} %collective-permute-done.3.refs_14_.refs_27_), channel_id=1, source_target_pairs={{0,4},{4,0},{8,12},{12,8},{16,20},{20,16},{24,28},{28,24},{1,5},{5... | collective-permute-start | bytes 3538952 | tf_op jit(solution)/shard_map/ppermute | solution.py:963
  86.8 30.8 %collective-permute-start.12 = (bf16[2,384,768]{2,1,0:T(8,128)(2,1)}, bf16[2,384,768]{2,1,0:T(8,128)(2,1)S(1)}, u32[]{:S(2)}, u32[]{:S(2)}) collective-permute-start(bf16[2,384,768]{2,1,0:T(8,128)(2,1)} %pad_maximum_fusion.2), channel_id=1, source_target_pairs={{0,2},{1,3},{2,0},{3,1},{4,6},{5,7},{6,4},{7,5},{8,10},{9,11},{10,... | collective-permute-start | bytes 3538952 | tf_op jit(solution)/shard_map/ppermute | solution.py:963
  117.7 33.7 %collective-permute-start.19 = (bf16[2,384,768]{2,1,0:T(8,128)(2,1)S(1)}, bf16[2,384,768]{2,1,0:T(8,128)(2,1)S(1)}, u32[]{:S(2)}, u32[]{:S(2)}) collective-permute-start(bf16[2,384,768]{2,1,0:T(8,128)(2,1)S(1)} %collective-permute-done.12.refs_14_.refs_28_), channel_id=1, source_target_pairs={{0,4},{4,0},{8,12},{12,8},{16,20},{20,16},{24,28},{28,24},{1,5},{5... | collective-permute-start | bytes 3538952 | tf_op jit(solution)/shard_map/ppermute | solution.py:963
  185.7 14.2 %collective-permute-start.22 = (bf16[112,768]{1,0:T(8,128)(2,1)}, bf16[112,768]{1,0:T(8,128)(2,1)S(1)}, u32[]{:S(2)}, u32[]{:S(2)}) collective-permute-start(bf16[112,768]{1,0:T(8,128)(2,1)} %get-tuple-element.413), channel_id=1, source_target_pairs={{0,1},{1,0},{2,3},{3,2},{4,5},{5,4},{6,7},{7,6},{8,9},{9,8},{10,11... | collective-permute-start | bytes 516104 | tf_op jit(solution)/shard_map/ppermute | solution.py:842
  186.1 13.7 %collective-permute-start.23 = (bf16[112,768]{1,0:T(8,128)(2,1)}, bf16[112,768]{1,0:T(8,128)(2,1)S(1)}, u32[]{:S(2)}, u32[]{:S(2)}) collective-permute-start(bf16[112,768]{1,0:T(8,128)(2,1)} %get-tuple-element.414), channel_id=1, source_target_pairs={{0,2},{1,3},{2,0},{3,1},{4,6},{5,7},{6,4},{7,5},{8,10},{9,11},{10,... | collective-permute-start | bytes 516104 | tf_op jit(solution)/shard_map/ppermute | solution.py:842
  187.6 12.2 %collective-permute-start.24 = (bf16[112,768]{1,0:T(8,128)(2,1)}, bf16[112,768]{1,0:T(8,128)(2,1)S(1)}, u32[]{:S(2)}, u32[]{:S(2)}) collective-permute-start(bf16[112,768]{1,0:T(8,128)(2,1)} %get-tuple-element.415), channel_id=1, source_target_pairs={{0,3},{1,2},{2,1},{3,0},{4,7},{5,6},{6,5},{7,4},{8,11},{9,10},{10,... | collective-permute-start | bytes 516104 | tf_op jit(solution)/shard_map/ppermute | solution.py:842
  200.6 178.0 %reduce-scatter.5.cloned.1.call-start = ((), (), s32[]{:S(2)}) async-start(), calls=%async_computation.3 | async-start | bytes 2654208 | tf_op jit(solution)/shard_map/reduce_scatter | solution.py:1281
  214.2 10.3 %collective-permute-start.25 = (bf16[112,768]{1,0:T(8,128)(2,1)}, bf16[112,768]{1,0:T(8,128)(2,1)S(1)}, u32[]{:S(2)}, u32[]{:S(2)}) collective-permute-start(bf16[112,768]{1,0:T(8,128)(2,1)} %get-tuple-element.432), channel_id=1, source_target_pairs={{0,1},{1,0},{2,3},{3,2},{4,5},{5,4},{6,7},{7,6},{8,9},{9,8},{10,11... | collective-permute-start | bytes 516104 | tf_op jit(solution)/shard_map/ppermute | solution.py:842
  267.0 18.6 %collective-permute-start.32 = (bf16[768,1920]{1,0:T(8,128)(2,1)}, bf16[768,1920]{1,0:T(8,128)(2,1)}, u32[]{:S(2)}, u32[]{:S(2)}) collective-permute-start(bf16[768,1920]{1,0:T(8,128)(2,1)} %get-tuple-element.487), channel_id=1, source_target_pairs={{0,1},{1,0},{2,3},{3,2},{4,5},{5,4},{6,7},{7,6},{8,9},{9,8},{10,11... | collective-permute-start | bytes 8847368 | tf_op jit(solution)/shard_map/ppermute | solution.py:963
  267.7 17.9 %collective-permute-start.31 = (bf16[768,1536]{1,0:T(8,128)(2,1)}, bf16[768,1536]{1,0:T(8,128)(2,1)}, u32[]{:S(2)}, u32[]{:S(2)}) collective-permute-start(bf16[768,1536]{1,0:T(8,128)(2,1)} %get-tuple-element.486), channel_id=1, source_target_pairs={{0,1},{1,0},{2,3},{3,2},{4,5},{5,4},{6,7},{7,6},{8,9},{9,8},{10,11... | collective-permute-start | bytes 7077896 | tf_op jit(solution)/shard_map/ppermute | solution.py:963
  267.8 14.3 %collective-permute-start.28 = (bf16[112,768]{1,0:T(8,128)(2,1)}, bf16[112,768]{1,0:T(8,128)(2,1)S(1)}, u32[]{:S(2)}, u32[]{:S(2)}) collective-permute-start(bf16[112,768]{1,0:T(8,128)(2,1)} %get-tuple-element.456), channel_id=1, source_target_pairs={{0,1},{1,0},{2,3},{3,2},{4,5},{5,4},{6,7},{7,6},{8,9},{9,8},{10,11... | collective-permute-start | bytes 516104 | tf_op jit(solution)/shard_map/ppermute | solution.py:842
  268.3 13.9 %collective-permute-start.29 = (bf16[112,768]{1,0:T(8,128)(2,1)}, bf16[112,768]{1,0:T(8,128)(2,1)S(1)}, u32[]{:S(2)}, u32[]{:S(2)}) collective-permute-start(bf16[112,768]{1,0:T(8,128)(2,1)} %get-tuple-element.457), channel_id=1, source_target_pairs={{0,2},{1,3},{2,0},{3,1},{4,6},{5,7},{6,4},{7,5},{8,10},{9,11},{10,... | collective-permute-start | bytes 516104 | tf_op jit(solution)/shard_map/ppermute | solution.py:842
  269.7 15.0 %collective-permute-start.30 = (bf16[112,768]{1,0:T(8,128)(2,1)}, bf16[112,768]{1,0:T(8,128)(2,1)S(1)}, u32[]{:S(2)}, u32[]{:S(2)}) collective-permute-start(bf16[112,768]{1,0:T(8,128)(2,1)} %get-tuple-element.458), channel_id=1, source_target_pairs={{0,3},{1,2},{2,1},{3,0},{4,7},{5,6},{6,5},{7,4},{8,11},{9,10},{10,... | collective-permute-start | bytes 516104 | tf_op jit(solution)/shard_map/ppermute | solution.py:842
  296.7 23.3 %collective-permute-start.33 = (bf16[2,768,1536]{2,1,0:T(8,128)(2,1)}, bf16[2,768,1536]{2,1,0:T(8,128)(2,1)}, u32[]{:S(2)}, u32[]{:S(2)}) collective-permute-start(bf16[2,768,1536]{2,1,0:T(8,128)(2,1)} %get-tuple-element.516), channel_id=1, source_target_pairs={{0,1},{1,0},{2,3},{3,2},{4,5},{5,4},{6,7},{7,6},{8,9},{9,8},{10,11... | collective-permute-start | bytes 14155784 | tf_op jit(solution)/shard_map/ppermute | solution.py:963
  296.7 40.8 %collective-permute-start.38 = (bf16[2,2,2,48,1792]{4,3,1,0,2:T(8,128)(2,1)}, bf16[2,2,2,48,1792]{4,3,1,0,2:T(8,128)(2,1)}, u32[]{:S(2)}, u32[]{:S(2)}) collective-permute-start(bf16[2,2,2,48,1792]{4,3,1,0,2:T(8,128)(2,1)} %bitcast.166), channel_id=1, source_target_pairs={{0,4},{4,0},{8,12},{12,8},{16,20},{20,16},{24,28},{28,24},{1,5},{5... | collective-permute-start | bytes 4128776 | tf_op jit(solution)/shard_map/ppermute | solution.py:963
  299.0 31.2 %collective-permute-start.37 = (bf16[2,2,2,48,1664]{4,3,1,0,2:T(8,128)(2,1)}, bf16[2,2,2,48,1664]{4,3,1,0,2:T(8,128)(2,1)}, u32[]{:S(2)}, u32[]{:S(2)}) collective-permute-start(bf16[2,2,2,48,1664]{4,3,1,0,2:T(8,128)(2,1)} %bitcast.167), channel_id=1, source_target_pairs={{0,2},{1,3},{2,0},{3,1},{4,6},{5,7},{6,4},{7,5},{8,10},{9,11},{10,... | collective-permute-start | bytes 3833864 | tf_op jit(solution)/shard_map/ppermute | solution.py:963
  320.0 17.5 %collective-permute-start.34 = (bf16[112,768]{1,0:T(8,128)(2,1)S(1)}, bf16[112,768]{1,0:T(8,128)(2,1)S(1)}, u32[]{:S(2)}, u32[]{:S(2)}) collective-permute-start(bf16[112,768]{1,0:T(8,128)(2,1)S(1)} %copy-done.72), channel_id=1, source_target_pairs={{0,1},{1,0},{2,3},{3,2},{4,5},{5,4},{6,7},{7,6},{8,9},{9,8},{10,11... | collective-permute-start | bytes 516104 | tf_op jit(solution)/shard_map/ppermute | solution.py:842
  320.3 17.2 %collective-permute-start.35 = (bf16[112,768]{1,0:T(8,128)(2,1)S(1)}, bf16[112,768]{1,0:T(8,128)(2,1)S(1)}, u32[]{:S(2)}, u32[]{:S(2)}) collective-permute-start(bf16[112,768]{1,0:T(8,128)(2,1)S(1)} %copy-done.71), channel_id=1, source_target_pairs={{0,2},{1,3},{2,0},{3,1},{4,6},{5,7},{6,4},{7,5},{8,10},{9,11},{10,... | collective-permute-start | bytes 516104 | tf_op jit(solution)/shard_map/ppermute | solution.py:842
  322.2 15.3 %collective-permute-start.36 = (bf16[112,768]{1,0:T(8,128)(2,1)S(1)}, bf16[112,768]{1,0:T(8,128)(2,1)S(1)}, u32[]{:S(2)}, u32[]{:S(2)}) collective-permute-start(bf16[112,768]{1,0:T(8,128)(2,1)S(1)} %copy-done.70), channel_id=1, source_target_pairs={{0,3},{1,2},{2,1},{3,0},{4,7},{5,6},{6,5},{7,4},{8,11},{9,10},{10,... | collective-permute-start | bytes 516104 | tf_op jit(solution)/shard_map/ppermute | solution.py:842
  343.8 47.1 %collective-permute-start.43 = (bf16[768,1536]{1,0:T(8,128)(2,1)}, bf16[768,1536]{1,0:T(8,128)(2,1)}, u32[]{:S(2)}, u32[]{:S(2)}) collective-permute-start(bf16[768,1536]{1,0:T(8,128)(2,1)} %get-tuple-element.558), channel_id=1, source_target_pairs={{0,1},{1,0},{2,3},{3,2},{4,5},{5,4},{6,7},{7,6},{8,9},{9,8},{10,11... | collective-permute-start | bytes 7077896 | tf_op jit(solution)/shard_map/ppermute | solution.py:963
  343.8 47.1 %collective-permute-start.41 = (bf16[2,2,2,96,768]{4,3,2,1,0:T(8,128)(2,1)}, bf16[2,2,2,96,768]{4,3,2,1,0:T(8,128)(2,1)S(1)}, u32[]{:S(2)}, u32[]{:S(2)}) collective-permute-start(bf16[2,2,2,96,768]{4,3,2,1,0:T(8,128)(2,1)} %slice_bitcast_fusion.1), channel_id=1, source_target_pairs={{0,2},{1,3},{2,0},{3,1},{4,6},{5,7},{6,4},{7,5},{8,10},{9,11},{10,... | collective-permute-start | bytes 3538952 | tf_op jit(solution)/shard_map/ppermute | solution.py:963
  343.8 47.1 %collective-permute-start.42 = (bf16[2,2,2,96,768]{4,3,2,1,0:T(8,128)(2,1)}, bf16[2,2,2,96,768]{4,3,2,1,0:T(8,128)(2,1)}, u32[]{:S(2)}, u32[]{:S(2)}) collective-permute-start(bf16[2,2,2,96,768]{4,3,2,1,0:T(8,128)(2,1)} %dynamic-slice_bitcast_fusion), channel_id=1, source_target_pairs={{0,4},{4,0},{8,12},{12,8},{16,20},{20,16},{24,28},{28,24},{1,5},{5... | collective-permute-start | bytes 3538952 | tf_op jit(solution)/shard_map/ppermute | solution.py:963
  346.3 44.6 %collective-permute-start.40 = (bf16[2,2,48,1792]{3,2,1,0:T(8,128)(2,1)}, bf16[2,2,48,1792]{3,2,1,0:T(8,128)(2,1)}, u32[]{:S(2)}, u32[]{:S(2)}) collective-permute-start(bf16[2,2,48,1792]{3,2,1,0:T(8,128)(2,1)} %dynamic-slice_bitcast_fusion.1), channel_id=1, source_target_pairs={{0,2},{1,3},{2,0},{3,1},{4,6},{5,7},{6,4},{7,5},{8,10},{9,11},{10,... | collective-permute-start | bytes 2064392 | tf_op jit(solution)/shard_map/ppermute | solution.py:963
  348.4 42.4 %collective-permute-start.39 = (bf16[2,2,48,1664]{3,2,1,0:T(8,128)(2,1)}, bf16[2,2,48,1664]{3,2,1,0:T(8,128)(2,1)}, u32[]{:S(2)}, u32[]{:S(2)}) collective-permute-start(bf16[2,2,48,1664]{3,2,1,0:T(8,128)(2,1)} %dynamic-slice_bitcast_fusion.2), channel_id=1, source_target_pairs={{0,4},{4,0},{8,12},{12,8},{16,20},{20,16},{24,28},{28,24},{1,5},{5... | collective-permute-start | bytes 1916936 | tf_op jit(solution)/shard_map/ppermute | solution.py:963
  390.8 31.4 %collective-permute-start.47 = (bf16[768,1920]{1,0:T(8,128)(2,1)}, bf16[768,1920]{1,0:T(8,128)(2,1)}, u32[]{:S(2)}, u32[]{:S(2)}) collective-permute-start(bf16[768,1920]{1,0:T(8,128)(2,1)} %get-tuple-element.570), channel_id=1, source_target_pairs={{0,1},{1,0},{2,3},{3,2},{4,5},{5,4},{6,7},{7,6},{8,9},{9,8},{10,11... | collective-permute-start | bytes 8847368 | tf_op jit(solution)/shard_map/ppermute | solution.py:963
  404.7 16.0 %collective-permute-start.45 = (bf16[2,2,96,768]{3,2,1,0:T(8,128)(2,1)}, bf16[2,2,96,768]{3,2,1,0:T(8,128)(2,1)}, u32[]{:S(2)}, u32[]{:S(2)}) collective-permute-start(bf16[2,2,96,768]{3,2,1,0:T(8,128)(2,1)} %dynamic-slice_bitcast_fusion.4), channel_id=1, source_target_pairs={{0,4},{4,0},{8,12},{12,8},{16,20},{20,16},{24,28},{28,24},{1,5},{5... | collective-permute-start | bytes 1769480 | tf_op jit(solution)/shard_map/ppermute | solution.py:963
  405.8 16.4 %collective-permute-start.46 = (bf16[2,2,96,768]{3,2,1,0:T(8,128)(2,1)}, bf16[2,2,96,768]{3,2,1,0:T(8,128)(2,1)S(1)}, u32[]{:S(2)}, u32[]{:S(2)}) collective-permute-start(bf16[2,2,96,768]{3,2,1,0:T(8,128)(2,1)} %slice_bitcast_fusion.3), channel_id=1, source_target_pairs={{0,2},{1,3},{2,0},{3,1},{4,6},{5,7},{6,4},{7,5},{8,10},{9,11},{10,... | collective-permute-start | bytes 1769480 | tf_op jit(solution)/shard_map/ppermute | solution.py:963
  407.6 17.2 %collective-permute-start.44 = (bf16[2,48,3456]{2,1,0:T(8,128)(2,1)S(1)}, bf16[2,48,3456]{2,1,0:T(8,128)(2,1)S(1)}, u32[]{:S(2)}, u32[]{:S(2)}) collective-permute-start(bf16[2,48,3456]{2,1,0:T(8,128)(2,1)S(1)} %fusion.5), channel_id=1, source_target_pairs={{0,8},{4,12},{8,0},{12,4},{16,24},{20,28},{24,16},{28,20},{1,9},{5... | collective-permute-start | bytes 1990664 | tf_op jit(solution)/shard_map/ppermute | solution.py:963
  410.7 38.9 %collective-permute-start.48 = (bf16[2,2,2,48,1536]{4,3,1,0,2:T(8,128)(2,1)}, bf16[2,2,2,48,1536]{4,3,1,0,2:T(8,128)(2,1)}, u32[]{:S(2)}, u32[]{:S(2)}) collective-permute-start(bf16[2,2,2,48,1536]{4,3,1,0,2:T(8,128)(2,1)} %bitcast.168), channel_id=1, source_target_pairs={{0,2},{1,3},{2,0},{3,1},{4,6},{5,7},{6,4},{7,5},{8,10},{9,11},{10,... | collective-permute-start | bytes 3538952 | tf_op jit(solution)/shard_map/ppermute | solution.py:963
  437.4 24.2 %collective-permute-start.50 = (bf16[2,2,2,48,1024]{4,3,1,0,2:T(8,128)(2,1)}, bf16[2,2,2,48,1024]{4,3,1,0,2:T(8,128)(2,1)}, u32[]{:S(2)}, u32[]{:S(2)}) collective-permute-start(bf16[2,2,2,48,1024]{4,3,1,0,2:T(8,128)(2,1)} %bitcast.169), channel_id=1, source_target_pairs={{0,4},{4,0},{8,12},{12,8},{16,20},{20,16},{24,28},{28,24},{1,5},{5... | collective-permute-start | bytes 2359304 | tf_op jit(solution)/shard_map/ppermute | solution.py:963
  437.8 23.8 %collective-permute-start.49 = (bf16[2,2,2,48,896]{4,3,1,0,2:T(8,128)(2,1)}, bf16[2,2,2,48,896]{4,3,1,0,2:T(8,128)(2,1)}, u32[]{:S(2)}, u32[]{:S(2)}) collective-permute-start(bf16[2,2,2,48,896]{4,3,1,0,2:T(8,128)(2,1)} %bitcast.170), channel_id=1, source_target_pairs={{0,2},{1,3},{2,0},{3,1},{4,6},{5,7},{6,4},{7,5},{8,10},{9,11},{10,... | collective-permute-start | bytes 2064392 | tf_op jit(solution)/shard_map/ppermute | solution.py:963
  445.7 21.1 %collective-permute-start.52 = (bf16[48,3456]{1,0:T(8,128)(2,1)S(1)}, bf16[48,3456]{1,0:T(8,128)(2,1)S(1)}, u32[]{:S(2)}, u32[]{:S(2)}) collective-permute-start(bf16[48,3456]{1,0:T(8,128)(2,1)S(1)} %copy-done.38), channel_id=1, source_target_pairs={{0,16},{4,20},{8,24},{12,28},{16,0},{20,4},{24,8},{28,12},{1,17},{... | collective-permute-start | bytes 995336 | tf_op jit(solution)/shard_map/ppermute | solution.py:963
  448.4 21.4 %collective-permute-start.53 = (bf16[2,96,1536]{2,1,0:T(8,128)(2,1)S(1)}, bf16[2,96,1536]{2,1,0:T(8,128)(2,1)S(1)}, u32[]{:S(2)}, u32[]{:S(2)}) collective-permute-start(bf16[2,96,1536]{2,1,0:T(8,128)(2,1)S(1)} %copy-done.37), channel_id=1, source_target_pairs={{0,8},{4,12},{8,0},{12,4},{16,24},{20,28},{24,16},{28,20},{1,9},{5... | collective-permute-start | bytes 1769480 | tf_op jit(solution)/shard_map/ppermute | solution.py:963
  471.5 11.0 %collective-permute-start.55 = (bf16[2,2,48,896]{3,2,1,0:T(8,128)(2,1)S(1)}, bf16[2,2,48,896]{3,2,1,0:T(8,128)(2,1)S(1)}, u32[]{:S(2)}, u32[]{:S(2)}) collective-permute-start(bf16[2,2,48,896]{3,2,1,0:T(8,128)(2,1)S(1)} %dynamic-slice_bitcast_fusion.6), channel_id=1, source_target_pairs={{0,4},{4,0},{8,12},{12,8},{16,20},{20,16},{24,28},{28,24},{1,5},{5... | collective-permute-start | bytes 1032200 | tf_op jit(solution)/shard_map/ppermute | solution.py:963
  473.2 12.1 %collective-permute-start.56 = (bf16[2,2,48,1024]{3,2,1,0:T(8,128)(2,1)S(1)}, bf16[2,2,48,1024]{3,2,1,0:T(8,128)(2,1)S(1)}, u32[]{:S(2)}, u32[]{:S(2)}) collective-permute-start(bf16[2,2,48,1024]{3,2,1,0:T(8,128)(2,1)S(1)} %dynamic-slice_bitcast_fusion.5), channel_id=1, source_target_pairs={{0,2},{1,3},{2,0},{3,1},{4,6},{5,7},{6,4},{7,5},{8,10},{9,11},{10,... | collective-permute-start | bytes 1179656 | tf_op jit(solution)/shard_map/ppermute | solution.py:963
  473.5 19.8 %collective-permute-start.54 = (bf16[2,2,48,1536]{3,2,1,0:T(8,128)(2,1)S(1)}, bf16[2,2,48,1536]{3,2,1,0:T(8,128)(2,1)S(1)}, u32[]{:S(2)}, u32[]{:S(2)}) collective-permute-start(bf16[2,2,48,1536]{3,2,1,0:T(8,128)(2,1)S(1)} %dynamic-slice_bitcast_fusion.3), channel_id=1, source_target_pairs={{0,4},{4,0},{8,12},{12,8},{16,20},{20,16},{24,28},{28,24},{1,5},{5... | collective-permute-start | bytes 1769480 | tf_op jit(solution)/shard_map/ppermute | solution.py:963
  474.2 19.4 %collective-permute-start.59 = (bf16[96,1536]{1,0:T(8,128)(2,1)S(1)}, bf16[96,1536]{1,0:T(8,128)(2,1)S(1)}, u32[]{:S(2)}, u32[]{:S(2)}) collective-permute-start(bf16[96,1536]{1,0:T(8,128)(2,1)S(1)} %dynamic-slice_bitcast_fusion.9), channel_id=1, source_target_pairs={{0,16},{4,20},{8,24},{12,28},{16,0},{20,4},{24,8},{28,12},{1,17},{... | collective-permute-start | bytes 884744 | tf_op jit(solution)/shard_map/ppermute | solution.py:963
  475.5 18.0 %collective-permute-start.58 = (bf16[48,3456]{1,0:T(8,128)(2,1)S(1)}, bf16[48,3456]{1,0:T(8,128)(2,1)S(1)}, u32[]{:S(2)}, u32[]{:S(2)}) collective-permute-start(bf16[48,3456]{1,0:T(8,128)(2,1)S(1)} %bitcast_add_fusion.12), channel_id=1, source_target_pairs={{0,2},{1,3},{2,0},{3,1},{4,6},{5,7},{6,4},{7,5},{8,10},{9,11},{10,... | collective-permute-start | bytes 995336 | tf_op jit(solution)/shard_map/ppermute | solution.py:963
  495.5 13.6 %collective-permute-start.61 = (bf16[2,48,1920]{2,1,0:T(8,128)(2,1)S(1)}, bf16[2,48,1920]{2,1,0:T(8,128)(2,1)S(1)}, u32[]{:S(2)}, u32[]{:S(2)}) collective-permute-start(bf16[2,48,1920]{2,1,0:T(8,128)(2,1)S(1)} %fusion.16), channel_id=1, source_target_pairs={{0,8},{4,12},{8,0},{12,4},{16,24},{20,28},{24,16},{28,20},{1,9},{5... | collective-permute-start | bytes 1105928 | tf_op jit(solution)/shard_map/ppermute | solution.py:963
  497.7 16.4 %collective-permute-start.63 = (bf16[96,3456]{1,0:T(8,128)(2,1)S(1)}, bf16[96,3456]{1,0:T(8,128)(2,1)S(1)}, u32[]{:S(2)}, u32[]{:S(2)}) collective-permute-start(bf16[96,3456]{1,0:T(8,128)(2,1)S(1)} %maximum_select_fusion), channel_id=1, source_target_pairs={{0,1},{1,0},{2,3},{3,2},{4,5},{5,4},{6,7},{7,6},{8,9},{9,8},{10,11... | collective-permute-start | bytes 1990664 | tf_op jit(solution)/shard_map/ppermute | solution.py:963
  511.1 11.5 %collective-permute-start.64 = (bf16[48,1536]{1,0:T(8,128)(2,1)S(1)}, bf16[48,1536]{1,0:T(8,128)(2,1)S(1)}, u32[]{:S(2)}, u32[]{:S(2)}) collective-permute-start(bf16[48,1536]{1,0:T(8,128)(2,1)S(1)} %dynamic-slice_bitcast_fusion.11), channel_id=1, source_target_pairs={{0,16},{4,20},{8,24},{12,28},{16,0},{20,4},{24,8},{28,12},{1,17},{... | collective-permute-start | bytes 442376 | tf_op jit(solution)/shard_map/ppermute | solution.py:963
  512.4 13.6 %collective-permute-start.65 = (bf16[48,1920]{1,0:T(8,128)(2,1)S(1)}, bf16[48,1920]{1,0:T(8,128)(2,1)S(1)}, u32[]{:S(2)}, u32[]{:S(2)}) collective-permute-start(bf16[48,1920]{1,0:T(8,128)(2,1)S(1)} %dynamic-slice_bitcast_fusion.10), channel_id=1, source_target_pairs={{0,16},{4,20},{8,24},{12,28},{16,0},{20,4},{24,8},{28,12},{1,17},{... | collective-permute-start | bytes 552968 | tf_op jit(solution)/shard_map/ppermute | solution.py:963
  (102 other events, 605.9 us)
Sparse Core Ops, SparseCore 0:
  200.1 85.5 reduce-scatter.2
  299.2 76.7 reduce-scatter.4

commit v5 on v4

--- a/solution.py
+++ b/solution.py
@@ -1191,7 +1191,6 @@
         )
 
     saved = []
-    grad_rows = rows_of(patch_cotangent, class_cotangent)
     time = call_steps(time_step(0, patch_rows))
     for layer in range(layers):
         pieces = time[6:10]
@@ -1206,7 +1205,11 @@
             core_shards = (arrived_here("up"), arrived_here("down"))
             first = arrived_here("x0")
             send("y0", first, by_y)
-            send("x1", both_matrices(hidden_up, hidden_down, 1, near), by_x)
+            arrived, later_near, cotangent = lax.optimization_barrier(
+                (arrived, near, patch_cotangent)
+            )
+            send("x1", both_matrices(hidden_up, hidden_down, 1, later_near), by_x)
+            grad_rows = rows_of(cotangent, class_cotangent)
         arrived = flights.leave(arrived)
         space = call(
             partial(space_forward, dims, layer),

time: 561 us -> 562 us (level)
    unnamed x158 -> x153, local copies, waits for them, and re-layouts: 18.4 us -> 17.1 us
  transfers between devices with their start and end apart: 74 -> 74, of which waited for: 35 -> 33; matrix products, arithmetic and copies ran while one was open for 11% -> 12% of each run, Pallas kernels for 36% -> 36%
where the time goes in v5:
time: 562 us; the launch traced here: 552 us
  Pallas kernels  227 us (40%)
  waiting for transfers between devices  143 us (25%)
  starting transfers between devices  61.2 us (11%)
  local copies, waits for them, and re-layouts  56.8 us (10%)
  other arithmetic  48.9 us (9%)
  between operations  15.8 us (3%)
    pallas_call x9, Pallas kernels, run(): pl.pallas_call(whole, out_shape=[jax.ShapeDtypeStruct(shape, kind) for sh...  170 us
    ppermute x48, waiting for transfers between devices, leave(): lax.ppermute(send, *way)  101 us
    pallas_call x6, Pallas kernels, outer_group(): pl.pallas_call(kernel, out_shape=[jax.ShapeDtypeStruct(shape, HALF)] * re...  56.8 us
    ppermute x48, starting transfers between devices, leave(): lax.ppermute(send, *way)  45.9 us
    ppermute x24, waiting for transfers between devices, swap(): return lax.ppermute(values, *exchange(axis, bit))  40.2 us
    unnamed x153, local copies, waits for them, and re-layouts  17.1 us
    add x5, other arithmetic, reduce_group(): sums = [keep + other for (send, keep), other in zip(groups, others)]  15.9 us
    ppermute x24, starting transfers between devices, swap(): return lax.ppermute(values, *exchange(axis, bit))  14.8 us
  transfers between devices with their start and end apart: 74, of which 33 were waited for; matrix products, arithmetic and copies ran while one was open for 12% of the time, Pallas kernels for 36%

profile of v5, /device:TPU:0, one launch (start us, length us, event | category | flops | bytes accessed | tf_op | source)
XLA Modules:
  0.0 552.4 jit_solution(5286634683808548070)
XLA Ops:
  10.8 3.2 fusion.20
  18.1 2.9 collective-permute-start.3
  25.4 14.8 %shard_map.237 = (bf16[400,768]{1,0:T(8,128)(2,1)}, bf16[400,2304]{1,0:T(8,128)(2,1)}, f32[400,128]{1,0:T(8,128)}, bf16[400,768]{1,0:T(8,128)(2,1)}, bf16[400,76...) custom-call(s32[2]{0:T(128)} %pad_add_fusion.refs_0_.refs_18_.place_, ...), custom_call_target="tpu_custom_call" | custom-call | flops 14 | bytes 14 | tf_op jit(solution)/shard_map/pallas_call | solution.py:736
  42.2 9.5 %collective-permute-done.1.refs_5_ = bf16[112,768]{1,0:T(8,128)(2,1)S(1)} collective-permute-done((bf16[112,768]{1,0:T(8,128)(2,1)}, bf16[112,768]{1,0:T(8,128)(2,1)S(1)}, u32[]{:S(2)}, u32[]{:S(2)}) %collective-permute-start.1) | collective-permute-done | bytes 172064 | tf_op jit(solution)/shard_map/ppermute | solution.py:842
  51.7 2.4 collective-permute-done.2.refs_6_
  58.7 11.4 %shard_map.238 = (bf16[416,768]{1,0:T(8,128)(2,1)}, bf16[416,2304]{1,0:T(8,128)(2,1)}, f32[416,128]{1,0:T(8,128)}, bf16[112,768]{1,0:T(8,128)(2,1)}, bf16[112,76...) custom-call(s32[2]{0:T(128)} %pad_add_fusion.refs_0_.refs_18_.place_ref.refs_16_, s32[8]{0:T(128)} %copy-done.60, ...), custom_call_target="tpu_custom_call" | custom-call | flops 9 | bytes 9 | tf_op jit(solution)/shard_map/pallas_call | solution.py:736
  72.1 5.9 %collective-permute-done.7.refs_3_ = bf16[112,768]{1,0:T(8,128)(2,1)S(1)} collective-permute-done((bf16[112,768]{1,0:T(8,128)(2,1)}, bf16[112,768]{1,0:T(8,128)(2,1)S(1)}, u32[]{:S(2)}, u32[]{:S(2)}) %collective-permute-start.7) | collective-permute-done | bytes 172064 | tf_op jit(solution)/shard_map/ppermute | solution.py:842
  80.0 5.6 %collective-permute-done.9.refs_15_.refs_28_ = bf16[2,384,768]{2,1,0:T(8,128)(2,1)S(1)} collective-permute-done((bf16[2,384,768]{2,1,0:T(8,128)(2,1)S(1)}, bf16[2,384,768]{2,1,0:T(8,128)(2,1)S(1)}, u32[]{:S(2)}, u32[]{:S(2)}) %collective-permute-start.9) | collective-permute-done | bytes 1179680 | tf_op jit(solution)/shard_map/ppermute | solution.py:963
  91.1 25.8 %shard_map.239 = (bf16[400,768]{1,0:T(8,128)(2,1)}, f32[400,768]{1,0:T(8,128)}, bf16[400,768]{1,0:T(8,128)(2,1)}, bf16[400,3072]{1,0:T(8,128)(2,1)}, bf16[400,30...) custom-call(s32[2]{0:T(128)} %pad_add_fusion.refs_0_.refs_18_.place_, ...), custom_call_target="tpu_custom_call" | custom-call | flops 29 | bytes 29 | tf_op jit(solution)/shard_map/pallas_call | solution.py:736
  120.7 5.5 collective-permute-done.14.refs_5_
  126.2 2.9 collective-permute-done.15.refs_6_
  129.8 11.0 %shard_map.240 = (bf16[416,768]{1,0:T(8,128)(2,1)}, bf16[416,2304]{1,0:T(8,128)(2,1)}, f32[416,128]{1,0:T(8,128)}, bf16[112,768]{1,0:T(8,128)(2,1)}, bf16[112,76...) custom-call(s32[2]{0:T(128)} %pad_add_fusion.refs_0_.refs_18_.place_ref.refs_16_, s32[8]{0:T(128)} %copy-done.60, ...), custom_call_target="tpu_custom_call" | custom-call | flops 9 | bytes 9 | tf_op jit(solution)/shard_map/pallas_call | solution.py:736
  142.9 5.9 %collective-permute-done.17.refs_3_ = bf16[112,768]{1,0:T(8,128)(2,1)S(1)} collective-permute-done((bf16[112,768]{1,0:T(8,128)(2,1)}, bf16[112,768]{1,0:T(8,128)(2,1)S(1)}, u32[]{:S(2)}, u32[]{:S(2)}) %collective-permute-start.17) | collective-permute-done | bytes 172064 | tf_op jit(solution)/shard_map/ppermute | solution.py:842
  154.7 2.3 maximum_convert_fusion.3.refs_20_
  158.5 28.2 %shard_map.241 = (bf16[400,768]{1,0:T(8,128)(2,1)}, f32[400,768]{1,0:T(8,128)}, bf16[400,768]{1,0:T(8,128)(2,1)}, bf16[400,3072]{1,0:T(8,128)(2,1)}, bf16[400,30...) custom-call(s32[2]{0:T(128)} %pad_add_fusion.refs_0_.refs_18_.place_, ...), custom_call_target="tpu_custom_call" | custom-call | flops 38 | bytes 38 | tf_op jit(solution)/shard_map/pallas_call | solution.py:736
  188.7 12.2 %shard_map.242 = bf16[4,768,1536]{2,1,0:T(8,128)(2,1)} custom-call(s32[2]{0:T(128)} %pad_add_fusion.refs_0_.refs_18_.place_ref.refs_16_, bf16[400,768]{1,0:T(8,128)(2,1)} %get-tuple-element.428.refs_0_, bf16[400,768]{1,0:T(8,128)(2,1)} %get-tuple-element.429.refs_1_, bf16[400,3072]{1,0:T(8,128)(2,1)} %get-tuple-element.430.refs_2_, ...), custom_call_target="tpu_custom_call" | custom-call | flops 10 | bytes 10 | tf_op jit(solution)/shard_map/pallas_call | solution.py:819
  202.1 13.1 %shard_map.243 = (bf16[416,2304]{1,0:T(8,128)(2,1)}, bf16[112,768]{1,0:T(8,128)(2,1)}, bf16[112,768]{1,0:T(8,128)(2,1)}, bf16[112,768]{1,0:T(8,128)(2,1)}, bf16[112,768]{1,0:T(8,128)(2,1)}) custom-call(bf16[112,768]{1,0:T(8,128)(2,1)} %get-tuple-element.436.refs_0_, bf16[112,768]{1,0:T(8,128)(2,1)} %copy-done.54, bf16[112,768]{1,0:T(8,128)(2,1)} %copy-done.55, ...), custom_call_target="tpu_custom_call" | custom-call | flops 29 | bytes 29 | tf_op jit(solution)/shard_map/pallas_call | solution.py:736
  218.1 7.4 %shard_map.244 = (bf16[768,1536]{1,0:T(8,128)(2,1)}, bf16[768,1536]{1,0:T(8,128)(2,1)}) custom-call(s32[2]{0:T(128)} %pad_add_fusion.refs_0_.refs_18_.place_ref.refs_16_, bf16[416,768]{1,0:T(8,128)(2,1)} %get-tuple-element.451.refs_0_, bf16[400,768]{1,0:T(8,128)(2,1)} %get-tuple-element.452.refs_1_, bf16[416,2304]{1,0:T(8,128)(2,1)} %get-tuple-element.453.refs_2_, ...), custom_call_target="tpu_custom_call" | custom-call | flops 8 | bytes 8 | tf_op jit(solution)/shard_map/pallas_call | solution.py:819
  226.3 33.1 %shard_map.245 = (bf16[400,768]{1,0:T(8,128)(2,1)}, bf16[400,768]{1,0:T(8,128)(2,1)}, bf16[400,2304]{1,0:T(8,128)(2,1)}, f32[400,768]{1,0:T(8,128)}, f32[8,768]{...) custom-call(s32[2]{0:T(128)} %pad_add_fusion.refs_0_.refs_18_.place_, ...), custom_call_target="tpu_custom_call" | custom-call | flops 37 | bytes 37 | tf_op jit(solution)/shard_map/pallas_call | solution.py:736
  259.4 8.6 %shard_map.246 = (bf16[768,1920]{1,0:T(8,128)(2,1)}, bf16[768,1920]{1,0:T(8,128)(2,1)}) custom-call(s32[2]{0:T(128)} %pad_add_fusion.refs_0_.refs_18_.place_ref.refs_16_, bf16[400,768]{1,0:T(8,128)(2,1)} %get-tuple-element.491.refs_0_, bf16[400,768]{1,0:T(8,128)(2,1)} %get-tuple-element.492.refs_1_, bf16[400,768]{1,0:T(8,128)(2,1)} %get-tuple-element.493.refs_2_, ...), custom_call_target="tpu_custom_call" | custom-call | flops 9 | bytes 9 | tf_op jit(solution)/shard_map/pallas_call | solution.py:819
  270.8 12.4 %shard_map.247 = (bf16[2,768,1536]{2,1,0:T(8,128)(2,1)}, bf16[2,768,1536]{2,1,0:T(8,128)(2,1)}) custom-call(s32[2]{0:T(128)} %pad_add_fusion.refs_0_.refs_18_.place_ref.refs_16_, bf16[400,768]{1,0:T(8,128)(2,1)} %get-tuple-element.512.refs_0_, bf16[400,768]{1,0:T(8,128)(2,1)} %get-tuple-element.513.refs_1_, bf16[400,3072]{1,0:T(8,128)(2,1)} %get-tuple-element.514.refs_2_, ...), custom_call_target="tpu_custom_call" | custom-call | flops 10 | bytes 10 | tf_op jit(solution)/shard_map/pallas_call | solution.py:819
  283.3 2.6 collective-permute-done.30.refs_3_
  286.9 2.7 add.263
  289.7 2.7 add.262
  300.3 13.3 %shard_map.248 = (bf16[416,2304]{1,0:T(8,128)(2,1)}, bf16[112,768]{1,0:T(8,128)(2,1)}, bf16[112,768]{1,0:T(8,128)(2,1)}, bf16[112,768]{1,0:T(8,128)(2,1)}, bf16[112,768]{1,0:T(8,128)(2,1)}) custom-call(bf16[112,768]{1,0:T(8,128)(2,1)} %get-tuple-element.517.refs_0_, bf16[112,768]{1,0:T(8,128)(2,1)} %copy-done.51, bf16[112,768]{1,0:T(8,128)(2,1)} %copy-done.52, ...), custom_call_target="tpu_custom_call" | custom-call | flops 29 | bytes 29 | tf_op jit(solution)/shard_map/pallas_call | solution.py:736
  313.6 7.5 %shard_map.249 = (bf16[768,1536]{1,0:T(8,128)(2,1)}, bf16[768,1536]{1,0:T(8,128)(2,1)}) custom-call(s32[2]{0:T(128)} %pad_add_fusion.refs_0_.refs_18_.place_ref.refs_16_, bf16[416,768]{1,0:T(8,128)(2,1)} %get-tuple-element.541.refs_0_, bf16[400,768]{1,0:T(8,128)(2,1)} %get-tuple-element.542.refs_1_, bf16[416,2304]{1,0:T(8,128)(2,1)} %get-tuple-element.543.refs_2_, ...), custom_call_target="tpu_custom_call" | custom-call | flops 8 | bytes 8 | tf_op jit(solution)/shard_map/pallas_call | solution.py:819
  323.5 3.9 add.266
  331.5 7.1 %collective-permute-done.38 = bf16[2,2,2,48,1792]{4,3,1,0,2:T(8,128)(2,1)} collective-permute-done((bf16[2,2,2,48,1792]{4,3,1,0,2:T(8,128)(2,1)}, bf16[2,2,2,48,1792]{4,3,1,0,2:T(8,128)(2,1)}, u32[]{:S(2)}, u32[]{:S(2)}) %collective-permute-start.38) | collective-permute-done | bytes 1376288 | tf_op jit(solution)/shard_map/ppermute | solution.py:963
  345.0 2.5 collective-permute-start.42
  350.3 19.5 %shard_map.250 = (bf16[400,768]{1,0:T(8,128)(2,1)}, bf16[400,768]{1,0:T(8,128)(2,1)}, bf16[400,2304]{1,0:T(8,128)(2,1)}, f32[400,768]{1,0:T(8,128)}, f32[8,768]{1,0:T(8,128)}) custom-call(s32[2]{0:T(128)} %pad_add_fusion.refs_0_.refs_18_.place_ref.refs_16_, bf16[112,768]{1,0:T(8,128)(2,1)} %get-tuple-element.548.refs_1_, bf16[112,768]{1,0:T(8,128)(2,1)} %copy-done.57, ...), custom_call_target="tpu_custom_call" | custom-call | flops 14 | bytes 14 | tf_op jit(solution)/shard_map/pallas_call | solution.py:736
  369.8 8.6 %shard_map.251 = (bf16[768,1920]{1,0:T(8,128)(2,1)}, bf16[768,1920]{1,0:T(8,128)(2,1)}) custom-call(s32[2]{0:T(128)} %pad_add_fusion.refs_0_.refs_18_.place_ref.refs_16_, bf16[400,768]{1,0:T(8,128)(2,1)} %get-tuple-element.556.refs_0_, bf16[400,768]{1,0:T(8,128)(2,1)} %get-tuple-element.557.refs_1_, bf16[400,768]{1,0:T(8,128)(2,1)} %get-tuple-element.558.refs_2_, ...), custom_call_target="tpu_custom_call" | custom-call | flops 9 | bytes 9 | tf_op jit(solution)/shard_map/pallas_call | solution.py:819
  379.8 12.3 %collective-permute-done.39 = bf16[2,2,48,1664]{3,2,1,0:T(8,128)(2,1)} collective-permute-done((bf16[2,2,48,1664]{3,2,1,0:T(8,128)(2,1)}, bf16[2,2,48,1664]{3,2,1,0:T(8,128)(2,1)}, u32[]{:S(2)}, u32[]{:S(2)}) %collective-permute-start.39) | collective-permute-done | bytes 639008 | tf_op jit(solution)/shard_map/ppermute | solution.py:963
  392.2 3.0 add.277
  412.2 9.8 %collective-permute-done.45 = bf16[2,2,96,768]{3,2,1,0:T(8,128)(2,1)} collective-permute-done((bf16[2,2,96,768]{3,2,1,0:T(8,128)(2,1)}, bf16[2,2,96,768]{3,2,1,0:T(8,128)(2,1)}, u32[]{:S(2)}, u32[]{:S(2)}) %collective-permute-start.45) | collective-permute-done | bytes 589856 | tf_op jit(solution)/shard_map/ppermute | solution.py:963
  423.3 2.6 collective-permute-done.44
  425.9 3.7 add.283
  446.9 2.7 collective-permute-start.52
  450.8 11.9 %collective-permute-done.49 = bf16[2,2,2,48,896]{4,3,1,0,2:T(8,128)(2,1)} collective-permute-done((bf16[2,2,2,48,896]{4,3,1,0,2:T(8,128)(2,1)}, bf16[2,2,2,48,896]{4,3,1,0,2:T(8,128)(2,1)}, u32[]{:S(2)}, u32[]{:S(2)}) %collective-permute-start.49) | collective-permute-done | bytes 688160 | tf_op jit(solution)/shard_map/ppermute | solution.py:963
  467.9 3.2 collective-permute-done.53
  478.4 5.4 collective-permute-done.55
  483.7 2.7 collective-permute-done.56
  486.4 8.0 %collective-permute-done.54 = bf16[2,2,48,1536]{3,2,1,0:T(8,128)(2,1)S(1)} collective-permute-done((bf16[2,2,48,1536]{3,2,1,0:T(8,128)(2,1)S(1)}, bf16[2,2,48,1536]{3,2,1,0:T(8,128)(2,1)S(1)}, u32[]{:S(2)}, u32[]{:S(2)}) %collective-permute-start.54) | collective-permute-done | bytes 589856 | tf_op jit(solution)/shard_map/ppermute | solution.py:963
  501.3 3.6 collective-permute-done.60
  504.9 5.4 collective-permute-done.61
  515.3 8.5 %collective-permute-done.64 = bf16[48,1536]{1,0:T(8,128)(2,1)S(1)} collective-permute-done((bf16[48,1536]{1,0:T(8,128)(2,1)S(1)}, bf16[48,1536]{1,0:T(8,128)(2,1)S(1)}, u32[]{:S(2)}, u32[]{:S(2)}) %collective-permute-start.64) | collective-permute-done | bytes 147488 | tf_op jit(solution)/shard_map/ppermute | solution.py:963
  523.8 3.3 collective-permute-done.65
  529.7 4.4 collective-permute-done.67
  534.1 2.4 collective-permute-done.68
  (410 shorter events, 149.0 us)
Async XLA Ops:
  7.2 279.7 %reduce-scatter.3.cloned.1.call-start = ((), (), s32[]{:S(2)}) async-start(), calls=%async_computation.2 | async-start | bytes 11796480 | tf_op jit(solution)/shard_map/reduce_scatter | solution.py:1290
  17.6 36.5 %collective-permute-start.4 = (bf16[2,768,768]{2,1,0:T(8,128)(2,1)S(1)}, bf16[2,768,768]{2,1,0:T(8,128)(2,1)}, u32[]{:S(2)}, u32[]{:S(2)}) collective-permute-start(bf16[2,768,768]{2,1,0:T(8,128)(2,1)S(1)} %copy-done), channel_id=1, source_target_pairs={{0,1},{1,0},{2,3},{3,2},{4,5},{5,4},{6,7},{7,6},{8,9},{9,8},{10,11... | collective-permute-start | bytes 7077896 | tf_op jit(solution)/shard_map/ppermute | solution.py:963
  18.0 36.1 %collective-permute-start.5 = (bf16[2,768,768]{2,1,0:T(8,128)(2,1)}, bf16[2,768,768]{2,1,0:T(8,128)(2,1)}, u32[]{:S(2)}, u32[]{:S(2)}) collective-permute-start(bf16[2,768,768]{2,1,0:T(8,128)(2,1)} %refs_24_.5), channel_id=1, source_target_pairs={{0,1},{1,0},{2,3},{3,2},{4,5},{5,4},{6,7},{7,6},{8,9},{9,8},{10,11... | collective-permute-start | bytes 7077896 | tf_op jit(solution)/shard_map/ppermute | solution.py:963
  18.1 36.0 %collective-permute-start.3 = (bf16[2,384,768]{2,1,0:T(8,128)(2,1)}, bf16[2,384,768]{2,1,0:T(8,128)(2,1)S(1)}, u32[]{:S(2)}, u32[]{:S(2)}) collective-permute-start(bf16[2,384,768]{2,1,0:T(8,128)(2,1)} %pad_maximum_fusion.1), channel_id=1, source_target_pairs={{0,2},{1,3},{2,0},{3,1},{4,6},{5,7},{6,4},{7,5},{8,10},{9,11},{10,... | collective-permute-start | bytes 3538952 | tf_op jit(solution)/shard_map/ppermute | solution.py:963
  40.3 11.4 %collective-permute-start.1 = (bf16[112,768]{1,0:T(8,128)(2,1)}, bf16[112,768]{1,0:T(8,128)(2,1)S(1)}, u32[]{:S(2)}, u32[]{:S(2)}) collective-permute-start(bf16[112,768]{1,0:T(8,128)(2,1)} %get-tuple-element.340), channel_id=1, source_target_pairs={{0,2},{1,3},{2,0},{3,1},{4,6},{5,7},{6,4},{7,5},{8,10},{9,11},{10,... | collective-permute-start | bytes 516104 | tf_op jit(solution)/shard_map/ppermute | solution.py:842
  41.9 12.2 %collective-permute-start.2 = (bf16[112,768]{1,0:T(8,128)(2,1)}, bf16[112,768]{1,0:T(8,128)(2,1)S(1)}, u32[]{:S(2)}, u32[]{:S(2)}) collective-permute-start(bf16[112,768]{1,0:T(8,128)(2,1)} %get-tuple-element.341), channel_id=1, source_target_pairs={{0,3},{1,2},{2,1},{3,0},{4,7},{5,6},{6,5},{7,4},{8,11},{9,10},{10,... | collective-permute-start | bytes 516104 | tf_op jit(solution)/shard_map/ppermute | solution.py:842
  57.1 28.4 %collective-permute-start.9 = (bf16[2,384,768]{2,1,0:T(8,128)(2,1)S(1)}, bf16[2,384,768]{2,1,0:T(8,128)(2,1)S(1)}, u32[]{:S(2)}, u32[]{:S(2)}) collective-permute-start(bf16[2,384,768]{2,1,0:T(8,128)(2,1)S(1)} %collective-permute-done.3.refs_14_.refs_27_), channel_id=1, source_target_pairs={{0,4},{4,0},{8,12},{12,8},{16,20},{20,16},{24,28},{28,24},{1,5},{5... | collective-permute-start | bytes 3538952 | tf_op jit(solution)/shard_map/ppermute | solution.py:963
  86.1 30.9 %collective-permute-start.12 = (bf16[2,384,768]{2,1,0:T(8,128)(2,1)S(1)}, bf16[2,384,768]{2,1,0:T(8,128)(2,1)}, u32[]{:S(2)}, u32[]{:S(2)}) collective-permute-start(bf16[2,384,768]{2,1,0:T(8,128)(2,1)S(1)} %pad_maximum_fusion.2), channel_id=1, source_target_pairs={{0,2},{1,3},{2,0},{3,1},{4,6},{5,7},{6,4},{7,5},{8,10},{9,11},{10,... | collective-permute-start | bytes 3538952 | tf_op jit(solution)/shard_map/ppermute | solution.py:963
  117.0 33.8 %collective-permute-start.19 = (bf16[2,384,768]{2,1,0:T(8,128)(2,1)}, bf16[2,384,768]{2,1,0:T(8,128)(2,1)S(1)}, u32[]{:S(2)}, u32[]{:S(2)}) collective-permute-start(bf16[2,384,768]{2,1,0:T(8,128)(2,1)} %collective-permute-done.12.refs_14_.refs_28_), channel_id=1, source_target_pairs={{0,4},{4,0},{8,12},{12,8},{16,20},{20,16},{24,28},{28,24},{1,5},{5... | collective-permute-start | bytes 3538952 | tf_op jit(solution)/shard_map/ppermute | solution.py:963
  186.7 14.2 %collective-permute-start.22 = (bf16[112,768]{1,0:T(8,128)(2,1)}, bf16[112,768]{1,0:T(8,128)(2,1)S(1)}, u32[]{:S(2)}, u32[]{:S(2)}) collective-permute-start(bf16[112,768]{1,0:T(8,128)(2,1)} %get-tuple-element.425), channel_id=1, source_target_pairs={{0,1},{1,0},{2,3},{3,2},{4,5},{5,4},{6,7},{7,6},{8,9},{9,8},{10,11... | collective-permute-start | bytes 516104 | tf_op jit(solution)/shard_map/ppermute | solution.py:842
  187.2 13.7 %collective-permute-start.23 = (bf16[112,768]{1,0:T(8,128)(2,1)}, bf16[112,768]{1,0:T(8,128)(2,1)S(1)}, u32[]{:S(2)}, u32[]{:S(2)}) collective-permute-start(bf16[112,768]{1,0:T(8,128)(2,1)} %get-tuple-element.426), channel_id=1, source_target_pairs={{0,2},{1,3},{2,0},{3,1},{4,6},{5,7},{6,4},{7,5},{8,10},{9,11},{10,... | collective-permute-start | bytes 516104 | tf_op jit(solution)/shard_map/ppermute | solution.py:842
  188.7 12.2 %collective-permute-start.24 = (bf16[112,768]{1,0:T(8,128)(2,1)}, bf16[112,768]{1,0:T(8,128)(2,1)S(1)}, u32[]{:S(2)}, u32[]{:S(2)}) collective-permute-start(bf16[112,768]{1,0:T(8,128)(2,1)} %get-tuple-element.427), channel_id=1, source_target_pairs={{0,3},{1,2},{2,1},{3,0},{4,7},{5,6},{6,5},{7,4},{8,11},{9,10},{10,... | collective-permute-start | bytes 516104 | tf_op jit(solution)/shard_map/ppermute | solution.py:842
  201.7 178.1 %reduce-scatter.5.cloned.1.call-start = ((), (), s32[]{:S(2)}) async-start(), calls=%async_computation.3 | async-start | bytes 2654208 | tf_op jit(solution)/shard_map/reduce_scatter | solution.py:1284
  215.2 10.3 %collective-permute-start.25 = (bf16[112,768]{1,0:T(8,128)(2,1)}, bf16[112,768]{1,0:T(8,128)(2,1)S(1)}, u32[]{:S(2)}, u32[]{:S(2)}) collective-permute-start(bf16[112,768]{1,0:T(8,128)(2,1)} %get-tuple-element.444), channel_id=1, source_target_pairs={{0,1},{1,0},{2,3},{3,2},{4,5},{5,4},{6,7},{7,6},{8,9},{9,8},{10,11... | collective-permute-start | bytes 516104 | tf_op jit(solution)/shard_map/ppermute | solution.py:842
  268.1 18.8 %collective-permute-start.32 = (bf16[768,1920]{1,0:T(8,128)(2,1)}, bf16[768,1920]{1,0:T(8,128)(2,1)}, u32[]{:S(2)}, u32[]{:S(2)}) collective-permute-start(bf16[768,1920]{1,0:T(8,128)(2,1)} %get-tuple-element.499), channel_id=1, source_target_pairs={{0,1},{1,0},{2,3},{3,2},{4,5},{5,4},{6,7},{7,6},{8,9},{9,8},{10,11... | collective-permute-start | bytes 8847368 | tf_op jit(solution)/shard_map/ppermute | solution.py:963
  268.8 18.1 %collective-permute-start.31 = (bf16[768,1536]{1,0:T(8,128)(2,1)}, bf16[768,1536]{1,0:T(8,128)(2,1)}, u32[]{:S(2)}, u32[]{:S(2)}) collective-permute-start(bf16[768,1536]{1,0:T(8,128)(2,1)} %get-tuple-element.498), channel_id=1, source_target_pairs={{0,1},{1,0},{2,3},{3,2},{4,5},{5,4},{6,7},{7,6},{8,9},{9,8},{10,11... | collective-permute-start | bytes 7077896 | tf_op jit(solution)/shard_map/ppermute | solution.py:963
  268.8 14.4 %collective-permute-start.28 = (bf16[112,768]{1,0:T(8,128)(2,1)}, bf16[112,768]{1,0:T(8,128)(2,1)S(1)}, u32[]{:S(2)}, u32[]{:S(2)}) collective-permute-start(bf16[112,768]{1,0:T(8,128)(2,1)} %get-tuple-element.468), channel_id=1, source_target_pairs={{0,1},{1,0},{2,3},{3,2},{4,5},{5,4},{6,7},{7,6},{8,9},{9,8},{10,11... | collective-permute-start | bytes 516104 | tf_op jit(solution)/shard_map/ppermute | solution.py:842
  269.3 14.0 %collective-permute-start.29 = (bf16[112,768]{1,0:T(8,128)(2,1)}, bf16[112,768]{1,0:T(8,128)(2,1)S(1)}, u32[]{:S(2)}, u32[]{:S(2)}) collective-permute-start(bf16[112,768]{1,0:T(8,128)(2,1)} %get-tuple-element.469), channel_id=1, source_target_pairs={{0,2},{1,3},{2,0},{3,1},{4,6},{5,7},{6,4},{7,5},{8,10},{9,11},{10,... | collective-permute-start | bytes 516104 | tf_op jit(solution)/shard_map/ppermute | solution.py:842
  270.8 15.1 %collective-permute-start.30 = (bf16[112,768]{1,0:T(8,128)(2,1)}, bf16[112,768]{1,0:T(8,128)(2,1)S(1)}, u32[]{:S(2)}, u32[]{:S(2)}) collective-permute-start(bf16[112,768]{1,0:T(8,128)(2,1)} %get-tuple-element.470), channel_id=1, source_target_pairs={{0,3},{1,2},{2,1},{3,0},{4,7},{5,6},{6,5},{7,4},{8,11},{9,10},{10,... | collective-permute-start | bytes 516104 | tf_op jit(solution)/shard_map/ppermute | solution.py:842
  298.0 23.1 %collective-permute-start.33 = (bf16[2,768,1536]{2,1,0:T(8,128)(2,1)}, bf16[2,768,1536]{2,1,0:T(8,128)(2,1)}, u32[]{:S(2)}, u32[]{:S(2)}) collective-permute-start(bf16[2,768,1536]{2,1,0:T(8,128)(2,1)} %get-tuple-element.528), channel_id=1, source_target_pairs={{0,1},{1,0},{2,3},{3,2},{4,5},{5,4},{6,7},{7,6},{8,9},{9,8},{10,11... | collective-permute-start | bytes 14155784 | tf_op jit(solution)/shard_map/ppermute | solution.py:963
  298.0 40.6 %collective-permute-start.38 = (bf16[2,2,2,48,1792]{4,3,1,0,2:T(8,128)(2,1)}, bf16[2,2,2,48,1792]{4,3,1,0,2:T(8,128)(2,1)}, u32[]{:S(2)}, u32[]{:S(2)}) collective-permute-start(bf16[2,2,2,48,1792]{4,3,1,0,2:T(8,128)(2,1)} %bitcast.166), channel_id=1, source_target_pairs={{0,4},{4,0},{8,12},{12,8},{16,20},{20,16},{24,28},{28,24},{1,5},{5... | collective-permute-start | bytes 4128776 | tf_op jit(solution)/shard_map/ppermute | solution.py:963
  300.3 31.2 %collective-permute-start.37 = (bf16[2,2,2,48,1664]{4,3,1,0,2:T(8,128)(2,1)}, bf16[2,2,2,48,1664]{4,3,1,0,2:T(8,128)(2,1)}, u32[]{:S(2)}, u32[]{:S(2)}) collective-permute-start(bf16[2,2,2,48,1664]{4,3,1,0,2:T(8,128)(2,1)} %bitcast.167), channel_id=1, source_target_pairs={{0,2},{1,3},{2,0},{3,1},{4,6},{5,7},{6,4},{7,5},{8,10},{9,11},{10,... | collective-permute-start | bytes 3833864 | tf_op jit(solution)/shard_map/ppermute | solution.py:963
  321.2 17.5 %collective-permute-start.34 = (bf16[112,768]{1,0:T(8,128)(2,1)S(1)}, bf16[112,768]{1,0:T(8,128)(2,1)S(1)}, u32[]{:S(2)}, u32[]{:S(2)}) collective-permute-start(bf16[112,768]{1,0:T(8,128)(2,1)S(1)} %copy-done.70), channel_id=1, source_target_pairs={{0,1},{1,0},{2,3},{3,2},{4,5},{5,4},{6,7},{7,6},{8,9},{9,8},{10,11... | collective-permute-start | bytes 516104 | tf_op jit(solution)/shard_map/ppermute | solution.py:842
  321.5 17.2 %collective-permute-start.35 = (bf16[112,768]{1,0:T(8,128)(2,1)S(1)}, bf16[112,768]{1,0:T(8,128)(2,1)S(1)}, u32[]{:S(2)}, u32[]{:S(2)}) collective-permute-start(bf16[112,768]{1,0:T(8,128)(2,1)S(1)} %copy-done.69), channel_id=1, source_target_pairs={{0,2},{1,3},{2,0},{3,1},{4,6},{5,7},{6,4},{7,5},{8,10},{9,11},{10,... | collective-permute-start | bytes 516104 | tf_op jit(solution)/shard_map/ppermute | solution.py:842
  323.4 15.3 %collective-permute-start.36 = (bf16[112,768]{1,0:T(8,128)(2,1)S(1)}, bf16[112,768]{1,0:T(8,128)(2,1)S(1)}, u32[]{:S(2)}, u32[]{:S(2)}) collective-permute-start(bf16[112,768]{1,0:T(8,128)(2,1)S(1)} %copy-done.68), channel_id=1, source_target_pairs={{0,3},{1,2},{2,1},{3,0},{4,7},{5,6},{6,5},{7,4},{8,11},{9,10},{10,... | collective-permute-start | bytes 516104 | tf_op jit(solution)/shard_map/ppermute | solution.py:842
  344.9 47.2 %collective-permute-start.43 = (bf16[768,1536]{1,0:T(8,128)(2,1)}, bf16[768,1536]{1,0:T(8,128)(2,1)}, u32[]{:S(2)}, u32[]{:S(2)}) collective-permute-start(bf16[768,1536]{1,0:T(8,128)(2,1)} %get-tuple-element.570), channel_id=1, source_target_pairs={{0,1},{1,0},{2,3},{3,2},{4,5},{5,4},{6,7},{7,6},{8,9},{9,8},{10,11... | collective-permute-start | bytes 7077896 | tf_op jit(solution)/shard_map/ppermute | solution.py:963
  345.0 47.2 %collective-permute-start.41 = (bf16[2,2,2,96,768]{4,3,2,1,0:T(8,128)(2,1)}, bf16[2,2,2,96,768]{4,3,2,1,0:T(8,128)(2,1)S(1)}, u32[]{:S(2)}, u32[]{:S(2)}) collective-permute-start(bf16[2,2,2,96,768]{4,3,2,1,0:T(8,128)(2,1)} %slice_bitcast_fusion.1), channel_id=1, source_target_pairs={{0,2},{1,3},{2,0},{3,1},{4,6},{5,7},{6,4},{7,5},{8,10},{9,11},{10,... | collective-permute-start | bytes 3538952 | tf_op jit(solution)/shard_map/ppermute | solution.py:963
  345.0 47.2 %collective-permute-start.42 = (bf16[2,2,2,96,768]{4,3,2,1,0:T(8,128)(2,1)}, bf16[2,2,2,96,768]{4,3,2,1,0:T(8,128)(2,1)}, u32[]{:S(2)}, u32[]{:S(2)}) collective-permute-start(bf16[2,2,2,96,768]{4,3,2,1,0:T(8,128)(2,1)} %dynamic-slice_bitcast_fusion), channel_id=1, source_target_pairs={{0,4},{4,0},{8,12},{12,8},{16,20},{20,16},{24,28},{28,24},{1,5},{5... | collective-permute-start | bytes 3538952 | tf_op jit(solution)/shard_map/ppermute | solution.py:963
  347.5 44.7 %collective-permute-start.40 = (bf16[2,2,48,1792]{3,2,1,0:T(8,128)(2,1)}, bf16[2,2,48,1792]{3,2,1,0:T(8,128)(2,1)}, u32[]{:S(2)}, u32[]{:S(2)}) collective-permute-start(bf16[2,2,48,1792]{3,2,1,0:T(8,128)(2,1)} %dynamic-slice_bitcast_fusion.1), channel_id=1, source_target_pairs={{0,2},{1,3},{2,0},{3,1},{4,6},{5,7},{6,4},{7,5},{8,10},{9,11},{10,... | collective-permute-start | bytes 2064392 | tf_op jit(solution)/shard_map/ppermute | solution.py:963
  349.5 42.6 %collective-permute-start.39 = (bf16[2,2,48,1664]{3,2,1,0:T(8,128)(2,1)}, bf16[2,2,48,1664]{3,2,1,0:T(8,128)(2,1)}, u32[]{:S(2)}, u32[]{:S(2)}) collective-permute-start(bf16[2,2,48,1664]{3,2,1,0:T(8,128)(2,1)} %dynamic-slice_bitcast_fusion.2), channel_id=1, source_target_pairs={{0,4},{4,0},{8,12},{12,8},{16,20},{20,16},{24,28},{28,24},{1,5},{5... | collective-permute-start | bytes 1916936 | tf_op jit(solution)/shard_map/ppermute | solution.py:963
  392.1 31.2 %collective-permute-start.47 = (bf16[768,1920]{1,0:T(8,128)(2,1)}, bf16[768,1920]{1,0:T(8,128)(2,1)}, u32[]{:S(2)}, u32[]{:S(2)}) collective-permute-start(bf16[768,1920]{1,0:T(8,128)(2,1)} %get-tuple-element.582), channel_id=1, source_target_pairs={{0,1},{1,0},{2,3},{3,2},{4,5},{5,4},{6,7},{7,6},{8,9},{9,8},{10,11... | collective-permute-start | bytes 8847368 | tf_op jit(solution)/shard_map/ppermute | solution.py:963
  406.0 16.0 %collective-permute-start.45 = (bf16[2,2,96,768]{3,2,1,0:T(8,128)(2,1)}, bf16[2,2,96,768]{3,2,1,0:T(8,128)(2,1)}, u32[]{:S(2)}, u32[]{:S(2)}) collective-permute-start(bf16[2,2,96,768]{3,2,1,0:T(8,128)(2,1)} %dynamic-slice_bitcast_fusion.4), channel_id=1, source_target_pairs={{0,4},{4,0},{8,12},{12,8},{16,20},{20,16},{24,28},{28,24},{1,5},{5... | collective-permute-start | bytes 1769480 | tf_op jit(solution)/shard_map/ppermute | solution.py:963
  406.9 16.4 %collective-permute-start.46 = (bf16[2,2,96,768]{3,2,1,0:T(8,128)(2,1)}, bf16[2,2,96,768]{3,2,1,0:T(8,128)(2,1)S(1)}, u32[]{:S(2)}, u32[]{:S(2)}) collective-permute-start(bf16[2,2,96,768]{3,2,1,0:T(8,128)(2,1)} %slice_bitcast_fusion.3), channel_id=1, source_target_pairs={{0,2},{1,3},{2,0},{3,1},{4,6},{5,7},{6,4},{7,5},{8,10},{9,11},{10,... | collective-permute-start | bytes 1769480 | tf_op jit(solution)/shard_map/ppermute | solution.py:963
  408.7 17.3 %collective-permute-start.44 = (bf16[2,48,3456]{2,1,0:T(8,128)(2,1)S(1)}, bf16[2,48,3456]{2,1,0:T(8,128)(2,1)S(1)}, u32[]{:S(2)}, u32[]{:S(2)}) collective-permute-start(bf16[2,48,3456]{2,1,0:T(8,128)(2,1)S(1)} %fusion.5), channel_id=1, source_target_pairs={{0,8},{4,12},{8,0},{12,4},{16,24},{20,28},{24,16},{28,20},{1,9},{5... | collective-permute-start | bytes 1990664 | tf_op jit(solution)/shard_map/ppermute | solution.py:963
  411.9 38.9 %collective-permute-start.48 = (bf16[2,2,2,48,1536]{4,3,1,0,2:T(8,128)(2,1)}, bf16[2,2,2,48,1536]{4,3,1,0,2:T(8,128)(2,1)}, u32[]{:S(2)}, u32[]{:S(2)}) collective-permute-start(bf16[2,2,2,48,1536]{4,3,1,0,2:T(8,128)(2,1)} %bitcast.168), channel_id=1, source_target_pairs={{0,2},{1,3},{2,0},{3,1},{4,6},{5,7},{6,4},{7,5},{8,10},{9,11},{10,... | collective-permute-start | bytes 3538952 | tf_op jit(solution)/shard_map/ppermute | solution.py:963
  438.6 24.1 %collective-permute-start.50 = (bf16[2,2,2,48,1024]{4,3,1,0,2:T(8,128)(2,1)}, bf16[2,2,2,48,1024]{4,3,1,0,2:T(8,128)(2,1)}, u32[]{:S(2)}, u32[]{:S(2)}) collective-permute-start(bf16[2,2,2,48,1024]{4,3,1,0,2:T(8,128)(2,1)} %bitcast.169), channel_id=1, source_target_pairs={{0,4},{4,0},{8,12},{12,8},{16,20},{20,16},{24,28},{28,24},{1,5},{5... | collective-permute-start | bytes 2359304 | tf_op jit(solution)/shard_map/ppermute | solution.py:963
  439.0 23.8 %collective-permute-start.49 = (bf16[2,2,2,48,896]{4,3,1,0,2:T(8,128)(2,1)}, bf16[2,2,2,48,896]{4,3,1,0,2:T(8,128)(2,1)}, u32[]{:S(2)}, u32[]{:S(2)}) collective-permute-start(bf16[2,2,2,48,896]{4,3,1,0,2:T(8,128)(2,1)} %bitcast.170), channel_id=1, source_target_pairs={{0,2},{1,3},{2,0},{3,1},{4,6},{5,7},{6,4},{7,5},{8,10},{9,11},{10,... | collective-permute-start | bytes 2064392 | tf_op jit(solution)/shard_map/ppermute | solution.py:963
  446.9 21.0 %collective-permute-start.52 = (bf16[48,3456]{1,0:T(8,128)(2,1)S(1)}, bf16[48,3456]{1,0:T(8,128)(2,1)S(1)}, u32[]{:S(2)}, u32[]{:S(2)}) collective-permute-start(bf16[48,3456]{1,0:T(8,128)(2,1)S(1)} %copy-done.35), channel_id=1, source_target_pairs={{0,16},{4,20},{8,24},{12,28},{16,0},{20,4},{24,8},{28,12},{1,17},{... | collective-permute-start | bytes 995336 | tf_op jit(solution)/shard_map/ppermute | solution.py:963
  449.6 21.5 %collective-permute-start.53 = (bf16[2,96,1536]{2,1,0:T(8,128)(2,1)S(1)}, bf16[2,96,1536]{2,1,0:T(8,128)(2,1)S(1)}, u32[]{:S(2)}, u32[]{:S(2)}) collective-permute-start(bf16[2,96,1536]{2,1,0:T(8,128)(2,1)S(1)} %copy-done.34), channel_id=1, source_target_pairs={{0,8},{4,12},{8,0},{12,4},{16,24},{20,28},{24,16},{28,20},{1,9},{5... | collective-permute-start | bytes 1769480 | tf_op jit(solution)/shard_map/ppermute | solution.py:963
  472.7 11.0 %collective-permute-start.55 = (bf16[2,2,48,896]{3,2,1,0:T(8,128)(2,1)S(1)}, bf16[2,2,48,896]{3,2,1,0:T(8,128)(2,1)S(1)}, u32[]{:S(2)}, u32[]{:S(2)}) collective-permute-start(bf16[2,2,48,896]{3,2,1,0:T(8,128)(2,1)S(1)} %dynamic-slice_bitcast_fusion.6), channel_id=1, source_target_pairs={{0,4},{4,0},{8,12},{12,8},{16,20},{20,16},{24,28},{28,24},{1,5},{5... | collective-permute-start | bytes 1032200 | tf_op jit(solution)/shard_map/ppermute | solution.py:963
  474.4 12.1 %collective-permute-start.56 = (bf16[2,2,48,1024]{3,2,1,0:T(8,128)(2,1)S(1)}, bf16[2,2,48,1024]{3,2,1,0:T(8,128)(2,1)S(1)}, u32[]{:S(2)}, u32[]{:S(2)}) collective-permute-start(bf16[2,2,48,1024]{3,2,1,0:T(8,128)(2,1)S(1)} %dynamic-slice_bitcast_fusion.5), channel_id=1, source_target_pairs={{0,2},{1,3},{2,0},{3,1},{4,6},{5,7},{6,4},{7,5},{8,10},{9,11},{10,... | collective-permute-start | bytes 1179656 | tf_op jit(solution)/shard_map/ppermute | solution.py:963
  474.7 19.8 %collective-permute-start.54 = (bf16[2,2,48,1536]{3,2,1,0:T(8,128)(2,1)S(1)}, bf16[2,2,48,1536]{3,2,1,0:T(8,128)(2,1)S(1)}, u32[]{:S(2)}, u32[]{:S(2)}) collective-permute-start(bf16[2,2,48,1536]{3,2,1,0:T(8,128)(2,1)S(1)} %dynamic-slice_bitcast_fusion.3), channel_id=1, source_target_pairs={{0,4},{4,0},{8,12},{12,8},{16,20},{20,16},{24,28},{28,24},{1,5},{5... | collective-permute-start | bytes 1769480 | tf_op jit(solution)/shard_map/ppermute | solution.py:963
  475.4 19.4 %collective-permute-start.59 = (bf16[96,1536]{1,0:T(8,128)(2,1)S(1)}, bf16[96,1536]{1,0:T(8,128)(2,1)S(1)}, u32[]{:S(2)}, u32[]{:S(2)}) collective-permute-start(bf16[96,1536]{1,0:T(8,128)(2,1)S(1)} %dynamic-slice_bitcast_fusion.9), channel_id=1, source_target_pairs={{0,16},{4,20},{8,24},{12,28},{16,0},{20,4},{24,8},{28,12},{1,17},{... | collective-permute-start | bytes 884744 | tf_op jit(solution)/shard_map/ppermute | solution.py:963
  476.7 18.1 %collective-permute-start.58 = (bf16[48,3456]{1,0:T(8,128)(2,1)S(1)}, bf16[48,3456]{1,0:T(8,128)(2,1)S(1)}, u32[]{:S(2)}, u32[]{:S(2)}) collective-permute-start(bf16[48,3456]{1,0:T(8,128)(2,1)S(1)} %bitcast_add_fusion.12), channel_id=1, source_target_pairs={{0,2},{1,3},{2,0},{3,1},{4,6},{5,7},{6,4},{7,5},{8,10},{9,11},{10,... | collective-permute-start | bytes 995336 | tf_op jit(solution)/shard_map/ppermute | solution.py:963
  496.7 13.6 %collective-permute-start.61 = (bf16[2,48,1920]{2,1,0:T(8,128)(2,1)S(1)}, bf16[2,48,1920]{2,1,0:T(8,128)(2,1)S(1)}, u32[]{:S(2)}, u32[]{:S(2)}) collective-permute-start(bf16[2,48,1920]{2,1,0:T(8,128)(2,1)S(1)} %fusion.16), channel_id=1, source_target_pairs={{0,8},{4,12},{8,0},{12,4},{16,24},{20,28},{24,16},{28,20},{1,9},{5... | collective-permute-start | bytes 1105928 | tf_op jit(solution)/shard_map/ppermute | solution.py:963
  498.9 16.3 %collective-permute-start.63 = (bf16[96,3456]{1,0:T(8,128)(2,1)S(1)}, bf16[96,3456]{1,0:T(8,128)(2,1)S(1)}, u32[]{:S(2)}, u32[]{:S(2)}) collective-permute-start(bf16[96,3456]{1,0:T(8,128)(2,1)S(1)} %maximum_select_fusion), channel_id=1, source_target_pairs={{0,1},{1,0},{2,3},{3,2},{4,5},{5,4},{6,7},{7,6},{8,9},{9,8},{10,11... | collective-permute-start | bytes 1990664 | tf_op jit(solution)/shard_map/ppermute | solution.py:963
  512.3 11.5 %collective-permute-start.64 = (bf16[48,1536]{1,0:T(8,128)(2,1)S(1)}, bf16[48,1536]{1,0:T(8,128)(2,1)S(1)}, u32[]{:S(2)}, u32[]{:S(2)}) collective-permute-start(bf16[48,1536]{1,0:T(8,128)(2,1)S(1)} %dynamic-slice_bitcast_fusion.11), channel_id=1, source_target_pairs={{0,16},{4,20},{8,24},{12,28},{16,0},{20,4},{24,8},{28,12},{1,17},{... | collective-permute-start | bytes 442376 | tf_op jit(solution)/shard_map/ppermute | solution.py:963
  513.5 13.7 %collective-permute-start.65 = (bf16[48,1920]{1,0:T(8,128)(2,1)S(1)}, bf16[48,1920]{1,0:T(8,128)(2,1)S(1)}, u32[]{:S(2)}, u32[]{:S(2)}) collective-permute-start(bf16[48,1920]{1,0:T(8,128)(2,1)S(1)} %dynamic-slice_bitcast_fusion.10), channel_id=1, source_target_pairs={{0,16},{4,20},{8,24},{12,28},{16,0},{20,4},{24,8},{28,12},{1,17},{... | collective-permute-start | bytes 552968 | tf_op jit(solution)/shard_map/ppermute | solution.py:963
  (100 other events, 564.2 us)
Sparse Core Ops, SparseCore 0:
  201.1 85.7 reduce-scatter.2
  300.4 76.8 reduce-scatter.4
